TPU v7x, 32 devices: a whole 2x2x4 slice. The times are simulated.
32 devices in a mesh: fsdp: 8 (over z, x), seq: 4 (over y, core).
Axes of the slice: x: 2, y: 2, z: 4, core: 2. Of those that a mesh axis runs over, the one named last changes fastest.
Arguments:
- hidden: bfloat16 [2, 8, 512, 576], P(None, 'fsdp', 'seq'), may hold values from -6 to 6
- w_qkv: bfloat16 [576, 960], P('fsdp'), may hold values from -0.25 to 0.25
- b_qkv: bfloat16 [960], P('fsdp'), may hold values from -3 to 3
- w_out: bfloat16 [576, 576], P('fsdp'), may hold values from -1 to 1
- w_gate_up: bfloat16 [576, 3072], P('fsdp'), may hold values from -0.25 to 0.25
- w_down: bfloat16 [1536, 576], P('fsdp'), may hold values from -0.15625 to 0.15625
- norm_gains: bfloat16 [2, 576], P(None, 'fsdp'), may hold values from 0.5 to 1.5
- segment_ids: int32 [2, 8, 512], P(None, 'fsdp', 'seq'), may hold values from 0 to 3, as said below
- token_counts: int32 [2], replicated, may hold values from 2048 to 4096
- cotangent: bfloat16 [2, 8, 512, 576], P(None, 'fsdp', 'seq'), may hold values from -6 to 6
Outputs:
- block_out: bfloat16 [2, 8, 512, 576], P(None, 'fsdp', 'seq')
- hidden_grad: float32 [2, 8, 512, 576], P(None, 'fsdp', 'seq')
- w_qkv_grad: float32 [576, 960], P('fsdp')
- b_qk_grad: float32 [768], P('fsdp')
- b_v_grad: float32 [192], P('fsdp')
- w_out_grad: float32 [576, 576], P('fsdp')
- w_gate_up_grad: float32 [576, 3072], P('fsdp')
- w_down_grad: float32 [1536, 576], P('fsdp')
- norm_gains_grad: float32 [2, 576], P(None, 'fsdp')
Inputs may be any that keep to these rules, and one draw needn't show every extreme that they name: `segment_ids`: in each sequence the ids start at 0 and never fall; equal ids mark one document of 200 to 2000 tokens, which the sequence's ends may cut.
All inputs are finite; a program needn't handle non-finite values.
Results may differ from a plain program's by a relative error of at most 0.017.
Values may be sent and summed in bfloat16 or wider, within the bound.
No kernel may reach another device: no remote copies, remote signals or barrier semaphores. Data moves between devices by JAX's collectives and lax.ppermute only.
A program may use at most 128 MiB of HBM per device.

v0:
```python
import functools

import jax
import jax.numpy as jnp
import numpy as np
from jax import lax
from jax.experimental import pallas as pl
from jax.experimental.pallas import tpu as pltpu
from jax.sharding import PartitionSpec as P

HEADS = 9
KV_HEADS = 3
HEAD_DIM = 64
GROUP = HEADS // KV_HEADS
QW = HEADS * HEAD_DIM
KW = KV_HEADS * HEAD_DIM
EPS = 1e-05
ROPE_BASE = 100000.0
MASKED = -1000000000.0
BF = jnp.bfloat16
F32 = jnp.float32


def dot(a, b, ca, cb):
    return lax.dot_general(a, b, (((ca,), (cb,)), ((), ())), preferred_element_type=F32)


def rotary(values, cosine, sine):
    half = values.shape[-1] // 2
    a, b = values[..., :half], values[..., half:]
    return jnp.concatenate([a * cosine - b * sine, b * cosine + a * sine], axis=-1)


def norm_parts(values):
    factor = lax.rsqrt(jnp.mean(values * values, axis=-1, keepdims=True) + EPS)
    return factor, values * factor


def norm_back(grad_in, gain, factor, normed):
    scaled = grad_in * gain
    return factor * (scaled - normed * jnp.mean(scaled * normed, axis=-1, keepdims=True))


def whole(*shape_dtypes):
    return [pl.BlockSpec(memory_space=pltpu.VMEM) for _ in shape_dtypes]


def call(kernel, scalars, arrays, outs, flops, scratch=()):
    specs = [pl.BlockSpec(memory_space=pltpu.SMEM)] * len(scalars) + whole(*arrays)
    moved = sum(a.size * a.dtype.itemsize for a in arrays) + sum(
        int(np.prod(o.shape)) * o.dtype.itemsize for o in outs
    )
    return pl.pallas_call(
        kernel,
        out_shape=outs,
        in_specs=specs,
        out_specs=whole(*outs),
        scratch_shapes=[pltpu.VMEM(shape, F32) for shape in scratch],
        compiler_params=pltpu.CompilerParams(vmem_limit_bytes=52 * 1024 * 1024),
        cost_estimate=pl.CostEstimate(flops=flops, bytes_accessed=moved, transcendentals=0),
    )(*scalars, *arrays)


def sds(shape, dtype):
    return jax.ShapeDtypeStruct(shape, dtype)


def turn(x, cosine, sine):
    tiles = []
    low = lax.broadcasted_iota(jnp.int32, (1, 128), 1) % HEAD_DIM < HEAD_DIM // 2
    for t in range(x.shape[1] // 128):
        part = x[:, 128 * t : 128 * t + 128]
        other = jnp.where(low, pltpu.roll(part, 96, 1), pltpu.roll(part, 32, 1))
        tiles.append(part * cosine + other * sine)
    return tiles


def turn_kv(x, cosine, sine):
    lane = lax.broadcasted_iota(jnp.int32, (1, 128), 1)
    first, second = turn(x[:, :256], cosine, sine)
    second = jnp.where(lane < KW - 128, second, x[:, 128:256])
    return jnp.concatenate([first, second, x[:, 256:]], axis=1)


def tables(seq, order, cos_ref, sin_ref):
    cosine = jnp.concatenate([cos_ref[seq ^ o] for o in order], axis=0)
    sine = jnp.concatenate([sin_ref[seq ^ o] for o in order], axis=0)
    return cosine, sine


def heads_to_rows(x, g):
    return jnp.concatenate(
        [x[:, HEAD_DIM * h : HEAD_DIM * (h + 1)] for h in range(GROUP * g, GROUP * (g + 1))], axis=0
    )


def rows_to_heads(parts, length):
    return jnp.concatenate(
        [p[length * r : length * (r + 1)] for p in parts for r in range(GROUP)], axis=1
    )


def attention_forward(order, length, seq_ref, blocks, wq, wkv, bq, bkv, gain, cos, sin, mask,
                      att_o, q_o, k_o, v_o, lse_o):
    seq = seq_ref[0]
    cosine, sine = tables(seq, order, cos, sin)
    width = gain.shape[1]
    for b in range(blocks.shape[1] // length):
        x = blocks[:, b * length : (b + 1) * length, :width].astype(F32)
        x = x.reshape(len(order) * length, width)
        first = (norm_parts(x)[1] * gain[...]).astype(BF)
        kv = dot(first, wkv[...], 1, 0) + bkv[...]
        q = dot(first[:length], wq[...], 1, 0) + bq[...]
        q = jnp.concatenate(turn(q, cosine[:length], sine[:length]), axis=1).astype(BF)
        q = q * jnp.asarray(HEAD_DIM ** (-0.5), BF)
        kv = turn_kv(kv, cosine, sine).astype(BF)
        allowed = jnp.concatenate([mask[b]] * GROUP, axis=0) > 0.0
        parts = []
        for g in range(KV_HEADS):
            qg = heads_to_rows(q, g)
            kg = kv[:, HEAD_DIM * g : HEAD_DIM * (g + 1)]
            vg = kv[:, KW + HEAD_DIM * g : KW + HEAD_DIM * (g + 1)]
            q_o[b, g] = qg
            k_o[b, g] = kg
            v_o[b, g] = vg
            scores = jnp.where(allowed, dot(qg, kg, 1, 1), MASKED)
            top = jnp.max(scores, axis=-1, keepdims=True)
            e = jnp.exp(scores - top)
            total = jnp.sum(e, axis=-1, keepdims=True)
            lse_o[b, g] = jnp.log(total) + top
            probs = (e * (1.0 / total)).astype(BF)
            parts.append(dot(probs, vg, 1, 0))
        att_o[b * length : (b + 1) * length, :] = rows_to_heads(parts, length).astype(BF)


def feed_forward(attended, source, wo, wgu, wd, gain, cot, weight,
                 out_o, down_o, gu_o, mid_o, wout_o, attg_o, gain_o):
    units = wd.shape[0]
    step = units // 3
    att = attended[...]
    middle = source[...].astype(F32) + dot(att, wo[...], 1, 0)
    scale_two, normed = norm_parts(middle)
    g2 = gain[...]
    second = (normed * g2).astype(BF)
    out_grad = cot[...].astype(F32) * weight[...]
    feed_grad = out_grad.astype(BF)
    feed = None
    back = None
    for j in range(0, units, step):
        wg = wgu[:, j : j + step]
        wu = wgu[:, units + j : units + j + step]
        wdj = wd[j : j + step, :]
        gate = dot(second, wg, 1, 0)
        up = dot(second, wu, 1, 0)
        sig = jax.nn.sigmoid(gate)
        act = gate * sig
        product = (act * up).astype(BF)
        part = dot(product, wdj, 1, 0)
        feed = part if feed is None else feed + part
        down_o[j : j + step, :] = dot(product, feed_grad, 0, 0).astype(BF)
        pgrad = dot(feed_grad, wdj, 1, 1)
        ggrad = (pgrad * up * (sig * (1.0 + gate * (1.0 - sig)))).astype(BF)
        ugrad = (pgrad * act).astype(BF)
        gu_o[:, j : j + step] = dot(second, ggrad, 0, 0).astype(BF)
        gu_o[:, units + j : units + j + step] = dot(second, ugrad, 0, 0).astype(BF)
        part = dot(ggrad, wg, 1, 1) + dot(ugrad, wu, 1, 1)
        back = part if back is None else back + part
    out_o[...] = (middle + feed).astype(BF)
    gain_o[...] = jnp.sum(back * normed, axis=0, keepdims=True)
    middle_grad = out_grad + norm_back(back, g2, scale_two, normed)
    mid_o[...] = middle_grad
    branch = middle_grad.astype(BF)
    wout_o[...] = dot(att, branch, 0, 0).astype(BF)
    attg_o[...] = dot(branch, wo[...], 1, 1).astype(BF)


def attention_backward(order, length, seq_ref, blocks, wq, wkv, gain, cos, sin, mask, q_i, k_i, v_i,
                       lse, attg, dq_o, dkv_o, wgrad_o, bias_o, gain_o):
    seq = seq_ref[0]
    cosine, sine = tables(seq, order, cos, sin)
    width = gain.shape[1]
    q_wgrad = kv_wgrad = bias_q = bias_kv = gain_sum = None
    for b in range(blocks.shape[1] // length):
        x = blocks[:, b * length : (b + 1) * length, :width].astype(F32)
        x = x.reshape(len(order) * length, width)
        normed = norm_parts(x)[1]
        first = (normed * gain[...]).astype(BF)
        allowed = jnp.concatenate([mask[b]] * GROUP, axis=0) > 0.0
        ag = attg[b * length : (b + 1) * length, :]
        dqs, dks, dvs = [], [], []
        for g in range(KV_HEADS):
            qg, kg, vg = q_i[b, g], k_i[b, g], v_i[b, g]
            agg = heads_to_rows(ag, g)
            p = jnp.exp(jnp.where(allowed, dot(qg, kg, 1, 1), MASKED) - lse[b, g])
            dvs.append(dot(p.astype(BF), agg, 0, 0))
            pg = dot(agg, vg, 1, 1)
            inner = jnp.sum(p * pg, axis=-1, keepdims=True)
            ds = (p * (pg - inner)).astype(BF)
            dqs.append(dot(ds, kg, 1, 0) * HEAD_DIM ** (-0.5))
            dks.append(dot(ds, qg, 0, 0))
        dq = rows_to_heads(dqs, length)
        dq = jnp.concatenate([dq, jnp.zeros((length, 64), F32)], axis=1)
        dq = jnp.concatenate(turn(dq, cosine[:length], -sine[:length]), axis=1).astype(BF)
        dkv = jnp.concatenate(dks + dvs, axis=1)
        dkv = turn_kv(dkv, cosine, -sine).astype(BF)
        dq_o[b * length : (b + 1) * length, :] = dq
        for r in range(len(order)):
            dkv_o[r, b * length : (b + 1) * length, :] = dkv[r * length : (r + 1) * length, :]
        wq_part = dot(first[:length], dq, 0, 0)
        wkv_part = dot(first, dkv, 0, 0)
        bq_part = jnp.sum(dq.astype(F32), axis=0, keepdims=True)
        bkv_part = jnp.sum(dkv.astype(F32), axis=0, keepdims=True)
        e_kv = dot(dkv, wkv[...], 1, 1) * normed
        e_q = dot(dq[:, :QW], wq[:, :QW], 1, 1) * normed[:length]
        g_part = jnp.sum(e_kv, axis=0, keepdims=True) + jnp.sum(e_q, axis=0, keepdims=True)
        if q_wgrad is None:
            q_wgrad, kv_wgrad, bias_q, bias_kv, gain_sum = wq_part, wkv_part, bq_part, bkv_part, g_part
        else:
            q_wgrad, kv_wgrad = q_wgrad + wq_part, kv_wgrad + wkv_part
            bias_q, bias_kv, gain_sum = bias_q + bq_part, bias_kv + bkv_part, gain_sum + g_part
    wgrad_o[...] = jnp.concatenate([q_wgrad[:, :QW], kv_wgrad], axis=1).astype(BF)
    bias_o[...] = jnp.concatenate([bias_q[:, :QW], bias_kv], axis=1)
    gain_o[...] = gain_sum


def input_gradient(dq, own, a, b, c, source, mid, wq, wkv, gain, out_o):
    kv = own[...].astype(F32) + a[...].astype(F32) + b[...].astype(F32) + c[...].astype(F32)
    first_grad = dot(dq[:, :QW], wq[:, :QW], 1, 1) + dot(kv.astype(BF), wkv[...], 1, 1)
    scale_one, normed = norm_parts(source[...].astype(F32))
    out_o[...] = mid[...] + norm_back(first_grad, gain[...], scale_one, normed)

def chosen(flag, a, b):
    return jnp.where(flag != 0, b, a)


def first_forward(order, length, d_rows, n_bias, meta, blocks, am, ao, cos, sin, mask,
                  att_o, q_o, k_o, v_o, lse_o, w_o, gain_o, w_s, b_s):
    core = meta[0] & 1
    cut = am.shape[1]
    bias, gains = [], [[], []]
    for f in range(am.shape[0]):
        mine, other = am[f].astype(F32), ao[f].astype(F32)
        low, high = chosen(core, mine, other), chosen(core, other, mine)
        w_s[d_rows * f : d_rows * f + cut, :] = low
        w_s[d_rows * f + cut : d_rows * (f + 1), :] = high[: d_rows - cut]
        line = high[d_rows - cut : d_rows - cut + 1]
        bias.append(line[:, :n_bias])
        for i in range(2):
            gains[i].append(line[:, n_bias + d_rows * i : n_bias + d_rows * (i + 1)])
    w_o[...] = w_s[...].astype(BF)
    b_s[...] = jnp.concatenate(bias, axis=1)
    for i in range(2):
        gain_o[i : i + 1, :] = jnp.concatenate(gains[i], axis=1)
    wide = QW + 64
    attention_forward(order, length, meta, blocks, w_o[:, :wide], w_o[:, QW:], b_s[:, :wide], b_s[:, QW:],
                      gain_o[0:1, :], cos, sin, mask, att_o, q_o, k_o, v_o, lse_o)


def rel(meta, f):
    r = f ^ meta[1]
    return r & 1, (r >> 1) & 1, (r >> 2) & 1


def feed_forward_pieces(d_rows, ff_rows, meta, attended, source, bm, bo, c00, c10, c01, c11, gains, cot, weight,
                        out_o, gk_o, gg_o, dk_o, dg_o, mid_o, attg_o, gain_o, down_s, wout_s):
    core, y = meta[0] & 1, (meta[0] >> 1) & 1
    n_f = bm.shape[0]
    hf = n_f // 2
    part_d = ff_rows // 4
    part_o = d_rows // 3
    cut = bm.shape[1] - ff_rows // 2
    wo = []
    for f in range(n_f):
        mine, other = bm[f, ff_rows // 2 :, :].astype(F32), bo[f, ff_rows // 2 :, :].astype(F32)
        wo.append(chosen(core, mine, other))
        wo.append(chosen(core, other, mine)[: d_rows - cut])
    wo = jnp.concatenate(wo, axis=0).astype(BF)
    att = attended[...]
    middle = source[...].astype(F32) + dot(att, wo, 1, 0)
    scale_two, normed = norm_parts(middle)
    g2 = gains[1:2, :]
    second = (normed * g2).astype(BF)
    out_grad = cot[...].astype(F32) * weight[...]
    feed_grad = out_grad.astype(BF)
    feed = back = None
    for c_rel in (1, 0):
        first_q, second_q = (c01, c11) if c_rel else (c00, c10)
        wg = chosen(y, first_q[...], second_q[...])
        wu = chosen(y, second_q[...], first_q[...])
        h = core ^ c_rel
        wd = []
        for i in range(hf):
            mine, other = bm[hf * h + i, : ff_rows // 2, :], bo[hf * h + i, : ff_rows // 2, :]
            wd += [chosen(core, mine, other), chosen(core, other, mine)]
        wd = jnp.concatenate(wd, axis=0)
        gate = dot(second, wg, 1, 0)
        up = dot(second, wu, 1, 0)
        sig = jax.nn.sigmoid(gate)
        act = gate * sig
        product = (act * up).astype(BF)
        part = dot(product, wd, 1, 0)
        feed = part if feed is None else feed + part
        down_s[...] = dot(product, feed_grad, 0, 0)
        pgrad = dot(feed_grad, wd, 1, 1)
        ggrad = (pgrad * up * (sig * (1.0 + gate * (1.0 - sig)))).astype(BF)
        ugrad = (pgrad * act).astype(BF)
        part = dot(ggrad, wg, 1, 1) + dot(ugrad, wu, 1, 1)
        back = part if back is None else back + part
        for i in range(hf):
            x, z0, z1 = rel(meta, hf * h + i)
            for yy in range(2):
                for c_to, to in ((0, dk_o), (1, dg_o)):
                    at = pl.multiple_of(i * ff_rows + (yy * 2 + (core ^ c_to)) * part_d, 16)
                    to[y ^ yy, x, z0, z1, :part_d, :] = down_s[pl.ds(at, part_d), :].astype(BF)
        to = gg_o if c_rel else gk_o
        for yy, grad in ((0, ggrad), (1, ugrad)):
            wgrad = dot(second, grad, 0, 0)
            for f in range(n_f):
                x, z0, z1 = rel(meta, f)
                to[x, y ^ yy, z0, z1] = wgrad[d_rows * f : d_rows * (f + 1), :].astype(BF)
    out_o[...] = (middle + feed).astype(BF)
    gain_o[...] = jnp.sum(back * normed, axis=0, keepdims=True)
    middle_grad = out_grad + norm_back(back, g2, scale_two, normed)
    mid_o[...] = middle_grad
    branch = middle_grad.astype(BF)
    attg_o[...] = dot(branch, wo, 1, 1).astype(BF)
    wout = dot(att, branch, 0, 0)
    for f in range(n_f):
        wout_s[f, :d_rows, :] = wout[d_rows * f : d_rows * (f + 1), :]
        wout_s[f, d_rows:, :] = jnp.zeros((part_o, wout.shape[1]), F32)
    for f in range(n_f):
        x, z0, z1 = rel(meta, f)
        for yy in range(2):
            for c_to, to in ((0, dk_o), (1, dg_o)):
                at = pl.multiple_of((yy * 2 + (core ^ c_to)) * part_o, 8)
                to[y ^ yy, x, z0, z1, part_d:, :] = wout_s[f, pl.ds(at, part_o), :].astype(BF)


def attention_backward_pieces(order, length, d_rows, meta, blocks, w, gains, cos, sin, mask, q_i, k_i, v_i,
                              lse, attg, gain_two, dq_o, dk_o, dg_o, rk_o, rg_o, w_s, bias_s, gain_s, small_s):
    class Rows:
        def __init__(self, ref, base):
            self.ref, self.base = ref, base

        def __setitem__(self, key, value):
            if key is not Ellipsis:
                self.ref[(key[0] - self.base,) + key[1:]] = value

    half = len(order) // 2

    class Blocks:
        def __setitem__(self, key, value):
            ref = dk_o if key[0] < half else dg_o
            ref[(key[0] % half,) + key[1:]] = value

    class Wgrad:
        def __setitem__(self, key, value):
            w_s[:, : 2 * KW] = value[:, QW:].astype(F32)
            w_s[:, 2 * KW : 2 * KW + QW] = value[:, :QW].astype(F32)
            w_s[:, 2 * KW + QW :] = jnp.zeros((value.shape[0], 64), F32)

    wide = QW + 64
    attention_backward(order, length, meta, blocks, w[:, :wide], w[:, QW:], gains[0:1, :], cos, sin, mask,
                       q_i, k_i, v_i, lse, attg, dq_o, Blocks(), Wgrad(), bias_s, gain_s)
    n_f = small_s.shape[0]
    qk, v = (QW + KW) // n_f, KW // n_f
    bias, g1, g2 = bias_s[...], gain_s[...], gain_two[...]
    for f in range(n_f):
        line = jnp.concatenate(
            [
                bias[:, qk * f : qk * (f + 1)],
                bias[:, QW + KW + v * f : QW + KW + v * (f + 1)],
                g1[:, d_rows * f : d_rows * (f + 1)],
                jnp.zeros((1, 256 - qk - v - d_rows), F32),
                g2[:, d_rows * f : d_rows * (f + 1)],
                jnp.zeros((1, 768 - d_rows), F32),
            ],
            axis=1,
        )
        small_s[f] = jnp.broadcast_to(line, (8, 1024))
    core, y = meta[0] & 1, (meta[0] >> 1) & 1
    for f in range(n_f):
        x, z0, z1 = rel(meta, f)
        for yy in range(2):
            for c_to, to in ((0, rk_o), (1, rg_o)):
                at = pl.multiple_of((yy * 2 + (core ^ c_to)) * 256, 256)
                block = [w_s[d_rows * f : d_rows * (f + 1), pl.ds(at, 256)], small_s[f, :, pl.ds(at, 256)]]
                to[x, y ^ yy, z0, z1] = jnp.concatenate(block, axis=0).astype(BF)


def input_gradient_two(dq, own, other, source, mid, w, gains, out_o):
    kv = (own[...].astype(F32) + other[...].astype(F32)).astype(BF)
    first_grad = dot(dq[:, :QW], w[:, :QW], 1, 1) + dot(kv, w[:, QW:], 1, 1)
    scale_one, normed = norm_parts(source[...].astype(F32))
    out_o[...] = mid[...] + norm_back(first_grad, gains[0:1, :], scale_one, normed)


def place_gate(meta, p00, p10, pc, out_o):
    seq = meta[0]
    n = p00.shape[1]
    for piece, o in ((p00[...], 0), (p10[...], 2), (pc[0], 1), (pc[1], 3)):
        out_o[:, pl.ds(pl.multiple_of((seq ^ o) * n, 128), n)] = piece.astype(F32)


def place_down(part_d, meta, p00, p10, pc, out_o, wout_o):
    seq = meta[0]
    part_o = p00.shape[0] - part_d
    for piece, o in ((p00[...], 0), (p10[...], 2), (pc[0], 1), (pc[1], 3)):
        piece = piece.astype(F32)
        to = seq ^ o
        out_o[pl.ds(pl.multiple_of(to * part_d, 16), part_d), :] = piece[:part_d]

        @pl.when(to < 3)
        def _():
            wout_o[pl.ds(pl.multiple_of(to * part_o, 8), part_o), :] = piece[part_d:]


def place_qkv(qk, v, meta, p00, p10, pc, w_o, bqk_o, bv_o, gains_o, all_s):
    seq = meta[0]
    n = p00.shape[1]
    for piece, o in ((p00[...], 0), (p10[...], 2), (pc[0], 1), (pc[1], 3)):
        all_s[:, pl.ds(pl.multiple_of((seq ^ o) * n, 128), n)] = piece.astype(F32)
    d_rows = w_o.shape[0]
    w_o[:, :QW] = all_s[:d_rows, 2 * KW : 2 * KW + QW]
    w_o[:, QW:] = all_s[:d_rows, : 2 * KW]
    line = all_s[d_rows : d_rows + 1, :]
    bqk_o[...] = line[:, :qk]
    bv_o[...] = line[:, qk : qk + v]
    gains_o[0:1, :] = line[:, qk + v : qk + v + d_rows]
    gains_o[1:2, :] = line[:, 256 : 256 + d_rows]


class Net:
    def __init__(self, n_fsdp, n_seq):
        self.n_fsdp, self.n_seq = n_fsdp, n_seq
        self.total = n_fsdp * n_seq
        f, s = lax.axis_index("fsdp"), lax.axis_index("seq")
        self.index = f * n_seq + s
        self.seq_bits = [1 << b for b in range(n_seq.bit_length() - 1)]
        self.fsdp_bits = [n_seq << b for b in range(n_fsdp.bit_length() - 1)]

    def swap(self, value, mask):
        pairs = [(i, i ^ mask) for i in range(self.total)]
        return lax.ppermute(value, ("fsdp", "seq"), pairs)

    def bit(self, mask):
        return (self.index & mask) != 0

    def both(self, mine, mask, axis):
        other = self.swap(mine, mask)
        high = self.bit(mask)
        return jnp.stack([jnp.where(high, other, mine), jnp.where(high, mine, other)], axis=axis)

    def half(self, value, mask, axis):
        return lax.dynamic_index_in_dim(
            value, self.bit(mask).astype(jnp.int32), axis, keepdims=False
        )

    def add_half(self, value, mask, axis):
        mine = self.bit(mask).astype(jnp.int32)
        keep = lax.dynamic_index_in_dim(value, mine, axis, keepdims=False)
        give = lax.dynamic_index_in_dim(value, 1 - mine, axis, keepdims=False)
        got = self.swap(give, mask)
        return (keep.astype(F32) + got.astype(F32)).astype(value.dtype)

    def gather_fsdp(self, value):
        for step, mask in enumerate(reversed(self.fsdp_bits)):
            value = self.both(value, mask, step)
        return value

    def scatter_fsdp(self, value, first_axis=0):
        count = len(self.fsdp_bits)
        for step, mask in enumerate(self.fsdp_bits):
            value = self.add_half(value, mask, first_axis + count - 1 - step)
        return value


def on_device(
    hidden, w_qkv, b_qkv, w_out, w_gate_up, w_down, norm_gains, segment_ids, token_counts, cotangent,
    n_fsdp, n_seq,
):
    net = Net(n_fsdp, n_seq)
    micro, batch, length, width = hidden.shape
    full_length = length * n_seq
    tokens_micro = batch * n_fsdp * full_length
    scale = HEAD_DIM ** (-0.5)
    rows = micro * batch * length
    d_rows = w_qkv.shape[0]
    ff_rows = w_down.shape[0]
    units = w_gate_up.shape[1] // 2
    qkv_w = w_qkv.shape[1]
    core = net.seq_bits[0]
    f_lead = (2,) * len(net.fsdp_bits)

    ids = segment_ids.reshape(rows, 1).astype(BF)
    block = jnp.concatenate(
        [hidden.reshape(rows, width), jnp.broadcast_to(ids, (rows, 64))], axis=1
    )
    blocks = block[None]
    for mask in reversed(net.seq_bits):
        blocks = jnp.concatenate([blocks, net.swap(blocks, mask)], axis=0)
    order = [0]
    for mask in reversed(net.seq_bits):
        order = order + [o ^ mask for o in order]
    seq_index = lax.axis_index("seq")
    block_ids = [seq_index ^ o for o in order]

    pad_rows = -(d_rows + 1) % 16 + 1
    extra = jnp.zeros((pad_rows, qkv_w), BF)
    small = jnp.concatenate([b_qkv, norm_gains.reshape(-1)])
    extra = extra.at[0, : small.shape[0]].set(small)
    shard_a = jnp.concatenate([w_qkv, extra], axis=0).reshape(2, -1, qkv_w)
    got_a = net.gather_fsdp(net.half(shard_a, core, 0))
    full_a = net.both(got_a, core, len(f_lead)).reshape(n_fsdp, d_rows + pad_rows, qkv_w)
    wf_qkv = full_a[:, :d_rows].reshape(n_fsdp * d_rows, qkv_w)
    smalls = full_a[:, d_rows]
    n_bias = b_qkv.shape[0]
    bias = smalls[:, :n_bias].reshape(-1).astype(F32)
    gains = smalls[:, n_bias : n_bias + 2 * d_rows].reshape(n_fsdp, 2, d_rows).astype(F32)
    gain_one = gains[:, 0].reshape(-1)
    gain_two = gains[:, 1].reshape(-1)

    pad_b = -(d_rows + ff_rows) % 16
    shard_b = jnp.concatenate([w_out, w_down, jnp.zeros((pad_b, width), BF)], axis=0)
    shard_b = shard_b.reshape(2, -1, width)
    got_b = net.gather_fsdp(net.half(shard_b, core, 0))

    parts = n_seq
    shard_c = w_gate_up.reshape(d_rows, parts, -1)
    got_c = net.gather_fsdp(lax.dynamic_index_in_dim(shard_c, seq_index, 1, keepdims=False))
    full_b = net.both(got_b, core, len(f_lead)).reshape(n_fsdp, -1, width)
    wf_out = full_b[:, :d_rows].reshape(n_fsdp * d_rows, width)
    wf_down = full_b[:, d_rows : d_rows + ff_rows].reshape(n_fsdp * ff_rows, width)
    got_c = got_c.reshape(n_fsdp * d_rows, -1)
    for mask in reversed(net.seq_bits):
        got_c = net.both(got_c, mask, got_c.ndim - 1)
    wf_gate_up = got_c.reshape(n_fsdp * d_rows, 2 * units)

    places = np.arange(full_length, dtype=np.float32)
    speeds = np.power(ROPE_BASE, -2.0 * np.arange(HEAD_DIM // 2, dtype=np.float32) / HEAD_DIM)
    angles = places[:, None] * speeds.astype(np.float32)[None, :]
    cos_t = np.tile(np.cos(angles), (1, 4)).reshape(n_seq, length, 128)
    sin_t = np.concatenate([-np.sin(angles), np.sin(angles)] * 2, axis=1).reshape(n_seq, length, 128)
    cos_t, sin_t = jnp.asarray(cos_t, F32), jnp.asarray(sin_t, F32)
    seqs = micro * batch
    seg_all = blocks[..., width].reshape(n_seq, seqs, length).transpose(1, 0, 2)
    own_places = seq_index * length + jnp.arange(length, dtype=jnp.int32)
    key_places = jnp.stack(block_ids)[:, None] * length + jnp.arange(length, dtype=jnp.int32)
    allowed = (seg_all[:, 0, :, None] == seg_all.reshape(seqs, 1, -1)) & (
        own_places[None, :, None] >= key_places.reshape(1, 1, -1)
    )
    allowed = allowed.astype(F32)
    seq_scalar = seq_index.astype(jnp.int32).reshape(1)
    wq, wkv = wf_qkv[:, : QW + 64], wf_qkv[:, QW:]
    gain_one, gain_two = gain_one[None], gain_two[None]
    source = hidden.reshape(rows, width)
    n_all = n_seq * rows
    attended, q_s, k_s, v_s, lse = call(
        functools.partial(attention_forward, order, length),
        [seq_scalar],
        [blocks, wq, wkv, bias[None, : QW + 64], bias[None, QW:], gain_one, cos_t, sin_t, allowed],
        [
            sds((rows, QW), BF),
            sds((seqs, KV_HEADS, GROUP * length, HEAD_DIM), BF),
            sds((seqs, KV_HEADS, full_length, HEAD_DIM), BF),
            sds((seqs, KV_HEADS, full_length, HEAD_DIM), BF),
            sds((seqs, KV_HEADS, GROUP * length, 1), F32),
        ],
        2 * n_all * width * 2 * KW + 2 * rows * width * QW + 4 * rows * full_length * QW,
    )

    weight = tokens_micro / token_counts.astype(F32)
    weight = jnp.repeat(weight, batch * length)[:, None]
    block_out, down_grad, gate_up_wgrad, middle_grad, out_wgrad, attended_grad, gain_two_grad = call(
        feed_forward,
        [],
        [attended, source, wf_out, wf_gate_up, wf_down, gain_two, cotangent.reshape(rows, width), weight],
        [
            sds((rows, width), BF),
            sds((units, width), BF),
            sds((width, 2 * units), BF),
            sds((rows, width), F32),
            sds((QW, width), BF),
            sds((rows, QW), BF),
            sds((1, width), F32),
        ],
        6 * rows * width * 3 * units + 6 * rows * width * QW,
    )
    block_out = block_out.reshape(hidden.shape)

    def seq_axes(value, axis, masks):
        for mask in masks:
            value = net.add_half(value, mask, axis)
        return value

    quarter = (2,) * len(net.seq_bits)
    n_f = len(f_lead)
    red_down = down_grad.reshape(f_lead + quarter + (ff_rows // n_seq, width))
    for step, mask in enumerate(net.seq_bits):
        red_down = net.add_half(red_down, mask, n_f + len(quarter) - 1 - step)
    red_down = net.scatter_fsdp(red_down)

    red_gate = gate_up_wgrad.reshape(f_lead + (d_rows,) + quarter + (2 * units // n_seq,))
    red_gate = net.add_half(red_gate, core, n_f + len(quarter))
    red_gate = net.add_half(red_gate, net.fsdp_bits[0], n_f - 1)
    for step, mask in enumerate(net.seq_bits[1:]):
        red_gate = net.add_half(red_gate, mask, n_f - 1 + len(quarter) - 1 - step)
    for step, mask in enumerate(net.fsdp_bits[1:]):
        red_gate = net.add_half(red_gate, mask, n_f - 2 - step)

    dq, dkv, qkv_wgrad, bias_grad, gain_one_grad = call(
        functools.partial(attention_backward, order, length),
        [seq_scalar],
        [blocks, wq, wkv, gain_one, cos_t, sin_t, allowed, q_s, k_s, v_s, lse, attended_grad],
        [
            sds((rows, QW + 64), BF),
            sds((n_seq, rows, 2 * KW), BF),
            sds((width, qkv_w), BF),
            sds((1, qkv_w), F32),
            sds((1, width), F32),
        ],
        4 * n_all * width * 2 * KW + 4 * rows * width * QW + 10 * rows * full_length * QW,
    )
    kv_parts = [dkv[0]]
    for place, mask_bits in enumerate(order):
        if mask_bits:
            kv_parts.append(net.swap(dkv[place], mask_bits))
    (hidden_grad,) = call(
        input_gradient,
        [],
        [dq, *kv_parts, source, middle_grad, wq, wkv, gain_one],
        [sds((rows, width), F32)],
        2 * rows * width * qkv_w,
    )
    hidden_grad = hidden_grad.reshape(hidden.shape)
    bias_grad, gain_one_grad, gain_two_grad = bias_grad[0], gain_one_grad[0], gain_two_grad[0]

    qk_rows, v_rows = (QW + KW) // n_fsdp, KW // n_fsdp
    small_grads = jnp.concatenate(
        [
            bias_grad[: QW + KW].reshape(n_fsdp, qk_rows),
            bias_grad[QW + KW :].reshape(n_fsdp, v_rows),
            gain_one_grad.reshape(n_fsdp, d_rows),
            gain_two_grad.reshape(n_fsdp, d_rows),
        ],
        axis=1,
    ).astype(BF)
    wide = qkv_w + width
    small_pad = jnp.zeros((n_fsdp, pad_rows, wide), BF)
    small_pad = small_pad.at[:, 0, : small_grads.shape[1]].set(small_grads)
    rest = jnp.concatenate([qkv_wgrad, out_wgrad], axis=1)
    rest = jnp.concatenate([rest.reshape(n_fsdp, d_rows, wide), small_pad], axis=1)
    rest = rest.reshape(f_lead + (d_rows + pad_rows,) + quarter + (wide // n_seq,))
    for step, mask in enumerate(net.seq_bits):
        rest = net.add_half(rest, mask, n_f + 1 + len(quarter) - 1 - step)
    rest = net.scatter_fsdp(rest)

    def seq_back(value, axis):
        for step, mask in enumerate(reversed(net.seq_bits)):
            value = net.both(value, mask, axis + step)
        return value

    out_down = seq_back(red_down, 0).reshape(ff_rows, width).astype(F32)
    out_gate = seq_back(red_gate, 1).reshape(d_rows, 2 * units).astype(F32)
    out_rest = seq_back(rest, 1).reshape(d_rows + pad_rows, wide).astype(F32)
    line = out_rest[d_rows]
    edge = qk_rows + v_rows
    return (
        block_out,
        hidden_grad,
        out_rest[:d_rows, :qkv_w],
        line[:qk_rows],
        line[qk_rows:edge],
        out_rest[:d_rows, qkv_w:],
        out_gate,
        out_down,
        line[edge : edge + 2 * d_rows].reshape(2, d_rows),
    )


def after(value, *others):
    return lax.optimization_barrier((value, *others))[0]


def rope_tables(full_length, n_seq):
    places = np.arange(full_length, dtype=np.float32)
    speeds = np.power(ROPE_BASE, -2.0 * np.arange(HEAD_DIM // 2, dtype=np.float32) / HEAD_DIM)
    angles = places[:, None] * speeds.astype(np.float32)[None, :]
    cos_t = np.tile(np.cos(angles), (1, 4)).reshape(n_seq, -1, 128)
    sin_t = np.concatenate([-np.sin(angles), np.sin(angles)] * 2, axis=1).reshape(n_seq, -1, 128)
    return jnp.asarray(cos_t, F32), jnp.asarray(sin_t, F32)


def on_device_tiled(
    hidden, w_qkv, b_qkv, w_out, w_gate_up, w_down, norm_gains, segment_ids, token_counts, cotangent,
    n_fsdp, n_seq,
):
    net = Net(n_fsdp, n_seq)
    micro, batch, length, width = hidden.shape
    full_length = length * n_seq
    tokens_micro = batch * n_fsdp * full_length
    rows = micro * batch * length
    seqs = micro * batch
    d_rows, qkv_w = w_qkv.shape
    ff_rows = w_down.shape[0]
    units = w_gate_up.shape[1] // 2
    n_bias = b_qkv.shape[0]
    core, ybit = net.seq_bits
    xbit, znear, zfar = net.fsdp_bits
    order = [0, 2, 1, 3]
    seq_index = lax.axis_index("seq")
    meta = jnp.stack([seq_index, lax.axis_index("fsdp")]).astype(jnp.int32)
    source = hidden.reshape(rows, width)

    small = jnp.concatenate([b_qkv, norm_gains.reshape(-1)])
    extra = jnp.zeros((8, qkv_w), BF).at[:, : small.shape[0]].set(small[None])
    shard_a = jnp.concatenate([w_qkv, extra], axis=0).reshape(2, -1, qkv_w)
    a = net.half(shard_a, core, 0)
    a = net.both(a, zfar, 0)

    ids = segment_ids.reshape(rows, 1).astype(BF)
    block = jnp.concatenate([source, jnp.broadcast_to(ids, (rows, 64))], axis=1)
    blocks = jnp.stack([block, net.swap(block, ybit)])
    blocks = jnp.concatenate([blocks, net.swap(blocks, core)], axis=0)

    gu = lax.dynamic_slice_in_dim(
        w_gate_up, seq_index * (2 * units // n_seq), 2 * units // n_seq, axis=1
    )
    gu = after(gu, a)
    half_b = jnp.concatenate(
        [
            w_down.reshape(2, ff_rows // 2, width),
            jnp.concatenate([w_out, jnp.zeros((8, width), BF)], axis=0).reshape(2, -1, width),
        ],
        axis=1,
    )
    b = after(net.half(half_b, core, 0), a)
    gu = net.both(gu, zfar, 0)
    b = net.both(b, zfar, 0)
    a = net.both(a, znear, 1)
    a = net.both(a, xbit, 2).reshape(n_fsdp, -1, qkv_w)
    gu = net.both(gu, znear, 1)
    b = net.both(b, znear, 1)
    a_other = net.swap(a, core)
    gu = net.both(gu, xbit, 2).reshape(n_fsdp * d_rows, -1)
    b = net.both(b, xbit, 2).reshape(n_fsdp, -1, width)
    gu_c = net.swap(gu, core)
    gu_y = net.swap(gu, ybit)
    b_other = net.swap(b, core)
    gu_yc = net.swap(gu_y, core)

    cos_t, sin_t = rope_tables(full_length, n_seq)
    block_ids = [seq_index ^ o for o in order]
    seg_all = blocks[..., width].reshape(n_seq, seqs, length).transpose(1, 0, 2)
    own_places = seq_index * length + jnp.arange(length, dtype=jnp.int32)
    key_places = jnp.stack(block_ids)[:, None] * length + jnp.arange(length, dtype=jnp.int32)
    allowed = (seg_all[:, 0, :, None] == seg_all.reshape(seqs, 1, -1)) & (
        own_places[None, :, None] >= key_places.reshape(1, 1, -1)
    )
    allowed = allowed.astype(F32)
    n_all = n_seq * rows
    attended, q_s, k_s, v_s, lse, wf, gains = call(
        functools.partial(first_forward, order, length, d_rows, n_bias),
        [meta],
        [blocks, a, a_other, cos_t, sin_t, allowed],
        [
            sds((rows, QW), BF),
            sds((seqs, KV_HEADS, GROUP * length, HEAD_DIM), BF),
            sds((seqs, KV_HEADS, full_length, HEAD_DIM), BF),
            sds((seqs, KV_HEADS, full_length, HEAD_DIM), BF),
            sds((seqs, KV_HEADS, GROUP * length, 1), F32),
            sds((width, qkv_w), BF),
            sds((2, width), F32),
        ],
        2 * n_all * width * 2 * KW + 2 * rows * width * QW + 4 * rows * full_length * QW,
        [(width, qkv_w), (1, qkv_w)],
    )

    weight = tokens_micro / token_counts.astype(F32)
    weight = jnp.repeat(weight, batch * length)[:, None]
    lead = (2, 2, 2, 2)
    block_out, gate_keep, gate_give, down_keep, down_give, middle_grad, attended_grad, gain_two = call(
        functools.partial(feed_forward_pieces, d_rows, ff_rows),
        [meta],
        [attended, source, b, b_other, gu, gu_y, gu_c, gu_yc, gains, cotangent.reshape(rows, width), weight],
        [
            sds((rows, width), BF),
            sds(lead + (d_rows, units // 2), BF),
            sds(lead + (d_rows, units // 2), BF),
            sds(lead + (ff_rows // 4 + d_rows // 3, width), BF),
            sds(lead + (ff_rows // 4 + d_rows // 3, width), BF),
            sds((rows, width), F32),
            sds((rows, QW), BF),
            sds((1, width), F32),
        ],
        6 * rows * width * 3 * units + 6 * rows * width * QW,
        [(units // 2, width), (n_fsdp, d_rows + d_rows // 3, width)],
    )
    block_out = block_out.reshape(hidden.shape)

    def add(keep, got):
        return (keep.astype(F32) + got.astype(F32)).astype(BF)

    gate = add(gate_keep, net.swap(gate_give, core))
    down = add(down_keep, net.swap(down_give, core))
    attended_grad = after(attended_grad, gate, down)
    gate_got = net.swap(gate[1], xbit)
    down_got = net.swap(down[1], ybit)

    dq, dkv_keep, dkv_give, rest_keep, rest_give = call(
        functools.partial(attention_backward_pieces, order, length, d_rows),
        [meta],
        [blocks, wf, gains, cos_t, sin_t, allowed, q_s, k_s, v_s, lse, attended_grad, gain_two],
        [
            sds((rows, QW + 64), BF),
            sds((2, rows, 2 * KW), BF),
            sds((2, rows, 2 * KW), BF),
            sds(lead + (d_rows + 8, 256), BF),
            sds(lead + (d_rows + 8, 256), BF),
        ],
        4 * n_all * width * 2 * KW + 4 * rows * width * QW + 10 * rows * full_length * QW,
        [(width, 1024), (1, qkv_w), (1, width), (n_fsdp, 8, 1024)],
    )
    rest = add(rest_keep, net.swap(rest_give, core))
    dkv = add(dkv_keep, net.swap(dkv_give, core))
    rest_got = net.swap(rest[1], xbit)
    dkv_got = net.swap(dkv[1], ybit)

    gate = add(gate[0], gate_got)
    down = add(down[0], down_got)
    gate_got = net.swap(gate[1], ybit)
    down_got = net.swap(down[1], xbit)
    rest = add(rest[0], rest_got)
    rest_got = net.swap(rest[1], ybit)
    (hidden_grad,) = call(
        input_gradient_two,
        [],
        [dq, dkv[0], dkv_got, source, middle_grad, wf, gains],
        [sds((rows, width), F32)],
        2 * rows * width * qkv_w,
    )
    hidden_grad = hidden_grad.reshape(hidden.shape)
    gate = add(gate[0], gate_got)
    down = add(down[0], down_got)
    rest = add(rest[0], rest_got)
    for mask in (znear, zfar):
        gots = [net.swap(part[1], mask) for part in (gate, down, rest)]
        gate, down, rest = [add(part[0], got) for part, got in zip((gate, down, rest), gots)]

    def spread(part):
        other = net.swap(part, ybit)
        return [part, other, net.swap(jnp.stack([part, other]), core)]

    (out_gate,) = call(place_gate, [meta], spread(gate), [sds((d_rows, 2 * units), F32)], 0)
    out_down, out_wout = call(
        functools.partial(place_down, ff_rows // 4),
        [meta],
        spread(down),
        [sds((ff_rows, width), F32), sds((d_rows, width), F32)],
        0,
    )
    qk, v = (QW + KW) // n_fsdp, KW // n_fsdp
    out_qkv, b_qk, b_v, out_gains = call(
        functools.partial(place_qkv, qk, v),
        [meta],
        spread(rest),
        [sds((d_rows, qkv_w), F32), sds((1, qk), F32), sds((1, v), F32), sds((2, d_rows), F32)],
        0,
        [(d_rows + 8, 1024)],
    )
    return (
        block_out,
        hidden_grad,
        out_qkv,
        b_qk.reshape(qk),
        b_v.reshape(v),
        out_wout,
        out_gate,
        out_down,
        out_gains,
    )


def solution(mesh):
    n_fsdp, n_seq = mesh.shape["fsdp"], mesh.shape["seq"]
    in_specs = (
        P(None, "fsdp", "seq", None),
        P("fsdp", None),
        P("fsdp"),
        P("fsdp", None),
        P("fsdp", None),
        P("fsdp", None),
        P(None, "fsdp"),
        P(None, "fsdp", "seq"),
        P(),
        P(None, "fsdp", "seq", None),
    )
    out_specs = (
        P(None, "fsdp", "seq", None),
        P(None, "fsdp", "seq", None),
        P("fsdp", None),
        P("fsdp"),
        P("fsdp"),
        P("fsdp", None),
        P("fsdp", None),
        P("fsdp", None),
        P(None, "fsdp"),
    )

    def local(*args):
        body = on_device_tiled if (n_fsdp, n_seq) == (8, 4) else on_device
        return body(*args, n_fsdp=n_fsdp, n_seq=n_seq)

    return jax.shard_map(local, mesh=mesh, in_specs=in_specs, out_specs=out_specs, check_vma=False)
```

profile of v0, /device:TPU:0, one launch (start us, length us, event | category | flops | bytes accessed | tf_op | source)
XLA Modules:
  0.0 204.6 jit_solution(6041616880246811856)
XLA Ops:
  4.4 4.1 %collective-permute-start.2 = (bf16[40,960]{1,0:T(8,128)(2,1)S(1)}, bf16[40,960]{1,0:T(8,128)(2,1)S(1)}, u32[]{:S(2)}, u32[]{:S(2)}) collective-permute-start(bf16[40,960]{1,0:T(8,128)(2,1)S(1)} %dynamic-slice_bitcast_fusion), channel_id=1, source_target_pairs={{0,16},{1,17},{2,18},{3,19},{4,20},{5,21},{6,22},{7,23},{8,24},{9,... | collective-permute-start | bytes 230408 | tf_op jit(solution)/shard_map/ppermute | solution.py:444
  14.0 3.0 %collective-permute-start.3 = (bf16[2,40,960]{2,1,0:T(8,128)(2,1)S(1)}, bf16[2,40,960]{2,1,0:T(8,128)(2,1)S(1)}, u32[]{:S(2)}, u32[]{:S(2)}) collective-permute-start(bf16[2,40,960]{2,1,0:T(8,128)(2,1)S(1)} %pad_maximum_fusion.14), channel_id=1, source_target_pairs={{0,8},{1,9},{2,10},{3,11},{4,12},{5,13},{6,14},{7,15},{8,0},{9,1},... | collective-permute-start | bytes 460808 | tf_op jit(solution)/shard_map/ppermute | solution.py:444
  17.8 2.9 %collective-permute-done.10 = bf16[72,768]{1,0:T(8,128)(2,1)S(1)} collective-permute-done((bf16[72,768]{1,0:T(8,128)(2,1)S(1)}, bf16[72,768]{1,0:T(8,128)(2,1)S(1)}, u32[]{:S(2)}, u32[]{:S(2)}) %collective-permute-start.10) | collective-permute-done | bytes 110624 | tf_op jit(solution)/shard_map/ppermute | solution.py:444
  21.8 6.2 %collective-permute-done.6 = bf16[136,576]{1,0:T(8,128)(2,1)S(1)} collective-permute-done((bf16[136,576]{1,0:T(8,128)(2,1)S(1)}, bf16[136,576]{1,0:T(8,128)(2,1)S(1)}, u32[]{:S(2)}, u32[]{:S(2)}) %collective-permute-start.6) | collective-permute-done | bytes 156704 | tf_op jit(solution)/shard_map/ppermute | solution.py:444
  29.1 2.5 %collective-permute-done.11 = bf16[2,72,768]{2,1,0:T(8,128)(2,1)S(1)} collective-permute-done((bf16[2,72,768]{2,1,0:T(8,128)(2,1)S(1)}, bf16[2,72,768]{2,1,0:T(8,128)(2,1)S(1)}, u32[]{:S(2)}, u32[]{:S(2)}) %collective-permute-start.11) | collective-permute-done | bytes 221216 | tf_op jit(solution)/shard_map/ppermute | solution.py:444
  31.7 1.6 collective-permute-start.12
  33.3 4.8 %collective-permute-done.7 = bf16[2,136,576]{2,1,0:T(8,128)(2,1)S(1)} collective-permute-done((bf16[2,136,576]{2,1,0:T(8,128)(2,1)S(1)}, bf16[2,136,576]{2,1,0:T(8,128)(2,1)S(1)}, u32[]{:S(2)}, u32[]{:S(2)}) %collective-permute-start.7) | collective-permute-done | bytes 313376 | tf_op jit(solution)/shard_map/ppermute | solution.py:444
  39.9 4.0 %collective-permute-done.12 = bf16[2,2,72,768]{3,2,0,1:T(8,128)(2,1)S(1)} collective-permute-done((bf16[2,2,72,768]{3,2,0,1:T(8,128)(2,1)S(1)}, bf16[2,2,72,768]{3,2,0,1:T(8,128)(2,1)S(1)}, u32[]{:S(2)}, u32[]{:S(2)}) %collective-permute-start.12) | collective-permute-done | bytes 442400 | tf_op jit(solution)/shard_map/ppermute | solution.py:444
  45.0 1.8 collective-permute-start.13
  48.4 10.4 %collective-permute-done.8 = bf16[2,2,136,576]{3,2,1,0:T(8,128)(2,1)S(1)} collective-permute-done((bf16[2,2,136,576]{3,2,1,0:T(8,128)(2,1)S(1)}, bf16[2,2,136,576]{3,2,1,0:T(8,128)(2,1)S(1)}, u32[]{:S(2)}, u32[]{:S(2)}) %collective-permute-start.8) | collective-permute-done | bytes 626720 | tf_op jit(solution)/shard_map/ppermute | solution.py:444
  61.9 2.0 collective-permute-done.4
  68.9 11.3 %shard_map.187 = (bf16[256,576]{1,0:T(8,128)(2,1)S(1)}, bf16[2,3,384,64]{3,2,1,0:T(8,128)(2,1)S(1)}, bf16[2,3,512,64]{3,2,1,0:T(8,128)(2,1)}, bf16[2,3,512,64]{3...) custom-call(s32[2]{0:T(128)S(1)} %pad_add_fusion.meta, ...), custom_call_target="tpu_custom_call" | custom-call | flops 924844032 | bytes 6084096 | tf_op jit(solution)/shard_map/pallas_call | solution.py:53
  81.1 12.9 %shard_map.188 = (bf16[256,576]{1,0:T(8,128)(2,1)S(1)}, bf16[2,2,2,2,72,768]{5,4,3,2,1,0:T(8,128)(2,1)}, bf16[2,2,2,2,72,768]{5,4,3,2,1,0:T(8,128)(2,1)}, bf16[2...) custom-call(s32[2]{0:T(128)S(1)} %pad_add_fusion.meta, ...), custom_call_target="tpu_custom_call" | custom-call | flops 4586471424 | bytes 14311168 | tf_op jit(solution)/shard_map/pallas_call | solution.py:53
  94.6 3.0 %collective-permute-done.17 = bf16[2,2,2,2,72,576]{5,4,3,2,1,0:T(8,128)(2,1)S(1)} collective-permute-done((bf16[2,2,2,2,72,576]{5,4,3,2,1,0:T(8,128)(2,1)}, bf16[2,2,2,2,72,576]{5,4,3,2,1,0:T(8,128)(2,1)S(1)}, u32[]{:S(2)}, u32[]{:S(2)}) %collective-permute-start.17) | collective-permute-done | bytes 1327136 | tf_op jit(solution)/shard_map/ppermute | solution.py:444
  97.5 1.9 add_convert_fusion.1
  102.3 12.9 %shard_map.189 = (bf16[256,640]{1,0:T(8,128)(2,1)S(1)}, bf16[2,256,384]{2,1,0:T(8,128)(2,1)S(1)}, bf16[2,256,384]{2,1,0:T(8,128)(2,1)S(1)}, bf16[2,2,2,2,80,256]...) custom-call(s32[2]{0:T(128)S(1)} %pad_add_fusion.meta, bf16[4,256,640]{2,1,0:T(8,128)(2,1)} %copy-done.5, ...), custom_call_target="tpu_custom_call" | custom-call | flops 2000683008 | bytes 7282432 | tf_op jit(solution)/shard_map/pallas_call | solution.py:53
  117.3 2.1 %collective-permute-done.27 = bf16[2,2,2,72,576]{4,3,2,1,0:T(8,128)(2,1)} collective-permute-done((bf16[2,2,2,72,576]{4,3,2,1,0:T(8,128)(2,1)}, bf16[2,2,2,72,576]{4,3,2,1,0:T(8,128)(2,1)}, u32[]{:S(2)}, u32[]{:S(2)}) %collective-permute-start.27) | collective-permute-done | bytes 663584 | tf_op jit(solution)/shard_map/ppermute | solution.py:444
  120.8 1.6 collective-permute-start.28
  122.5 1.6 collective-permute-start.19
  124.1 21.3 %collective-permute-done.28 = bf16[2,2,72,576]{3,2,1,0:T(8,128)(2,1)S(1)} collective-permute-done((bf16[2,2,72,576]{3,2,1,0:T(8,128)(2,1)S(1)}, bf16[2,2,72,576]{3,2,1,0:T(8,128)(2,1)S(1)}, u32[]{:S(2)}, u32[]{:S(2)}) %collective-permute-start.28) | collective-permute-done | bytes 331808 | tf_op jit(solution)/shard_map/ppermute | solution.py:444
  145.9 5.5 %collective-permute-done.29 = bf16[2,72,576]{2,1,0:T(8,128)(2,1)S(1)} collective-permute-done((bf16[2,72,576]{2,1,0:T(8,128)(2,1)S(1)}, bf16[2,72,576]{2,1,0:T(8,128)(2,1)S(1)}, u32[]{:S(2)}, u32[]{:S(2)}) %collective-permute-start.29) | collective-permute-done | bytes 165920 | tf_op jit(solution)/shard_map/ppermute | solution.py:444
  151.4 1.9 collective-permute-start.30
  154.9 3.0 %collective-permute-done.30 = bf16[72,576]{1,0:T(8,128)(2,1)S(1)} collective-permute-done((bf16[72,576]{1,0:T(8,128)(2,1)S(1)}, bf16[72,576]{1,0:T(8,128)(2,1)S(1)}, u32[]{:S(2)}, u32[]{:S(2)}) %collective-permute-start.30) | collective-permute-done | bytes 82976 | tf_op jit(solution)/shard_map/ppermute | solution.py:444
  158.7 2.6 %collective-permute-done.21 = bf16[2,2,2,80,256]{4,3,2,1,0:T(8,128)(2,1)S(1)} collective-permute-done((bf16[2,2,2,80,256]{4,3,2,1,0:T(8,128)(2,1)S(1)}, bf16[2,2,2,80,256]{4,3,2,1,0:T(8,128)(2,1)S(1)}, u32[]{:S(2)}, u32[]{:S(2)}) %collective-permute-start.21) | collective-permute-done | bytes 327712 | tf_op jit(solution)/shard_map/ppermute | solution.py:444
  163.6 5.0 %collective-permute-done.22 = bf16[2,2,80,256]{3,2,1,0:T(8,128)(2,1)S(1)} collective-permute-done((bf16[2,2,80,256]{3,2,1,0:T(8,128)(2,1)S(1)}, bf16[2,2,80,256]{3,2,1,0:T(8,128)(2,1)S(1)}, u32[]{:S(2)}, u32[]{:S(2)}) %collective-permute-start.22) | collective-permute-done | bytes 163872 | tf_op jit(solution)/shard_map/ppermute | solution.py:444
  168.6 1.6 collective-permute-start.23
  170.2 5.1 %collective-permute-done.34 = bf16[2,2,72,768]{3,2,1,0:T(8,128)(2,1)S(1)} collective-permute-done((bf16[2,2,72,768]{3,2,1,0:T(8,128)(2,1)S(1)}, bf16[2,2,72,768]{3,2,1,0:T(8,128)(2,1)S(1)}, u32[]{:S(2)}, u32[]{:S(2)}) %collective-permute-start.34) | collective-permute-done | bytes 442400 | tf_op jit(solution)/shard_map/ppermute | solution.py:444
  175.9 5.7 %collective-permute-done.35 = bf16[2,72,768]{2,1,0:T(8,128)(2,1)S(1)} collective-permute-done((bf16[2,72,768]{2,1,0:T(8,128)(2,1)S(1)}, bf16[2,72,768]{2,1,0:T(8,128)(2,1)S(1)}, u32[]{:S(2)}, u32[]{:S(2)}) %collective-permute-start.35) | collective-permute-done | bytes 221216 | tf_op jit(solution)/shard_map/ppermute | solution.py:444
  182.7 2.0 collective-permute-start.24
  184.7 4.3 %collective-permute-done.36 = bf16[72,768]{1,0:T(8,128)(2,1)S(1)} collective-permute-done((bf16[72,768]{1,0:T(8,128)(2,1)S(1)}, bf16[72,768]{1,0:T(8,128)(2,1)S(1)}, u32[]{:S(2)}, u32[]{:S(2)}) %collective-permute-start.36) | collective-permute-done | bytes 110624 | tf_op jit(solution)/shard_map/ppermute | solution.py:444
  191.2 2.6 %collective-permute-done.37.p10 = bf16[72,768]{1,0:T(8,128)(2,1)S(1)} collective-permute-done((bf16[72,768]{1,0:T(8,128)(2,1)S(1)}, bf16[72,768]{1,0:T(8,128)(2,1)S(1)}, u32[]{:S(2)}, u32[]{:S(2)}) %collective-permute-start.37) | collective-permute-done | bytes 110624 | tf_op jit(solution)/shard_map/ppermute | solution.py:444
  196.7 2.4 %shard_map.190 = f32[256,576]{1,0:T(8,128)S(1)} custom-call(bf16[256,640]{1,0:T(8,128)(2,1)S(1)} %get-tuple-element.67.dq, bf16[256,384]{1,0:T(8,128)(2,1)S(1)} %get-tuple-element.117.own, bf16[256,384]{1,0:T(8,128)(2,1)S(1)} %collective-permute-done.19.other, bf16[256,576]{1,0:T(8,128)(2,1)S(1)} %bitcast.180, f32[256,576]{1,0:T(8,128)} %get-tuple-element.70.mid, ...), custom_call_target="tpu_custom_call" | custom-call | flops 283115520 | bytes 3305984 | tf_op jit(solution)/shard_map/pallas_call | solution.py:53
  (161 shorter events, 49.9 us)
Async XLA Ops:
  4.4 8.7 %collective-permute-start.2 = (bf16[40,960]{1,0:T(8,128)(2,1)S(1)}, bf16[40,960]{1,0:T(8,128)(2,1)S(1)}, u32[]{:S(2)}, u32[]{:S(2)}) collective-permute-start(bf16[40,960]{1,0:T(8,128)(2,1)S(1)} %dynamic-slice_bitcast_fusion), channel_id=1, source_target_pairs={{0,16},{1,17},{2,18},{3,19},{4,20},{5,21},{6,22},{7,23},{8,24},{9,... | collective-permute-start | bytes 230408 | tf_op jit(solution)/shard_map/ppermute | solution.py:444
  11.3 49.1 %collective-permute-start = (bf16[256,640]{1,0:T(8,128)(2,1)}, bf16[256,640]{1,0:T(8,128)(2,1)S(1)}, u32[]{:S(2)}, u32[]{:S(2)}) collective-permute-start(bf16[256,640]{1,0:T(8,128)(2,1)} %get-tuple-element.119), channel_id=1, source_target_pairs={{0,2},{1,3},{2,0},{3,1},{4,6},{5,7},{6,4},{7,5},{8,10},{9,11},{10,... | collective-permute-start | bytes 983048 | tf_op jit(solution)/shard_map/ppermute | solution.py:444
  13.2 7.6 %collective-permute-start.10 = (bf16[72,768]{1,0:T(8,128)(2,1)S(1)}, bf16[72,768]{1,0:T(8,128)(2,1)S(1)}, u32[]{:S(2)}, u32[]{:S(2)}) collective-permute-start(bf16[72,768]{1,0:T(8,128)(2,1)S(1)} %constant_dynamic-slice_fusion), channel_id=1, source_target_pairs={{0,16},{1,17},{2,18},{3,19},{4,20},{5,21},{6,22},{7,23},{8,24},{9,... | collective-permute-start | bytes 331784 | tf_op jit(solution)/shard_map/ppermute | solution.py:444
  14.0 25.8 %collective-permute-start.3 = (bf16[2,40,960]{2,1,0:T(8,128)(2,1)S(1)}, bf16[2,40,960]{2,1,0:T(8,128)(2,1)S(1)}, u32[]{:S(2)}, u32[]{:S(2)}) collective-permute-start(bf16[2,40,960]{2,1,0:T(8,128)(2,1)S(1)} %pad_maximum_fusion.14), channel_id=1, source_target_pairs={{0,8},{1,9},{2,10},{3,11},{4,12},{5,13},{6,14},{7,15},{8,0},{9,1},... | collective-permute-start | bytes 460808 | tf_op jit(solution)/shard_map/ppermute | solution.py:444
  17.0 11.0 %collective-permute-start.6 = (bf16[136,576]{1,0:T(8,128)(2,1)S(1)}, bf16[136,576]{1,0:T(8,128)(2,1)S(1)}, u32[]{:S(2)}, u32[]{:S(2)}) collective-permute-start(bf16[136,576]{1,0:T(8,128)(2,1)S(1)} %fusion.11), channel_id=1, source_target_pairs={{0,16},{1,17},{2,18},{3,19},{4,20},{5,21},{6,22},{7,23},{8,24},{9,... | collective-permute-start | bytes 470024 | tf_op jit(solution)/shard_map/ppermute | solution.py:444
  20.8 10.9 %collective-permute-start.11 = (bf16[2,72,768]{2,1,0:T(8,128)(2,1)S(1)}, bf16[2,72,768]{2,1,0:T(8,128)(2,1)S(1)}, u32[]{:S(2)}, u32[]{:S(2)}) collective-permute-start(bf16[2,72,768]{2,1,0:T(8,128)(2,1)S(1)} %pad_maximum_fusion.10), channel_id=1, source_target_pairs={{0,8},{1,9},{2,10},{3,11},{4,12},{5,13},{6,14},{7,15},{8,0},{9,1},... | collective-permute-start | bytes 663560 | tf_op jit(solution)/shard_map/ppermute | solution.py:444
  28.1 10.0 %collective-permute-start.7 = (bf16[2,136,576]{2,1,0:T(8,128)(2,1)S(1)}, bf16[2,136,576]{2,1,0:T(8,128)(2,1)S(1)}, u32[]{:S(2)}, u32[]{:S(2)}) collective-permute-start(bf16[2,136,576]{2,1,0:T(8,128)(2,1)S(1)} %pad_maximum_fusion.7), channel_id=1, source_target_pairs={{0,8},{1,9},{2,10},{3,11},{4,12},{5,13},{6,14},{7,15},{8,0},{9,1},... | collective-permute-start | bytes 940040 | tf_op jit(solution)/shard_map/ppermute | solution.py:444
  31.7 12.2 %collective-permute-start.12 = (bf16[2,2,72,768]{3,2,0,1:T(8,128)(2,1)S(1)}, bf16[2,2,72,768]{3,2,0,1:T(8,128)(2,1)S(1)}, u32[]{:S(2)}, u32[]{:S(2)}) collective-permute-start(bf16[2,2,72,768]{3,2,0,1:T(8,128)(2,1)S(1)} %pad_maximum_fusion.6), channel_id=1, source_target_pairs={{0,4},{1,5},{2,6},{3,7},{4,0},{5,1},{6,2},{7,3},{8,12},{9,13},{10,... | collective-permute-start | bytes 1327112 | tf_op jit(solution)/shard_map/ppermute | solution.py:444
  38.3 20.5 %collective-permute-start.8 = (bf16[2,2,136,576]{3,2,1,0:T(8,128)(2,1)S(1)}, bf16[2,2,136,576]{3,2,1,0:T(8,128)(2,1)S(1)}, u32[]{:S(2)}, u32[]{:S(2)}) collective-permute-start(bf16[2,2,136,576]{3,2,1,0:T(8,128)(2,1)S(1)} %pad_maximum_fusion.3), channel_id=1, source_target_pairs={{0,4},{1,5},{2,6},{3,7},{4,0},{5,1},{6,2},{7,3},{8,12},{9,13},{10,... | collective-permute-start | bytes 1880072 | tf_op jit(solution)/shard_map/ppermute | solution.py:444
  45.0 19.0 %collective-permute-start.13 = (bf16[576,768]{1,0:T(8,128)(2,1)}, bf16[576,768]{1,0:T(8,128)(2,1)}, u32[]{:S(2)}, u32[]{:S(2)}) collective-permute-start(bf16[576,768]{1,0:T(8,128)(2,1)} %bitcast.41.c00), channel_id=1, source_target_pairs={{0,2},{1,3},{2,0},{3,1},{4,6},{5,7},{6,4},{7,5},{8,10},{9,11},{10,... | collective-permute-start | bytes 2654216 | tf_op jit(solution)/shard_map/ppermute | solution.py:444
  46.8 17.0 %collective-permute-start.4 = (bf16[2,2,40,960]{3,2,1,0:T(8,128)(2,1)S(1)}, bf16[2,2,40,960]{3,2,1,0:T(8,128)(2,1)S(1)}, u32[]{:S(2)}, u32[]{:S(2)}) collective-permute-start(bf16[2,2,40,960]{3,2,1,0:T(8,128)(2,1)S(1)} %pad_maximum_fusion.9), channel_id=1, source_target_pairs={{0,4},{1,5},{2,6},{3,7},{4,0},{5,1},{6,2},{7,3},{8,12},{9,13},{10,... | collective-permute-start | bytes 921608 | tf_op jit(solution)/shard_map/ppermute | solution.py:444
  60.4 20.7 %collective-permute-start.9 = (bf16[8,136,576]{2,1,0:T(8,128)(2,1)}, bf16[8,136,576]{2,1,0:T(8,128)(2,1)}, u32[]{:S(2)}, u32[]{:S(2)}) collective-permute-start(bf16[8,136,576]{2,1,0:T(8,128)(2,1)} %bitcast.34.bm), channel_id=1, source_target_pairs={{0,1},{1,0},{2,3},{3,2},{4,5},{5,4},{6,7},{7,6},{8,9},{9,8},{10,11... | collective-permute-start | bytes 3760136 | tf_op jit(solution)/shard_map/ppermute | solution.py:444
  63.9 17.2 %collective-permute-start.14 = (bf16[576,768]{1,0:T(8,128)(2,1)}, bf16[576,768]{1,0:T(8,128)(2,1)}, u32[]{:S(2)}, u32[]{:S(2)}) collective-permute-start(bf16[576,768]{1,0:T(8,128)(2,1)} %bitcast.41.c00), channel_id=1, source_target_pairs={{0,1},{1,0},{2,3},{3,2},{4,5},{5,4},{6,7},{7,6},{8,9},{9,8},{10,11... | collective-permute-start | bytes 2654216 | tf_op jit(solution)/shard_map/ppermute | solution.py:444
  64.0 17.1 %collective-permute-start.15 = (bf16[576,768]{1,0:T(8,128)(2,1)}, bf16[576,768]{1,0:T(8,128)(2,1)}, u32[]{:S(2)}, u32[]{:S(2)}) collective-permute-start(bf16[576,768]{1,0:T(8,128)(2,1)} %collective-permute-done.13.c10), channel_id=1, source_target_pairs={{0,1},{1,0},{2,3},{3,2},{4,5},{5,4},{6,7},{7,6},{8,9},{9,8},{10,11... | collective-permute-start | bytes 2654216 | tf_op jit(solution)/shard_map/ppermute | solution.py:444
  94.4 7.4 %collective-permute-start.16 = (bf16[2,2,2,2,72,768]{5,4,3,2,1,0:T(8,128)(2,1)}, bf16[2,2,2,2,72,768]{5,4,3,2,1,0:T(8,128)(2,1)S(1)}, u32[]{:S(2)}, u32[]{:S(2)}) collective-permute-start(bf16[2,2,2,2,72,768]{5,4,3,2,1,0:T(8,128)(2,1)} %get-tuple-element.62), channel_id=1, source_target_pairs={{0,1},{1,0},{2,3},{3,2},{4,5},{5,4},{6,7},{7,6},{8,9},{9,8},{10,11... | collective-permute-start | bytes 5308424 | tf_op jit(solution)/shard_map/ppermute | solution.py:444
  100.3 19.1 %collective-permute-start.27 = (bf16[2,2,2,72,576]{4,3,2,1,0:T(8,128)(2,1)}, bf16[2,2,2,72,576]{4,3,2,1,0:T(8,128)(2,1)}, u32[]{:S(2)}, u32[]{:S(2)}) collective-permute-start(bf16[2,2,2,72,576]{4,3,2,1,0:T(8,128)(2,1)} %slice_bitcast_fusion.2), channel_id=1, source_target_pairs={{0,2},{1,3},{2,0},{3,1},{4,6},{5,7},{6,4},{7,5},{8,10},{9,11},{10,... | collective-permute-start | bytes 1990664 | tf_op jit(solution)/shard_map/ppermute | solution.py:444
  115.2 7.1 %collective-permute-start.18 = (bf16[2,256,384]{2,1,0:T(8,128)(2,1)S(1)}, bf16[2,256,384]{2,1,0:T(8,128)(2,1)S(1)}, u32[]{:S(2)}, u32[]{:S(2)}) collective-permute-start(bf16[2,256,384]{2,1,0:T(8,128)(2,1)S(1)} %get-tuple-element.69), channel_id=1, source_target_pairs={{0,1},{1,0},{2,3},{3,2},{4,5},{5,4},{6,7},{7,6},{8,9},{9,8},{10,11... | collective-permute-start | bytes 1179656 | tf_op jit(solution)/shard_map/ppermute | solution.py:444
  115.3 30.4 %collective-permute-start.20 = (bf16[2,2,2,2,80,256]{5,4,3,2,1,0:T(8,128)(2,1)}, bf16[2,2,2,2,80,256]{5,4,3,2,1,0:T(8,128)(2,1)S(1)}, u32[]{:S(2)}, u32[]{:S(2)}) collective-permute-start(bf16[2,2,2,2,80,256]{5,4,3,2,1,0:T(8,128)(2,1)} %get-tuple-element.72), channel_id=1, source_target_pairs={{0,1},{1,0},{2,3},{3,2},{4,5},{5,4},{6,7},{7,6},{8,9},{9,8},{10,11... | collective-permute-start | bytes 1966088 | tf_op jit(solution)/shard_map/ppermute | solution.py:444
  115.8 42.7 %collective-permute-start.33 = (bf16[2,2,2,72,768]{4,3,2,1,0:T(8,128)(2,1)S(1)}, bf16[2,2,2,72,768]{4,3,2,1,0:T(8,128)(2,1)S(1)}, u32[]{:S(2)}, u32[]{:S(2)}) collective-permute-start(bf16[2,2,2,72,768]{4,3,2,1,0:T(8,128)(2,1)S(1)} %slice_bitcast_fusion), channel_id=1, source_target_pairs={{0,4},{1,5},{2,6},{3,7},{4,0},{5,1},{6,2},{7,3},{8,12},{9,13},{10,... | collective-permute-start | bytes 2654216 | tf_op jit(solution)/shard_map/ppermute | solution.py:444
  120.8 24.6 %collective-permute-start.28 = (bf16[2,2,72,576]{3,2,1,0:T(8,128)(2,1)S(1)}, bf16[2,2,72,576]{3,2,1,0:T(8,128)(2,1)S(1)}, u32[]{:S(2)}, u32[]{:S(2)}) collective-permute-start(bf16[2,2,72,576]{3,2,1,0:T(8,128)(2,1)S(1)} %slice_bitcast_fusion.6), channel_id=1, source_target_pairs={{0,4},{1,5},{2,6},{3,7},{4,0},{5,1},{6,2},{7,3},{8,12},{9,13},{10,... | collective-permute-start | bytes 995336 | tf_op jit(solution)/shard_map/ppermute | solution.py:444
  122.5 74.2 %collective-permute-start.19 = (bf16[256,384]{1,0:T(8,128)(2,1)S(1)}, bf16[256,384]{1,0:T(8,128)(2,1)S(1)}, u32[]{:S(2)}, u32[]{:S(2)}) collective-permute-start(bf16[256,384]{1,0:T(8,128)(2,1)S(1)} %get-tuple-element.116), channel_id=1, source_target_pairs={{0,2},{1,3},{2,0},{3,1},{4,6},{5,7},{6,4},{7,5},{8,10},{9,11},{10,... | collective-permute-start | bytes 589832 | tf_op jit(solution)/shard_map/ppermute | solution.py:444
  151.4 6.5 %collective-permute-start.30 = (bf16[72,576]{1,0:T(8,128)(2,1)S(1)}, bf16[72,576]{1,0:T(8,128)(2,1)S(1)}, u32[]{:S(2)}, u32[]{:S(2)}) collective-permute-start(bf16[72,576]{1,0:T(8,128)(2,1)S(1)} %slice_bitcast_fusion.20), channel_id=1, source_target_pairs={{0,16},{1,17},{2,18},{3,19},{4,20},{5,21},{6,22},{7,23},{8,24},{9,... | collective-permute-start | bytes 248840 | tf_op jit(solution)/shard_map/ppermute | solution.py:444
  153.3 7.9 %collective-permute-start.21 = (bf16[2,2,2,80,256]{4,3,2,1,0:T(8,128)(2,1)S(1)}, bf16[2,2,2,80,256]{4,3,2,1,0:T(8,128)(2,1)S(1)}, u32[]{:S(2)}, u32[]{:S(2)}) collective-permute-start(bf16[2,2,2,80,256]{4,3,2,1,0:T(8,128)(2,1)S(1)} %slice_bitcast_fusion.8), channel_id=1, source_target_pairs={{0,4},{1,5},{2,6},{3,7},{4,0},{5,1},{6,2},{7,3},{8,12},{9,13},{10,... | collective-permute-start | bytes 983048 | tf_op jit(solution)/shard_map/ppermute | solution.py:444
  157.9 36.0 %collective-permute-start.31 = (bf16[72,576]{1,0:T(8,128)(2,1)S(1)}, bf16[72,576]{1,0:T(8,128)(2,1)S(1)}, u32[]{:S(2)}, u32[]{:S(2)}) collective-permute-start(bf16[72,576]{1,0:T(8,128)(2,1)S(1)} %fusion.9.p00), channel_id=1, source_target_pairs={{0,2},{1,3},{2,0},{3,1},{4,6},{5,7},{6,4},{7,5},{8,10},{9,11},{10,... | collective-permute-start | bytes 248840 | tf_op jit(solution)/shard_map/ppermute | solution.py:444
  161.4 7.2 %collective-permute-start.22 = (bf16[2,2,80,256]{3,2,1,0:T(8,128)(2,1)S(1)}, bf16[2,2,80,256]{3,2,1,0:T(8,128)(2,1)S(1)}, u32[]{:S(2)}, u32[]{:S(2)}) collective-permute-start(bf16[2,2,80,256]{3,2,1,0:T(8,128)(2,1)S(1)} %slice_bitcast_fusion.16), channel_id=1, source_target_pairs={{0,2},{1,3},{2,0},{3,1},{4,6},{5,7},{6,4},{7,5},{8,10},{9,11},{10,... | collective-permute-start | bytes 491528 | tf_op jit(solution)/shard_map/ppermute | solution.py:444
  162.1 13.3 %collective-permute-start.34 = (bf16[2,2,72,768]{3,2,1,0:T(8,128)(2,1)S(1)}, bf16[2,2,72,768]{3,2,1,0:T(8,128)(2,1)S(1)}, u32[]{:S(2)}, u32[]{:S(2)}) collective-permute-start(bf16[2,2,72,768]{3,2,1,0:T(8,128)(2,1)S(1)} %slice_bitcast_fusion.4), channel_id=1, source_target_pairs={{0,2},{1,3},{2,0},{3,1},{4,6},{5,7},{6,4},{7,5},{8,10},{9,11},{10,... | collective-permute-start | bytes 1327112 | tf_op jit(solution)/shard_map/ppermute | solution.py:444
  168.6 7.2 %collective-permute-start.23 = (bf16[2,80,256]{2,1,0:T(8,128)(2,1)S(1)}, bf16[2,80,256]{2,1,0:T(8,128)(2,1)S(1)}, u32[]{:S(2)}, u32[]{:S(2)}) collective-permute-start(bf16[2,80,256]{2,1,0:T(8,128)(2,1)S(1)} %slice_bitcast_fusion.22), channel_id=1, source_target_pairs={{0,8},{1,9},{2,10},{3,11},{4,12},{5,13},{6,14},{7,15},{8,0},{9,1},... | collective-permute-start | bytes 245768 | tf_op jit(solution)/shard_map/ppermute | solution.py:444
  175.4 6.1 %collective-permute-start.35 = (bf16[2,72,768]{2,1,0:T(8,128)(2,1)S(1)}, bf16[2,72,768]{2,1,0:T(8,128)(2,1)S(1)}, u32[]{:S(2)}, u32[]{:S(2)}) collective-permute-start(bf16[2,72,768]{2,1,0:T(8,128)(2,1)S(1)} %slice_bitcast_fusion.10), channel_id=1, source_target_pairs={{0,8},{1,9},{2,10},{3,11},{4,12},{5,13},{6,14},{7,15},{8,0},{9,1},... | collective-permute-start | bytes 663560 | tf_op jit(solution)/shard_map/ppermute | solution.py:444
  181.7 7.3 %collective-permute-start.36 = (bf16[72,768]{1,0:T(8,128)(2,1)S(1)}, bf16[72,768]{1,0:T(8,128)(2,1)S(1)}, u32[]{:S(2)}, u32[]{:S(2)}) collective-permute-start(bf16[72,768]{1,0:T(8,128)(2,1)S(1)} %slice_bitcast_fusion.18), channel_id=1, source_target_pairs={{0,16},{1,17},{2,18},{3,19},{4,20},{5,21},{6,22},{7,23},{8,24},{9,... | collective-permute-start | bytes 331784 | tf_op jit(solution)/shard_map/ppermute | solution.py:444
  182.7 7.0 %collective-permute-start.24 = (bf16[80,256]{1,0:T(8,128)(2,1)S(1)}, bf16[80,256]{1,0:T(8,128)(2,1)S(1)}, u32[]{:S(2)}, u32[]{:S(2)}) collective-permute-start(bf16[80,256]{1,0:T(8,128)(2,1)S(1)} %slice_bitcast_fusion.24), channel_id=1, source_target_pairs={{0,16},{1,17},{2,18},{3,19},{4,20},{5,21},{6,22},{7,23},{8,24},{9,... | collective-permute-start | bytes 122888 | tf_op jit(solution)/shard_map/ppermute | solution.py:444
  193.9 9.2 %collective-permute-start.38 = (bf16[2,72,768]{2,1,0:T(8,128)(2,1)S(1)}, bf16[2,72,768]{2,1,0:T(8,128)(2,1)S(1)}, u32[]{:S(2)}, u32[]{:S(2)}) collective-permute-start(bf16[2,72,768]{2,1,0:T(8,128)(2,1)S(1)} %pad_maximum_fusion.11), channel_id=1, source_target_pairs={{0,1},{1,0},{2,3},{3,2},{4,5},{5,4},{6,7},{7,6},{8,9},{9,8},{10,11... | collective-permute-start | bytes 663560 | tf_op jit(solution)/shard_map/ppermute | solution.py:444
  195.8 5.9 %collective-permute-start.26 = (bf16[2,80,256]{2,1,0:T(8,128)(2,1)}, bf16[2,80,256]{2,1,0:T(8,128)(2,1)S(1)}, u32[]{:S(2)}, u32[]{:S(2)}) collective-permute-start(bf16[2,80,256]{2,1,0:T(8,128)(2,1)} %pad_maximum_fusion.15), channel_id=1, source_target_pairs={{0,1},{1,0},{2,3},{3,2},{4,5},{5,4},{6,7},{7,6},{8,9},{9,8},{10,11... | collective-permute-start | bytes 245768 | tf_op jit(solution)/shard_map/ppermute | solution.py:444
  (19 other events, 133.7 us)
where the time goes:
time: 205 us
  waiting for transfers between devices  93.1 us (45%)
  Pallas kernels  44 us (21%)
  starting transfers between devices  41.3 us (20%)
  other arithmetic  16.4 us (8%)
  local copies, waits for them, and re-layouts  8.78 us (4%)
    ppermute x39, waiting for transfers between devices, swap(): return lax.ppermute(value, ('fsdp', 'seq'), pairs)  93.1 us
    pallas_call x7, Pallas kernels, call(): pl.pallas_call(kernel, out_shape=outs, in_specs=specs, out_specs=whole(*o...  44 us
    ppermute x39, starting transfers between devices, swap(): return lax.ppermute(value, ('fsdp', 'seq'), pairs)  41.3 us
    unnamed x30, local copies, waits for them, and re-layouts  5.24 us
    convert_element_type x16, other arithmetic, add(): return (keep.astype(F32) + got.astype(F32)).astype(BF)  4.54 us
  transfers between devices with their start and end apart: 39, of which 18 were waited for; matrix products, arithmetic and copies ran while one was open for 10% of the time, Pallas kernels for 14%

commit v1 on v0

--- a/solution.py
+++ b/solution.py
@@ -57,7 +57,7 @@
         out_specs=whole(*outs),
         scratch_shapes=[pltpu.VMEM(shape, F32) for shape in scratch],
         compiler_params=pltpu.CompilerParams(vmem_limit_bytes=52 * 1024 * 1024),
-        cost_estimate=pl.CostEstimate(flops=flops, bytes_accessed=moved, transcendentals=0),
+        cost_estimate=pl.CostEstimate(flops=int(flops), bytes_accessed=moved, transcendentals=0),
     )(*scalars, *arrays)
 
 
@@ -233,47 +233,90 @@
     return jnp.where(flag != 0, b, a)
 
 
-def first_forward(order, length, d_rows, n_bias, meta, blocks, am, ao, cos, sin, mask,
+class Blocks:
+    def __init__(self, *refs):
+        self.refs = refs
+        self.shape = (len(refs),) + refs[0].shape
+
+    def __getitem__(self, key):
+        return jnp.stack([ref[key[1:]] for ref in self.refs])
+
+
+def cut_qkv(core_bit, meta, w, bias, gains, out_o, all_s):
+    rows = w.shape[0]
+    n = bias.shape[1]
+    all_s[:rows, :] = w[...].astype(F32)
+    all_s[rows:, :] = jnp.zeros((8, w.shape[1]), F32)
+    all_s[rows : rows + 1, :n] = bias[...].astype(F32)
+    for i in range(2):
+        all_s[rows : rows + 1, n + rows * i : n + rows * (i + 1)] = gains[i : i + 1, :].astype(F32)
+    half = out_o.shape[0]
+    at = pl.multiple_of((meta[0] & core_bit) * half, 8)
+    out_o[...] = all_s[pl.ds(at, half), :].astype(BF)
+
+
+def first_forward(order, length, d_rows, n_bias, meta, b0, b1, b2, b3, a00, a10, a01, a11, cos, sin, mask,
                   att_o, q_o, k_o, v_o, lse_o, w_o, gain_o, w_s, b_s):
-    core = meta[0] & 1
-    cut = am.shape[1]
-    bias, gains = [], [[], []]
-    for f in range(am.shape[0]):
-        mine, other = am[f].astype(F32), ao[f].astype(F32)
-        low, high = chosen(core, mine, other), chosen(core, other, mine)
-        w_s[d_rows * f : d_rows * f + cut, :] = low
-        w_s[d_rows * f + cut : d_rows * (f + 1), :] = high[: d_rows - cut]
-        line = high[d_rows - cut : d_rows - cut + 1]
-        bias.append(line[:, :n_bias])
-        for i in range(2):
-            gains[i].append(line[:, n_bias + d_rows * i : n_bias + d_rows * (i + 1)])
-    w_o[...] = w_s[...].astype(BF)
-    b_s[...] = jnp.concatenate(bias, axis=1)
+    blocks = Blocks(b0, b1, b2, b3)
+    core, x = meta[0] & 1, meta[1] & 1
+    cut = a00.shape[2]
+    for x_rel, c_rel, piece in ((0, 0, a00), (1, 0, a10), (0, 1, a01), (1, 1, a11)):
+        for z0 in range(2):
+            for z1 in range(2):
+                at = (z1 * 4 + z0 * 2 + (x ^ x_rel)) * 2 * cut + (core ^ c_rel) * cut
+                w_s[pl.ds(pl.multiple_of(at, 8), cut), :] = piece[z0, z1].astype(F32)
+    n_f = w_s.shape[0] // (2 * cut)
+    starts = [2 * cut * f for f in range(n_f)]
+    w_o[...] = jnp.concatenate([w_s[at : at + d_rows, :] for at in starts], axis=0).astype(BF)
+    lines = [w_s[at + d_rows : at + d_rows + 1, :] for at in starts]
+    b_s[...] = jnp.concatenate([line[:, :n_bias] for line in lines], axis=1)
     for i in range(2):
-        gain_o[i : i + 1, :] = jnp.concatenate(gains[i], axis=1)
+        at = n_bias + d_rows * i
+        gain_o[i : i + 1, :] = jnp.concatenate([line[:, at : at + d_rows] for line in lines], axis=1)
     wide = QW + 64
     attention_forward(order, length, meta, blocks, w_o[:, :wide], w_o[:, QW:], b_s[:, :wide], b_s[:, QW:],
                       gain_o[0:1, :], cos, sin, mask, att_o, q_o, k_o, v_o, lse_o)
 
 
+def turned(out, value):
+    length = out.shape[2]
+    for b in range(out.shape[0]):
+        out[b] = value[length * b : length * (b + 1)].T.astype(out.dtype)
+
+
 def rel(meta, f):
     r = f ^ meta[1]
     return r & 1, (r >> 1) & 1, (r >> 2) & 1
 
 
-def feed_forward_pieces(d_rows, ff_rows, meta, attended, source, bm, bo, c00, c10, c01, c11, gains, cot, weight,
+def feed_forward_pieces(d_rows, ff_rows, meta, attended, source, b00, b10, b01, b11,
+                        g000, g100, g010, g110, g001, g101, g011, g111, gains, cot, weight,
                         out_o, gk_o, gg_o, dk_o, dg_o, mid_o, attg_o, gain_o, down_s, wout_s):
-    core, y = meta[0] & 1, (meta[0] >> 1) & 1
-    n_f = bm.shape[0]
+    core, y, x_own = meta[0] & 1, (meta[0] >> 1) & 1, meta[1] & 1
+    n_f = 8
     hf = n_f // 2
     part_d = ff_rows // 4
     part_o = d_rows // 3
-    cut = bm.shape[1] - ff_rows // 2
+    cut = b00.shape[2] - ff_rows // 2
+
+    def b_rows(z0, z1, x, c, rows):
+        low = chosen(x_own ^ x, b00[z0, z1, rows, :], b10[z0, z1, rows, :])
+        high = chosen(x_own ^ x, b01[z0, z1, rows, :], b11[z0, z1, rows, :])
+        return chosen(core ^ c, low, high)
+
+    def quarter(near, far):
+        parts = []
+        for f in range(n_f):
+            z1, z0, x = f >> 2, (f >> 1) & 1, f & 1
+            mine, other = near[z0, z1].astype(F32), far[z0, z1].astype(F32)
+            parts.append(chosen(x_own ^ x, mine, other))
+        return jnp.concatenate(parts, axis=0).astype(BF)
+
     wo = []
     for f in range(n_f):
-        mine, other = bm[f, ff_rows // 2 :, :].astype(F32), bo[f, ff_rows // 2 :, :].astype(F32)
-        wo.append(chosen(core, mine, other))
-        wo.append(chosen(core, other, mine)[: d_rows - cut])
+        z1, z0, x = f >> 2, (f >> 1) & 1, f & 1
+        wo.append(b_rows(z0, z1, x, 0, slice(ff_rows // 2, None)).astype(F32))
+        wo.append(b_rows(z0, z1, x, 1, slice(ff_rows // 2, None)).astype(F32)[: d_rows - cut])
     wo = jnp.concatenate(wo, axis=0).astype(BF)
     att = attended[...]
     middle = source[...].astype(F32) + dot(att, wo, 1, 0)
@@ -284,14 +327,15 @@
     feed_grad = out_grad.astype(BF)
     feed = back = None
     for c_rel in (1, 0):
-        first_q, second_q = (c01, c11) if c_rel else (c00, c10)
-        wg = chosen(y, first_q[...], second_q[...])
-        wu = chosen(y, second_q[...], first_q[...])
+        first_q = quarter(g001, g101) if c_rel else quarter(g000, g100)
+        second_q = quarter(g011, g111) if c_rel else quarter(g010, g110)
+        wg = chosen(y, first_q, second_q)
+        wu = chosen(y, second_q, first_q)
         h = core ^ c_rel
         wd = []
         for i in range(hf):
-            mine, other = bm[hf * h + i, : ff_rows // 2, :], bo[hf * h + i, : ff_rows // 2, :]
-            wd += [chosen(core, mine, other), chosen(core, other, mine)]
+            for c in range(2):
+                wd.append(b_rows(i >> 1, h, i & 1, c, slice(0, ff_rows // 2)))
         wd = jnp.concatenate(wd, axis=0)
         gate = dot(second, wg, 1, 0)
         up = dot(second, wu, 1, 0)
@@ -318,7 +362,7 @@
             for f in range(n_f):
                 x, z0, z1 = rel(meta, f)
                 to[x, y ^ yy, z0, z1] = wgrad[d_rows * f : d_rows * (f + 1), :].astype(BF)
-    out_o[...] = (middle + feed).astype(BF)
+    turned(out_o, middle + feed)
     gain_o[...] = jnp.sum(back * normed, axis=0, keepdims=True)
     middle_grad = out_grad + norm_back(back, g2, scale_two, normed)
     mid_o[...] = middle_grad
@@ -336,19 +380,12 @@
                 to[y ^ yy, x, z0, z1, part_d:, :] = wout_s[f, pl.ds(at, part_o), :].astype(BF)
 
 
-def attention_backward_pieces(order, length, d_rows, meta, blocks, w, gains, cos, sin, mask, q_i, k_i, v_i,
+def attention_backward_pieces(order, length, d_rows, meta, b0, b1, b2, b3, w, gains, cos, sin, mask, q_i, k_i, v_i,
                               lse, attg, gain_two, dq_o, dk_o, dg_o, rk_o, rg_o, w_s, bias_s, gain_s, small_s):
-    class Rows:
-        def __init__(self, ref, base):
-            self.ref, self.base = ref, base
-
-        def __setitem__(self, key, value):
-            if key is not Ellipsis:
-                self.ref[(key[0] - self.base,) + key[1:]] = value
-
+    blocks = Blocks(b0, b1, b2, b3)
     half = len(order) // 2
 
-    class Blocks:
+    class Pieces:
         def __setitem__(self, key, value):
             ref = dk_o if key[0] < half else dg_o
             ref[(key[0] % half,) + key[1:]] = value
@@ -361,7 +398,7 @@
 
     wide = QW + 64
     attention_backward(order, length, meta, blocks, w[:, :wide], w[:, QW:], gains[0:1, :], cos, sin, mask,
-                       q_i, k_i, v_i, lse, attg, dq_o, Blocks(), Wgrad(), bias_s, gain_s)
+                       q_i, k_i, v_i, lse, attg, dq_o, Pieces(), Wgrad(), bias_s, gain_s)
     n_f = small_s.shape[0]
     qk, v = (QW + KW) // n_f, KW // n_f
     bias, g1, g2 = bias_s[...], gain_s[...], gain_two[...]
@@ -392,20 +429,20 @@
     kv = (own[...].astype(F32) + other[...].astype(F32)).astype(BF)
     first_grad = dot(dq[:, :QW], w[:, :QW], 1, 1) + dot(kv, w[:, QW:], 1, 1)
     scale_one, normed = norm_parts(source[...].astype(F32))
-    out_o[...] = mid[...] + norm_back(first_grad, gains[0:1, :], scale_one, normed)
-
-
-def place_gate(meta, p00, p10, pc, out_o):
+    turned(out_o, mid[...] + norm_back(first_grad, gains[0:1, :], scale_one, normed))
+
+
+def place_gate(meta, p00, p10, p01, p11, out_o):
     seq = meta[0]
     n = p00.shape[1]
-    for piece, o in ((p00[...], 0), (p10[...], 2), (pc[0], 1), (pc[1], 3)):
+    for piece, o in ((p00[...], 0), (p10[...], 2), (p01[...], 1), (p11[...], 3)):
         out_o[:, pl.ds(pl.multiple_of((seq ^ o) * n, 128), n)] = piece.astype(F32)
 
 
-def place_down(part_d, meta, p00, p10, pc, out_o, wout_o):
+def place_down(part_d, meta, p00, p10, p01, p11, out_o, wout_o):
     seq = meta[0]
     part_o = p00.shape[0] - part_d
-    for piece, o in ((p00[...], 0), (p10[...], 2), (pc[0], 1), (pc[1], 3)):
+    for piece, o in ((p00[...], 0), (p10[...], 2), (p01[...], 1), (p11[...], 3)):
         piece = piece.astype(F32)
         to = seq ^ o
         out_o[pl.ds(pl.multiple_of(to * part_d, 16), part_d), :] = piece[:part_d]
@@ -415,10 +452,10 @@
             wout_o[pl.ds(pl.multiple_of(to * part_o, 8), part_o), :] = piece[part_d:]
 
 
-def place_qkv(qk, v, meta, p00, p10, pc, w_o, bqk_o, bv_o, gains_o, all_s):
+def place_qkv(qk, v, meta, p00, p10, p01, p11, w_o, bqk_o, bv_o, gains_o, all_s):
     seq = meta[0]
     n = p00.shape[1]
-    for piece, o in ((p00[...], 0), (p10[...], 2), (pc[0], 1), (pc[1], 3)):
+    for piece, o in ((p00[...], 0), (p10[...], 2), (p01[...], 1), (p11[...], 3)):
         all_s[:, pl.ds(pl.multiple_of((seq ^ o) * n, 128), n)] = piece.astype(F32)
     d_rows = w_o.shape[0]
     w_o[:, :QW] = all_s[:d_rows, 2 * KW : 2 * KW + QW]
@@ -446,8 +483,8 @@
     def bit(self, mask):
         return (self.index & mask) != 0
 
-    def both(self, mine, mask, axis):
-        other = self.swap(mine, mask)
+    def both(self, mine, mask, axis, other=None):
+        other = self.swap(mine, mask) if other is None else other
         high = self.bit(mask)
         return jnp.stack([jnp.where(high, other, mine), jnp.where(high, mine, other)], axis=axis)
 
@@ -712,21 +749,24 @@
     meta = jnp.stack([seq_index, lax.axis_index("fsdp")]).astype(jnp.int32)
     source = hidden.reshape(rows, width)
 
-    small = jnp.concatenate([b_qkv, norm_gains.reshape(-1)])
-    extra = jnp.zeros((8, qkv_w), BF).at[:, : small.shape[0]].set(small[None])
-    shard_a = jnp.concatenate([w_qkv, extra], axis=0).reshape(2, -1, qkv_w)
-    a = net.half(shard_a, core, 0)
-    a = net.both(a, zfar, 0)
+    (a0,) = call(
+        functools.partial(cut_qkv, core),
+        [meta],
+        [w_qkv, b_qkv[None], norm_gains],
+        [sds(((d_rows + 8) // 2, qkv_w), BF)],
+        1e8,
+        [(d_rows + 8, qkv_w)],
+    )
+    a1 = net.both(a0, zfar, 0)
 
     ids = segment_ids.reshape(rows, 1).astype(BF)
     block = jnp.concatenate([source, jnp.broadcast_to(ids, (rows, 64))], axis=1)
-    blocks = jnp.stack([block, net.swap(block, ybit)])
-    blocks = jnp.concatenate([blocks, net.swap(blocks, core)], axis=0)
-
-    gu = lax.dynamic_slice_in_dim(
-        w_gate_up, seq_index * (2 * units // n_seq), 2 * units // n_seq, axis=1
-    )
-    gu = after(gu, a)
+    block = after(block, a0)
+    block_y = net.swap(block, ybit)
+    block_c = net.swap(block, core)
+
+    quarter = 2 * units // n_seq
+    gu0 = lax.dynamic_slice_in_dim(after(w_gate_up, a0), seq_index * quarter, quarter, axis=1)
     half_b = jnp.concatenate(
         [
             w_down.reshape(2, ff_rows // 2, width),
@@ -734,35 +774,39 @@
         ],
         axis=1,
     )
-    b = after(net.half(half_b, core, 0), a)
-    gu = net.both(gu, zfar, 0)
-    b = net.both(b, zfar, 0)
-    a = net.both(a, znear, 1)
-    a = net.both(a, xbit, 2).reshape(n_fsdp, -1, qkv_w)
-    gu = net.both(gu, znear, 1)
-    b = net.both(b, znear, 1)
-    a_other = net.swap(a, core)
-    gu = net.both(gu, xbit, 2).reshape(n_fsdp * d_rows, -1)
-    b = net.both(b, xbit, 2).reshape(n_fsdp, -1, width)
-    gu_c = net.swap(gu, core)
-    gu_y = net.swap(gu, ybit)
-    b_other = net.swap(b, core)
-    gu_yc = net.swap(gu_y, core)
+    b0 = net.half(after(half_b, a0), core, 0)
+    a2 = net.both(a1, znear, 0)
+    a_x = net.swap(a2, xbit)
+    a_c = net.swap(a2, core)
+    gu1 = net.both(gu0, zfar, 0)
+    b1 = net.both(b0, zfar, 0)
+    gu2 = net.both(after(gu1, a2), znear, 0)
+    b2 = net.both(after(b1, a2), znear, 0)
+    block_yc = net.swap(block_y, core)
+    a_xc = net.swap(a_x, core)
+    gu2 = after(gu2, a_x)
+    b2 = after(b2, a_x)
+    gu_x = net.swap(gu2, xbit)
+    gu_y = net.swap(gu2, ybit)
+    b_x = net.swap(b2, xbit)
+    gu_c = net.swap(gu2, core)
+    b_c = net.swap(b2, core)
+    a_xc = after(a_xc, gu2, b2)
 
     cos_t, sin_t = rope_tables(full_length, n_seq)
     block_ids = [seq_index ^ o for o in order]
-    seg_all = blocks[..., width].reshape(n_seq, seqs, length).transpose(1, 0, 2)
+    blocks = [block, block_y, block_c, block_yc]
+    seg_all = jnp.stack([b[:, width].reshape(seqs, length) for b in blocks], axis=1)
     own_places = seq_index * length + jnp.arange(length, dtype=jnp.int32)
     key_places = jnp.stack(block_ids)[:, None] * length + jnp.arange(length, dtype=jnp.int32)
     allowed = (seg_all[:, 0, :, None] == seg_all.reshape(seqs, 1, -1)) & (
         own_places[None, :, None] >= key_places.reshape(1, 1, -1)
     )
     allowed = allowed.astype(F32)
-    n_all = n_seq * rows
     attended, q_s, k_s, v_s, lse, wf, gains = call(
         functools.partial(first_forward, order, length, d_rows, n_bias),
         [meta],
-        [blocks, a, a_other, cos_t, sin_t, allowed],
+        [*blocks, a2, a_x, a_c, a_xc, cos_t, sin_t, allowed],
         [
             sds((rows, QW), BF),
             sds((seqs, KV_HEADS, GROUP * length, HEAD_DIM), BF),
@@ -772,9 +816,16 @@
             sds((width, qkv_w), BF),
             sds((2, width), F32),
         ],
-        2 * n_all * width * 2 * KW + 2 * rows * width * QW + 4 * rows * full_length * QW,
-        [(width, qkv_w), (1, qkv_w)],
-    )
+        1.2e10,
+        [(n_fsdp * (d_rows + 8), qkv_w), (1, qkv_w)],
+    )
+    gu_x, gu_y, b_x = after(gu_x, attended), after(gu_y, attended), after(b_x, attended)
+    gu_xy = net.swap(gu_x, ybit)
+    gu_yc = net.swap(gu_y, core)
+    gu_xc = net.swap(gu_x, core)
+    b_xc = net.swap(b_x, core)
+    gu_xyc = net.swap(gu_xy, core)
+    gate_up = [gu2, gu_x, gu_y, gu_xy, gu_c, gu_xc, gu_yc, gu_xyc]
 
     weight = tokens_micro / token_counts.astype(F32)
     weight = jnp.repeat(weight, batch * length)[:, None]
@@ -782,9 +833,9 @@
     block_out, gate_keep, gate_give, down_keep, down_give, middle_grad, attended_grad, gain_two = call(
         functools.partial(feed_forward_pieces, d_rows, ff_rows),
         [meta],
-        [attended, source, b, b_other, gu, gu_y, gu_c, gu_yc, gains, cotangent.reshape(rows, width), weight],
+        [attended, source, b2, b_x, b_c, b_xc, *gate_up, gains, cotangent.reshape(rows, width), weight],
         [
-            sds((rows, width), BF),
+            sds((seqs, width, length), BF),
             sds(lead + (d_rows, units // 2), BF),
             sds(lead + (d_rows, units // 2), BF),
             sds(lead + (ff_rows // 4 + d_rows // 3, width), BF),
@@ -793,24 +844,27 @@
             sds((rows, QW), BF),
             sds((1, width), F32),
         ],
-        6 * rows * width * 3 * units + 6 * rows * width * QW,
+        1.4e10,
         [(units // 2, width), (n_fsdp, d_rows + d_rows // 3, width)],
     )
-    block_out = block_out.reshape(hidden.shape)
+    block_out = block_out.reshape(micro, batch, width, length).swapaxes(2, 3)
 
     def add(keep, got):
         return (keep.astype(F32) + got.astype(F32)).astype(BF)
 
-    gate = add(gate_keep, net.swap(gate_give, core))
-    down = add(down_keep, net.swap(down_give, core))
-    attended_grad = after(attended_grad, gate, down)
-    gate_got = net.swap(gate[1], xbit)
-    down_got = net.swap(down[1], ybit)
+    def halves(keep, got):
+        return add(keep[0], got[0]), add(keep[1], got[1])
+
+    gate, gate_give = halves(gate_keep, net.swap(gate_give, core))
+    down, down_give = halves(down_keep, net.swap(down_give, core))
+    attended_grad = after(attended_grad, gate_give, down_give)
+    gate_got = net.swap(gate_give, xbit)
+    down_got = net.swap(down_give, ybit)
 
     dq, dkv_keep, dkv_give, rest_keep, rest_give = call(
         functools.partial(attention_backward_pieces, order, length, d_rows),
         [meta],
-        [blocks, wf, gains, cos_t, sin_t, allowed, q_s, k_s, v_s, lse, attended_grad, gain_two],
+        [*blocks, wf, gains, cos_t, sin_t, allowed, q_s, k_s, v_s, lse, attended_grad, gain_two],
         [
             sds((rows, QW + 64), BF),
             sds((2, rows, 2 * KW), BF),
@@ -818,38 +872,37 @@
             sds(lead + (d_rows + 8, 256), BF),
             sds(lead + (d_rows + 8, 256), BF),
         ],
-        4 * n_all * width * 2 * KW + 4 * rows * width * QW + 10 * rows * full_length * QW,
+        1.4e10,
         [(width, 1024), (1, qkv_w), (1, width), (n_fsdp, 8, 1024)],
     )
-    rest = add(rest_keep, net.swap(rest_give, core))
-    dkv = add(dkv_keep, net.swap(dkv_give, core))
-    rest_got = net.swap(rest[1], xbit)
-    dkv_got = net.swap(dkv[1], ybit)
-
-    gate = add(gate[0], gate_got)
-    down = add(down[0], down_got)
-    gate_got = net.swap(gate[1], ybit)
-    down_got = net.swap(down[1], xbit)
-    rest = add(rest[0], rest_got)
-    rest_got = net.swap(rest[1], ybit)
+    dkv, dkv_give = halves(dkv_keep, net.swap(dkv_give, core))
+    rest, rest_give = halves(rest_keep, after(net.swap(rest_give, core), gate_got))
+    dkv_got = net.swap(dkv_give, ybit)
+    rest_got = net.swap(rest_give, xbit)
+    down, down_give = halves(down, down_got)
+    down_got = net.swap(down_give, xbit)
+    gate, gate_give = halves(gate, gate_got)
+    gate_got = net.swap(gate_give, ybit)
     (hidden_grad,) = call(
         input_gradient_two,
         [],
-        [dq, dkv[0], dkv_got, source, middle_grad, wf, gains],
-        [sds((rows, width), F32)],
-        2 * rows * width * qkv_w,
-    )
-    hidden_grad = hidden_grad.reshape(hidden.shape)
-    gate = add(gate[0], gate_got)
-    down = add(down[0], down_got)
-    rest = add(rest[0], rest_got)
+        [dq, dkv, dkv_got, source, middle_grad, wf, gains],
+        [sds((seqs, width, length), F32)],
+        3e9,
+    )
+    rest_got = after(rest_got, hidden_grad)
+    hidden_grad = hidden_grad.reshape(micro, batch, width, length).swapaxes(2, 3)
+    rest, rest_give = halves(rest, rest_got)
+    rest_got = net.swap(rest_give, ybit)
+    parts, gots = [gate, down, rest], [gate_got, down_got, rest_got]
     for mask in (znear, zfar):
-        gots = [net.swap(part[1], mask) for part in (gate, down, rest)]
-        gate, down, rest = [add(part[0], got) for part, got in zip((gate, down, rest), gots)]
+        pairs = [halves(part, got) for part, got in zip(parts, gots)]
+        parts, gots = [keep for keep, _ in pairs], [net.swap(give, mask) for _, give in pairs]
+    gate, down, rest = [add(part, got) for part, got in zip(parts, gots)]
 
     def spread(part):
         other = net.swap(part, ybit)
-        return [part, other, net.swap(jnp.stack([part, other]), core)]
+        return [part, other, net.swap(part, core), net.swap(other, core)]
 
     (out_gate,) = call(place_gate, [meta], spread(gate), [sds((d_rows, 2 * units), F32)], 0)
     out_down, out_wout = call(

time: 205 us -> 177 us (0.86)
  waiting for transfers between devices: 93.1 us -> 82.2 us
  other arithmetic: 16.4 us -> 8.12 us
  starting transfers between devices: 41.3 us -> 35.3 us
  local copies, waits for them, and re-layouts: 8.78 us -> 5.45 us
    ppermute x39 -> x48, waiting for transfers between devices: 93.1 us -> 82.2 us  [swap(): return lax.ppermute(value, ('fsdp', 'seq'), pairs)]
    ppermute x39 -> x48, starting transfers between devices: 41.3 us -> 35.3 us  [swap(): return lax.ppermute(value, ('fsdp', 'seq'), pairs)]
    another operation x7 -> x0, other arithmetic: 5.14 us -> none
    concatenate x2, other arithmetic: 2.22 us -> 0.13 us  [the longest x1 0.09 us: on_device_tiled(): block = jnp.concatenate([source, jnp.broadcast_to(ids, (rows, 64))], axis=1)]
    pallas_call x7 -> x8, Pallas kernels: 44 us -> 45 us  [call(): pl.pallas_call(kernel, out_shape=outs, in_specs=specs, out_specs=whole(*o...]
    unnamed x30 -> x42, local copies, waits for them, and re-layouts: 5.24 us -> 4.39 us
  transfers between devices with their start and end apart: 39 -> 48, of which waited for: 18 -> 24; matrix products, arithmetic and copies ran while one was open for 10% -> 6% of each run, Pallas kernels for 14% -> 17%
where the time goes in v1:
time: 177 us
  waiting for transfers between devices  82.2 us (46%)
  Pallas kernels  45 us (25%)
  starting transfers between devices  35.3 us (20%)
  other arithmetic  8.12 us (5%)
  local copies, waits for them, and re-layouts  5.45 us (3%)
    ppermute x48, waiting for transfers between devices, swap(): return lax.ppermute(value, ('fsdp', 'seq'), pairs)  82.2 us
    pallas_call x8, Pallas kernels, call(): pl.pallas_call(kernel, out_shape=outs, in_specs=specs, out_specs=whole(*o...  45 us
    ppermute x48, starting transfers between devices, swap(): return lax.ppermute(value, ('fsdp', 'seq'), pairs)  35.3 us
    convert_element_type x16, other arithmetic, add(): return (keep.astype(F32) + got.astype(F32)).astype(BF)  4.57 us
    unnamed x42, local copies, waits for them, and re-layouts  4.39 us
  transfers between devices with their start and end apart: 48, of which 24 were waited for; matrix products, arithmetic and copies ran while one was open for 6% of the time, Pallas kernels for 17%

profile of v1, /device:TPU:0, one launch (start us, length us, event | category | flops | bytes accessed | tf_op | source)
XLA Modules:
  0.0 177.1 jit_solution(16369401093476941216)
XLA Ops:
  3.6 4.1 %collective-permute-start.3 = (bf16[40,960]{1,0:T(8,128)(2,1)S(1)}, bf16[40,960]{1,0:T(8,128)(2,1)S(1)}, u32[]{:S(2)}, u32[]{:S(2)}) collective-permute-start(bf16[40,960]{1,0:T(8,128)(2,1)S(1)} %shard_map.187), channel_id=1, source_target_pairs={{0,16},{1,17},{2,18},{3,19},{4,20},{5,21},{6,22},{7,23},{8,24},{9,... | collective-permute-start | bytes 230408 | tf_op jit(solution)/shard_map/ppermute | solution.py:481
  9.8 1.6 collective-permute-start
  11.9 2.7 %collective-permute-start.10 = (bf16[136,576]{1,0:T(8,128)(2,1)S(1)}, bf16[136,576]{1,0:T(8,128)(2,1)S(1)}, u32[]{:S(2)}, u32[]{:S(2)}) collective-permute-start(bf16[136,576]{1,0:T(8,128)(2,1)S(1)} %dynamic-slice_bitcast_fusion), channel_id=1, source_target_pairs={{0,16},{1,17},{2,18},{3,19},{4,20},{5,21},{6,22},{7,23},{8,24},{9,... | collective-permute-start | bytes 470024 | tf_op jit(solution)/shard_map/ppermute | solution.py:481
  15.1 1.6 collective-permute-start.4
  16.7 7.6 %collective-permute-done.8 = bf16[72,768]{1,0:T(8,128)(2,1)S(1)} collective-permute-done((bf16[72,768]{1,0:T(8,128)(2,1)S(1)}, bf16[72,768]{1,0:T(8,128)(2,1)S(1)}, u32[]{:S(2)}, u32[]{:S(2)}) %collective-permute-start.8) | collective-permute-done | bytes 110624 | tf_op jit(solution)/shard_map/ppermute | solution.py:481
  24.5 2.8 %collective-permute-done.10 = bf16[136,576]{1,0:T(8,128)(2,1)S(1)} collective-permute-done((bf16[136,576]{1,0:T(8,128)(2,1)S(1)}, bf16[136,576]{1,0:T(8,128)(2,1)S(1)}, u32[]{:S(2)}, u32[]{:S(2)}) %collective-permute-start.10) | collective-permute-done | bytes 156704 | tf_op jit(solution)/shard_map/ppermute | solution.py:481
  27.6 1.6 collective-permute-start.5
  29.2 2.0 %collective-permute-start.11 = (bf16[2,136,576]{2,1,0:T(8,128)(2,1)S(1)}, bf16[2,136,576]{2,1,0:T(8,128)(2,1)S(1)}, u32[]{:S(2)}, u32[]{:S(2)}) collective-permute-start(bf16[2,136,576]{2,1,0:T(8,128)(2,1)S(1)} %pad_maximum_fusion.3), channel_id=1, source_target_pairs={{0,8},{1,9},{2,10},{3,11},{4,12},{5,13},{6,14},{7,15},{8,0},{9,1},... | collective-permute-start | bytes 940040 | tf_op jit(solution)/shard_map/ppermute | solution.py:481
  31.6 5.8 %collective-permute-done.9 = bf16[2,72,768]{2,1,0:T(8,128)(2,1)S(1)} collective-permute-done((bf16[2,72,768]{2,1,0:T(8,128)(2,1)S(1)}, bf16[2,72,768]{2,1,0:T(8,128)(2,1)S(1)}, u32[]{:S(2)}, u32[]{:S(2)}) %collective-permute-start.9) | collective-permute-done | bytes 221216 | tf_op jit(solution)/shard_map/ppermute | solution.py:481
  38.2 5.9 %collective-permute-done.11 = bf16[2,136,576]{2,1,0:T(8,128)(2,1)S(1)} collective-permute-done((bf16[2,136,576]{2,1,0:T(8,128)(2,1)S(1)}, bf16[2,136,576]{2,1,0:T(8,128)(2,1)S(1)}, u32[]{:S(2)}, u32[]{:S(2)}) %collective-permute-start.11) | collective-permute-done | bytes 313376 | tf_op jit(solution)/shard_map/ppermute | solution.py:481
  47.3 1.5 collective-permute-start.12
  49.6 10.7 %shard_map.188 = (bf16[256,576]{1,0:T(8,128)(2,1)S(1)}, bf16[2,3,384,64]{3,2,1,0:T(8,128)(2,1)}, bf16[2,3,512,64]{3,2,1,0:T(8,128)(2,1)}, bf16[2,3,512,64]{3,2,1...) custom-call(s32[2]{0:T(128)S(1)} %pad_add_fusion.meta, ...), custom_call_target="tpu_custom_call" | custom-call | flops 12000000000 | bytes 6084096 | tf_op jit(solution)/shard_map/pallas_call | solution.py:53
  60.9 9.8 %collective-permute-done.12.b10 = bf16[2,2,136,576]{3,2,1,0:T(8,128)(2,1)} collective-permute-done((bf16[2,2,136,576]{3,2,1,0:T(8,128)(2,1)}, bf16[2,2,136,576]{3,2,1,0:T(8,128)(2,1)}, u32[]{:S(2)}, u32[]{:S(2)}) %collective-permute-start.12) | collective-permute-done | bytes 626720 | tf_op jit(solution)/shard_map/ppermute | solution.py:481
  75.1 13.5 %shard_map.189 = (bf16[2,576,128]{2,1,0:T(8,128)(2,1)}, bf16[2,2,2,2,72,768]{5,4,3,2,1,0:T(8,128)(2,1)}, bf16[2,2,2,2,72,768]{5,4,3,2,1,0:T(8,128)(2,1)}, bf16[2...) custom-call(s32[2]{0:T(128)S(1)} %pad_add_fusion.meta, ...), custom_call_target="tpu_custom_call" | custom-call | flops 14000000000 | bytes 14311168 | tf_op jit(solution)/shard_map/pallas_call | solution.py:53
  89.1 3.0 %collective-permute-done.23 = bf16[2,2,2,2,72,576]{5,4,3,2,1,0:T(8,128)(2,1)S(1)} collective-permute-done((bf16[2,2,2,2,72,576]{5,4,3,2,1,0:T(8,128)(2,1)}, bf16[2,2,2,2,72,576]{5,4,3,2,1,0:T(8,128)(2,1)S(1)}, u32[]{:S(2)}, u32[]{:S(2)}) %collective-permute-start.23) | collective-permute-done | bytes 1327136 | tf_op jit(solution)/shard_map/ppermute | solution.py:481
  92.1 1.9 %add_convert_fusion.2 = (bf16[1,2,2,2,72,576]{5,4,3,2,1,0:T(8,128)(2,1)S(1)}, bf16[2,2,2,72,576]{4,3,2,1,0:T(8,128)(2,1)S(1)}) fusion(bf16[2,2,2,2,72,576]{5,4,3,2,1,0:T(8,128)(2,1)S(1)} %collective-permute-done.23, bf16[2,2,2,2,72,576]{5,4,3,2,1,0:T(8,128)(2,1)} %get-tuple-element.71), kind=kLoop, calls=%fused_computation.2 | loop fusion | flops 2654208 | bytes 3981312 | tf_op jit(solution)/shard_map/convert_element_type | solution.py:853
  95.8 16.7 %collective-permute-done.35 = bf16[2,2,2,72,576]{4,3,2,1,0:T(8,128)(2,1)S(1)} collective-permute-done((bf16[2,2,2,72,576]{4,3,2,1,0:T(8,128)(2,1)S(1)}, bf16[2,2,2,72,576]{4,3,2,1,0:T(8,128)(2,1)S(1)}, u32[]{:S(2)}, u32[]{:S(2)}) %collective-permute-start.35) | collective-permute-done | bytes 663584 | tf_op jit(solution)/shard_map/ppermute | solution.py:481
  113.5 12.7 %shard_map.190 = (bf16[256,640]{1,0:T(8,128)(2,1)S(1)}, bf16[2,256,384]{2,1,0:T(8,128)(2,1)}, bf16[2,256,384]{2,1,0:T(8,128)(2,1)}, bf16[2,2,2,2,80,256]{5,4,3,2...) custom-call(s32[2]{0:T(128)S(1)} %pad_add_fusion.meta, bf16[256,640]{1,0:T(8,128)(2,1)S(1)} %pad_maximum_fusion.4.b0, ...), custom_call_target="tpu_custom_call" | custom-call | flops 14000000000 | bytes 7282432 | tf_op jit(solution)/shard_map/pallas_call | solution.py:53
  129.8 3.7 %collective-permute-done.37 = bf16[2,72,576]{2,1,0:T(8,128)(2,1)S(1)} collective-permute-done((bf16[2,72,576]{2,1,0:T(8,128)(2,1)S(1)}, bf16[2,72,576]{2,1,0:T(8,128)(2,1)S(1)}, u32[]{:S(2)}, u32[]{:S(2)}) %collective-permute-start.37) | collective-permute-done | bytes 165920 | tf_op jit(solution)/shard_map/ppermute | solution.py:481
  134.0 1.6 collective-permute-start.28
  136.4 3.2 %shard_map.191 = f32[2,576,128]{2,1,0:T(8,128)} custom-call(bf16[256,640]{1,0:T(8,128)(2,1)S(1)} %get-tuple-element.75.dq, bf16[256,384]{1,0:T(8,128)(2,1)S(1)} %get-tuple-element.120.own, bf16[256,384]{1,0:T(8,128)(2,1)S(1)} %collective-permute-done.25.other, bf16[256,576]{1,0:T(8,128)(2,1)S(1)} %bitcast.196, f32[256,576]{1,0:T(8,128)S(1)} %copy-done.5, ...), custom_call_target="tpu_custom_call" | custom-call | flops 3000000000 | bytes 3305984 | tf_op jit(solution)/shard_map/pallas_call | solution.py:53
  141.2 1.5 collective-permute-done.28
  142.7 4.9 %collective-permute-done.42 = bf16[2,2,72,768]{3,2,1,0:T(8,128)(2,1)S(1)} collective-permute-done((bf16[2,2,72,768]{3,2,1,0:T(8,128)(2,1)S(1)}, bf16[2,2,72,768]{3,2,1,0:T(8,128)(2,1)S(1)}, u32[]{:S(2)}, u32[]{:S(2)}) %collective-permute-start.42) | collective-permute-done | bytes 442400 | tf_op jit(solution)/shard_map/ppermute | solution.py:481
  147.7 1.5 collective-permute-start.43
  149.9 5.2 %collective-permute-done.43 = bf16[2,72,768]{2,1,0:T(8,128)(2,1)S(1)} collective-permute-done((bf16[2,72,768]{2,1,0:T(8,128)(2,1)S(1)}, bf16[2,72,768]{2,1,0:T(8,128)(2,1)S(1)}, u32[]{:S(2)}, u32[]{:S(2)}) %collective-permute-start.43) | collective-permute-done | bytes 221216 | tf_op jit(solution)/shard_map/ppermute | solution.py:481
  155.1 2.9 %collective-permute-start.44 = (bf16[72,768]{1,0:T(8,128)(2,1)S(1)}, bf16[72,768]{1,0:T(8,128)(2,1)S(1)}, u32[]{:S(2)}, u32[]{:S(2)}) collective-permute-start(bf16[72,768]{1,0:T(8,128)(2,1)S(1)} %fusion.29), channel_id=1, source_target_pairs={{0,16},{1,17},{2,18},{3,19},{4,20},{5,21},{6,22},{7,23},{8,24},{9,... | collective-permute-start | bytes 331784 | tf_op jit(solution)/shard_map/ppermute | solution.py:481
  158.9 3.6 %collective-permute-done.44 = bf16[72,768]{1,0:T(8,128)(2,1)S(1)} collective-permute-done((bf16[72,768]{1,0:T(8,128)(2,1)S(1)}, bf16[72,768]{1,0:T(8,128)(2,1)S(1)}, u32[]{:S(2)}, u32[]{:S(2)}) %collective-permute-start.44) | collective-permute-done | bytes 110624 | tf_op jit(solution)/shard_map/ppermute | solution.py:481
  164.9 2.5 %collective-permute-done.45.p10 = bf16[72,768]{1,0:T(8,128)(2,1)S(1)} collective-permute-done((bf16[72,768]{1,0:T(8,128)(2,1)S(1)}, bf16[72,768]{1,0:T(8,128)(2,1)S(1)}, u32[]{:S(2)}, u32[]{:S(2)}) %collective-permute-start.45) | collective-permute-done | bytes 110624 | tf_op jit(solution)/shard_map/ppermute | solution.py:481
  168.6 1.5 collective-permute-start.32
  170.1 2.6 %collective-permute-done.32.p10 = bf16[80,256]{1,0:T(8,128)(2,1)S(1)} collective-permute-done((bf16[80,256]{1,0:T(8,128)(2,1)S(1)}, bf16[80,256]{1,0:T(8,128)(2,1)S(1)}, u32[]{:S(2)}, u32[]{:S(2)}) %collective-permute-start.32) | collective-permute-done | bytes 40992 | tf_op jit(solution)/shard_map/ppermute | solution.py:481
  172.7 1.5 shard_map.193
  175.6 1.5 shard_map.194
  (163 shorter events, 33.1 us)
Async XLA Ops:
  3.6 11.5 %collective-permute-start.3 = (bf16[40,960]{1,0:T(8,128)(2,1)S(1)}, bf16[40,960]{1,0:T(8,128)(2,1)S(1)}, u32[]{:S(2)}, u32[]{:S(2)}) collective-permute-start(bf16[40,960]{1,0:T(8,128)(2,1)S(1)} %shard_map.187), channel_id=1, source_target_pairs={{0,16},{1,17},{2,18},{3,19},{4,20},{5,21},{6,22},{7,23},{8,24},{9,... | collective-permute-start | bytes 230408 | tf_op jit(solution)/shard_map/ppermute | solution.py:481
  9.7 21.7 %collective-permute-start.1 = (bf16[256,640]{1,0:T(8,128)(2,1)S(1)}, bf16[256,640]{1,0:T(8,128)(2,1)S(1)}, u32[]{:S(2)}, u32[]{:S(2)}) collective-permute-start(bf16[256,640]{1,0:T(8,128)(2,1)S(1)} %pad_maximum_fusion.4.b0), channel_id=1, source_target_pairs={{0,1},{1,0},{2,3},{3,2},{4,5},{5,4},{6,7},{7,6},{8,9},{9,8},{10,11... | collective-permute-start | bytes 983048 | tf_op jit(solution)/shard_map/ppermute | solution.py:481
  9.8 19.4 %collective-permute-start = (bf16[256,640]{1,0:T(8,128)(2,1)S(1)}, bf16[256,640]{1,0:T(8,128)(2,1)S(1)}, u32[]{:S(2)}, u32[]{:S(2)}) collective-permute-start(bf16[256,640]{1,0:T(8,128)(2,1)S(1)} %pad_maximum_fusion.4.b0), channel_id=1, source_target_pairs={{0,2},{1,3},{2,0},{3,1},{4,6},{5,7},{6,4},{7,5},{8,10},{9,11},{10,... | collective-permute-start | bytes 983048 | tf_op jit(solution)/shard_map/ppermute | solution.py:481
  11.4 13.0 %collective-permute-start.8 = (bf16[72,768]{1,0:T(8,128)(2,1)S(1)}, bf16[72,768]{1,0:T(8,128)(2,1)S(1)}, u32[]{:S(2)}, u32[]{:S(2)}) collective-permute-start(bf16[72,768]{1,0:T(8,128)(2,1)S(1)} %constant_dynamic-slice_fusion), channel_id=1, source_target_pairs={{0,16},{1,17},{2,18},{3,19},{4,20},{5,21},{6,22},{7,23},{8,24},{9,... | collective-permute-start | bytes 331784 | tf_op jit(solution)/shard_map/ppermute | solution.py:481
  11.9 15.4 %collective-permute-start.10 = (bf16[136,576]{1,0:T(8,128)(2,1)S(1)}, bf16[136,576]{1,0:T(8,128)(2,1)S(1)}, u32[]{:S(2)}, u32[]{:S(2)}) collective-permute-start(bf16[136,576]{1,0:T(8,128)(2,1)S(1)} %dynamic-slice_bitcast_fusion), channel_id=1, source_target_pairs={{0,16},{1,17},{2,18},{3,19},{4,20},{5,21},{6,22},{7,23},{8,24},{9,... | collective-permute-start | bytes 470024 | tf_op jit(solution)/shard_map/ppermute | solution.py:481
  15.1 12.3 %collective-permute-start.4 = (bf16[2,40,960]{2,1,0:T(8,128)(2,1)S(1)}, bf16[2,40,960]{2,1,0:T(8,128)(2,1)S(1)}, u32[]{:S(2)}, u32[]{:S(2)}) collective-permute-start(bf16[2,40,960]{2,1,0:T(8,128)(2,1)S(1)} %pad_maximum_fusion.7), channel_id=1, source_target_pairs={{0,8},{1,9},{2,10},{3,11},{4,12},{5,13},{6,14},{7,15},{8,0},{9,1},... | collective-permute-start | bytes 460808 | tf_op jit(solution)/shard_map/ppermute | solution.py:481
  27.5 21.3 %collective-permute-start.6 = (bf16[2,2,40,960]{3,2,1,0:T(8,128)(2,1)S(1)}, bf16[2,2,40,960]{3,2,1,0:T(8,128)(2,1)S(1)}, u32[]{:S(2)}, u32[]{:S(2)}) collective-permute-start(bf16[2,2,40,960]{3,2,1,0:T(8,128)(2,1)S(1)} %pad_maximum_fusion.5.a00), channel_id=1, source_target_pairs={{0,1},{1,0},{2,3},{3,2},{4,5},{5,4},{6,7},{7,6},{8,9},{9,8},{10,11... | collective-permute-start | bytes 921608 | tf_op jit(solution)/shard_map/ppermute | solution.py:481
  27.6 10.1 %collective-permute-start.5 = (bf16[2,2,40,960]{3,2,1,0:T(8,128)(2,1)S(1)}, bf16[2,2,40,960]{3,2,1,0:T(8,128)(2,1)S(1)}, u32[]{:S(2)}, u32[]{:S(2)}) collective-permute-start(bf16[2,2,40,960]{3,2,1,0:T(8,128)(2,1)S(1)} %pad_maximum_fusion.5.a00), channel_id=1, source_target_pairs={{0,4},{1,5},{2,6},{3,7},{4,0},{5,1},{6,2},{7,3},{8,12},{9,13},{10,... | collective-permute-start | bytes 921608 | tf_op jit(solution)/shard_map/ppermute | solution.py:481
  29.1 8.3 %collective-permute-start.9 = (bf16[2,72,768]{2,1,0:T(8,128)(2,1)S(1)}, bf16[2,72,768]{2,1,0:T(8,128)(2,1)S(1)}, u32[]{:S(2)}, u32[]{:S(2)}) collective-permute-start(bf16[2,72,768]{2,1,0:T(8,128)(2,1)S(1)} %pad_maximum_fusion.6), channel_id=1, source_target_pairs={{0,8},{1,9},{2,10},{3,11},{4,12},{5,13},{6,14},{7,15},{8,0},{9,1},... | collective-permute-start | bytes 663560 | tf_op jit(solution)/shard_map/ppermute | solution.py:481
  29.2 15.0 %collective-permute-start.11 = (bf16[2,136,576]{2,1,0:T(8,128)(2,1)S(1)}, bf16[2,136,576]{2,1,0:T(8,128)(2,1)S(1)}, u32[]{:S(2)}, u32[]{:S(2)}) collective-permute-start(bf16[2,136,576]{2,1,0:T(8,128)(2,1)S(1)} %pad_maximum_fusion.3), channel_id=1, source_target_pairs={{0,8},{1,9},{2,10},{3,11},{4,12},{5,13},{6,14},{7,15},{8,0},{9,1},... | collective-permute-start | bytes 940040 | tf_op jit(solution)/shard_map/ppermute | solution.py:481
  31.4 14.3 %collective-permute-start.2 = (bf16[256,640]{1,0:T(8,128)(2,1)S(1)}, bf16[256,640]{1,0:T(8,128)(2,1)S(1)}, u32[]{:S(2)}, u32[]{:S(2)}) collective-permute-start(bf16[256,640]{1,0:T(8,128)(2,1)S(1)} %collective-permute-done.b1), channel_id=1, source_target_pairs={{0,1},{1,0},{2,3},{3,2},{4,5},{5,4},{6,7},{7,6},{8,9},{9,8},{10,11... | collective-permute-start | bytes 983048 | tf_op jit(solution)/shard_map/ppermute | solution.py:481
  37.7 33.4 %collective-permute-start.18 = (bf16[2,2,72,768]{3,2,1,0:T(8,128)(2,1)S(1)}, bf16[2,2,72,768]{3,2,1,0:T(8,128)(2,1)S(1)}, u32[]{:S(2)}, u32[]{:S(2)}) collective-permute-start(bf16[2,2,72,768]{3,2,1,0:T(8,128)(2,1)S(1)} %pad_maximum_fusion.1.g000), channel_id=1, source_target_pairs={{0,1},{1,0},{2,3},{3,2},{4,5},{5,4},{6,7},{7,6},{8,9},{9,8},{10,11... | collective-permute-start | bytes 1327112 | tf_op jit(solution)/shard_map/ppermute | solution.py:481
  37.7 32.9 %collective-permute-start.16 = (bf16[2,2,72,768]{3,2,1,0:T(8,128)(2,1)S(1)}, bf16[2,2,72,768]{3,2,1,0:T(8,128)(2,1)}, u32[]{:S(2)}, u32[]{:S(2)}) collective-permute-start(bf16[2,2,72,768]{3,2,1,0:T(8,128)(2,1)S(1)} %pad_maximum_fusion.1.g000), channel_id=1, source_target_pairs={{0,2},{1,3},{2,0},{3,1},{4,6},{5,7},{6,4},{7,5},{8,10},{9,11},{10,... | collective-permute-start | bytes 1327112 | tf_op jit(solution)/shard_map/ppermute | solution.py:481
  44.1 16.2 %collective-permute-start.15 = (bf16[2,2,72,768]{3,2,1,0:T(8,128)(2,1)S(1)}, bf16[2,2,72,768]{3,2,1,0:T(8,128)(2,1)}, u32[]{:S(2)}, u32[]{:S(2)}) collective-permute-start(bf16[2,2,72,768]{3,2,1,0:T(8,128)(2,1)S(1)} %pad_maximum_fusion.1.g000), channel_id=1, source_target_pairs={{0,4},{1,5},{2,6},{3,7},{4,0},{5,1},{6,2},{7,3},{8,12},{9,13},{10,... | collective-permute-start | bytes 1327112 | tf_op jit(solution)/shard_map/ppermute | solution.py:481
  47.3 23.3 %collective-permute-start.12 = (bf16[2,2,136,576]{3,2,1,0:T(8,128)(2,1)}, bf16[2,2,136,576]{3,2,1,0:T(8,128)(2,1)}, u32[]{:S(2)}, u32[]{:S(2)}) collective-permute-start(bf16[2,2,136,576]{3,2,1,0:T(8,128)(2,1)} %pad_maximum_fusion.b00), channel_id=1, source_target_pairs={{0,4},{1,5},{2,6},{3,7},{4,0},{5,1},{6,2},{7,3},{8,12},{9,13},{10,... | collective-permute-start | bytes 1880072 | tf_op jit(solution)/shard_map/ppermute | solution.py:481
  60.3 12.3 %collective-permute-start.17 = (bf16[2,2,72,768]{3,2,1,0:T(8,128)(2,1)}, bf16[2,2,72,768]{3,2,1,0:T(8,128)(2,1)}, u32[]{:S(2)}, u32[]{:S(2)}) collective-permute-start(bf16[2,2,72,768]{3,2,1,0:T(8,128)(2,1)} %collective-permute-done.15.g100), channel_id=1, source_target_pairs={{0,2},{1,3},{2,0},{3,1},{4,6},{5,7},{6,4},{7,5},{8,10},{9,11},{10,... | collective-permute-start | bytes 1327112 | tf_op jit(solution)/shard_map/ppermute | solution.py:481
  60.9 12.2 %collective-permute-start.13 = (bf16[2,2,136,576]{3,2,1,0:T(8,128)(2,1)}, bf16[2,2,136,576]{3,2,1,0:T(8,128)(2,1)}, u32[]{:S(2)}, u32[]{:S(2)}) collective-permute-start(bf16[2,2,136,576]{3,2,1,0:T(8,128)(2,1)} %pad_maximum_fusion.b00), channel_id=1, source_target_pairs={{0,1},{1,0},{2,3},{3,2},{4,5},{5,4},{6,7},{7,6},{8,9},{9,8},{10,11... | collective-permute-start | bytes 1880072 | tf_op jit(solution)/shard_map/ppermute | solution.py:481
  94.0 18.6 %collective-permute-start.35 = (bf16[2,2,2,72,576]{4,3,2,1,0:T(8,128)(2,1)S(1)}, bf16[2,2,2,72,576]{4,3,2,1,0:T(8,128)(2,1)S(1)}, u32[]{:S(2)}, u32[]{:S(2)}) collective-permute-start(bf16[2,2,2,72,576]{4,3,2,1,0:T(8,128)(2,1)S(1)} %get-tuple-element.110), channel_id=1, source_target_pairs={{0,2},{1,3},{2,0},{3,1},{4,6},{5,7},{6,4},{7,5},{8,10},{9,11},{10,... | collective-permute-start | bytes 1990664 | tf_op jit(solution)/shard_map/ppermute | solution.py:481
  95.1 38.7 %collective-permute-start.27 = (bf16[2,2,2,72,768]{4,3,2,1,0:T(8,128)(2,1)S(1)}, bf16[2,2,2,72,768]{4,3,2,1,0:T(8,128)(2,1)S(1)}, u32[]{:S(2)}, u32[]{:S(2)}) collective-permute-start(bf16[2,2,2,72,768]{4,3,2,1,0:T(8,128)(2,1)S(1)} %get-tuple-element.108), channel_id=1, source_target_pairs={{0,4},{1,5},{2,6},{3,7},{4,0},{5,1},{6,2},{7,3},{8,12},{9,13},{10,... | collective-permute-start | bytes 2654216 | tf_op jit(solution)/shard_map/ppermute | solution.py:481
  112.7 13.9 %collective-permute-start.36 = (bf16[2,2,72,576]{3,2,1,0:T(8,128)(2,1)S(1)}, bf16[2,2,72,576]{3,2,1,0:T(8,128)(2,1)S(1)}, u32[]{:S(2)}, u32[]{:S(2)}) collective-permute-start(bf16[2,2,72,576]{3,2,1,0:T(8,128)(2,1)S(1)} %get-tuple-element.114), channel_id=1, source_target_pairs={{0,4},{1,5},{2,6},{3,7},{4,0},{5,1},{6,2},{7,3},{8,12},{9,13},{10,... | collective-permute-start | bytes 995336 | tf_op jit(solution)/shard_map/ppermute | solution.py:481
  126.2 7.6 %collective-permute-start.26 = (bf16[2,2,2,2,80,256]{5,4,3,2,1,0:T(8,128)(2,1)}, bf16[2,2,2,2,80,256]{5,4,3,2,1,0:T(8,128)(2,1)S(1)}, u32[]{:S(2)}, u32[]{:S(2)}) collective-permute-start(bf16[2,2,2,2,80,256]{5,4,3,2,1,0:T(8,128)(2,1)} %get-tuple-element.80), channel_id=1, source_target_pairs={{0,1},{1,0},{2,3},{3,2},{4,5},{5,4},{6,7},{7,6},{8,9},{9,8},{10,11... | collective-permute-start | bytes 1966088 | tf_op jit(solution)/shard_map/ppermute | solution.py:481
  126.8 6.7 %collective-permute-start.37 = (bf16[2,72,576]{2,1,0:T(8,128)(2,1)S(1)}, bf16[2,72,576]{2,1,0:T(8,128)(2,1)S(1)}, u32[]{:S(2)}, u32[]{:S(2)}) collective-permute-start(bf16[2,72,576]{2,1,0:T(8,128)(2,1)S(1)} %get-tuple-element.122), channel_id=1, source_target_pairs={{0,8},{1,9},{2,10},{3,11},{4,12},{5,13},{6,14},{7,15},{8,0},{9,1},... | collective-permute-start | bytes 497672 | tf_op jit(solution)/shard_map/ppermute | solution.py:481
  129.2 7.2 %collective-permute-start.25 = (bf16[256,384]{1,0:T(8,128)(2,1)S(1)}, bf16[256,384]{1,0:T(8,128)(2,1)S(1)}, u32[]{:S(2)}, u32[]{:S(2)}) collective-permute-start(bf16[256,384]{1,0:T(8,128)(2,1)S(1)} %get-tuple-element.119), channel_id=1, source_target_pairs={{0,2},{1,3},{2,0},{3,1},{4,6},{5,7},{6,4},{7,5},{8,10},{9,11},{10,... | collective-permute-start | bytes 589832 | tf_op jit(solution)/shard_map/ppermute | solution.py:481
  134.0 8.7 %collective-permute-start.28 = (bf16[2,2,2,80,256]{4,3,2,1,0:T(8,128)(2,1)S(1)}, bf16[2,2,2,80,256]{4,3,2,1,0:T(8,128)(2,1)S(1)}, u32[]{:S(2)}, u32[]{:S(2)}) collective-permute-start(bf16[2,2,2,80,256]{4,3,2,1,0:T(8,128)(2,1)S(1)} %get-tuple-element.115), channel_id=1, source_target_pairs={{0,4},{1,5},{2,6},{3,7},{4,0},{5,1},{6,2},{7,3},{8,12},{9,13},{10,... | collective-permute-start | bytes 983048 | tf_op jit(solution)/shard_map/ppermute | solution.py:481
  135.8 11.8 %collective-permute-start.42 = (bf16[2,2,72,768]{3,2,1,0:T(8,128)(2,1)S(1)}, bf16[2,2,72,768]{3,2,1,0:T(8,128)(2,1)S(1)}, u32[]{:S(2)}, u32[]{:S(2)}) collective-permute-start(bf16[2,2,72,768]{3,2,1,0:T(8,128)(2,1)S(1)} %get-tuple-element.112), channel_id=1, source_target_pairs={{0,2},{1,3},{2,0},{3,1},{4,6},{5,7},{6,4},{7,5},{8,10},{9,11},{10,... | collective-permute-start | bytes 1327112 | tf_op jit(solution)/shard_map/ppermute | solution.py:481
  140.2 24.2 %collective-permute-start.39 = (bf16[72,576]{1,0:T(8,128)(2,1)S(1)}, bf16[72,576]{1,0:T(8,128)(2,1)S(1)}, u32[]{:S(2)}, u32[]{:S(2)}) collective-permute-start(bf16[72,576]{1,0:T(8,128)(2,1)S(1)} %fusion.23.p00), channel_id=1, source_target_pairs={{0,2},{1,3},{2,0},{3,1},{4,6},{5,7},{6,4},{7,5},{8,10},{9,11},{10,... | collective-permute-start | bytes 248840 | tf_op jit(solution)/shard_map/ppermute | solution.py:481
  147.7 7.4 %collective-permute-start.43 = (bf16[2,72,768]{2,1,0:T(8,128)(2,1)S(1)}, bf16[2,72,768]{2,1,0:T(8,128)(2,1)S(1)}, u32[]{:S(2)}, u32[]{:S(2)}) collective-permute-start(bf16[2,72,768]{2,1,0:T(8,128)(2,1)S(1)} %get-tuple-element.118), channel_id=1, source_target_pairs={{0,8},{1,9},{2,10},{3,11},{4,12},{5,13},{6,14},{7,15},{8,0},{9,1},... | collective-permute-start | bytes 663560 | tf_op jit(solution)/shard_map/ppermute | solution.py:481
  149.3 8.7 %collective-permute-start.29 = (bf16[2,2,80,256]{3,2,1,0:T(8,128)(2,1)S(1)}, bf16[2,2,80,256]{3,2,1,0:T(8,128)(2,1)S(1)}, u32[]{:S(2)}, u32[]{:S(2)}) collective-permute-start(bf16[2,2,80,256]{3,2,1,0:T(8,128)(2,1)S(1)} %get-tuple-element.126), channel_id=1, source_target_pairs={{0,2},{1,3},{2,0},{3,1},{4,6},{5,7},{6,4},{7,5},{8,10},{9,11},{10,... | collective-permute-start | bytes 491528 | tf_op jit(solution)/shard_map/ppermute | solution.py:481
  155.1 7.4 %collective-permute-start.44 = (bf16[72,768]{1,0:T(8,128)(2,1)S(1)}, bf16[72,768]{1,0:T(8,128)(2,1)S(1)}, u32[]{:S(2)}, u32[]{:S(2)}) collective-permute-start(bf16[72,768]{1,0:T(8,128)(2,1)S(1)} %fusion.29), channel_id=1, source_target_pairs={{0,16},{1,17},{2,18},{3,19},{4,20},{5,21},{6,22},{7,23},{8,24},{9,... | collective-permute-start | bytes 331784 | tf_op jit(solution)/shard_map/ppermute | solution.py:481
  164.4 8.3 %collective-permute-start.41 = (bf16[72,576]{1,0:T(8,128)(2,1)S(1)}, bf16[72,576]{1,0:T(8,128)(2,1)S(1)}, u32[]{:S(2)}, u32[]{:S(2)}) collective-permute-start(bf16[72,576]{1,0:T(8,128)(2,1)S(1)} %collective-permute-done.39.p10), channel_id=1, source_target_pairs={{0,1},{1,0},{2,3},{3,2},{4,5},{5,4},{6,7},{7,6},{8,9},{9,8},{10,11... | collective-permute-start | bytes 248840 | tf_op jit(solution)/shard_map/ppermute | solution.py:481
  164.9 10.6 %collective-permute-start.46 = (bf16[72,768]{1,0:T(8,128)(2,1)S(1)}, bf16[72,768]{1,0:T(8,128)(2,1)S(1)}, u32[]{:S(2)}, u32[]{:S(2)}) collective-permute-start(bf16[72,768]{1,0:T(8,128)(2,1)S(1)} %fusion.17.p00), channel_id=1, source_target_pairs={{0,1},{1,0},{2,3},{3,2},{4,5},{5,4},{6,7},{7,6},{8,9},{9,8},{10,11... | collective-permute-start | bytes 331784 | tf_op jit(solution)/shard_map/ppermute | solution.py:481
  167.4 8.2 %collective-permute-start.47 = (bf16[72,768]{1,0:T(8,128)(2,1)S(1)}, bf16[72,768]{1,0:T(8,128)(2,1)S(1)}, u32[]{:S(2)}, u32[]{:S(2)}) collective-permute-start(bf16[72,768]{1,0:T(8,128)(2,1)S(1)} %collective-permute-done.45.p10), channel_id=1, source_target_pairs={{0,1},{1,0},{2,3},{3,2},{4,5},{5,4},{6,7},{7,6},{8,9},{9,8},{10,11... | collective-permute-start | bytes 331784 | tf_op jit(solution)/shard_map/ppermute | solution.py:481
  (36 other events, 218.3 us)

commit v2 on v1

--- a/solution.py
+++ b/solution.py
@@ -361,7 +361,7 @@
             wgrad = dot(second, grad, 0, 0)
             for f in range(n_f):
                 x, z0, z1 = rel(meta, f)
-                to[x, y ^ yy, z0, z1] = wgrad[d_rows * f : d_rows * (f + 1), :].astype(BF)
+                to[x, z0, z1, yy] = wgrad[d_rows * f : d_rows * (f + 1), :].astype(BF)
     turned(out_o, middle + feed)
     gain_o[...] = jnp.sum(back * normed, axis=0, keepdims=True)
     middle_grad = out_grad + norm_back(back, g2, scale_two, normed)
@@ -422,7 +422,7 @@
             for c_to, to in ((0, rk_o), (1, rg_o)):
                 at = pl.multiple_of((yy * 2 + (core ^ c_to)) * 256, 256)
                 block = [w_s[d_rows * f : d_rows * (f + 1), pl.ds(at, 256)], small_s[f, :, pl.ds(at, 256)]]
-                to[x, y ^ yy, z0, z1] = jnp.concatenate(block, axis=0).astype(BF)
+                to[y ^ yy, x, z0, z1] = jnp.concatenate(block, axis=0).astype(BF)
 
 
 def input_gradient_two(dq, own, other, source, mid, w, gains, out_o):
@@ -432,11 +432,13 @@
     turned(out_o, mid[...] + norm_back(first_grad, gains[0:1, :], scale_one, normed))
 
 
-def place_gate(meta, p00, p10, p01, p11, out_o):
-    seq = meta[0]
-    n = p00.shape[1]
-    for piece, o in ((p00[...], 0), (p10[...], 2), (p01[...], 1), (p11[...], 3)):
-        out_o[:, pl.ds(pl.multiple_of((seq ^ o) * n, 128), n)] = piece.astype(F32)
+def place_gate(meta, near, far, out_o):
+    core = meta[0] & 1
+    n = near.shape[2]
+    for pieces, c_rel in ((near, 0), (far, 1)):
+        for yy in range(2):
+            at = pl.multiple_of((yy * 2 + (core ^ c_rel)) * n, 128)
+            out_o[:, pl.ds(at, n)] = pieces[yy].astype(F32)
 
 
 def place_down(part_d, meta, p00, p10, p01, p11, out_o, wout_o):
@@ -465,6 +467,13 @@
     bv_o[...] = line[:, qk : qk + v]
     gains_o[0:1, :] = line[:, qk + v : qk + v + d_rows]
     gains_o[1:2, :] = line[:, 256 : 256 + d_rows]
+
+
+def place_all(part_d, qk, v, meta, near, far, d0, d1, d2, d3, r0, r1, r2, r3,
+              gate_o, down_o, wout_o, w_o, bqk_o, bv_o, gains_o, all_s):
+    place_gate(meta, near, far, gate_o)
+    place_down(part_d, meta, d0, d1, d2, d3, down_o, wout_o)
+    place_qkv(qk, v, meta, r0, r1, r2, r3, w_o, bqk_o, bv_o, gains_o, all_s)
 
 
 class Net:
@@ -774,8 +783,8 @@
         ],
         axis=1,
     )
-    b0 = net.half(after(half_b, a0), core, 0)
     a2 = net.both(a1, znear, 0)
+    b0 = net.half(after(half_b, a2), core, 0)
     a_x = net.swap(a2, xbit)
     a_c = net.swap(a2, core)
     gu1 = net.both(gu0, zfar, 0)
@@ -875,14 +884,14 @@
         1.4e10,
         [(width, 1024), (1, qkv_w), (1, width), (n_fsdp, 8, 1024)],
     )
-    dkv, dkv_give = halves(dkv_keep, net.swap(dkv_give, core))
-    rest, rest_give = halves(rest_keep, after(net.swap(rest_give, core), gate_got))
+    gate, gate_give = halves(gate, after(gate_got, dq))
+    gate_got = net.swap(gate_give, znear)
+    dkv, dkv_give = halves(dkv_keep, after(net.swap(dkv_give, core), gate_give))
+    rest, rest_give = halves(rest_keep, after(net.swap(rest_give, core), gate_give))
+    down, down_give = halves(down, after(down_got, gate_give))
     dkv_got = net.swap(dkv_give, ybit)
-    rest_got = net.swap(rest_give, xbit)
-    down, down_give = halves(down, down_got)
+    rest_got = net.swap(rest_give, ybit)
     down_got = net.swap(down_give, xbit)
-    gate, gate_give = halves(gate, gate_got)
-    gate_got = net.swap(gate_give, ybit)
     (hidden_grad,) = call(
         input_gradient_two,
         [],
@@ -893,32 +902,43 @@
     rest_got = after(rest_got, hidden_grad)
     hidden_grad = hidden_grad.reshape(micro, batch, width, length).swapaxes(2, 3)
     rest, rest_give = halves(rest, rest_got)
-    rest_got = net.swap(rest_give, ybit)
-    parts, gots = [gate, down, rest], [gate_got, down_got, rest_got]
-    for mask in (znear, zfar):
-        pairs = [halves(part, got) for part, got in zip(parts, gots)]
-        parts, gots = [keep for keep, _ in pairs], [net.swap(give, mask) for _, give in pairs]
-    gate, down, rest = [add(part, got) for part, got in zip(parts, gots)]
+    rest_got = net.swap(rest_give, xbit)
+    gate, gate_give = halves(gate, gate_got)
+    gate_got = net.swap(gate_give, zfar)
+    down, down_give = halves(down, down_got)
+    down_got = net.swap(down_give, znear)
+    rest, rest_give = halves(rest, rest_got)
+    rest_got = net.swap(rest_give, znear)
+    gate = add(gate, gate_got)
+    gate_got = net.swap(gate, ybit)
+    down, down_give = halves(down, down_got)
+    down_got = net.swap(down_give, zfar)
+    rest, rest_give = halves(rest, rest_got)
+    rest_got = net.swap(rest_give, zfar)
+    down = add(down, down_got)
+    rest = add(rest, rest_got)
 
     def spread(part):
         other = net.swap(part, ybit)
         return [part, other, net.swap(part, core), net.swap(other, core)]
 
-    (out_gate,) = call(place_gate, [meta], spread(gate), [sds((d_rows, 2 * units), F32)], 0)
-    out_down, out_wout = call(
-        functools.partial(place_down, ff_rows // 4),
+    gate = add(gate, gate_got)
+    gate = [gate, net.swap(gate, core)]
+    qk, v = (QW + KW) // n_fsdp, KW // n_fsdp
+    out_gate, out_down, out_wout, out_qkv, b_qk, b_v, out_gains = call(
+        functools.partial(place_all, ff_rows // 4, qk, v),
         [meta],
-        spread(down),
-        [sds((ff_rows, width), F32), sds((d_rows, width), F32)],
-        0,
-    )
-    qk, v = (QW + KW) // n_fsdp, KW // n_fsdp
-    out_qkv, b_qk, b_v, out_gains = call(
-        functools.partial(place_qkv, qk, v),
-        [meta],
-        spread(rest),
-        [sds((d_rows, qkv_w), F32), sds((1, qk), F32), sds((1, v), F32), sds((2, d_rows), F32)],
-        0,
+        [*gate, *spread(down), *spread(rest)],
+        [
+            sds((d_rows, 2 * units), F32),
+            sds((ff_rows, width), F32),
+            sds((d_rows, width), F32),
+            sds((d_rows, qkv_w), F32),
+            sds((1, qk), F32),
+            sds((1, v), F32),
+            sds((2, d_rows), F32),
+        ],
+        3e9,
         [(d_rows + 8, 1024)],
     )
     return (

time: 177 us -> 164 us (0.927)
  waiting for transfers between devices: 82.2 us -> 71.1 us
  Pallas kernels: 45 us -> 42.4 us
    ppermute x48 -> x46, waiting for transfers between devices: 82.2 us -> 71.1 us  [swap(): return lax.ppermute(value, ('fsdp', 'seq'), pairs)]
    pallas_call x8 -> x6, Pallas kernels: 45 us -> 42.4 us  [call(): pl.pallas_call(kernel, out_shape=outs, in_specs=specs, out_specs=whole(*o...]
    ppermute x48 -> x46, starting transfers between devices: 35.3 us -> 36.6 us  [swap(): return lax.ppermute(value, ('fsdp', 'seq'), pairs)]
    unnamed x42 -> x44, local copies, waits for them, and re-layouts: 4.39 us -> 4.56 us
  transfers between devices with their start and end apart: 48 -> 46, of which waited for: 24 -> 18; matrix products, arithmetic and copies ran while one was open for 6% -> 6% of each run, Pallas kernels for 17% -> 16%
where the time goes in v2:
time: 164 us
  waiting for transfers between devices  71.1 us (43%)
  Pallas kernels  42.4 us (26%)
  starting transfers between devices  36.6 us (22%)
  other arithmetic  6.93 us (4%)
  local copies, waits for them, and re-layouts  5.61 us (3%)
    ppermute x46, waiting for transfers between devices, swap(): return lax.ppermute(value, ('fsdp', 'seq'), pairs)  71.1 us
    pallas_call x6, Pallas kernels, call(): pl.pallas_call(kernel, out_shape=outs, in_specs=specs, out_specs=whole(*o...  42.4 us
    ppermute x46, starting transfers between devices, swap(): return lax.ppermute(value, ('fsdp', 'seq'), pairs)  36.6 us
    unnamed x44, local copies, waits for them, and re-layouts  4.56 us
    convert_element_type x16, other arithmetic, add(): return (keep.astype(F32) + got.astype(F32)).astype(BF)  3.42 us
  transfers between devices with their start and end apart: 46, of which 18 were waited for; matrix products, arithmetic and copies ran while one was open for 6% of the time, Pallas kernels for 16%

profile of v2, /device:TPU:0, one launch (start us, length us, event | category | flops | bytes accessed | tf_op | source)
XLA Modules:
  0.0 163.7 jit_solution(4309290453223308946)
XLA Ops:
  3.6 4.1 %collective-permute-start.3 = (bf16[40,960]{1,0:T(8,128)(2,1)S(1)}, bf16[40,960]{1,0:T(8,128)(2,1)S(1)}, u32[]{:S(2)}, u32[]{:S(2)}) collective-permute-start(bf16[40,960]{1,0:T(8,128)(2,1)S(1)} %shard_map.187), channel_id=1, source_target_pairs={{0,16},{1,17},{2,18},{3,19},{4,20},{5,21},{6,22},{7,23},{8,24},{9,... | collective-permute-start | bytes 230408 | tf_op jit(solution)/shard_map/ppermute | solution.py:490
  9.8 1.6 collective-permute-start
  12.4 1.6 %collective-permute-start.4 = (bf16[2,40,960]{2,1,0:T(8,128)(2,1)S(1)}, bf16[2,40,960]{2,1,0:T(8,128)(2,1)S(1)}, u32[]{:S(2)}, u32[]{:S(2)}) collective-permute-start(bf16[2,40,960]{2,1,0:T(8,128)(2,1)S(1)} %pad_maximum_fusion.7), channel_id=1, source_target_pairs={{0,8},{1,9},{2,10},{3,11},{4,12},{5,13},{6,14},{7,15},{8,0},{9,1},... | collective-permute-start | bytes 460808 | tf_op jit(solution)/shard_map/ppermute | solution.py:490
  14.0 6.0 %collective-permute-done.8 = bf16[72,768]{1,0:T(8,128)(2,1)S(1)} collective-permute-done((bf16[72,768]{1,0:T(8,128)(2,1)S(1)}, bf16[72,768]{1,0:T(8,128)(2,1)S(1)}, u32[]{:S(2)}, u32[]{:S(2)}) %collective-permute-start.8) | collective-permute-done | bytes 110624 | tf_op jit(solution)/shard_map/ppermute | solution.py:490
  21.0 1.6 collective-permute-start.5
  22.6 4.1 %collective-permute-start.10 = (bf16[136,576]{1,0:T(8,128)(2,1)S(1)}, bf16[136,576]{1,0:T(8,128)(2,1)S(1)}, u32[]{:S(2)}, u32[]{:S(2)}) collective-permute-start(bf16[136,576]{1,0:T(8,128)(2,1)S(1)} %dynamic-slice_bitcast_fusion), channel_id=1, source_target_pairs={{0,16},{1,17},{2,18},{3,19},{4,20},{5,21},{6,22},{7,23},{8,24},{9,... | collective-permute-start | bytes 470024 | tf_op jit(solution)/shard_map/ppermute | solution.py:490
  27.1 4.5 %collective-permute-done.10 = bf16[136,576]{1,0:T(8,128)(2,1)S(1)} collective-permute-done((bf16[136,576]{1,0:T(8,128)(2,1)S(1)}, bf16[136,576]{1,0:T(8,128)(2,1)S(1)}, u32[]{:S(2)}, u32[]{:S(2)}) %collective-permute-start.10) | collective-permute-done | bytes 156704 | tf_op jit(solution)/shard_map/ppermute | solution.py:490
  31.7 4.5 %collective-permute-start.11 = (bf16[2,136,576]{2,1,0:T(8,128)(2,1)S(1)}, bf16[2,136,576]{2,1,0:T(8,128)(2,1)S(1)}, u32[]{:S(2)}, u32[]{:S(2)}) collective-permute-start(bf16[2,136,576]{2,1,0:T(8,128)(2,1)S(1)} %pad_maximum_fusion.3), channel_id=1, source_target_pairs={{0,8},{1,9},{2,10},{3,11},{4,12},{5,13},{6,14},{7,15},{8,0},{9,1},... | collective-permute-start | bytes 940040 | tf_op jit(solution)/shard_map/ppermute | solution.py:490
  39.0 5.2 %collective-permute-done.11 = bf16[2,136,576]{2,1,0:T(8,128)(2,1)S(1)} collective-permute-done((bf16[2,136,576]{2,1,0:T(8,128)(2,1)S(1)}, bf16[2,136,576]{2,1,0:T(8,128)(2,1)S(1)}, u32[]{:S(2)}, u32[]{:S(2)}) %collective-permute-start.11) | collective-permute-done | bytes 313376 | tf_op jit(solution)/shard_map/ppermute | solution.py:490
  47.3 10.7 %shard_map.188 = (bf16[256,576]{1,0:T(8,128)(2,1)S(1)}, bf16[2,3,384,64]{3,2,1,0:T(8,128)(2,1)}, bf16[2,3,512,64]{3,2,1,0:T(8,128)(2,1)}, bf16[2,3,512,64]{3,2,1...) custom-call(s32[2]{0:T(128)S(1)} %pad_add_fusion.meta, ...), custom_call_target="tpu_custom_call" | custom-call | flops 12000000000 | bytes 6084096 | tf_op jit(solution)/shard_map/pallas_call | solution.py:53
  58.8 5.8 %collective-permute-done.12.b10 = bf16[2,2,136,576]{3,2,1,0:T(8,128)(2,1)} collective-permute-done((bf16[2,2,136,576]{3,2,1,0:T(8,128)(2,1)}, bf16[2,2,136,576]{3,2,1,0:T(8,128)(2,1)}, u32[]{:S(2)}, u32[]{:S(2)}) %collective-permute-start.12) | collective-permute-done | bytes 626720 | tf_op jit(solution)/shard_map/ppermute | solution.py:490
  65.1 5.4 %collective-permute-done.17.g110 = bf16[2,2,72,768]{3,2,1,0:T(8,128)(2,1)} collective-permute-done((bf16[2,2,72,768]{3,2,1,0:T(8,128)(2,1)}, bf16[2,2,72,768]{3,2,1,0:T(8,128)(2,1)}, u32[]{:S(2)}, u32[]{:S(2)}) %collective-permute-start.17) | collective-permute-done | bytes 442400 | tf_op jit(solution)/shard_map/ppermute | solution.py:490
  71.0 1.6 %collective-permute-done.21.g111 = bf16[2,2,72,768]{3,2,1,0:T(8,128)(2,1)} collective-permute-done((bf16[2,2,72,768]{3,2,1,0:T(8,128)(2,1)}, bf16[2,2,72,768]{3,2,1,0:T(8,128)(2,1)}, u32[]{:S(2)}, u32[]{:S(2)}) %collective-permute-start.21) | collective-permute-done | bytes 442400 | tf_op jit(solution)/shard_map/ppermute | solution.py:490
  72.7 13.3 %shard_map.189 = (bf16[2,576,128]{2,1,0:T(8,128)(2,1)}, bf16[2,2,2,2,72,768]{5,4,3,2,1,0:T(8,128)(2,1)}, bf16[2,2,2,2,72,768]{5,4,3,2,1,0:T(8,128)(2,1)}, bf16[2...) custom-call(s32[2]{0:T(128)S(1)} %pad_add_fusion.meta, ...), custom_call_target="tpu_custom_call" | custom-call | flops 14000000000 | bytes 14311168 | tf_op jit(solution)/shard_map/pallas_call | solution.py:53
  86.6 5.5 %collective-permute-done.23 = bf16[2,2,2,2,72,576]{5,4,3,2,1,0:T(8,128)(2,1)S(1)} collective-permute-done((bf16[2,2,2,2,72,576]{5,4,3,2,1,0:T(8,128)(2,1)}, bf16[2,2,2,2,72,576]{5,4,3,2,1,0:T(8,128)(2,1)S(1)}, u32[]{:S(2)}, u32[]{:S(2)}) %collective-permute-start.23) | collective-permute-done | bytes 1327136 | tf_op jit(solution)/shard_map/ppermute | solution.py:490
  92.1 1.8 %add_convert_fusion.2 = (bf16[1,2,2,2,72,576]{5,4,3,2,1,0:T(8,128)(2,1)S(1)}, bf16[2,2,2,72,576]{4,3,2,1,0:T(8,128)(2,1)S(1)}) fusion(bf16[2,2,2,2,72,576]{5,4,3,2,1,0:T(8,128)(2,1)S(1)} %collective-permute-done.23, bf16[2,2,2,2,72,576]{5,4,3,2,1,0:T(8,128)(2,1)} %get-tuple-element.75), kind=kLoop, calls=%fused_computation.2 | loop fusion | flops 2654208 | bytes 3981312 | tf_op jit(solution)/shard_map/convert_element_type | solution.py:862
  96.3 12.6 %shard_map.190 = (bf16[256,640]{1,0:T(8,128)(2,1)S(1)}, bf16[2,256,384]{2,1,0:T(8,128)(2,1)}, bf16[2,256,384]{2,1,0:T(8,128)(2,1)}, bf16[2,2,2,2,80,256]{5,4,3,2...) custom-call(s32[2]{0:T(128)S(1)} %pad_add_fusion.meta, bf16[256,640]{1,0:T(8,128)(2,1)S(1)} %pad_maximum_fusion.4.b0, ...), custom_call_target="tpu_custom_call" | custom-call | flops 14000000000 | bytes 7282432 | tf_op jit(solution)/shard_map/pallas_call | solution.py:53
  109.4 7.2 %collective-permute-done.25 = bf16[2,2,2,72,768]{4,3,2,1,0:T(8,128)(2,1)S(1)} collective-permute-done((bf16[2,2,2,72,768]{4,3,2,1,0:T(8,128)(2,1)S(1)}, bf16[2,2,2,72,768]{4,3,2,1,0:T(8,128)(2,1)S(1)}, u32[]{:S(2)}, u32[]{:S(2)}) %collective-permute-start.25) | collective-permute-done | bytes 884768 | tf_op jit(solution)/shard_map/ppermute | solution.py:490
  116.9 1.8 %collective-permute-start.27 = (bf16[2,2,72,768]{3,2,1,0:T(8,128)(2,1)S(1)}, bf16[2,2,72,768]{3,2,1,0:T(8,128)(2,1)S(1)}, u32[]{:S(2)}, u32[]{:S(2)}) collective-permute-start(bf16[2,2,72,768]{3,2,1,0:T(8,128)(2,1)S(1)} %get-tuple-element.120), channel_id=1, source_target_pairs={{0,8},{1,9},{2,10},{3,11},{4,12},{5,13},{6,14},{7,15},{8,0},{9,1},... | collective-permute-start | bytes 1327112 | tf_op jit(solution)/shard_map/ppermute | solution.py:490
  118.8 1.3 collective-permute-start.26
  122.4 4.3 %collective-permute-done.26.other = bf16[256,384]{1,0:T(8,128)(2,1)S(1)} collective-permute-done((bf16[256,384]{1,0:T(8,128)(2,1)S(1)}, bf16[256,384]{1,0:T(8,128)(2,1)S(1)}, u32[]{:S(2)}, u32[]{:S(2)}) %collective-permute-start.26) | collective-permute-done | bytes 196640 | tf_op jit(solution)/shard_map/ppermute | solution.py:490
  126.7 3.2 %shard_map.191 = f32[2,576,128]{2,1,0:T(8,128)} custom-call(bf16[256,640]{1,0:T(8,128)(2,1)S(1)} %get-tuple-element.79.dq, bf16[256,384]{1,0:T(8,128)(2,1)S(1)} %get-tuple-element.126.own, bf16[256,384]{1,0:T(8,128)(2,1)S(1)} %collective-permute-done.26.other, bf16[256,576]{1,0:T(8,128)(2,1)S(1)} %bitcast.184, f32[256,576]{1,0:T(8,128)S(1)} %copy-done.5, ...), custom_call_target="tpu_custom_call" | custom-call | flops 3000000000 | bytes 3305984 | tf_op jit(solution)/shard_map/pallas_call | solution.py:53
  129.9 1.5 collective-permute-done.39
  133.1 1.5 collective-permute-start.28
  134.7 6.3 %collective-permute-done.33 = bf16[2,72,576]{2,1,0:T(8,128)(2,1)S(1)} collective-permute-done((bf16[2,72,576]{2,1,0:T(8,128)(2,1)S(1)}, bf16[2,72,576]{2,1,0:T(8,128)(2,1)S(1)}, u32[]{:S(2)}, u32[]{:S(2)}) %collective-permute-start.33) | collective-permute-done | bytes 165920 | tf_op jit(solution)/shard_map/ppermute | solution.py:490
  141.3 6.2 %collective-permute-done.34 = bf16[72,576]{1,0:T(8,128)(2,1)S(1)} collective-permute-done((bf16[72,576]{1,0:T(8,128)(2,1)S(1)}, bf16[72,576]{1,0:T(8,128)(2,1)S(1)}, u32[]{:S(2)}, u32[]{:S(2)}) %collective-permute-start.34) | collective-permute-done | bytes 82976 | tf_op jit(solution)/shard_map/ppermute | solution.py:490
  147.6 1.3 collective-permute-start.35
  150.0 3.1 %collective-permute-done.35.d1 = bf16[72,576]{1,0:T(8,128)(2,1)S(1)} collective-permute-done((bf16[72,576]{1,0:T(8,128)(2,1)S(1)}, bf16[72,576]{1,0:T(8,128)(2,1)S(1)}, u32[]{:S(2)}, u32[]{:S(2)}) %collective-permute-start.35) | collective-permute-done | bytes 82976 | tf_op jit(solution)/shard_map/ppermute | solution.py:490
  153.1 3.2 %collective-permute-done.29 = bf16[2,72,768]{2,1,0:T(8,128)(2,1)S(1)} collective-permute-done((bf16[2,72,768]{2,1,0:T(8,128)(2,1)S(1)}, bf16[2,72,768]{2,1,0:T(8,128)(2,1)S(1)}, u32[]{:S(2)}, u32[]{:S(2)}) %collective-permute-start.29) | collective-permute-done | bytes 221216 | tf_op jit(solution)/shard_map/ppermute | solution.py:490
  157.9 2.7 %collective-permute-done.43.r1 = bf16[80,256]{1,0:T(8,128)(2,1)S(1)} collective-permute-done((bf16[80,256]{1,0:T(8,128)(2,1)S(1)}, bf16[80,256]{1,0:T(8,128)(2,1)S(1)}, u32[]{:S(2)}, u32[]{:S(2)}) %collective-permute-start.43) | collective-permute-done | bytes 40992 | tf_op jit(solution)/shard_map/ppermute | solution.py:490
  160.6 1.2 collective-permute-done.45.r3
  161.8 1.9 %shard_map.192 = (f32[72,3072]{1,0:T(8,128)}, f32[192,576]{1,0:T(8,128)}, f32[72,576]{1,0:T(8,128)}, f32[72,960]{1,0:T(8,128)}, f32[1,96]{1,0:T(1,128)}, /*index=5*/f32[1,24]{1,0:T(1,128)}, f32[2,72]{1,0:T(2,128)}) custom-call(s32[2]{0:T(128)S(1)} %pad_add_fusion.meta, bf16[2,72,768]{2,1,0:T(8,128)(2,1)S(1)} %add_convert_fusion.6.near, ...), custom_call_target="tpu_custom_call" | custom-call | flops 3000000000 | bytes 2708512 | tf_op jit(solution)/shard_map/pallas_call | solution.py:53
  (159 shorter events, 25.9 us)
Async XLA Ops:
  3.6 8.8 %collective-permute-start.3 = (bf16[40,960]{1,0:T(8,128)(2,1)S(1)}, bf16[40,960]{1,0:T(8,128)(2,1)S(1)}, u32[]{:S(2)}, u32[]{:S(2)}) collective-permute-start(bf16[40,960]{1,0:T(8,128)(2,1)S(1)} %shard_map.187), channel_id=1, source_target_pairs={{0,16},{1,17},{2,18},{3,19},{4,20},{5,21},{6,22},{7,23},{8,24},{9,... | collective-permute-start | bytes 230408 | tf_op jit(solution)/shard_map/ppermute | solution.py:490
  9.7 17.1 %collective-permute-start.1 = (bf16[256,640]{1,0:T(8,128)(2,1)S(1)}, bf16[256,640]{1,0:T(8,128)(2,1)S(1)}, u32[]{:S(2)}, u32[]{:S(2)}) collective-permute-start(bf16[256,640]{1,0:T(8,128)(2,1)S(1)} %pad_maximum_fusion.4.b0), channel_id=1, source_target_pairs={{0,1},{1,0},{2,3},{3,2},{4,5},{5,4},{6,7},{7,6},{8,9},{9,8},{10,11... | collective-permute-start | bytes 983048 | tf_op jit(solution)/shard_map/ppermute | solution.py:490
  9.8 12.8 %collective-permute-start = (bf16[256,640]{1,0:T(8,128)(2,1)S(1)}, bf16[256,640]{1,0:T(8,128)(2,1)S(1)}, u32[]{:S(2)}, u32[]{:S(2)}) collective-permute-start(bf16[256,640]{1,0:T(8,128)(2,1)S(1)} %pad_maximum_fusion.4.b0), channel_id=1, source_target_pairs={{0,2},{1,3},{2,0},{3,1},{4,6},{5,7},{6,4},{7,5},{8,10},{9,11},{10,... | collective-permute-start | bytes 983048 | tf_op jit(solution)/shard_map/ppermute | solution.py:490
  11.4 8.6 %collective-permute-start.8 = (bf16[72,768]{1,0:T(8,128)(2,1)S(1)}, bf16[72,768]{1,0:T(8,128)(2,1)S(1)}, u32[]{:S(2)}, u32[]{:S(2)}) collective-permute-start(bf16[72,768]{1,0:T(8,128)(2,1)S(1)} %constant_dynamic-slice_fusion), channel_id=1, source_target_pairs={{0,16},{1,17},{2,18},{3,19},{4,20},{5,21},{6,22},{7,23},{8,24},{9,... | collective-permute-start | bytes 331784 | tf_op jit(solution)/shard_map/ppermute | solution.py:490
  12.4 8.4 %collective-permute-start.4 = (bf16[2,40,960]{2,1,0:T(8,128)(2,1)S(1)}, bf16[2,40,960]{2,1,0:T(8,128)(2,1)S(1)}, u32[]{:S(2)}, u32[]{:S(2)}) collective-permute-start(bf16[2,40,960]{2,1,0:T(8,128)(2,1)S(1)} %pad_maximum_fusion.7), channel_id=1, source_target_pairs={{0,8},{1,9},{2,10},{3,11},{4,12},{5,13},{6,14},{7,15},{8,0},{9,1},... | collective-permute-start | bytes 460808 | tf_op jit(solution)/shard_map/ppermute | solution.py:490
  20.9 25.5 %collective-permute-start.6 = (bf16[2,2,40,960]{3,2,1,0:T(8,128)(2,1)S(1)}, bf16[2,2,40,960]{3,2,1,0:T(8,128)(2,1)S(1)}, u32[]{:S(2)}, u32[]{:S(2)}) collective-permute-start(bf16[2,2,40,960]{3,2,1,0:T(8,128)(2,1)S(1)} %pad_maximum_fusion.5.a00), channel_id=1, source_target_pairs={{0,1},{1,0},{2,3},{3,2},{4,5},{5,4},{6,7},{7,6},{8,9},{9,8},{10,11... | collective-permute-start | bytes 921608 | tf_op jit(solution)/shard_map/ppermute | solution.py:490
  21.0 15.3 %collective-permute-start.5 = (bf16[2,2,40,960]{3,2,1,0:T(8,128)(2,1)S(1)}, bf16[2,2,40,960]{3,2,1,0:T(8,128)(2,1)S(1)}, u32[]{:S(2)}, u32[]{:S(2)}) collective-permute-start(bf16[2,2,40,960]{3,2,1,0:T(8,128)(2,1)S(1)} %pad_maximum_fusion.5.a00), channel_id=1, source_target_pairs={{0,4},{1,5},{2,6},{3,7},{4,0},{5,1},{6,2},{7,3},{8,12},{9,13},{10,... | collective-permute-start | bytes 921608 | tf_op jit(solution)/shard_map/ppermute | solution.py:490
  22.5 13.7 %collective-permute-start.9 = (bf16[2,72,768]{2,1,0:T(8,128)(2,1)S(1)}, bf16[2,72,768]{2,1,0:T(8,128)(2,1)S(1)}, u32[]{:S(2)}, u32[]{:S(2)}) collective-permute-start(bf16[2,72,768]{2,1,0:T(8,128)(2,1)S(1)} %pad_maximum_fusion.6), channel_id=1, source_target_pairs={{0,8},{1,9},{2,10},{3,11},{4,12},{5,13},{6,14},{7,15},{8,0},{9,1},... | collective-permute-start | bytes 663560 | tf_op jit(solution)/shard_map/ppermute | solution.py:490
  22.6 9.0 %collective-permute-start.10 = (bf16[136,576]{1,0:T(8,128)(2,1)S(1)}, bf16[136,576]{1,0:T(8,128)(2,1)S(1)}, u32[]{:S(2)}, u32[]{:S(2)}) collective-permute-start(bf16[136,576]{1,0:T(8,128)(2,1)S(1)} %dynamic-slice_bitcast_fusion), channel_id=1, source_target_pairs={{0,16},{1,17},{2,18},{3,19},{4,20},{5,21},{6,22},{7,23},{8,24},{9,... | collective-permute-start | bytes 470024 | tf_op jit(solution)/shard_map/ppermute | solution.py:490
  26.8 10.4 %collective-permute-start.2 = (bf16[256,640]{1,0:T(8,128)(2,1)S(1)}, bf16[256,640]{1,0:T(8,128)(2,1)S(1)}, u32[]{:S(2)}, u32[]{:S(2)}) collective-permute-start(bf16[256,640]{1,0:T(8,128)(2,1)S(1)} %collective-permute-done.b1), channel_id=1, source_target_pairs={{0,1},{1,0},{2,3},{3,2},{4,5},{5,4},{6,7},{7,6},{8,9},{9,8},{10,11... | collective-permute-start | bytes 983048 | tf_op jit(solution)/shard_map/ppermute | solution.py:490
  31.7 12.5 %collective-permute-start.11 = (bf16[2,136,576]{2,1,0:T(8,128)(2,1)S(1)}, bf16[2,136,576]{2,1,0:T(8,128)(2,1)S(1)}, u32[]{:S(2)}, u32[]{:S(2)}) collective-permute-start(bf16[2,136,576]{2,1,0:T(8,128)(2,1)S(1)} %pad_maximum_fusion.3), channel_id=1, source_target_pairs={{0,8},{1,9},{2,10},{3,11},{4,12},{5,13},{6,14},{7,15},{8,0},{9,1},... | collective-permute-start | bytes 940040 | tf_op jit(solution)/shard_map/ppermute | solution.py:490
  36.3 28.7 %collective-permute-start.18 = (bf16[2,2,72,768]{3,2,1,0:T(8,128)(2,1)S(1)}, bf16[2,2,72,768]{3,2,1,0:T(8,128)(2,1)S(1)}, u32[]{:S(2)}, u32[]{:S(2)}) collective-permute-start(bf16[2,2,72,768]{3,2,1,0:T(8,128)(2,1)S(1)} %pad_maximum_fusion.1.g000), channel_id=1, source_target_pairs={{0,1},{1,0},{2,3},{3,2},{4,5},{5,4},{6,7},{7,6},{8,9},{9,8},{10,11... | collective-permute-start | bytes 1327112 | tf_op jit(solution)/shard_map/ppermute | solution.py:490
  36.4 28.1 %collective-permute-start.16 = (bf16[2,2,72,768]{3,2,1,0:T(8,128)(2,1)S(1)}, bf16[2,2,72,768]{3,2,1,0:T(8,128)(2,1)}, u32[]{:S(2)}, u32[]{:S(2)}) collective-permute-start(bf16[2,2,72,768]{3,2,1,0:T(8,128)(2,1)S(1)} %pad_maximum_fusion.1.g000), channel_id=1, source_target_pairs={{0,2},{1,3},{2,0},{3,1},{4,6},{5,7},{6,4},{7,5},{8,10},{9,11},{10,... | collective-permute-start | bytes 1327112 | tf_op jit(solution)/shard_map/ppermute | solution.py:490
  37.2 20.7 %collective-permute-start.15 = (bf16[2,2,72,768]{3,2,1,0:T(8,128)(2,1)S(1)}, bf16[2,2,72,768]{3,2,1,0:T(8,128)(2,1)}, u32[]{:S(2)}, u32[]{:S(2)}) collective-permute-start(bf16[2,2,72,768]{3,2,1,0:T(8,128)(2,1)S(1)} %pad_maximum_fusion.1.g000), channel_id=1, source_target_pairs={{0,4},{1,5},{2,6},{3,7},{4,0},{5,1},{6,2},{7,3},{8,12},{9,13},{10,... | collective-permute-start | bytes 1327112 | tf_op jit(solution)/shard_map/ppermute | solution.py:490
  45.8 18.7 %collective-permute-start.12 = (bf16[2,2,136,576]{3,2,1,0:T(8,128)(2,1)}, bf16[2,2,136,576]{3,2,1,0:T(8,128)(2,1)}, u32[]{:S(2)}, u32[]{:S(2)}) collective-permute-start(bf16[2,2,136,576]{3,2,1,0:T(8,128)(2,1)} %pad_maximum_fusion.b00), channel_id=1, source_target_pairs={{0,4},{1,5},{2,6},{3,7},{4,0},{5,1},{6,2},{7,3},{8,12},{9,13},{10,... | collective-permute-start | bytes 1880072 | tf_op jit(solution)/shard_map/ppermute | solution.py:490
  57.9 12.6 %collective-permute-start.17 = (bf16[2,2,72,768]{3,2,1,0:T(8,128)(2,1)}, bf16[2,2,72,768]{3,2,1,0:T(8,128)(2,1)}, u32[]{:S(2)}, u32[]{:S(2)}) collective-permute-start(bf16[2,2,72,768]{3,2,1,0:T(8,128)(2,1)} %collective-permute-done.15.g100), channel_id=1, source_target_pairs={{0,2},{1,3},{2,0},{3,1},{4,6},{5,7},{6,4},{7,5},{8,10},{9,11},{10,... | collective-permute-start | bytes 1327112 | tf_op jit(solution)/shard_map/ppermute | solution.py:490
  58.7 12.2 %collective-permute-start.13 = (bf16[2,2,136,576]{3,2,1,0:T(8,128)(2,1)}, bf16[2,2,136,576]{3,2,1,0:T(8,128)(2,1)}, u32[]{:S(2)}, u32[]{:S(2)}) collective-permute-start(bf16[2,2,136,576]{3,2,1,0:T(8,128)(2,1)} %pad_maximum_fusion.b00), channel_id=1, source_target_pairs={{0,1},{1,0},{2,3},{3,2},{4,5},{5,4},{6,7},{7,6},{8,9},{9,8},{10,11... | collective-permute-start | bytes 1880072 | tf_op jit(solution)/shard_map/ppermute | solution.py:490
  64.5 8.1 %collective-permute-start.14 = (bf16[2,2,136,576]{3,2,1,0:T(8,128)(2,1)}, bf16[2,2,136,576]{3,2,1,0:T(8,128)(2,1)}, u32[]{:S(2)}, u32[]{:S(2)}) collective-permute-start(bf16[2,2,136,576]{3,2,1,0:T(8,128)(2,1)} %collective-permute-done.12.b10), channel_id=1, source_target_pairs={{0,1},{1,0},{2,3},{3,2},{4,5},{5,4},{6,7},{7,6},{8,9},{9,8},{10,11... | collective-permute-start | bytes 1880072 | tf_op jit(solution)/shard_map/ppermute | solution.py:490
  86.0 8.7 %collective-permute-start.22 = (bf16[2,2,2,2,72,768]{5,4,3,2,1,0:T(8,128)(2,1)}, bf16[2,2,2,2,72,768]{5,4,3,2,1,0:T(8,128)(2,1)S(1)}, u32[]{:S(2)}, u32[]{:S(2)}) collective-permute-start(bf16[2,2,2,2,72,768]{5,4,3,2,1,0:T(8,128)(2,1)} %get-tuple-element.74), channel_id=1, source_target_pairs={{0,1},{1,0},{2,3},{3,2},{4,5},{5,4},{6,7},{7,6},{8,9},{9,8},{10,11... | collective-permute-start | bytes 5308424 | tf_op jit(solution)/shard_map/ppermute | solution.py:490
  93.9 24.8 %collective-permute-start.31 = (bf16[2,2,2,72,576]{4,3,2,1,0:T(8,128)(2,1)S(1)}, bf16[2,2,2,72,576]{4,3,2,1,0:T(8,128)(2,1)S(1)}, u32[]{:S(2)}, u32[]{:S(2)}) collective-permute-start(bf16[2,2,2,72,576]{4,3,2,1,0:T(8,128)(2,1)S(1)} %get-tuple-element.118), channel_id=1, source_target_pairs={{0,2},{1,3},{2,0},{3,1},{4,6},{5,7},{6,4},{7,5},{8,10},{9,11},{10,... | collective-permute-start | bytes 1990664 | tf_op jit(solution)/shard_map/ppermute | solution.py:490
  95.2 21.5 %collective-permute-start.25 = (bf16[2,2,2,72,768]{4,3,2,1,0:T(8,128)(2,1)S(1)}, bf16[2,2,2,72,768]{4,3,2,1,0:T(8,128)(2,1)S(1)}, u32[]{:S(2)}, u32[]{:S(2)}) collective-permute-start(bf16[2,2,2,72,768]{4,3,2,1,0:T(8,128)(2,1)S(1)} %get-tuple-element.116), channel_id=1, source_target_pairs={{0,4},{1,5},{2,6},{3,7},{4,0},{5,1},{6,2},{7,3},{8,12},{9,13},{10,... | collective-permute-start | bytes 2654216 | tf_op jit(solution)/shard_map/ppermute | solution.py:490
  108.9 9.8 %collective-permute-start.38 = (bf16[2,2,2,2,80,256]{5,4,3,2,1,0:T(8,128)(2,1)}, bf16[2,2,2,2,80,256]{5,4,3,2,1,0:T(8,128)(2,1)S(1)}, u32[]{:S(2)}, u32[]{:S(2)}) collective-permute-start(bf16[2,2,2,2,80,256]{5,4,3,2,1,0:T(8,128)(2,1)} %get-tuple-element.87), channel_id=1, source_target_pairs={{0,1},{1,0},{2,3},{3,2},{4,5},{5,4},{6,7},{7,6},{8,9},{9,8},{10,11... | collective-permute-start | bytes 1966088 | tf_op jit(solution)/shard_map/ppermute | solution.py:490
  108.9 9.8 %collective-permute-start.24 = (bf16[2,256,384]{2,1,0:T(8,128)(2,1)}, bf16[2,256,384]{2,1,0:T(8,128)(2,1)S(1)}, u32[]{:S(2)}, u32[]{:S(2)}) collective-permute-start(bf16[2,256,384]{2,1,0:T(8,128)(2,1)} %get-tuple-element.81), channel_id=1, source_target_pairs={{0,1},{1,0},{2,3},{3,2},{4,5},{5,4},{6,7},{7,6},{8,9},{9,8},{10,11... | collective-permute-start | bytes 1179656 | tf_op jit(solution)/shard_map/ppermute | solution.py:490
  116.9 16.2 %collective-permute-start.27 = (bf16[2,2,72,768]{3,2,1,0:T(8,128)(2,1)S(1)}, bf16[2,2,72,768]{3,2,1,0:T(8,128)(2,1)S(1)}, u32[]{:S(2)}, u32[]{:S(2)}) collective-permute-start(bf16[2,2,72,768]{3,2,1,0:T(8,128)(2,1)S(1)} %get-tuple-element.120), channel_id=1, source_target_pairs={{0,8},{1,9},{2,10},{3,11},{4,12},{5,13},{6,14},{7,15},{8,0},{9,1},... | collective-permute-start | bytes 1327112 | tf_op jit(solution)/shard_map/ppermute | solution.py:490
  120.3 11.1 %collective-permute-start.39 = (bf16[2,2,2,80,256]{4,3,2,1,0:T(8,128)(2,1)S(1)}, bf16[2,2,2,80,256]{4,3,2,1,0:T(8,128)(2,1)S(1)}, u32[]{:S(2)}, u32[]{:S(2)}) collective-permute-start(bf16[2,2,2,80,256]{4,3,2,1,0:T(8,128)(2,1)S(1)} %get-tuple-element.123), channel_id=1, source_target_pairs={{0,2},{1,3},{2,0},{3,1},{4,6},{5,7},{6,4},{7,5},{8,10},{9,11},{10,... | collective-permute-start | bytes 983048 | tf_op jit(solution)/shard_map/ppermute | solution.py:490
  121.3 11.3 %collective-permute-start.32 = (bf16[2,2,72,576]{3,2,1,0:T(8,128)(2,1)S(1)}, bf16[2,2,72,576]{3,2,1,0:T(8,128)(2,1)S(1)}, u32[]{:S(2)}, u32[]{:S(2)}) collective-permute-start(bf16[2,2,72,576]{3,2,1,0:T(8,128)(2,1)S(1)} %get-tuple-element.122), channel_id=1, source_target_pairs={{0,4},{1,5},{2,6},{3,7},{4,0},{5,1},{6,2},{7,3},{8,12},{9,13},{10,... | collective-permute-start | bytes 995336 | tf_op jit(solution)/shard_map/ppermute | solution.py:490
  131.5 9.7 %collective-permute-start.40 = (bf16[2,2,80,256]{3,2,1,0:T(8,128)(2,1)S(1)}, bf16[2,2,80,256]{3,2,1,0:T(8,128)(2,1)S(1)}, u32[]{:S(2)}, u32[]{:S(2)}) collective-permute-start(bf16[2,2,80,256]{3,2,1,0:T(8,128)(2,1)S(1)} %get-tuple-element.132), channel_id=1, source_target_pairs={{0,4},{1,5},{2,6},{3,7},{4,0},{5,1},{6,2},{7,3},{8,12},{9,13},{10,... | collective-permute-start | bytes 491528 | tf_op jit(solution)/shard_map/ppermute | solution.py:490
  132.7 8.3 %collective-permute-start.33 = (bf16[2,72,576]{2,1,0:T(8,128)(2,1)S(1)}, bf16[2,72,576]{2,1,0:T(8,128)(2,1)S(1)}, u32[]{:S(2)}, u32[]{:S(2)}) collective-permute-start(bf16[2,72,576]{2,1,0:T(8,128)(2,1)S(1)} %get-tuple-element.128), channel_id=1, source_target_pairs={{0,8},{1,9},{2,10},{3,11},{4,12},{5,13},{6,14},{7,15},{8,0},{9,1},... | collective-permute-start | bytes 497672 | tf_op jit(solution)/shard_map/ppermute | solution.py:490
  133.1 15.8 %collective-permute-start.28 = (bf16[2,72,768]{2,1,0:T(8,128)(2,1)S(1)}, bf16[2,72,768]{2,1,0:T(8,128)(2,1)S(1)}, u32[]{:S(2)}, u32[]{:S(2)}) collective-permute-start(bf16[2,72,768]{2,1,0:T(8,128)(2,1)S(1)} %fusion.17), channel_id=1, source_target_pairs={{0,16},{1,17},{2,18},{3,19},{4,20},{5,21},{6,22},{7,23},{8,24},{9,... | collective-permute-start | bytes 663560 | tf_op jit(solution)/shard_map/ppermute | solution.py:490
  141.2 8.6 %collective-permute-start.41 = (bf16[2,80,256]{2,1,0:T(8,128)(2,1)S(1)}, bf16[2,80,256]{2,1,0:T(8,128)(2,1)S(1)}, u32[]{:S(2)}, u32[]{:S(2)}) collective-permute-start(bf16[2,80,256]{2,1,0:T(8,128)(2,1)S(1)} %get-tuple-element.138), channel_id=1, source_target_pairs={{0,8},{1,9},{2,10},{3,11},{4,12},{5,13},{6,14},{7,15},{8,0},{9,1},... | collective-permute-start | bytes 245768 | tf_op jit(solution)/shard_map/ppermute | solution.py:490
  149.9 10.6 %collective-permute-start.36 = (bf16[72,576]{1,0:T(8,128)(2,1)S(1)}, bf16[72,576]{1,0:T(8,128)(2,1)S(1)}, u32[]{:S(2)}, u32[]{:S(2)}) collective-permute-start(bf16[72,576]{1,0:T(8,128)(2,1)S(1)} %fusion.22.d0), channel_id=1, source_target_pairs={{0,1},{1,0},{2,3},{3,2},{4,5},{5,4},{6,7},{7,6},{8,9},{9,8},{10,11... | collective-permute-start | bytes 248840 | tf_op jit(solution)/shard_map/ppermute | solution.py:490
  153.1 8.7 %collective-permute-start.37 = (bf16[72,576]{1,0:T(8,128)(2,1)S(1)}, bf16[72,576]{1,0:T(8,128)(2,1)S(1)}, u32[]{:S(2)}, u32[]{:S(2)}) collective-permute-start(bf16[72,576]{1,0:T(8,128)(2,1)S(1)} %collective-permute-done.35.d1), channel_id=1, source_target_pairs={{0,1},{1,0},{2,3},{3,2},{4,5},{5,4},{6,7},{7,6},{8,9},{9,8},{10,11... | collective-permute-start | bytes 248840 | tf_op jit(solution)/shard_map/ppermute | solution.py:490
  (35 other events, 235.5 us)

commit v3 on v2

--- a/solution.py
+++ b/solution.py
@@ -45,7 +45,7 @@
     return [pl.BlockSpec(memory_space=pltpu.VMEM) for _ in shape_dtypes]
 
 
-def call(kernel, scalars, arrays, outs, flops, scratch=()):
+def call(kernel, scalars, arrays, outs, flops, scratch=(), mib=52):
     specs = [pl.BlockSpec(memory_space=pltpu.SMEM)] * len(scalars) + whole(*arrays)
     moved = sum(a.size * a.dtype.itemsize for a in arrays) + sum(
         int(np.prod(o.shape)) * o.dtype.itemsize for o in outs
@@ -56,7 +56,7 @@
         in_specs=specs,
         out_specs=whole(*outs),
         scratch_shapes=[pltpu.VMEM(shape, F32) for shape in scratch],
-        compiler_params=pltpu.CompilerParams(vmem_limit_bytes=52 * 1024 * 1024),
+        compiler_params=pltpu.CompilerParams(vmem_limit_bytes=mib * 1024 * 1024),
         cost_estimate=pl.CostEstimate(flops=int(flops), bytes_accessed=moved, transcendentals=0),
     )(*scalars, *arrays)
 
@@ -242,7 +242,13 @@
         return jnp.stack([ref[key[1:]] for ref in self.refs])
 
 
-def cut_qkv(core_bit, meta, w, bias, gains, out_o, all_s):
+def cut_qkv(core_bit, meta, w_hbm, bias_hbm, gains_hbm, out_o, w, bias, gains, all_s, sems):
+    pairs = ((w_hbm, w), (bias_hbm, bias), (gains_hbm, gains))
+    copies = [pltpu.make_async_copy(a, b, sems.at[i]) for i, (a, b) in enumerate(pairs)]
+    for copy in copies:
+        copy.start()
+    for copy in copies:
+        copy.wait()
     rows = w.shape[0]
     n = bias.shape[1]
     all_s[:rows, :] = w[...].astype(F32)
@@ -292,7 +298,7 @@
 def feed_forward_pieces(d_rows, ff_rows, meta, attended, source, b00, b10, b01, b11,
                         g000, g100, g010, g110, g001, g101, g011, g111, gains, cot, weight,
                         out_o, gk_o, gg_o, dk_o, dg_o, mid_o, attg_o, gain_o, down_s, wout_s):
-    core, y, x_own = meta[0] & 1, (meta[0] >> 1) & 1, meta[1] & 1
+    core, y, x_own, z0_own = meta[0] & 1, (meta[0] >> 1) & 1, meta[1] & 1, (meta[1] >> 1) & 1
     n_f = 8
     hf = n_f // 2
     part_d = ff_rows // 4
@@ -300,8 +306,8 @@
     cut = b00.shape[2] - ff_rows // 2
 
     def b_rows(z0, z1, x, c, rows):
-        low = chosen(x_own ^ x, b00[z0, z1, rows, :], b10[z0, z1, rows, :])
-        high = chosen(x_own ^ x, b01[z0, z1, rows, :], b11[z0, z1, rows, :])
+        low = chosen(z0_own ^ z0, b00[z1, x, rows, :], b10[z1, x, rows, :])
+        high = chosen(z0_own ^ z0, b01[z1, x, rows, :], b11[z1, x, rows, :])
         return chosen(core ^ c, low, high)
 
     def quarter(near, far):
@@ -758,14 +764,19 @@
     meta = jnp.stack([seq_index, lax.axis_index("fsdp")]).astype(jnp.int32)
     source = hidden.reshape(rows, width)
 
-    (a0,) = call(
+    small = [w_qkv, b_qkv[None], norm_gains]
+    a0 = pl.pallas_call(
         functools.partial(cut_qkv, core),
-        [meta],
-        [w_qkv, b_qkv[None], norm_gains],
-        [sds(((d_rows + 8) // 2, qkv_w), BF)],
-        1e8,
-        [(d_rows + 8, qkv_w)],
-    )
+        out_shape=sds(((d_rows + 8) // 2, qkv_w), BF),
+        in_specs=[pl.BlockSpec(memory_space=pltpu.SMEM)] + [pl.BlockSpec(memory_space=pl.ANY)] * 3,
+        out_specs=pl.BlockSpec(memory_space=pltpu.VMEM),
+        scratch_shapes=[
+            *[pltpu.VMEM(v.shape, BF) for v in small],
+            pltpu.VMEM((d_rows + 8, qkv_w), F32),
+            pltpu.SemaphoreType.DMA((3,)),
+        ],
+        compiler_params=pltpu.CompilerParams(vmem_limit_bytes=4 * 1024 * 1024),
+    )(meta, *small)
     a1 = net.both(a0, zfar, 0)
 
     ids = segment_ids.reshape(rows, 1).astype(BF)
@@ -784,23 +795,23 @@
         axis=1,
     )
     a2 = net.both(a1, znear, 0)
-    b0 = net.half(after(half_b, a2), core, 0)
+    b0 = net.half(after(half_b, a0), core, 0)
+    bx = net.both(b0, xbit, 0)
     a_x = net.swap(a2, xbit)
     a_c = net.swap(a2, core)
     gu1 = net.both(gu0, zfar, 0)
-    b1 = net.both(b0, zfar, 0)
+    b1 = net.both(after(bx, a2), zfar, 0)
     gu2 = net.both(after(gu1, a2), znear, 0)
-    b2 = net.both(after(b1, a2), znear, 0)
     block_yc = net.swap(block_y, core)
     a_xc = net.swap(a_x, core)
     gu2 = after(gu2, a_x)
-    b2 = after(b2, a_x)
     gu_x = net.swap(gu2, xbit)
     gu_y = net.swap(gu2, ybit)
-    b_x = net.swap(b2, xbit)
     gu_c = net.swap(gu2, core)
-    b_c = net.swap(b2, core)
-    a_xc = after(a_xc, gu2, b2)
+    b_z = net.swap(b1, znear)
+    b_c = net.swap(b1, core)
+    gu_xy = net.swap(gu_x, ybit)
+    a_xc = after(a_xc, gu_x, b1)
 
     cos_t, sin_t = rope_tables(full_length, n_seq)
     block_ids = [seq_index ^ o for o in order]
@@ -827,12 +838,12 @@
         ],
         1.2e10,
         [(n_fsdp * (d_rows + 8), qkv_w), (1, qkv_w)],
-    )
-    gu_x, gu_y, b_x = after(gu_x, attended), after(gu_y, attended), after(b_x, attended)
-    gu_xy = net.swap(gu_x, ybit)
+        20,
+    )
+    gu_xy, b_z = after(gu_xy, attended), after(b_z, attended)
     gu_yc = net.swap(gu_y, core)
     gu_xc = net.swap(gu_x, core)
-    b_xc = net.swap(b_x, core)
+    b_zc = net.swap(b_z, core)
     gu_xyc = net.swap(gu_xy, core)
     gate_up = [gu2, gu_x, gu_y, gu_xy, gu_c, gu_xc, gu_yc, gu_xyc]
 
@@ -842,7 +853,7 @@
     block_out, gate_keep, gate_give, down_keep, down_give, middle_grad, attended_grad, gain_two = call(
         functools.partial(feed_forward_pieces, d_rows, ff_rows),
         [meta],
-        [attended, source, b2, b_x, b_c, b_xc, *gate_up, gains, cotangent.reshape(rows, width), weight],
+        [attended, source, b1, b_z, b_c, b_zc, *gate_up, gains, cotangent.reshape(rows, width), weight],
         [
             sds((seqs, width, length), BF),
             sds(lead + (d_rows, units // 2), BF),
@@ -855,6 +866,7 @@
         ],
         1.4e10,
         [(units // 2, width), (n_fsdp, d_rows + d_rows // 3, width)],
+        32,
     )
     block_out = block_out.reshape(micro, batch, width, length).swapaxes(2, 3)
 
@@ -864,10 +876,12 @@
     def halves(keep, got):
         return add(keep[0], got[0]), add(keep[1], got[1])
 
-    gate, gate_give = halves(gate_keep, net.swap(gate_give, core))
-    down, down_give = halves(down_keep, net.swap(down_give, core))
+    gate_got = net.swap(gate_give, core)
+    down_got = net.swap(after(down_give, gate_got), core)
+    gate, gate_give = halves(gate_keep, gate_got)
+    gate_got = net.swap(gate_give, xbit)
+    down, down_give = halves(down_keep, down_got)
     attended_grad = after(attended_grad, gate_give, down_give)
-    gate_got = net.swap(gate_give, xbit)
     down_got = net.swap(down_give, ybit)
 
     dq, dkv_keep, dkv_give, rest_keep, rest_give = call(
@@ -883,46 +897,47 @@
         ],
         1.4e10,
         [(width, 1024), (1, qkv_w), (1, width), (n_fsdp, 8, 1024)],
+        24,
     )
     gate, gate_give = halves(gate, after(gate_got, dq))
     gate_got = net.swap(gate_give, znear)
-    dkv, dkv_give = halves(dkv_keep, after(net.swap(dkv_give, core), gate_give))
-    rest, rest_give = halves(rest_keep, after(net.swap(rest_give, core), gate_give))
     down, down_give = halves(down, after(down_got, gate_give))
+    dkv, dkv_give = halves(dkv_keep, after(net.swap(dkv_give, core), down_give))
+    rest, rest_give = halves(rest_keep, after(net.swap(rest_give, core), down_give))
     dkv_got = net.swap(dkv_give, ybit)
     rest_got = net.swap(rest_give, ybit)
     down_got = net.swap(down_give, xbit)
+    gate, gate_give = halves(gate, gate_got)
+    gate_got = net.swap(gate_give, zfar)
+    rest, rest_give = halves(rest, after(rest_got, gate_give))
+    rest_got = net.swap(rest_give, xbit)
     (hidden_grad,) = call(
         input_gradient_two,
         [],
-        [dq, dkv, dkv_got, source, middle_grad, wf, gains],
+        [dq, dkv, after(dkv_got, rest_give), source, middle_grad, wf, gains],
         [sds((seqs, width, length), F32)],
         3e9,
-    )
-    rest_got = after(rest_got, hidden_grad)
+        mib=16,
+    )
+    down, down_give = halves(down, after(down_got, hidden_grad))
     hidden_grad = hidden_grad.reshape(micro, batch, width, length).swapaxes(2, 3)
-    rest, rest_give = halves(rest, rest_got)
-    rest_got = net.swap(rest_give, xbit)
-    gate, gate_give = halves(gate, gate_got)
-    gate_got = net.swap(gate_give, zfar)
-    down, down_give = halves(down, down_got)
     down_got = net.swap(down_give, znear)
-    rest, rest_give = halves(rest, rest_got)
-    rest_got = net.swap(rest_give, znear)
     gate = add(gate, gate_got)
     gate_got = net.swap(gate, ybit)
-    down, down_give = halves(down, down_got)
+    rest, rest_give = halves(rest, after(rest_got, gate))
+    rest_got = net.swap(rest_give, znear)
+    down, down_give = halves(down, after(down_got, rest_give))
     down_got = net.swap(down_give, zfar)
+    gate = add(gate, gate_got)
     rest, rest_give = halves(rest, rest_got)
     rest_got = net.swap(rest_give, zfar)
-    down = add(down, down_got)
+    down = add(down, after(down_got, rest_give))
     rest = add(rest, rest_got)
 
     def spread(part):
         other = net.swap(part, ybit)
         return [part, other, net.swap(part, core), net.swap(other, core)]
 
-    gate = add(gate, gate_got)
     gate = [gate, net.swap(gate, core)]
     qk, v = (QW + KW) // n_fsdp, KW // n_fsdp
     out_gate, out_down, out_wout, out_qkv, b_qk, b_v, out_gains = call(
@@ -940,6 +955,7 @@
         ],
         3e9,
         [(d_rows + 8, 1024)],
+        16,
     )
     return (
         block_out,

time: 164 us -> 175 us (1.067)
  waiting for transfers between devices: 71.1 us -> 81.7 us
  local copies, waits for them, and re-layouts: 5.61 us -> 15.4 us
  Pallas kernels: 42.4 us -> 34 us
  other arithmetic: 6.93 us -> 3.97 us
  starting transfers between devices: 36.6 us -> 38.4 us
    ppermute x46, waiting for transfers between devices: 71.1 us -> 81.7 us  [swap(): return lax.ppermute(value, ('fsdp', 'seq'), pairs)]
    unnamed x44 -> x56, local copies, waits for them, and re-layouts: 4.56 us -> 14.3 us
    pallas_call x6 -> x5, Pallas kernels: 42.4 us -> 33.2 us  [call(): pl.pallas_call(kernel, out_shape=outs, in_specs=specs, out_specs=whole(*o...]
    ppermute x46, starting transfers between devices: 36.6 us -> 38.4 us  [swap(): return lax.ppermute(value, ('fsdp', 'seq'), pairs)]
  transfers between devices with their start and end apart: 46 -> 46, of which waited for: 18 -> 22; matrix products, arithmetic and copies ran while one was open for 6% -> 4% of each run, Pallas kernels for 16% -> 12%
where the time goes in v3:
time: 175 us
  waiting for transfers between devices  81.7 us (47%)
  starting transfers between devices  38.4 us (22%)
  Pallas kernels  34 us (19%)
  local copies, waits for them, and re-layouts  15.4 us (9%)
  other arithmetic  3.97 us (2%)
    ppermute x46, waiting for transfers between devices, swap(): return lax.ppermute(value, ('fsdp', 'seq'), pairs)  81.7 us
    ppermute x46, starting transfers between devices, swap(): return lax.ppermute(value, ('fsdp', 'seq'), pairs)  38.4 us
    pallas_call x5, Pallas kernels, call(): pl.pallas_call(kernel, out_shape=outs, in_specs=specs, out_specs=whole(*o...  33.2 us
    unnamed x56, local copies, waits for them, and re-layouts  14.3 us
  transfers between devices with their start and end apart: 46, of which 22 were waited for; matrix products, arithmetic and copies ran while one was open for 4% of the time, Pallas kernels for 12%

profile of v3, /device:TPU:0, one launch (start us, length us, event | category | flops | bytes accessed | tf_op | source)
XLA Modules:
  0.0 174.6 jit_solution(15384250853777236769)
XLA Ops:
  3.8 4.1 %collective-permute-start.3 = (bf16[40,960]{1,0:T(8,128)(2,1)S(1)}, bf16[40,960]{1,0:T(8,128)(2,1)S(1)}, u32[]{:S(2)}, u32[]{:S(2)}) collective-permute-start(bf16[40,960]{1,0:T(8,128)(2,1)S(1)} %shard_map.187), channel_id=1, source_target_pairs={{0,16},{1,17},{2,18},{3,19},{4,20},{5,21},{6,22},{7,23},{8,24},{9,... | collective-permute-start | bytes 230408 | tf_op jit(solution)/shard_map/ppermute | solution.py:496
  10.0 1.6 collective-permute-start
  12.1 1.6 collective-permute-start.11
  14.2 1.6 collective-permute-start.4
  15.9 4.3 %collective-permute-done.8 = bf16[72,768]{1,0:T(8,128)(2,1)S(1)} collective-permute-done((bf16[72,768]{1,0:T(8,128)(2,1)S(1)}, bf16[72,768]{1,0:T(8,128)(2,1)S(1)}, u32[]{:S(2)}, u32[]{:S(2)}) %collective-permute-start.8) | collective-permute-done | bytes 110624 | tf_op jit(solution)/shard_map/ppermute | solution.py:496
  23.0 4.2 %collective-permute-start.12 = (bf16[2,136,576]{2,1,0:T(8,128)(2,1)S(1)}, bf16[2,136,576]{2,1,0:T(8,128)(2,1)S(1)}, u32[]{:S(2)}, u32[]{:S(2)}) collective-permute-start(bf16[2,136,576]{2,1,0:T(8,128)(2,1)S(1)} %pad_maximum_fusion.3), channel_id=1, source_target_pairs={{0,16},{1,17},{2,18},{3,19},{4,20},{5,21},{6,22},{7,23},{8,24},{9,... | collective-permute-start | bytes 940040 | tf_op jit(solution)/shard_map/ppermute | solution.py:496
  27.6 7.4 %collective-permute-done.9 = bf16[2,72,768]{2,1,0:T(8,128)(2,1)S(1)} collective-permute-done((bf16[2,72,768]{2,1,0:T(8,128)(2,1)S(1)}, bf16[2,72,768]{2,1,0:T(8,128)(2,1)S(1)}, u32[]{:S(2)}, u32[]{:S(2)}) %collective-permute-start.9) | collective-permute-done | bytes 221216 | tf_op jit(solution)/shard_map/ppermute | solution.py:496
  35.7 7.1 %collective-permute-done.12 = bf16[2,136,576]{2,1,0:T(8,128)(2,1)S(1)} collective-permute-done((bf16[2,136,576]{2,1,0:T(8,128)(2,1)S(1)}, bf16[2,136,576]{2,1,0:T(8,128)(2,1)S(1)}, u32[]{:S(2)}, u32[]{:S(2)}) %collective-permute-start.12) | collective-permute-done | bytes 313376 | tf_op jit(solution)/shard_map/ppermute | solution.py:496
  45.4 8.9 %collective-permute-done.10.g100 = bf16[2,2,72,768]{3,2,1,0:T(8,128)(2,1)} collective-permute-done((bf16[2,2,72,768]{3,2,1,0:T(8,128)(2,1)S(1)}, bf16[2,2,72,768]{3,2,1,0:T(8,128)(2,1)}, u32[]{:S(2)}, u32[]{:S(2)}) %collective-permute-start.10) | collective-permute-done | bytes 442400 | tf_op jit(solution)/shard_map/ppermute | solution.py:496
  54.9 8.3 %shard_map.188 = (bf16[256,576]{1,0:T(8,128)(2,1)S(1)}, bf16[2,3,384,64]{3,2,1,0:T(8,128)(2,1)S(1)}, bf16[2,3,512,64]{3,2,1,0:T(8,128)(2,1)S(1)}, bf16[2,3,512,6...) custom-call(s32[2]{0:T(128)S(1)} %pad_add_fusion.meta, ...), custom_call_target="tpu_custom_call" | custom-call | flops 12000000000 | bytes 6084096 | tf_op jit(solution)/shard_map/pallas_call | solution.py:53
  68.6 1.8 %collective-permute-done.13.b10 = bf16[2,2,136,576]{3,2,1,0:T(8,128)(2,1)} collective-permute-done((bf16[2,2,136,576]{3,2,1,0:T(8,128)(2,1)S(1)}, bf16[2,2,136,576]{3,2,1,0:T(8,128)(2,1)}, u32[]{:S(2)}, u32[]{:S(2)}) %collective-permute-start.13) | collective-permute-done | bytes 626720 | tf_op jit(solution)/shard_map/ppermute | solution.py:496
  76.8 11.1 %shard_map.189 = (bf16[2,576,128]{2,1,0:T(8,128)(2,1)}, bf16[2,2,2,2,72,768]{5,4,3,2,1,0:T(8,128)(2,1)S(1)}, bf16[2,2,2,2,72,768]{5,4,3,2,1,0:T(8,128)(2,1)S(1)}...) custom-call(s32[2]{0:T(128)S(1)} %pad_add_fusion.meta, ...), custom_call_target="tpu_custom_call" | custom-call | flops 14000000000 | bytes 14311168 | tf_op jit(solution)/shard_map/pallas_call | solution.py:53
  88.1 3.5 %collective-permute-done.22 = bf16[2,2,2,2,72,768]{5,4,3,2,1,0:T(8,128)(2,1)S(1)} collective-permute-done((bf16[2,2,2,2,72,768]{5,4,3,2,1,0:T(8,128)(2,1)S(1)}, bf16[2,2,2,2,72,768]{5,4,3,2,1,0:T(8,128)(2,1)S(1)}, u32[]{:S(2)}, u32[]{:S(2)}) %collective-permute-start.22) | collective-permute-done | bytes 1769504 | tf_op jit(solution)/shard_map/ppermute | solution.py:496
  92.9 2.0 %collective-permute-done.23 = bf16[2,2,2,2,72,576]{5,4,3,2,1,0:T(8,128)(2,1)S(1)} collective-permute-done((bf16[2,2,2,2,72,576]{5,4,3,2,1,0:T(8,128)(2,1)S(1)}, bf16[2,2,2,2,72,576]{5,4,3,2,1,0:T(8,128)(2,1)S(1)}, u32[]{:S(2)}, u32[]{:S(2)}) %collective-permute-start.23) | collective-permute-done | bytes 1327136 | tf_op jit(solution)/shard_map/ppermute | solution.py:496
  97.0 9.8 %shard_map.190 = (bf16[256,640]{1,0:T(8,128)(2,1)S(1)}, bf16[2,256,384]{2,1,0:T(8,128)(2,1)S(1)}, bf16[2,256,384]{2,1,0:T(8,128)(2,1)S(1)}, bf16[2,2,2,2,80,256]...) custom-call(s32[2]{0:T(128)S(1)} %pad_add_fusion.meta, bf16[256,640]{1,0:T(8,128)(2,1)S(1)} %pad_maximum_fusion.4.b0, ...), custom_call_target="tpu_custom_call" | custom-call | flops 14000000000 | bytes 7282432 | tf_op jit(solution)/shard_map/pallas_call | solution.py:53
  106.8 7.4 %collective-permute-done.26 = bf16[2,2,2,72,768]{4,3,2,1,0:T(8,128)(2,1)S(1)} collective-permute-done((bf16[2,2,2,72,768]{4,3,2,1,0:T(8,128)(2,1)S(1)}, bf16[2,2,2,72,768]{4,3,2,1,0:T(8,128)(2,1)S(1)}, u32[]{:S(2)}, u32[]{:S(2)}) %collective-permute-start.26) | collective-permute-done | bytes 884768 | tf_op jit(solution)/shard_map/ppermute | solution.py:496
  116.7 9.4 %collective-permute-done.30 = bf16[2,2,72,768]{3,2,1,0:T(8,128)(2,1)S(1)} collective-permute-done((bf16[2,2,72,768]{3,2,1,0:T(8,128)(2,1)S(1)}, bf16[2,2,72,768]{3,2,1,0:T(8,128)(2,1)S(1)}, u32[]{:S(2)}, u32[]{:S(2)}) %collective-permute-start.30) | collective-permute-done | bytes 442400 | tf_op jit(solution)/shard_map/ppermute | solution.py:496
  127.4 5.1 %collective-permute-done.25 = bf16[2,2,2,72,576]{4,3,2,1,0:T(8,128)(2,1)S(1)} collective-permute-done((bf16[2,2,2,72,576]{4,3,2,1,0:T(8,128)(2,1)S(1)}, bf16[2,2,2,72,576]{4,3,2,1,0:T(8,128)(2,1)S(1)}, u32[]{:S(2)}, u32[]{:S(2)}) %collective-permute-start.25) | collective-permute-done | bytes 663584 | tf_op jit(solution)/shard_map/ppermute | solution.py:496
  135.8 1.8 %collective-permute-done.31 = bf16[2,72,768]{2,1,0:T(8,128)(2,1)S(1)} collective-permute-done((bf16[2,72,768]{2,1,0:T(8,128)(2,1)S(1)}, bf16[2,72,768]{2,1,0:T(8,128)(2,1)S(1)}, u32[]{:S(2)}, u32[]{:S(2)}) %collective-permute-start.31) | collective-permute-done | bytes 221216 | tf_op jit(solution)/shard_map/ppermute | solution.py:496
  138.6 5.7 %collective-permute-done.29 = bf16[2,2,2,80,256]{4,3,2,1,0:T(8,128)(2,1)S(1)} collective-permute-done((bf16[2,2,2,80,256]{4,3,2,1,0:T(8,128)(2,1)S(1)}, bf16[2,2,2,80,256]{4,3,2,1,0:T(8,128)(2,1)S(1)}, u32[]{:S(2)}, u32[]{:S(2)}) %collective-permute-start.29) | collective-permute-done | bytes 327712 | tf_op jit(solution)/shard_map/ppermute | solution.py:496
  144.3 1.6 collective-permute-start.36
  145.9 2.0 %collective-permute-done.27.other = bf16[256,384]{1,0:T(8,128)(2,1)S(1)} collective-permute-done((bf16[256,384]{1,0:T(8,128)(2,1)S(1)}, bf16[256,384]{1,0:T(8,128)(2,1)S(1)}, u32[]{:S(2)}, u32[]{:S(2)}) %collective-permute-start.27) | collective-permute-done | bytes 196640 | tf_op jit(solution)/shard_map/ppermute | solution.py:496
  147.9 1.9 %shard_map.191 = f32[2,576,128]{2,1,0:T(8,128)} custom-call(bf16[256,640]{1,0:T(8,128)(2,1)S(1)} %get-tuple-element.82.dq, bf16[256,384]{1,0:T(8,128)(2,1)S(1)} %get-tuple-element.134.own, bf16[256,384]{1,0:T(8,128)(2,1)S(1)} %collective-permute-done.27.other, bf16[256,576]{1,0:T(8,128)(2,1)S(1)} %bitcast.184, f32[256,576]{1,0:T(8,128)S(1)} %get-tuple-element.93.mid, ...), custom_call_target="tpu_custom_call" | custom-call | flops 3000000000 | bytes 3305984 | tf_op jit(solution)/shard_map/pallas_call | solution.py:53
  150.0 1.7 collective-permute-start.35
  152.2 4.4 %collective-permute-done.35 = bf16[2,72,576]{2,1,0:T(8,128)(2,1)S(1)} collective-permute-done((bf16[2,72,576]{2,1,0:T(8,128)(2,1)S(1)}, bf16[2,72,576]{2,1,0:T(8,128)(2,1)S(1)}, u32[]{:S(2)}, u32[]{:S(2)}) %collective-permute-start.35) | collective-permute-done | bytes 165920 | tf_op jit(solution)/shard_map/ppermute | solution.py:496
  156.6 1.8 %collective-permute-start.37 = (bf16[72,576]{1,0:T(8,128)(2,1)S(1)}, bf16[72,576]{1,0:T(8,128)(2,1)S(1)}, u32[]{:S(2)}, u32[]{:S(2)}) collective-permute-start(bf16[72,576]{1,0:T(8,128)(2,1)S(1)} %fusion.28), channel_id=1, source_target_pairs={{0,16},{1,17},{2,18},{3,19},{4,20},{5,21},{6,22},{7,23},{8,24},{9,... | collective-permute-start | bytes 248840 | tf_op jit(solution)/shard_map/ppermute | solution.py:496
  159.6 2.5 %collective-permute-done.37 = bf16[72,576]{1,0:T(8,128)(2,1)S(1)} collective-permute-done((bf16[72,576]{1,0:T(8,128)(2,1)S(1)}, bf16[72,576]{1,0:T(8,128)(2,1)S(1)}, u32[]{:S(2)}, u32[]{:S(2)}) %collective-permute-start.37) | collective-permute-done | bytes 82976 | tf_op jit(solution)/shard_map/ppermute | solution.py:496
  162.1 2.4 %collective-permute-start.39 = (bf16[72,576]{1,0:T(8,128)(2,1)S(1)}, bf16[72,576]{1,0:T(8,128)(2,1)S(1)}, u32[]{:S(2)}, u32[]{:S(2)}) collective-permute-start(bf16[72,576]{1,0:T(8,128)(2,1)S(1)} %fusion.22.d0), channel_id=1, source_target_pairs={{0,2},{1,3},{2,0},{3,1},{4,6},{5,7},{6,4},{7,5},{8,10},{9,11},{10,... | collective-permute-start | bytes 248840 | tf_op jit(solution)/shard_map/ppermute | solution.py:496
  165.1 1.9 %collective-permute-done.39.d1 = bf16[72,576]{1,0:T(8,128)(2,1)S(1)} collective-permute-done((bf16[72,576]{1,0:T(8,128)(2,1)S(1)}, bf16[72,576]{1,0:T(8,128)(2,1)S(1)}, u32[]{:S(2)}, u32[]{:S(2)}) %collective-permute-start.39) | collective-permute-done | bytes 82976 | tf_op jit(solution)/shard_map/ppermute | solution.py:496
  167.1 2.1 %collective-permute-start.43 = (bf16[80,256]{1,0:T(8,128)(2,1)S(1)}, bf16[80,256]{1,0:T(8,128)(2,1)S(1)}, u32[]{:S(2)}, u32[]{:S(2)}) collective-permute-start(bf16[80,256]{1,0:T(8,128)(2,1)S(1)} %fusion.30.r0), channel_id=1, source_target_pairs={{0,2},{1,3},{2,0},{3,1},{4,6},{5,7},{6,4},{7,5},{8,10},{9,11},{10,... | collective-permute-start | bytes 122888 | tf_op jit(solution)/shard_map/ppermute | solution.py:496
  169.4 2.0 %collective-permute-done.43.r1 = bf16[80,256]{1,0:T(8,128)(2,1)S(1)} collective-permute-done((bf16[80,256]{1,0:T(8,128)(2,1)S(1)}, bf16[80,256]{1,0:T(8,128)(2,1)S(1)}, u32[]{:S(2)}, u32[]{:S(2)}) %collective-permute-start.43) | collective-permute-done | bytes 40992 | tf_op jit(solution)/shard_map/ppermute | solution.py:496
  172.6 1.9 %shard_map.192 = (f32[72,3072]{1,0:T(8,128)}, f32[192,576]{1,0:T(8,128)}, f32[72,576]{1,0:T(8,128)}, f32[72,960]{1,0:T(8,128)}, f32[1,96]{1,0:T(1,128)}, /*index=5*/f32[1,24]{1,0:T(1,128)}, f32[2,72]{1,0:T(2,128)}) custom-call(s32[2]{0:T(128)S(1)} %pad_add_fusion.meta, bf16[2,72,768]{2,1,0:T(8,128)(2,1)S(1)} %add_convert_fusion.6.near, ...), custom_call_target="tpu_custom_call" | custom-call | flops 3000000000 | bytes 2708512 | tf_op jit(solution)/shard_map/pallas_call | solution.py:53
  (171 shorter events, 40.6 us)
Async XLA Ops:
  3.8 10.4 %collective-permute-start.3 = (bf16[40,960]{1,0:T(8,128)(2,1)S(1)}, bf16[40,960]{1,0:T(8,128)(2,1)S(1)}, u32[]{:S(2)}, u32[]{:S(2)}) collective-permute-start(bf16[40,960]{1,0:T(8,128)(2,1)S(1)} %shard_map.187), channel_id=1, source_target_pairs={{0,16},{1,17},{2,18},{3,19},{4,20},{5,21},{6,22},{7,23},{8,24},{9,... | collective-permute-start | bytes 230408 | tf_op jit(solution)/shard_map/ppermute | solution.py:496
  10.0 17.4 %collective-permute-start.1 = (bf16[256,640]{1,0:T(8,128)(2,1)S(1)}, bf16[256,640]{1,0:T(8,128)(2,1)S(1)}, u32[]{:S(2)}, u32[]{:S(2)}) collective-permute-start(bf16[256,640]{1,0:T(8,128)(2,1)S(1)} %pad_maximum_fusion.4.b0), channel_id=1, source_target_pairs={{0,1},{1,0},{2,3},{3,2},{4,5},{5,4},{6,7},{7,6},{8,9},{9,8},{10,11... | collective-permute-start | bytes 983048 | tf_op jit(solution)/shard_map/ppermute | solution.py:496
  10.0 12.9 %collective-permute-start = (bf16[256,640]{1,0:T(8,128)(2,1)S(1)}, bf16[256,640]{1,0:T(8,128)(2,1)S(1)}, u32[]{:S(2)}, u32[]{:S(2)}) collective-permute-start(bf16[256,640]{1,0:T(8,128)(2,1)S(1)} %pad_maximum_fusion.4.b0), channel_id=1, source_target_pairs={{0,2},{1,3},{2,0},{3,1},{4,6},{5,7},{6,4},{7,5},{8,10},{9,11},{10,... | collective-permute-start | bytes 983048 | tf_op jit(solution)/shard_map/ppermute | solution.py:496
  11.6 8.6 %collective-permute-start.8 = (bf16[72,768]{1,0:T(8,128)(2,1)S(1)}, bf16[72,768]{1,0:T(8,128)(2,1)S(1)}, u32[]{:S(2)}, u32[]{:S(2)}) collective-permute-start(bf16[72,768]{1,0:T(8,128)(2,1)S(1)} %constant_dynamic-slice_fusion), channel_id=1, source_target_pairs={{0,16},{1,17},{2,18},{3,19},{4,20},{5,21},{6,22},{7,23},{8,24},{9,... | collective-permute-start | bytes 331784 | tf_op jit(solution)/shard_map/ppermute | solution.py:496
  12.1 8.1 %collective-permute-start.11 = (bf16[136,576]{1,0:T(8,128)(2,1)S(1)}, bf16[136,576]{1,0:T(8,128)(2,1)S(1)}, u32[]{:S(2)}, u32[]{:S(2)}) collective-permute-start(bf16[136,576]{1,0:T(8,128)(2,1)S(1)} %dynamic-slice_bitcast_fusion), channel_id=1, source_target_pairs={{0,4},{1,5},{2,6},{3,7},{4,0},{5,1},{6,2},{7,3},{8,12},{9,13},{10,... | collective-permute-start | bytes 470024 | tf_op jit(solution)/shard_map/ppermute | solution.py:496
  14.2 7.0 %collective-permute-start.4 = (bf16[2,40,960]{2,1,0:T(8,128)(2,1)S(1)}, bf16[2,40,960]{2,1,0:T(8,128)(2,1)S(1)}, u32[]{:S(2)}, u32[]{:S(2)}) collective-permute-start(bf16[2,40,960]{2,1,0:T(8,128)(2,1)S(1)} %pad_maximum_fusion.7), channel_id=1, source_target_pairs={{0,8},{1,9},{2,10},{3,11},{4,12},{5,13},{6,14},{7,15},{8,0},{9,1},... | collective-permute-start | bytes 460808 | tf_op jit(solution)/shard_map/ppermute | solution.py:496
  21.3 33.0 %collective-permute-start.6 = (bf16[2,2,40,960]{3,2,1,0:T(8,128)(2,1)S(1)}, bf16[2,2,40,960]{3,2,1,0:T(8,128)(2,1)S(1)}, u32[]{:S(2)}, u32[]{:S(2)}) collective-permute-start(bf16[2,2,40,960]{3,2,1,0:T(8,128)(2,1)S(1)} %pad_maximum_fusion.5.a00), channel_id=1, source_target_pairs={{0,1},{1,0},{2,3},{3,2},{4,5},{5,4},{6,7},{7,6},{8,9},{9,8},{10,11... | collective-permute-start | bytes 921608 | tf_op jit(solution)/shard_map/ppermute | solution.py:496
  21.4 13.7 %collective-permute-start.5 = (bf16[2,2,40,960]{3,2,1,0:T(8,128)(2,1)S(1)}, bf16[2,2,40,960]{3,2,1,0:T(8,128)(2,1)S(1)}, u32[]{:S(2)}, u32[]{:S(2)}) collective-permute-start(bf16[2,2,40,960]{3,2,1,0:T(8,128)(2,1)S(1)} %pad_maximum_fusion.5.a00), channel_id=1, source_target_pairs={{0,4},{1,5},{2,6},{3,7},{4,0},{5,1},{6,2},{7,3},{8,12},{9,13},{10,... | collective-permute-start | bytes 921608 | tf_op jit(solution)/shard_map/ppermute | solution.py:496
  23.0 12.0 %collective-permute-start.9 = (bf16[2,72,768]{2,1,0:T(8,128)(2,1)S(1)}, bf16[2,72,768]{2,1,0:T(8,128)(2,1)S(1)}, u32[]{:S(2)}, u32[]{:S(2)}) collective-permute-start(bf16[2,72,768]{2,1,0:T(8,128)(2,1)S(1)} %pad_maximum_fusion.6), channel_id=1, source_target_pairs={{0,8},{1,9},{2,10},{3,11},{4,12},{5,13},{6,14},{7,15},{8,0},{9,1},... | collective-permute-start | bytes 663560 | tf_op jit(solution)/shard_map/ppermute | solution.py:496
  23.0 19.9 %collective-permute-start.12 = (bf16[2,136,576]{2,1,0:T(8,128)(2,1)S(1)}, bf16[2,136,576]{2,1,0:T(8,128)(2,1)S(1)}, u32[]{:S(2)}, u32[]{:S(2)}) collective-permute-start(bf16[2,136,576]{2,1,0:T(8,128)(2,1)S(1)} %pad_maximum_fusion.3), channel_id=1, source_target_pairs={{0,16},{1,17},{2,18},{3,19},{4,20},{5,21},{6,22},{7,23},{8,24},{9,... | collective-permute-start | bytes 940040 | tf_op jit(solution)/shard_map/ppermute | solution.py:496
  27.3 16.2 %collective-permute-start.2 = (bf16[256,640]{1,0:T(8,128)(2,1)S(1)}, bf16[256,640]{1,0:T(8,128)(2,1)S(1)}, u32[]{:S(2)}, u32[]{:S(2)}) collective-permute-start(bf16[256,640]{1,0:T(8,128)(2,1)S(1)} %collective-permute-done.b1), channel_id=1, source_target_pairs={{0,1},{1,0},{2,3},{3,2},{4,5},{5,4},{6,7},{7,6},{8,9},{9,8},{10,11... | collective-permute-start | bytes 983048 | tf_op jit(solution)/shard_map/ppermute | solution.py:496
  35.1 35.9 %collective-permute-start.18 = (bf16[2,2,72,768]{3,2,1,0:T(8,128)(2,1)S(1)}, bf16[2,2,72,768]{3,2,1,0:T(8,128)(2,1)S(1)}, u32[]{:S(2)}, u32[]{:S(2)}) collective-permute-start(bf16[2,2,72,768]{3,2,1,0:T(8,128)(2,1)S(1)} %pad_maximum_fusion.1.g000), channel_id=1, source_target_pairs={{0,1},{1,0},{2,3},{3,2},{4,5},{5,4},{6,7},{7,6},{8,9},{9,8},{10,11... | collective-permute-start | bytes 1327112 | tf_op jit(solution)/shard_map/ppermute | solution.py:496
  35.2 35.2 %collective-permute-start.16 = (bf16[2,2,72,768]{3,2,1,0:T(8,128)(2,1)S(1)}, bf16[2,2,72,768]{3,2,1,0:T(8,128)(2,1)}, u32[]{:S(2)}, u32[]{:S(2)}) collective-permute-start(bf16[2,2,72,768]{3,2,1,0:T(8,128)(2,1)S(1)} %pad_maximum_fusion.1.g000), channel_id=1, source_target_pairs={{0,2},{1,3},{2,0},{3,1},{4,6},{5,7},{6,4},{7,5},{8,10},{9,11},{10,... | collective-permute-start | bytes 1327112 | tf_op jit(solution)/shard_map/ppermute | solution.py:496
  42.8 11.5 %collective-permute-start.10 = (bf16[2,2,72,768]{3,2,1,0:T(8,128)(2,1)S(1)}, bf16[2,2,72,768]{3,2,1,0:T(8,128)(2,1)}, u32[]{:S(2)}, u32[]{:S(2)}) collective-permute-start(bf16[2,2,72,768]{3,2,1,0:T(8,128)(2,1)S(1)} %pad_maximum_fusion.1.g000), channel_id=1, source_target_pairs={{0,4},{1,5},{2,6},{3,7},{4,0},{5,1},{6,2},{7,3},{8,12},{9,13},{10,... | collective-permute-start | bytes 1327112 | tf_op jit(solution)/shard_map/ppermute | solution.py:496
  45.3 28.3 %collective-permute-start.14 = (bf16[2,2,136,576]{3,2,1,0:T(8,128)(2,1)S(1)}, bf16[2,2,136,576]{3,2,1,0:T(8,128)(2,1)}, u32[]{:S(2)}, u32[]{:S(2)}) collective-permute-start(bf16[2,2,136,576]{3,2,1,0:T(8,128)(2,1)S(1)} %pad_maximum_fusion.b00), channel_id=1, source_target_pairs={{0,1},{1,0},{2,3},{3,2},{4,5},{5,4},{6,7},{7,6},{8,9},{9,8},{10,11... | collective-permute-start | bytes 1880072 | tf_op jit(solution)/shard_map/ppermute | solution.py:496
  54.3 16.0 %collective-permute-start.13 = (bf16[2,2,136,576]{3,2,1,0:T(8,128)(2,1)S(1)}, bf16[2,2,136,576]{3,2,1,0:T(8,128)(2,1)}, u32[]{:S(2)}, u32[]{:S(2)}) collective-permute-start(bf16[2,2,136,576]{3,2,1,0:T(8,128)(2,1)S(1)} %pad_maximum_fusion.b00), channel_id=1, source_target_pairs={{0,8},{1,9},{2,10},{3,11},{4,12},{5,13},{6,14},{7,15},{8,0},{9,1},... | collective-permute-start | bytes 1880072 | tf_op jit(solution)/shard_map/ppermute | solution.py:496
  54.4 16.5 %collective-permute-start.17 = (bf16[2,2,72,768]{3,2,1,0:T(8,128)(2,1)}, bf16[2,2,72,768]{3,2,1,0:T(8,128)(2,1)}, u32[]{:S(2)}, u32[]{:S(2)}) collective-permute-start(bf16[2,2,72,768]{3,2,1,0:T(8,128)(2,1)} %collective-permute-done.10.g100), channel_id=1, source_target_pairs={{0,2},{1,3},{2,0},{3,1},{4,6},{5,7},{6,4},{7,5},{8,10},{9,11},{10,... | collective-permute-start | bytes 1327112 | tf_op jit(solution)/shard_map/ppermute | solution.py:496
  92.3 22.0 %collective-permute-start.26 = (bf16[2,2,2,72,768]{4,3,2,1,0:T(8,128)(2,1)S(1)}, bf16[2,2,2,72,768]{4,3,2,1,0:T(8,128)(2,1)S(1)}, u32[]{:S(2)}, u32[]{:S(2)}) collective-permute-start(bf16[2,2,2,72,768]{4,3,2,1,0:T(8,128)(2,1)S(1)} %get-tuple-element.124), channel_id=1, source_target_pairs={{0,4},{1,5},{2,6},{3,7},{4,0},{5,1},{6,2},{7,3},{8,12},{9,13},{10,... | collective-permute-start | bytes 2654216 | tf_op jit(solution)/shard_map/ppermute | solution.py:496
  114.4 11.7 %collective-permute-start.30 = (bf16[2,2,72,768]{3,2,1,0:T(8,128)(2,1)S(1)}, bf16[2,2,72,768]{3,2,1,0:T(8,128)(2,1)S(1)}, u32[]{:S(2)}, u32[]{:S(2)}) collective-permute-start(bf16[2,2,72,768]{3,2,1,0:T(8,128)(2,1)S(1)} %get-tuple-element.128), channel_id=1, source_target_pairs={{0,8},{1,9},{2,10},{3,11},{4,12},{5,13},{6,14},{7,15},{8,0},{9,1},... | collective-permute-start | bytes 1327112 | tf_op jit(solution)/shard_map/ppermute | solution.py:496
  114.8 17.7 %collective-permute-start.25 = (bf16[2,2,2,72,576]{4,3,2,1,0:T(8,128)(2,1)S(1)}, bf16[2,2,2,72,576]{4,3,2,1,0:T(8,128)(2,1)S(1)}, u32[]{:S(2)}, u32[]{:S(2)}) collective-permute-start(bf16[2,2,2,72,576]{4,3,2,1,0:T(8,128)(2,1)S(1)} %get-tuple-element.126), channel_id=1, source_target_pairs={{0,2},{1,3},{2,0},{3,1},{4,6},{5,7},{6,4},{7,5},{8,10},{9,11},{10,... | collective-permute-start | bytes 1990664 | tf_op jit(solution)/shard_map/ppermute | solution.py:496
  116.2 17.1 %collective-permute-start.28 = (bf16[2,2,2,2,80,256]{5,4,3,2,1,0:T(8,128)(2,1)S(1)}, bf16[2,2,2,2,80,256]{5,4,3,2,1,0:T(8,128)(2,1)S(1)}, u32[]{:S(2)}, u32[]{:S(2)}) collective-permute-start(bf16[2,2,2,2,80,256]{5,4,3,2,1,0:T(8,128)(2,1)S(1)} %get-tuple-element.89), channel_id=1, source_target_pairs={{0,1},{1,0},{2,3},{3,2},{4,5},{5,4},{6,7},{7,6},{8,9},{9,8},{10,11... | collective-permute-start | bytes 1966088 | tf_op jit(solution)/shard_map/ppermute | solution.py:496
  116.2 17.1 %collective-permute-start.24 = (bf16[2,256,384]{2,1,0:T(8,128)(2,1)S(1)}, bf16[2,256,384]{2,1,0:T(8,128)(2,1)S(1)}, u32[]{:S(2)}, u32[]{:S(2)}) collective-permute-start(bf16[2,256,384]{2,1,0:T(8,128)(2,1)S(1)} %get-tuple-element.84), channel_id=1, source_target_pairs={{0,1},{1,0},{2,3},{3,2},{4,5},{5,4},{6,7},{7,6},{8,9},{9,8},{10,11... | collective-permute-start | bytes 1179656 | tf_op jit(solution)/shard_map/ppermute | solution.py:496
  126.2 11.4 %collective-permute-start.31 = (bf16[2,72,768]{2,1,0:T(8,128)(2,1)S(1)}, bf16[2,72,768]{2,1,0:T(8,128)(2,1)S(1)}, u32[]{:S(2)}, u32[]{:S(2)}) collective-permute-start(bf16[2,72,768]{2,1,0:T(8,128)(2,1)S(1)} %fusion.16), channel_id=1, source_target_pairs={{0,16},{1,17},{2,18},{3,19},{4,20},{5,21},{6,22},{7,23},{8,24},{9,... | collective-permute-start | bytes 663560 | tf_op jit(solution)/shard_map/ppermute | solution.py:496
  132.7 17.2 %collective-permute-start.34 = (bf16[2,2,72,576]{3,2,1,0:T(8,128)(2,1)S(1)}, bf16[2,2,72,576]{3,2,1,0:T(8,128)(2,1)S(1)}, u32[]{:S(2)}, u32[]{:S(2)}) collective-permute-start(bf16[2,2,72,576]{3,2,1,0:T(8,128)(2,1)S(1)} %get-tuple-element.130), channel_id=1, source_target_pairs={{0,4},{1,5},{2,6},{3,7},{4,0},{5,1},{6,2},{7,3},{8,12},{9,13},{10,... | collective-permute-start | bytes 995336 | tf_op jit(solution)/shard_map/ppermute | solution.py:496
  133.5 10.7 %collective-permute-start.29 = (bf16[2,2,2,80,256]{4,3,2,1,0:T(8,128)(2,1)S(1)}, bf16[2,2,2,80,256]{4,3,2,1,0:T(8,128)(2,1)S(1)}, u32[]{:S(2)}, u32[]{:S(2)}) collective-permute-start(bf16[2,2,2,80,256]{4,3,2,1,0:T(8,128)(2,1)S(1)} %get-tuple-element.131), channel_id=1, source_target_pairs={{0,2},{1,3},{2,0},{3,1},{4,6},{5,7},{6,4},{7,5},{8,10},{9,11},{10,... | collective-permute-start | bytes 983048 | tf_op jit(solution)/shard_map/ppermute | solution.py:496
  135.0 12.9 %collective-permute-start.27 = (bf16[256,384]{1,0:T(8,128)(2,1)S(1)}, bf16[256,384]{1,0:T(8,128)(2,1)S(1)}, u32[]{:S(2)}, u32[]{:S(2)}) collective-permute-start(bf16[256,384]{1,0:T(8,128)(2,1)S(1)} %get-tuple-element.133), channel_id=1, source_target_pairs={{0,2},{1,3},{2,0},{3,1},{4,6},{5,7},{6,4},{7,5},{8,10},{9,11},{10,... | collective-permute-start | bytes 589832 | tf_op jit(solution)/shard_map/ppermute | solution.py:496
  137.7 26.9 %collective-permute-start.32 = (bf16[2,72,768]{2,1,0:T(8,128)(2,1)S(1)}, bf16[2,72,768]{2,1,0:T(8,128)(2,1)S(1)}, u32[]{:S(2)}, u32[]{:S(2)}) collective-permute-start(bf16[2,72,768]{2,1,0:T(8,128)(2,1)S(1)} %fusion.7), channel_id=1, source_target_pairs={{0,2},{1,3},{2,0},{3,1},{4,6},{5,7},{6,4},{7,5},{8,10},{9,11},{10,... | collective-permute-start | bytes 663560 | tf_op jit(solution)/shard_map/ppermute | solution.py:496
  144.3 7.3 %collective-permute-start.36 = (bf16[2,2,80,256]{3,2,1,0:T(8,128)(2,1)S(1)}, bf16[2,2,80,256]{3,2,1,0:T(8,128)(2,1)S(1)}, u32[]{:S(2)}, u32[]{:S(2)}) collective-permute-start(bf16[2,2,80,256]{3,2,1,0:T(8,128)(2,1)S(1)} %get-tuple-element.140), channel_id=1, source_target_pairs={{0,4},{1,5},{2,6},{3,7},{4,0},{5,1},{6,2},{7,3},{8,12},{9,13},{10,... | collective-permute-start | bytes 491528 | tf_op jit(solution)/shard_map/ppermute | solution.py:496
  151.7 6.7 %collective-permute-start.38 = (bf16[2,80,256]{2,1,0:T(8,128)(2,1)S(1)}, bf16[2,80,256]{2,1,0:T(8,128)(2,1)S(1)}, u32[]{:S(2)}, u32[]{:S(2)}) collective-permute-start(bf16[2,80,256]{2,1,0:T(8,128)(2,1)S(1)} %get-tuple-element.146), channel_id=1, source_target_pairs={{0,8},{1,9},{2,10},{3,11},{4,12},{5,13},{6,14},{7,15},{8,0},{9,1},... | collective-permute-start | bytes 245768 | tf_op jit(solution)/shard_map/ppermute | solution.py:496
  158.4 8.7 %collective-permute-start.42 = (bf16[80,256]{1,0:T(8,128)(2,1)S(1)}, bf16[80,256]{1,0:T(8,128)(2,1)S(1)}, u32[]{:S(2)}, u32[]{:S(2)}) collective-permute-start(bf16[80,256]{1,0:T(8,128)(2,1)S(1)} %fusion.33), channel_id=1, source_target_pairs={{0,16},{1,17},{2,18},{3,19},{4,20},{5,21},{6,22},{7,23},{8,24},{9,... | collective-permute-start | bytes 122888 | tf_op jit(solution)/shard_map/ppermute | solution.py:496
  164.6 6.8 %collective-permute-start.33 = (bf16[2,72,768]{2,1,0:T(8,128)(2,1)S(1)}, bf16[2,72,768]{2,1,0:T(8,128)(2,1)S(1)}, u32[]{:S(2)}, u32[]{:S(2)}) collective-permute-start(bf16[2,72,768]{2,1,0:T(8,128)(2,1)S(1)} %add_convert_fusion.6.near), channel_id=1, source_target_pairs={{0,1},{1,0},{2,3},{3,2},{4,5},{5,4},{6,7},{7,6},{8,9},{9,8},{10,11... | collective-permute-start | bytes 663560 | tf_op jit(solution)/shard_map/ppermute | solution.py:496
  164.7 6.8 %collective-permute-start.40 = (bf16[72,576]{1,0:T(8,128)(2,1)S(1)}, bf16[72,576]{1,0:T(8,128)(2,1)S(1)}, u32[]{:S(2)}, u32[]{:S(2)}) collective-permute-start(bf16[72,576]{1,0:T(8,128)(2,1)S(1)} %fusion.22.d0), channel_id=1, source_target_pairs={{0,1},{1,0},{2,3},{3,2},{4,5},{5,4},{6,7},{7,6},{8,9},{9,8},{10,11... | collective-permute-start | bytes 248840 | tf_op jit(solution)/shard_map/ppermute | solution.py:496
  (41 other events, 193.4 us)

commit v4 on v3

--- a/solution.py
+++ b/solution.py
@@ -45,8 +45,10 @@
     return [pl.BlockSpec(memory_space=pltpu.VMEM) for _ in shape_dtypes]
 
 
-def call(kernel, scalars, arrays, outs, flops, scratch=(), mib=52):
+def call(kernel, scalars, arrays, outs, flops, scratch=(), mib=52, fetched=()):
     specs = [pl.BlockSpec(memory_space=pltpu.SMEM)] * len(scalars) + whole(*arrays)
+    specs += [pl.BlockSpec(memory_space=pl.ANY)] * len(fetched)
+    arrays = [*arrays, *fetched]
     moved = sum(a.size * a.dtype.itemsize for a in arrays) + sum(
         int(np.prod(o.shape)) * o.dtype.itemsize for o in outs
     )
@@ -55,7 +57,11 @@
         out_shape=outs,
         in_specs=specs,
         out_specs=whole(*outs),
-        scratch_shapes=[pltpu.VMEM(shape, F32) for shape in scratch],
+        scratch_shapes=[
+            *[pltpu.VMEM(shape, F32) for shape in scratch],
+            *[pltpu.VMEM(v.shape, v.dtype) for v in fetched],
+            *([pltpu.SemaphoreType.DMA((len(fetched),))] if fetched else []),
+        ],
         compiler_params=pltpu.CompilerParams(vmem_limit_bytes=mib * 1024 * 1024),
         cost_estimate=pl.CostEstimate(flops=int(flops), bytes_accessed=moved, transcendentals=0),
     )(*scalars, *arrays)
@@ -295,19 +301,24 @@
     return r & 1, (r >> 1) & 1, (r >> 2) & 1
 
 
-def feed_forward_pieces(d_rows, ff_rows, meta, attended, source, b00, b10, b01, b11,
-                        g000, g100, g010, g110, g001, g101, g011, g111, gains, cot, weight,
-                        out_o, gk_o, gg_o, dk_o, dg_o, mid_o, attg_o, gain_o, down_s, wout_s):
-    core, y, x_own, z0_own = meta[0] & 1, (meta[0] >> 1) & 1, meta[1] & 1, (meta[1] >> 1) & 1
+def feed_forward_pieces(d_rows, ff_rows, meta, attended, source, gains, cot, weight, *refs):
+    out_o, gk_o, gg_o, dk_o, dg_o, mid_o, attg_o, gain_o, down_s, wout_s = refs[12:22]
+    copies = [pltpu.make_async_copy(refs[i], refs[22 + i], refs[34].at[i]) for i in range(12)]
+    for copy in copies:
+        copy.start()
+    b00, b10, b01, b11, g001, g101, g011, g111, g000, g100, g010, g110 = refs[22:34]
+    core, y, x_own = meta[0] & 1, (meta[0] >> 1) & 1, meta[1] & 1
     n_f = 8
     hf = n_f // 2
     part_d = ff_rows // 4
     part_o = d_rows // 3
     cut = b00.shape[2] - ff_rows // 2
+    for copy in copies[:4]:
+        copy.wait()
 
     def b_rows(z0, z1, x, c, rows):
-        low = chosen(z0_own ^ z0, b00[z1, x, rows, :], b10[z1, x, rows, :])
-        high = chosen(z0_own ^ z0, b01[z1, x, rows, :], b11[z1, x, rows, :])
+        low = chosen(x_own ^ x, b00[z0, z1, rows, :], b10[z0, z1, rows, :])
+        high = chosen(x_own ^ x, b01[z0, z1, rows, :], b11[z0, z1, rows, :])
         return chosen(core ^ c, low, high)
 
     def quarter(near, far):
@@ -333,6 +344,8 @@
     feed_grad = out_grad.astype(BF)
     feed = back = None
     for c_rel in (1, 0):
+        for copy in copies[8 - 4 * c_rel : 12 - 4 * c_rel]:
+            copy.wait()
         first_q = quarter(g001, g101) if c_rel else quarter(g000, g100)
         second_q = quarter(g011, g111) if c_rel else quarter(g010, g110)
         wg = chosen(y, first_q, second_q)
@@ -428,7 +441,7 @@
             for c_to, to in ((0, rk_o), (1, rg_o)):
                 at = pl.multiple_of((yy * 2 + (core ^ c_to)) * 256, 256)
                 block = [w_s[d_rows * f : d_rows * (f + 1), pl.ds(at, 256)], small_s[f, :, pl.ds(at, 256)]]
-                to[y ^ yy, x, z0, z1] = jnp.concatenate(block, axis=0).astype(BF)
+                to[x, z0, z1, yy] = jnp.concatenate(block, axis=0).astype(BF)
 
 
 def input_gradient_two(dq, own, other, source, mid, w, gains, out_o):
@@ -460,11 +473,8 @@
             wout_o[pl.ds(pl.multiple_of(to * part_o, 8), part_o), :] = piece[part_d:]
 
 
-def place_qkv(qk, v, meta, p00, p10, p01, p11, w_o, bqk_o, bv_o, gains_o, all_s):
-    seq = meta[0]
-    n = p00.shape[1]
-    for piece, o in ((p00[...], 0), (p10[...], 2), (p01[...], 1), (p11[...], 3)):
-        all_s[:, pl.ds(pl.multiple_of((seq ^ o) * n, 128), n)] = piece.astype(F32)
+def place_qkv(qk, v, meta, near, far, w_o, bqk_o, bv_o, gains_o, all_s):
+    place_gate(meta, near, far, all_s)
     d_rows = w_o.shape[0]
     w_o[:, :QW] = all_s[:d_rows, 2 * KW : 2 * KW + QW]
     w_o[:, QW:] = all_s[:d_rows, : 2 * KW]
@@ -475,11 +485,11 @@
     gains_o[1:2, :] = line[:, 256 : 256 + d_rows]
 
 
-def place_all(part_d, qk, v, meta, near, far, d0, d1, d2, d3, r0, r1, r2, r3,
+def place_all(part_d, qk, v, meta, near, far, d0, d1, d2, d3, r_near, r_far,
               gate_o, down_o, wout_o, w_o, bqk_o, bv_o, gains_o, all_s):
     place_gate(meta, near, far, gate_o)
     place_down(part_d, meta, d0, d1, d2, d3, down_o, wout_o)
-    place_qkv(qk, v, meta, r0, r1, r2, r3, w_o, bqk_o, bv_o, gains_o, all_s)
+    place_qkv(qk, v, meta, r_near, r_far, w_o, bqk_o, bv_o, gains_o, all_s)
 
 
 class Net:
@@ -775,7 +785,7 @@
             pltpu.VMEM((d_rows + 8, qkv_w), F32),
             pltpu.SemaphoreType.DMA((3,)),
         ],
-        compiler_params=pltpu.CompilerParams(vmem_limit_bytes=4 * 1024 * 1024),
+        compiler_params=pltpu.CompilerParams(vmem_limit_bytes=52 * 1024 * 1024),
     )(meta, *small)
     a1 = net.both(a0, zfar, 0)
 
@@ -795,12 +805,10 @@
         axis=1,
     )
     a2 = net.both(a1, znear, 0)
-    b0 = net.half(after(half_b, a0), core, 0)
-    bx = net.both(b0, xbit, 0)
+    b0 = net.half(after(half_b, a2), core, 0)
     a_x = net.swap(a2, xbit)
     a_c = net.swap(a2, core)
     gu1 = net.both(gu0, zfar, 0)
-    b1 = net.both(after(bx, a2), zfar, 0)
     gu2 = net.both(after(gu1, a2), znear, 0)
     block_yc = net.swap(block_y, core)
     a_xc = net.swap(a_x, core)
@@ -808,10 +816,9 @@
     gu_x = net.swap(gu2, xbit)
     gu_y = net.swap(gu2, ybit)
     gu_c = net.swap(gu2, core)
+    b1 = net.both(b0, zfar, 0, after(net.swap(b0, zfar), gu2))
     b_z = net.swap(b1, znear)
-    b_c = net.swap(b1, core)
-    gu_xy = net.swap(gu_x, ybit)
-    a_xc = after(a_xc, gu_x, b1)
+    a_xc = after(a_xc, b1)
 
     cos_t, sin_t = rope_tables(full_length, n_seq)
     block_ids = [seq_index ^ o for o in order]
@@ -840,12 +847,17 @@
         [(n_fsdp * (d_rows + 8), qkv_w), (1, qkv_w)],
         20,
     )
-    gu_xy, b_z = after(gu_xy, attended), after(b_z, attended)
+    gu_y = after(gu_y, attended)
+    gu_x, b_z = after(gu_x, gu_y), after(b_z, gu_y)
+    gu_xy = net.swap(gu_x, ybit)
+    b2 = net.both(b1, znear, 0, b_z)
+    b_x = net.swap(b2, xbit)
+    b_c = net.swap(b2, core)
     gu_yc = net.swap(gu_y, core)
     gu_xc = net.swap(gu_x, core)
-    b_zc = net.swap(b_z, core)
+    b_xc = net.swap(b_x, core)
     gu_xyc = net.swap(gu_xy, core)
-    gate_up = [gu2, gu_x, gu_y, gu_xy, gu_c, gu_xc, gu_yc, gu_xyc]
+    gate_up = [gu_c, gu_xc, gu_yc, gu_xyc, gu2, gu_x, gu_y, gu_xy]
 
     weight = tokens_micro / token_counts.astype(F32)
     weight = jnp.repeat(weight, batch * length)[:, None]
@@ -853,7 +865,7 @@
     block_out, gate_keep, gate_give, down_keep, down_give, middle_grad, attended_grad, gain_two = call(
         functools.partial(feed_forward_pieces, d_rows, ff_rows),
         [meta],
-        [attended, source, b1, b_z, b_c, b_zc, *gate_up, gains, cotangent.reshape(rows, width), weight],
+        [attended, source, gains, cotangent.reshape(rows, width), weight],
         [
             sds((seqs, width, length), BF),
             sds(lead + (d_rows, units // 2), BF),
@@ -866,7 +878,7 @@
         ],
         1.4e10,
         [(units // 2, width), (n_fsdp, d_rows + d_rows // 3, width)],
-        32,
+        fetched=[b2, b_x, b_c, b_xc, *gate_up],
     )
     block_out = block_out.reshape(micro, batch, width, length).swapaxes(2, 3)
 
@@ -897,53 +909,51 @@
         ],
         1.4e10,
         [(width, 1024), (1, qkv_w), (1, width), (n_fsdp, 8, 1024)],
-        24,
-    )
-    gate, gate_give = halves(gate, after(gate_got, dq))
+    )
+    gate, gate_give = halves(gate, after(gate_got, dq, down_got))
     gate_got = net.swap(gate_give, znear)
     down, down_give = halves(down, after(down_got, gate_give))
-    dkv, dkv_give = halves(dkv_keep, after(net.swap(dkv_give, core), down_give))
+    down_got = net.swap(down_give, xbit)
     rest, rest_give = halves(rest_keep, after(net.swap(rest_give, core), down_give))
+    rest_got = net.swap(rest_give, xbit)
+    dkv, dkv_give = halves(dkv_keep, after(net.swap(dkv_give, core), rest_give))
     dkv_got = net.swap(dkv_give, ybit)
-    rest_got = net.swap(rest_give, ybit)
-    down_got = net.swap(down_give, xbit)
-    gate, gate_give = halves(gate, gate_got)
-    gate_got = net.swap(gate_give, zfar)
-    rest, rest_give = halves(rest, after(rest_got, gate_give))
-    rest_got = net.swap(rest_give, xbit)
     (hidden_grad,) = call(
         input_gradient_two,
         [],
-        [dq, dkv, after(dkv_got, rest_give), source, middle_grad, wf, gains],
+        [dq, dkv, dkv_got, source, middle_grad, wf, gains],
         [sds((seqs, width, length), F32)],
         3e9,
         mib=16,
     )
-    down, down_give = halves(down, after(down_got, hidden_grad))
+    gate, gate_give = halves(gate, after(gate_got, hidden_grad))
+    gate_got = net.swap(gate_give, zfar)
     hidden_grad = hidden_grad.reshape(micro, batch, width, length).swapaxes(2, 3)
+    down, down_give = halves(down, after(down_got, gate_give))
     down_got = net.swap(down_give, znear)
-    gate = add(gate, gate_got)
+    rest, rest_give = halves(rest, after(rest_got, down_give))
+    rest_got = net.swap(rest_give, znear)
+    gate = add(gate, after(gate_got, rest_give))
     gate_got = net.swap(gate, ybit)
-    rest, rest_give = halves(rest, after(rest_got, gate))
-    rest_got = net.swap(rest_give, znear)
-    down, down_give = halves(down, after(down_got, rest_give))
+    down, down_give = halves(down, after(down_got, gate))
     down_got = net.swap(down_give, zfar)
-    gate = add(gate, gate_got)
-    rest, rest_give = halves(rest, rest_got)
+    rest, rest_give = halves(rest, after(rest_got, down_give))
     rest_got = net.swap(rest_give, zfar)
-    down = add(down, after(down_got, rest_give))
+    gate = add(gate, after(gate_got, rest_give))
+    gate_far = net.swap(gate, core)
+    down = add(down, after(down_got, gate))
+    down_y = net.swap(down, ybit)
+    down_c = net.swap(down, core)
+    rest = add(rest, after(rest_got, down))
+    rest_got = net.swap(rest, ybit)
+    down_yc = net.swap(down_y, core)
     rest = add(rest, rest_got)
-
-    def spread(part):
-        other = net.swap(part, ybit)
-        return [part, other, net.swap(part, core), net.swap(other, core)]
-
-    gate = [gate, net.swap(gate, core)]
+    rest_far = net.swap(rest, core)
     qk, v = (QW + KW) // n_fsdp, KW // n_fsdp
     out_gate, out_down, out_wout, out_qkv, b_qk, b_v, out_gains = call(
         functools.partial(place_all, ff_rows // 4, qk, v),
         [meta],
-        [*gate, *spread(down), *spread(rest)],
+        [gate, gate_far, down, down_y, down_c, down_yc, rest, rest_far],
         [
             sds((d_rows, 2 * units), F32),
             sds((ff_rows, width), F32),

time: 175 us -> 161 us (0.920)
  waiting for transfers between devices: 81.7 us -> 70.1 us
  local copies, waits for them, and re-layouts: 15.4 us -> 8.17 us
  Pallas kernels: 34 us -> 39.2 us
  starting transfers between devices: 38.4 us -> 36.1 us
  other arithmetic: 3.97 us -> 6.25 us
    ppermute x46 -> x44, waiting for transfers between devices: 81.7 us -> 70.1 us  [swap(): return lax.ppermute(value, ('fsdp', 'seq'), pairs)]
    unnamed x56 -> x50, local copies, waits for them, and re-layouts: 14.3 us -> 7.11 us
    pallas_call x5, Pallas kernels: 33.2 us -> 38.3 us  [call(): pl.pallas_call(kernel, out_shape=outs, in_specs=specs, out_specs=whole(*o...]
    ppermute x46 -> x44, starting transfers between devices: 38.4 us -> 36.1 us  [swap(): return lax.ppermute(value, ('fsdp', 'seq'), pairs)]
  transfers between devices with their start and end apart: 46 -> 44, of which waited for: 22 -> 22; matrix products, arithmetic and copies ran while one was open for 4% -> 5% of each run, Pallas kernels for 12% -> 14%
where the time goes in v4:
time: 161 us
  waiting for transfers between devices  70.1 us (44%)
  Pallas kernels  39.2 us (24%)
  starting transfers between devices  36.1 us (22%)
  local copies, waits for them, and re-layouts  8.17 us (5%)
  other arithmetic  6.25 us (4%)
    ppermute x44, waiting for transfers between devices, swap(): return lax.ppermute(value, ('fsdp', 'seq'), pairs)  70.1 us
    pallas_call x5, Pallas kernels, call(): pl.pallas_call(kernel, out_shape=outs, in_specs=specs, out_specs=whole(*o...  38.3 us
    ppermute x44, starting transfers between devices, swap(): return lax.ppermute(value, ('fsdp', 'seq'), pairs)  36.1 us
    unnamed x50, local copies, waits for them, and re-layouts  7.11 us
    convert_element_type x16, other arithmetic, add(): return (keep.astype(F32) + got.astype(F32)).astype(BF)  3.49 us
  transfers between devices with their start and end apart: 44, of which 22 were waited for; matrix products, arithmetic and copies ran while one was open for 5% of the time, Pallas kernels for 14%

profile of v4, /device:TPU:0, one launch (start us, length us, event | category | flops | bytes accessed | tf_op | source)
XLA Modules:
  0.0 161.0 jit_solution(10065742487819603688)
XLA Ops:
  3.8 4.1 %collective-permute-start.3 = (bf16[40,960]{1,0:T(8,128)(2,1)S(1)}, bf16[40,960]{1,0:T(8,128)(2,1)S(1)}, u32[]{:S(2)}, u32[]{:S(2)}) collective-permute-start(bf16[40,960]{1,0:T(8,128)(2,1)S(1)} %shard_map.187), channel_id=1, source_target_pairs={{0,16},{1,17},{2,18},{3,19},{4,20},{5,21},{6,22},{7,23},{8,24},{9,... | collective-permute-start | bytes 230408 | tf_op jit(solution)/shard_map/ppermute | solution.py:506
  10.0 1.6 collective-permute-start
  12.6 1.6 %collective-permute-start.4 = (bf16[2,40,960]{2,1,0:T(8,128)(2,1)S(1)}, bf16[2,40,960]{2,1,0:T(8,128)(2,1)S(1)}, u32[]{:S(2)}, u32[]{:S(2)}) collective-permute-start(bf16[2,40,960]{2,1,0:T(8,128)(2,1)S(1)} %pad_maximum_fusion.7), channel_id=1, source_target_pairs={{0,8},{1,9},{2,10},{3,11},{4,12},{5,13},{6,14},{7,15},{8,0},{9,1},... | collective-permute-start | bytes 460808 | tf_op jit(solution)/shard_map/ppermute | solution.py:506
  14.3 6.0 %collective-permute-done.9 = bf16[72,768]{1,0:T(8,128)(2,1)S(1)} collective-permute-done((bf16[72,768]{1,0:T(8,128)(2,1)S(1)}, bf16[72,768]{1,0:T(8,128)(2,1)S(1)}, u32[]{:S(2)}, u32[]{:S(2)}) %collective-permute-start.9) | collective-permute-done | bytes 110624 | tf_op jit(solution)/shard_map/ppermute | solution.py:506
  21.2 1.6 collective-permute-start.5
  22.8 4.1 %collective-permute-start.8 = (bf16[136,576]{1,0:T(8,128)(2,1)S(1)}, bf16[136,576]{1,0:T(8,128)(2,1)S(1)}, u32[]{:S(2)}, u32[]{:S(2)}) collective-permute-start(bf16[136,576]{1,0:T(8,128)(2,1)S(1)} %dynamic-slice_bitcast_fusion), channel_id=1, source_target_pairs={{0,16},{1,17},{2,18},{3,19},{4,20},{5,21},{6,22},{7,23},{8,24},{9,... | collective-permute-start | bytes 470024 | tf_op jit(solution)/shard_map/ppermute | solution.py:506
  27.4 6.7 %collective-permute-done.10 = bf16[2,72,768]{2,1,0:T(8,128)(2,1)S(1)} collective-permute-done((bf16[2,72,768]{2,1,0:T(8,128)(2,1)S(1)}, bf16[2,72,768]{2,1,0:T(8,128)(2,1)S(1)}, u32[]{:S(2)}, u32[]{:S(2)}) %collective-permute-start.10) | collective-permute-done | bytes 221216 | tf_op jit(solution)/shard_map/ppermute | solution.py:506
  38.1 8.3 %shard_map.188 = (bf16[256,576]{1,0:T(8,128)(2,1)S(1)}, bf16[2,3,384,64]{3,2,1,0:T(8,128)(2,1)S(1)}, bf16[2,3,512,64]{3,2,1,0:T(8,128)(2,1)S(1)}, bf16[2,3,512,6...) custom-call(s32[2]{0:T(128)S(1)} %pad_add_fusion.meta, ...), custom_call_target="tpu_custom_call" | custom-call | flops 12000000000 | bytes 6084096 | tf_op jit(solution)/shard_map/pallas_call | solution.py:55
  50.7 1.6 collective-permute-start.20
  52.5 15.6 %collective-permute-done.13.refs_1_ = bf16[2,2,136,576]{3,2,1,0:T(8,128)(2,1)} collective-permute-done((bf16[2,2,136,576]{3,2,1,0:T(8,128)(2,1)}, bf16[2,2,136,576]{3,2,1,0:T(8,128)(2,1)}, u32[]{:S(2)}, u32[]{:S(2)}) %collective-permute-start.13) | collective-permute-done | bytes 626720 | tf_op jit(solution)/shard_map/ppermute | solution.py:506
  69.6 1.6 %collective-permute-done.18.refs_5_ = bf16[2,2,72,768]{3,2,1,0:T(8,128)(2,1)} collective-permute-done((bf16[2,2,72,768]{3,2,1,0:T(8,128)(2,1)}, bf16[2,2,72,768]{3,2,1,0:T(8,128)(2,1)}, u32[]{:S(2)}, u32[]{:S(2)}) %collective-permute-start.18) | collective-permute-done | bytes 442400 | tf_op jit(solution)/shard_map/ppermute | solution.py:506
  72.5 13.4 %shard_map.189 = (bf16[2,576,128]{2,1,0:T(8,128)(2,1)}, bf16[2,2,2,2,72,768]{5,4,3,2,1,0:T(8,128)(2,1)}, bf16[2,2,2,2,72,768]{5,4,3,2,1,0:T(8,128)(2,1)}, bf16[2...) custom-call(s32[2]{0:T(128)S(1)} %pad_add_fusion.meta, ...), custom_call_target="tpu_custom_call" | custom-call | flops 14000000000 | bytes 14311168 | tf_op jit(solution)/shard_map/pallas_call | solution.py:55
  86.2 3.8 %collective-permute-done.22 = bf16[2,2,2,2,72,768]{5,4,3,2,1,0:T(8,128)(2,1)S(1)} collective-permute-done((bf16[2,2,2,2,72,768]{5,4,3,2,1,0:T(8,128)(2,1)}, bf16[2,2,2,2,72,768]{5,4,3,2,1,0:T(8,128)(2,1)S(1)}, u32[]{:S(2)}, u32[]{:S(2)}) %collective-permute-start.22) | collective-permute-done | bytes 1769504 | tf_op jit(solution)/shard_map/ppermute | solution.py:506
  90.1 2.0 %add_convert_fusion = (bf16[1,2,2,2,72,768]{5,4,3,2,1,0:T(8,128)(2,1)S(1)}, bf16[2,2,2,72,768]{4,3,2,1,0:T(8,128)(2,1)S(1)}) fusion(bf16[2,2,2,2,72,768]{5,4,3,2,1,0:T(8,128)(2,1)S(1)} %collective-permute-done.22, bf16[2,2,2,2,72,768]{5,4,3,2,1,0:T(8,128)(2,1)} %get-tuple-element.80), kind=kLoop, calls=%fused_computation | loop fusion | flops 3538944 | bytes 5308416 | tf_op jit(solution)/shard_map/convert_element_type | solution.py:886
  94.7 12.7 %shard_map.190 = (bf16[256,640]{1,0:T(8,128)(2,1)S(1)}, bf16[2,256,384]{2,1,0:T(8,128)(2,1)}, bf16[2,256,384]{2,1,0:T(8,128)(2,1)}, bf16[2,2,2,2,80,256]{5,4,3,2...) custom-call(s32[2]{0:T(128)S(1)} %pad_add_fusion.meta, bf16[256,640]{1,0:T(8,128)(2,1)S(1)} %pad_maximum_fusion.4.b0, ...), custom_call_target="tpu_custom_call" | custom-call | flops 14000000000 | bytes 7282432 | tf_op jit(solution)/shard_map/pallas_call | solution.py:55
  107.8 6.2 %collective-permute-done.27 = bf16[2,2,2,72,768]{4,3,2,1,0:T(8,128)(2,1)S(1)} collective-permute-done((bf16[2,2,2,72,768]{4,3,2,1,0:T(8,128)(2,1)S(1)}, bf16[2,2,2,72,768]{4,3,2,1,0:T(8,128)(2,1)S(1)}, u32[]{:S(2)}, u32[]{:S(2)}) %collective-permute-start.27) | collective-permute-done | bytes 884768 | tf_op jit(solution)/shard_map/ppermute | solution.py:506
  116.5 1.7 %collective-permute-start.29 = (bf16[2,2,72,768]{3,2,1,0:T(8,128)(2,1)S(1)}, bf16[2,2,72,768]{3,2,1,0:T(8,128)(2,1)S(1)}, u32[]{:S(2)}, u32[]{:S(2)}) collective-permute-start(bf16[2,2,72,768]{3,2,1,0:T(8,128)(2,1)S(1)} %get-tuple-element.136), channel_id=1, source_target_pairs={{0,8},{1,9},{2,10},{3,11},{4,12},{5,13},{6,14},{7,15},{8,0},{9,1},... | collective-permute-start | bytes 1327112 | tf_op jit(solution)/shard_map/ppermute | solution.py:506
  118.3 1.5 collective-permute-start.31
  120.3 1.8 %collective-permute-done.28.other = bf16[256,384]{1,0:T(8,128)(2,1)S(1)} collective-permute-done((bf16[256,384]{1,0:T(8,128)(2,1)S(1)}, bf16[256,384]{1,0:T(8,128)(2,1)S(1)}, u32[]{:S(2)}, u32[]{:S(2)}) %collective-permute-start.28) | collective-permute-done | bytes 196640 | tf_op jit(solution)/shard_map/ppermute | solution.py:506
  122.1 1.9 %shard_map.191 = f32[2,576,128]{2,1,0:T(8,128)} custom-call(bf16[256,640]{1,0:T(8,128)(2,1)S(1)} %get-tuple-element.87.dq, bf16[256,384]{1,0:T(8,128)(2,1)S(1)} %get-tuple-element.142.own, bf16[256,384]{1,0:T(8,128)(2,1)S(1)} %collective-permute-done.28.other, bf16[256,576]{1,0:T(8,128)(2,1)S(1)} %bitcast.172, f32[256,576]{1,0:T(8,128)S(1)} %copy-done.9, ...), custom_call_target="tpu_custom_call" | custom-call | flops 3000000000 | bytes 3305984 | tf_op jit(solution)/shard_map/pallas_call | solution.py:55
  124.0 3.8 %collective-permute-done.29 = bf16[2,2,72,768]{3,2,1,0:T(8,128)(2,1)S(1)} collective-permute-done((bf16[2,2,72,768]{3,2,1,0:T(8,128)(2,1)S(1)}, bf16[2,2,72,768]{3,2,1,0:T(8,128)(2,1)S(1)}, u32[]{:S(2)}, u32[]{:S(2)}) %collective-permute-start.29) | collective-permute-done | bytes 442400 | tf_op jit(solution)/shard_map/ppermute | solution.py:506
  127.9 2.5 %collective-permute-start.30 = (bf16[2,72,768]{2,1,0:T(8,128)(2,1)S(1)}, bf16[2,72,768]{2,1,0:T(8,128)(2,1)S(1)}, u32[]{:S(2)}, u32[]{:S(2)}) collective-permute-start(bf16[2,72,768]{2,1,0:T(8,128)(2,1)S(1)} %fusion.17), channel_id=1, source_target_pairs={{0,16},{1,17},{2,18},{3,19},{4,20},{5,21},{6,22},{7,23},{8,24},{9,... | collective-permute-start | bytes 663560 | tf_op jit(solution)/shard_map/ppermute | solution.py:506
  130.4 4.3 %collective-permute-done.32 = bf16[2,2,72,576]{3,2,1,0:T(8,128)(2,1)S(1)} collective-permute-done((bf16[2,2,72,576]{3,2,1,0:T(8,128)(2,1)S(1)}, bf16[2,2,72,576]{3,2,1,0:T(8,128)(2,1)S(1)}, u32[]{:S(2)}, u32[]{:S(2)}) %collective-permute-start.32) | collective-permute-done | bytes 331808 | tf_op jit(solution)/shard_map/ppermute | solution.py:506
  135.3 1.8 %collective-permute-start.34 = (bf16[2,2,80,256]{3,2,1,0:T(8,128)(2,1)S(1)}, bf16[2,2,80,256]{3,2,1,0:T(8,128)(2,1)S(1)}, u32[]{:S(2)}, u32[]{:S(2)}) collective-permute-start(bf16[2,2,80,256]{3,2,1,0:T(8,128)(2,1)S(1)} %get-tuple-element.148), channel_id=1, source_target_pairs={{0,8},{1,9},{2,10},{3,11},{4,12},{5,13},{6,14},{7,15},{8,0},{9,1},... | collective-permute-start | bytes 491528 | tf_op jit(solution)/shard_map/ppermute | solution.py:506
  137.1 2.3 %collective-permute-done.30 = bf16[2,72,768]{2,1,0:T(8,128)(2,1)S(1)} collective-permute-done((bf16[2,72,768]{2,1,0:T(8,128)(2,1)S(1)}, bf16[2,72,768]{2,1,0:T(8,128)(2,1)S(1)}, u32[]{:S(2)}, u32[]{:S(2)}) %collective-permute-start.30) | collective-permute-done | bytes 221216 | tf_op jit(solution)/shard_map/ppermute | solution.py:506
  140.8 2.6 %collective-permute-done.35 = bf16[2,72,576]{2,1,0:T(8,128)(2,1)S(1)} collective-permute-done((bf16[2,72,576]{2,1,0:T(8,128)(2,1)S(1)}, bf16[2,72,576]{2,1,0:T(8,128)(2,1)S(1)}, u32[]{:S(2)}, u32[]{:S(2)}) %collective-permute-start.35) | collective-permute-done | bytes 165920 | tf_op jit(solution)/shard_map/ppermute | solution.py:506
  143.9 2.5 %collective-permute-done.34 = bf16[2,2,80,256]{3,2,1,0:T(8,128)(2,1)S(1)} collective-permute-done((bf16[2,2,80,256]{3,2,1,0:T(8,128)(2,1)S(1)}, bf16[2,2,80,256]{3,2,1,0:T(8,128)(2,1)S(1)}, u32[]{:S(2)}, u32[]{:S(2)}) %collective-permute-start.34) | collective-permute-done | bytes 163872 | tf_op jit(solution)/shard_map/ppermute | solution.py:506
  146.4 1.5 collective-permute-start.41
  148.0 2.8 %collective-permute-done.37 = bf16[72,576]{1,0:T(8,128)(2,1)S(1)} collective-permute-done((bf16[72,576]{1,0:T(8,128)(2,1)S(1)}, bf16[72,576]{1,0:T(8,128)(2,1)S(1)}, u32[]{:S(2)}, u32[]{:S(2)}) %collective-permute-start.37) | collective-permute-done | bytes 82976 | tf_op jit(solution)/shard_map/ppermute | solution.py:506
  151.5 1.6 %collective-permute-done.41 = bf16[2,80,256]{2,1,0:T(8,128)(2,1)S(1)} collective-permute-done((bf16[2,80,256]{2,1,0:T(8,128)(2,1)S(1)}, bf16[2,80,256]{2,1,0:T(8,128)(2,1)S(1)}, u32[]{:S(2)}, u32[]{:S(2)}) %collective-permute-start.41) | collective-permute-done | bytes 81952 | tf_op jit(solution)/shard_map/ppermute | solution.py:506
  155.5 2.2 %collective-permute-done.42 = bf16[2,80,256]{2,1,0:T(8,128)(2,1)S(1)} collective-permute-done((bf16[2,80,256]{2,1,0:T(8,128)(2,1)S(1)}, bf16[2,80,256]{2,1,0:T(8,128)(2,1)S(1)}, u32[]{:S(2)}, u32[]{:S(2)}) %collective-permute-start.42) | collective-permute-done | bytes 81952 | tf_op jit(solution)/shard_map/ppermute | solution.py:506
  159.1 1.9 %shard_map.192 = (f32[72,3072]{1,0:T(8,128)}, f32[192,576]{1,0:T(8,128)}, f32[72,576]{1,0:T(8,128)}, f32[72,960]{1,0:T(8,128)}, f32[1,96]{1,0:T(1,128)}, /*index=5*/f32[1,24]{1,0:T(1,128)}, f32[2,72]{1,0:T(2,128)}) custom-call(s32[2]{0:T(128)S(1)} %pad_add_fusion.meta, bf16[2,72,768]{2,1,0:T(8,128)(2,1)S(1)} %add_convert_fusion.6.near, ...), custom_call_target="tpu_custom_call" | custom-call | flops 3000000000 | bytes 2708512 | tf_op jit(solution)/shard_map/pallas_call | solution.py:55
  (161 shorter events, 32.0 us)
Async XLA Ops:
  3.8 8.8 %collective-permute-start.3 = (bf16[40,960]{1,0:T(8,128)(2,1)S(1)}, bf16[40,960]{1,0:T(8,128)(2,1)S(1)}, u32[]{:S(2)}, u32[]{:S(2)}) collective-permute-start(bf16[40,960]{1,0:T(8,128)(2,1)S(1)} %shard_map.187), channel_id=1, source_target_pairs={{0,16},{1,17},{2,18},{3,19},{4,20},{5,21},{6,22},{7,23},{8,24},{9,... | collective-permute-start | bytes 230408 | tf_op jit(solution)/shard_map/ppermute | solution.py:506
  10.0 17.1 %collective-permute-start.1 = (bf16[256,640]{1,0:T(8,128)(2,1)S(1)}, bf16[256,640]{1,0:T(8,128)(2,1)S(1)}, u32[]{:S(2)}, u32[]{:S(2)}) collective-permute-start(bf16[256,640]{1,0:T(8,128)(2,1)S(1)} %pad_maximum_fusion.4.b0), channel_id=1, source_target_pairs={{0,1},{1,0},{2,3},{3,2},{4,5},{5,4},{6,7},{7,6},{8,9},{9,8},{10,11... | collective-permute-start | bytes 983048 | tf_op jit(solution)/shard_map/ppermute | solution.py:506
  10.0 12.8 %collective-permute-start = (bf16[256,640]{1,0:T(8,128)(2,1)S(1)}, bf16[256,640]{1,0:T(8,128)(2,1)S(1)}, u32[]{:S(2)}, u32[]{:S(2)}) collective-permute-start(bf16[256,640]{1,0:T(8,128)(2,1)S(1)} %pad_maximum_fusion.4.b0), channel_id=1, source_target_pairs={{0,2},{1,3},{2,0},{3,1},{4,6},{5,7},{6,4},{7,5},{8,10},{9,11},{10,... | collective-permute-start | bytes 983048 | tf_op jit(solution)/shard_map/ppermute | solution.py:506
  11.6 8.6 %collective-permute-start.9 = (bf16[72,768]{1,0:T(8,128)(2,1)S(1)}, bf16[72,768]{1,0:T(8,128)(2,1)S(1)}, u32[]{:S(2)}, u32[]{:S(2)}) collective-permute-start(bf16[72,768]{1,0:T(8,128)(2,1)S(1)} %constant_dynamic-slice_fusion), channel_id=1, source_target_pairs={{0,16},{1,17},{2,18},{3,19},{4,20},{5,21},{6,22},{7,23},{8,24},{9,... | collective-permute-start | bytes 331784 | tf_op jit(solution)/shard_map/ppermute | solution.py:506
  12.6 8.4 %collective-permute-start.4 = (bf16[2,40,960]{2,1,0:T(8,128)(2,1)S(1)}, bf16[2,40,960]{2,1,0:T(8,128)(2,1)S(1)}, u32[]{:S(2)}, u32[]{:S(2)}) collective-permute-start(bf16[2,40,960]{2,1,0:T(8,128)(2,1)S(1)} %pad_maximum_fusion.7), channel_id=1, source_target_pairs={{0,8},{1,9},{2,10},{3,11},{4,12},{5,13},{6,14},{7,15},{8,0},{9,1},... | collective-permute-start | bytes 460808 | tf_op jit(solution)/shard_map/ppermute | solution.py:506
  21.1 17.0 %collective-permute-start.6 = (bf16[2,2,40,960]{3,2,1,0:T(8,128)(2,1)S(1)}, bf16[2,2,40,960]{3,2,1,0:T(8,128)(2,1)S(1)}, u32[]{:S(2)}, u32[]{:S(2)}) collective-permute-start(bf16[2,2,40,960]{3,2,1,0:T(8,128)(2,1)S(1)} %pad_maximum_fusion.5.a00), channel_id=1, source_target_pairs={{0,1},{1,0},{2,3},{3,2},{4,5},{5,4},{6,7},{7,6},{8,9},{9,8},{10,11... | collective-permute-start | bytes 921608 | tf_op jit(solution)/shard_map/ppermute | solution.py:506
  21.2 12.9 %collective-permute-start.5 = (bf16[2,2,40,960]{3,2,1,0:T(8,128)(2,1)S(1)}, bf16[2,2,40,960]{3,2,1,0:T(8,128)(2,1)S(1)}, u32[]{:S(2)}, u32[]{:S(2)}) collective-permute-start(bf16[2,2,40,960]{3,2,1,0:T(8,128)(2,1)S(1)} %pad_maximum_fusion.5.a00), channel_id=1, source_target_pairs={{0,4},{1,5},{2,6},{3,7},{4,0},{5,1},{6,2},{7,3},{8,12},{9,13},{10,... | collective-permute-start | bytes 921608 | tf_op jit(solution)/shard_map/ppermute | solution.py:506
  22.8 11.2 %collective-permute-start.10 = (bf16[2,72,768]{2,1,0:T(8,128)(2,1)S(1)}, bf16[2,72,768]{2,1,0:T(8,128)(2,1)S(1)}, u32[]{:S(2)}, u32[]{:S(2)}) collective-permute-start(bf16[2,72,768]{2,1,0:T(8,128)(2,1)S(1)} %pad_maximum_fusion.6), channel_id=1, source_target_pairs={{0,8},{1,9},{2,10},{3,11},{4,12},{5,13},{6,14},{7,15},{8,0},{9,1},... | collective-permute-start | bytes 663560 | tf_op jit(solution)/shard_map/ppermute | solution.py:506
  22.8 12.4 %collective-permute-start.8 = (bf16[136,576]{1,0:T(8,128)(2,1)S(1)}, bf16[136,576]{1,0:T(8,128)(2,1)S(1)}, u32[]{:S(2)}, u32[]{:S(2)}) collective-permute-start(bf16[136,576]{1,0:T(8,128)(2,1)S(1)} %dynamic-slice_bitcast_fusion), channel_id=1, source_target_pairs={{0,16},{1,17},{2,18},{3,19},{4,20},{5,21},{6,22},{7,23},{8,24},{9,... | collective-permute-start | bytes 470024 | tf_op jit(solution)/shard_map/ppermute | solution.py:506
  27.1 9.4 %collective-permute-start.2 = (bf16[256,640]{1,0:T(8,128)(2,1)S(1)}, bf16[256,640]{1,0:T(8,128)(2,1)S(1)}, u32[]{:S(2)}, u32[]{:S(2)}) collective-permute-start(bf16[256,640]{1,0:T(8,128)(2,1)S(1)} %collective-permute-done.b1), channel_id=1, source_target_pairs={{0,1},{1,0},{2,3},{3,2},{4,5},{5,4},{6,7},{7,6},{8,9},{9,8},{10,11... | collective-permute-start | bytes 983048 | tf_op jit(solution)/shard_map/ppermute | solution.py:506
  34.1 16.6 %collective-permute-start.17 = (bf16[2,2,72,768]{3,2,1,0:T(8,128)(2,1)S(1)}, bf16[2,2,72,768]{3,2,1,0:T(8,128)(2,1)}, u32[]{:S(2)}, u32[]{:S(2)}) collective-permute-start(bf16[2,2,72,768]{3,2,1,0:T(8,128)(2,1)S(1)} %pad_maximum_fusion.1.refs_8_), channel_id=1, source_target_pairs={{0,4},{1,5},{2,6},{3,7},{4,0},{5,1},{6,2},{7,3},{8,12},{9,13},{10,... | collective-permute-start | bytes 1327112 | tf_op jit(solution)/shard_map/ppermute | solution.py:506
  34.8 14.3 %collective-permute-start.12 = (bf16[2,2,72,768]{3,2,1,0:T(8,128)(2,1)S(1)}, bf16[2,2,72,768]{3,2,1,0:T(8,128)(2,1)}, u32[]{:S(2)}, u32[]{:S(2)}) collective-permute-start(bf16[2,2,72,768]{3,2,1,0:T(8,128)(2,1)S(1)} %pad_maximum_fusion.1.refs_8_), channel_id=1, source_target_pairs={{0,2},{1,3},{2,0},{3,1},{4,6},{5,7},{6,4},{7,5},{8,10},{9,11},{10,... | collective-permute-start | bytes 1327112 | tf_op jit(solution)/shard_map/ppermute | solution.py:506
  35.3 13.7 %collective-permute-start.11 = (bf16[2,136,576]{2,1,0:T(8,128)(2,1)S(1)}, bf16[2,136,576]{2,1,0:T(8,128)(2,1)S(1)}, u32[]{:S(2)}, u32[]{:S(2)}) collective-permute-start(bf16[2,136,576]{2,1,0:T(8,128)(2,1)S(1)} %pad_maximum_fusion.3), channel_id=1, source_target_pairs={{0,8},{1,9},{2,10},{3,11},{4,12},{5,13},{6,14},{7,15},{8,0},{9,1},... | collective-permute-start | bytes 940040 | tf_op jit(solution)/shard_map/ppermute | solution.py:506
  50.2 18.0 %collective-permute-start.13 = (bf16[2,2,136,576]{3,2,1,0:T(8,128)(2,1)}, bf16[2,2,136,576]{3,2,1,0:T(8,128)(2,1)}, u32[]{:S(2)}, u32[]{:S(2)}) collective-permute-start(bf16[2,2,136,576]{3,2,1,0:T(8,128)(2,1)} %pad_maximum_fusion.refs_0_), channel_id=1, source_target_pairs={{0,4},{1,5},{2,6},{3,7},{4,0},{5,1},{6,2},{7,3},{8,12},{9,13},{10,... | collective-permute-start | bytes 1880072 | tf_op jit(solution)/shard_map/ppermute | solution.py:506
  50.7 17.9 %collective-permute-start.16 = (bf16[2,2,72,768]{3,2,1,0:T(8,128)(2,1)S(1)}, bf16[2,2,72,768]{3,2,1,0:T(8,128)(2,1)S(1)}, u32[]{:S(2)}, u32[]{:S(2)}) collective-permute-start(bf16[2,2,72,768]{3,2,1,0:T(8,128)(2,1)S(1)} %pad_maximum_fusion.1.refs_8_), channel_id=1, source_target_pairs={{0,1},{1,0},{2,3},{3,2},{4,5},{5,4},{6,7},{7,6},{8,9},{9,8},{10,11... | collective-permute-start | bytes 1327112 | tf_op jit(solution)/shard_map/ppermute | solution.py:506
  50.7 17.9 %collective-permute-start.20 = (bf16[2,2,72,768]{3,2,1,0:T(8,128)(2,1)}, bf16[2,2,72,768]{3,2,1,0:T(8,128)(2,1)}, u32[]{:S(2)}, u32[]{:S(2)}) collective-permute-start(bf16[2,2,72,768]{3,2,1,0:T(8,128)(2,1)} %collective-permute-done.17.refs_9_), channel_id=1, source_target_pairs={{0,2},{1,3},{2,0},{3,1},{4,6},{5,7},{6,4},{7,5},{8,10},{9,11},{10,... | collective-permute-start | bytes 1327112 | tf_op jit(solution)/shard_map/ppermute | solution.py:506
  52.3 19.6 %collective-permute-start.14 = (bf16[2,2,136,576]{3,2,1,0:T(8,128)(2,1)}, bf16[2,2,136,576]{3,2,1,0:T(8,128)(2,1)}, u32[]{:S(2)}, u32[]{:S(2)}) collective-permute-start(bf16[2,2,136,576]{3,2,1,0:T(8,128)(2,1)} %pad_maximum_fusion.refs_0_), channel_id=1, source_target_pairs={{0,1},{1,0},{2,3},{3,2},{4,5},{5,4},{6,7},{7,6},{8,9},{9,8},{10,11... | collective-permute-start | bytes 1880072 | tf_op jit(solution)/shard_map/ppermute | solution.py:506
  92.1 22.0 %collective-permute-start.27 = (bf16[2,2,2,72,768]{4,3,2,1,0:T(8,128)(2,1)S(1)}, bf16[2,2,2,72,768]{4,3,2,1,0:T(8,128)(2,1)S(1)}, u32[]{:S(2)}, u32[]{:S(2)}) collective-permute-start(bf16[2,2,2,72,768]{4,3,2,1,0:T(8,128)(2,1)S(1)} %get-tuple-element.132), channel_id=1, source_target_pairs={{0,4},{1,5},{2,6},{3,7},{4,0},{5,1},{6,2},{7,3},{8,12},{9,13},{10,... | collective-permute-start | bytes 2654216 | tf_op jit(solution)/shard_map/ppermute | solution.py:506
  93.8 20.3 %collective-permute-start.26 = (bf16[2,2,2,72,576]{4,3,2,1,0:T(8,128)(2,1)S(1)}, bf16[2,2,2,72,576]{4,3,2,1,0:T(8,128)(2,1)S(1)}, u32[]{:S(2)}, u32[]{:S(2)}) collective-permute-start(bf16[2,2,2,72,576]{4,3,2,1,0:T(8,128)(2,1)S(1)} %get-tuple-element.134), channel_id=1, source_target_pairs={{0,2},{1,3},{2,0},{3,1},{4,6},{5,7},{6,4},{7,5},{8,10},{9,11},{10,... | collective-permute-start | bytes 1990664 | tf_op jit(solution)/shard_map/ppermute | solution.py:506
  107.3 7.2 %collective-permute-start.25 = (bf16[2,2,2,2,80,256]{5,4,3,2,1,0:T(8,128)(2,1)}, bf16[2,2,2,2,80,256]{5,4,3,2,1,0:T(8,128)(2,1)S(1)}, u32[]{:S(2)}, u32[]{:S(2)}) collective-permute-start(bf16[2,2,2,2,80,256]{5,4,3,2,1,0:T(8,128)(2,1)} %get-tuple-element.91), channel_id=1, source_target_pairs={{0,1},{1,0},{2,3},{3,2},{4,5},{5,4},{6,7},{7,6},{8,9},{9,8},{10,11... | collective-permute-start | bytes 1966088 | tf_op jit(solution)/shard_map/ppermute | solution.py:506
  107.3 8.2 %collective-permute-start.24 = (bf16[2,256,384]{2,1,0:T(8,128)(2,1)}, bf16[2,256,384]{2,1,0:T(8,128)(2,1)S(1)}, u32[]{:S(2)}, u32[]{:S(2)}) collective-permute-start(bf16[2,256,384]{2,1,0:T(8,128)(2,1)} %get-tuple-element.89), channel_id=1, source_target_pairs={{0,1},{1,0},{2,3},{3,2},{4,5},{5,4},{6,7},{7,6},{8,9},{9,8},{10,11... | collective-permute-start | bytes 1179656 | tf_op jit(solution)/shard_map/ppermute | solution.py:506
  115.7 6.4 %collective-permute-start.28 = (bf16[256,384]{1,0:T(8,128)(2,1)S(1)}, bf16[256,384]{1,0:T(8,128)(2,1)S(1)}, u32[]{:S(2)}, u32[]{:S(2)}) collective-permute-start(bf16[256,384]{1,0:T(8,128)(2,1)S(1)} %get-tuple-element.141), channel_id=1, source_target_pairs={{0,2},{1,3},{2,0},{3,1},{4,6},{5,7},{6,4},{7,5},{8,10},{9,11},{10,... | collective-permute-start | bytes 589832 | tf_op jit(solution)/shard_map/ppermute | solution.py:506
  116.5 11.4 %collective-permute-start.29 = (bf16[2,2,72,768]{3,2,1,0:T(8,128)(2,1)S(1)}, bf16[2,2,72,768]{3,2,1,0:T(8,128)(2,1)S(1)}, u32[]{:S(2)}, u32[]{:S(2)}) collective-permute-start(bf16[2,2,72,768]{3,2,1,0:T(8,128)(2,1)S(1)} %get-tuple-element.136), channel_id=1, source_target_pairs={{0,8},{1,9},{2,10},{3,11},{4,12},{5,13},{6,14},{7,15},{8,0},{9,1},... | collective-permute-start | bytes 1327112 | tf_op jit(solution)/shard_map/ppermute | solution.py:506
  118.3 17.0 %collective-permute-start.31 = (bf16[2,2,2,80,256]{4,3,2,1,0:T(8,128)(2,1)S(1)}, bf16[2,2,2,80,256]{4,3,2,1,0:T(8,128)(2,1)S(1)}, u32[]{:S(2)}, u32[]{:S(2)}) collective-permute-start(bf16[2,2,2,80,256]{4,3,2,1,0:T(8,128)(2,1)S(1)} %get-tuple-element.140), channel_id=1, source_target_pairs={{0,4},{1,5},{2,6},{3,7},{4,0},{5,1},{6,2},{7,3},{8,12},{9,13},{10,... | collective-permute-start | bytes 983048 | tf_op jit(solution)/shard_map/ppermute | solution.py:506
  119.8 15.0 %collective-permute-start.32 = (bf16[2,2,72,576]{3,2,1,0:T(8,128)(2,1)S(1)}, bf16[2,2,72,576]{3,2,1,0:T(8,128)(2,1)S(1)}, u32[]{:S(2)}, u32[]{:S(2)}) collective-permute-start(bf16[2,2,72,576]{3,2,1,0:T(8,128)(2,1)S(1)} %get-tuple-element.138), channel_id=1, source_target_pairs={{0,4},{1,5},{2,6},{3,7},{4,0},{5,1},{6,2},{7,3},{8,12},{9,13},{10,... | collective-permute-start | bytes 995336 | tf_op jit(solution)/shard_map/ppermute | solution.py:506
  127.9 11.5 %collective-permute-start.30 = (bf16[2,72,768]{2,1,0:T(8,128)(2,1)S(1)}, bf16[2,72,768]{2,1,0:T(8,128)(2,1)S(1)}, u32[]{:S(2)}, u32[]{:S(2)}) collective-permute-start(bf16[2,72,768]{2,1,0:T(8,128)(2,1)S(1)} %fusion.17), channel_id=1, source_target_pairs={{0,16},{1,17},{2,18},{3,19},{4,20},{5,21},{6,22},{7,23},{8,24},{9,... | collective-permute-start | bytes 663560 | tf_op jit(solution)/shard_map/ppermute | solution.py:506
  134.9 8.6 %collective-permute-start.35 = (bf16[2,72,576]{2,1,0:T(8,128)(2,1)S(1)}, bf16[2,72,576]{2,1,0:T(8,128)(2,1)S(1)}, u32[]{:S(2)}, u32[]{:S(2)}) collective-permute-start(bf16[2,72,576]{2,1,0:T(8,128)(2,1)S(1)} %get-tuple-element.144), channel_id=1, source_target_pairs={{0,8},{1,9},{2,10},{3,11},{4,12},{5,13},{6,14},{7,15},{8,0},{9,1},... | collective-permute-start | bytes 497672 | tf_op jit(solution)/shard_map/ppermute | solution.py:506
  135.3 11.1 %collective-permute-start.34 = (bf16[2,2,80,256]{3,2,1,0:T(8,128)(2,1)S(1)}, bf16[2,2,80,256]{3,2,1,0:T(8,128)(2,1)S(1)}, u32[]{:S(2)}, u32[]{:S(2)}) collective-permute-start(bf16[2,2,80,256]{3,2,1,0:T(8,128)(2,1)S(1)} %get-tuple-element.148), channel_id=1, source_target_pairs={{0,8},{1,9},{2,10},{3,11},{4,12},{5,13},{6,14},{7,15},{8,0},{9,1},... | collective-permute-start | bytes 491528 | tf_op jit(solution)/shard_map/ppermute | solution.py:506
  139.5 8.4 %collective-permute-start.33 = (bf16[2,72,768]{2,1,0:T(8,128)(2,1)S(1)}, bf16[2,72,768]{2,1,0:T(8,128)(2,1)S(1)}, u32[]{:S(2)}, u32[]{:S(2)}) collective-permute-start(bf16[2,72,768]{2,1,0:T(8,128)(2,1)S(1)} %fusion.8), channel_id=1, source_target_pairs={{0,2},{1,3},{2,0},{3,1},{4,6},{5,7},{6,4},{7,5},{8,10},{9,11},{10,... | collective-permute-start | bytes 663560 | tf_op jit(solution)/shard_map/ppermute | solution.py:506
  143.5 7.4 %collective-permute-start.37 = (bf16[72,576]{1,0:T(8,128)(2,1)S(1)}, bf16[72,576]{1,0:T(8,128)(2,1)S(1)}, u32[]{:S(2)}, u32[]{:S(2)}) collective-permute-start(bf16[72,576]{1,0:T(8,128)(2,1)S(1)} %fusion.28), channel_id=1, source_target_pairs={{0,16},{1,17},{2,18},{3,19},{4,20},{5,21},{6,22},{7,23},{8,24},{9,... | collective-permute-start | bytes 248840 | tf_op jit(solution)/shard_map/ppermute | solution.py:506
  146.4 6.7 %collective-permute-start.41 = (bf16[2,80,256]{2,1,0:T(8,128)(2,1)S(1)}, bf16[2,80,256]{2,1,0:T(8,128)(2,1)S(1)}, u32[]{:S(2)}, u32[]{:S(2)}) collective-permute-start(bf16[2,80,256]{2,1,0:T(8,128)(2,1)S(1)} %fusion.30), channel_id=1, source_target_pairs={{0,16},{1,17},{2,18},{3,19},{4,20},{5,21},{6,22},{7,23},{8,24},{9,... | collective-permute-start | bytes 245768 | tf_op jit(solution)/shard_map/ppermute | solution.py:506
  154.2 4.9 %collective-permute-start.36 = (bf16[2,72,768]{2,1,0:T(8,128)(2,1)S(1)}, bf16[2,72,768]{2,1,0:T(8,128)(2,1)S(1)}, u32[]{:S(2)}, u32[]{:S(2)}) collective-permute-start(bf16[2,72,768]{2,1,0:T(8,128)(2,1)S(1)} %add_convert_fusion.6.near), channel_id=1, source_target_pairs={{0,1},{1,0},{2,3},{3,2},{4,5},{5,4},{6,7},{7,6},{8,9},{9,8},{10,11... | collective-permute-start | bytes 663560 | tf_op jit(solution)/shard_map/ppermute | solution.py:506
  (36 other events, 223.9 us)

commit v5 on v4

--- a/solution.py
+++ b/solution.py
@@ -45,7 +45,7 @@
     return [pl.BlockSpec(memory_space=pltpu.VMEM) for _ in shape_dtypes]
 
 
-def call(kernel, scalars, arrays, outs, flops, scratch=(), mib=52, fetched=()):
+def call(kernel, scalars, arrays, outs, flops, scratch=(), mib=52, fetched=(), landing=()):
     specs = [pl.BlockSpec(memory_space=pltpu.SMEM)] * len(scalars) + whole(*arrays)
     specs += [pl.BlockSpec(memory_space=pl.ANY)] * len(fetched)
     arrays = [*arrays, *fetched]
@@ -59,7 +59,7 @@
         out_specs=whole(*outs),
         scratch_shapes=[
             *[pltpu.VMEM(shape, F32) for shape in scratch],
-            *[pltpu.VMEM(v.shape, v.dtype) for v in fetched],
+            *[pltpu.VMEM(shape, BF) for shape in landing],
             *([pltpu.SemaphoreType.DMA((len(fetched),))] if fetched else []),
         ],
         compiler_params=pltpu.CompilerParams(vmem_limit_bytes=mib * 1024 * 1024),
@@ -301,97 +301,128 @@
     return r & 1, (r >> 1) & 1, (r >> 2) & 1
 
 
-def feed_forward_pieces(d_rows, ff_rows, meta, attended, source, gains, cot, weight, *refs):
-    out_o, gk_o, gg_o, dk_o, dg_o, mid_o, attg_o, gain_o, down_s, wout_s = refs[12:22]
-    copies = [pltpu.make_async_copy(refs[i], refs[22 + i], refs[34].at[i]) for i in range(12)]
+def fetch_pieces(t, meta, refs, b_s, g_s, sems):
+    core, y, x, z0 = meta[0] & 1, (meta[0] >> 1) & 1, meta[1] & 1, (meta[1] >> 1) & 1
+    n = g_s.shape[-1]
+    copies = []
+    for i in range(8):
+        at = (z0 ^ (i >> 2), x ^ ((i >> 1) & 1), core ^ (i & 1))
+        copies.append(pltpu.make_async_copy(refs[i], b_s.at[at], sems.at[i]))
+    for i in range(8):
+        at = (y ^ ((i >> 1) & 1), core ^ (i & 1), x ^ (i >> 2))
+        source = refs[8 + i].at[:, :, :, pl.ds(t * n, n)]
+        copies.append(pltpu.make_async_copy(source, g_s.at[at], sems.at[8 + i]))
     for copy in copies:
         copy.start()
-    b00, b10, b01, b11, g001, g101, g011, g111, g000, g100, g010, g110 = refs[22:34]
-    core, y, x_own = meta[0] & 1, (meta[0] >> 1) & 1, meta[1] & 1
-    n_f = 8
-    hf = n_f // 2
+    return copies
+
+
+def hidden_block(t, d_rows, ff_rows, meta, second, feed_grad, b_s, g_s, down_s, gk_o, gg_o, put_down):
+    core, y, x_own, z1_own = meta[0] & 1, (meta[0] >> 1) & 1, meta[1] & 1, (meta[1] >> 2) & 1
     part_d = ff_rows // 4
-    part_o = d_rows // 3
-    cut = b00.shape[2] - ff_rows // 2
-    for copy in copies[:4]:
-        copy.wait()
-
-    def b_rows(z0, z1, x, c, rows):
-        low = chosen(x_own ^ x, b00[z0, z1, rows, :], b10[z0, z1, rows, :])
-        high = chosen(x_own ^ x, b01[z0, z1, rows, :], b11[z0, z1, rows, :])
-        return chosen(core ^ c, low, high)
-
-    def quarter(near, far):
-        parts = []
-        for f in range(n_f):
-            z1, z0, x = f >> 2, (f >> 1) & 1, f & 1
-            mine, other = near[z0, z1].astype(F32), far[z0, z1].astype(F32)
-            parts.append(chosen(x_own ^ x, mine, other))
-        return jnp.concatenate(parts, axis=0).astype(BF)
-
-    wo = []
-    for f in range(n_f):
-        z1, z0, x = f >> 2, (f >> 1) & 1, f & 1
-        wo.append(b_rows(z0, z1, x, 0, slice(ff_rows // 2, None)).astype(F32))
-        wo.append(b_rows(z0, z1, x, 1, slice(ff_rows // 2, None)).astype(F32)[: d_rows - cut])
-    wo = jnp.concatenate(wo, axis=0).astype(BF)
-    att = attended[...]
-    middle = source[...].astype(F32) + dot(att, wo, 1, 0)
-    scale_two, normed = norm_parts(middle)
-    g2 = gains[1:2, :]
-    second = (normed * g2).astype(BF)
-    out_grad = cot[...].astype(F32) * weight[...]
-    feed_grad = out_grad.astype(BF)
     feed = back = None
     for c_rel in (1, 0):
-        for copy in copies[8 - 4 * c_rel : 12 - 4 * c_rel]:
-            copy.wait()
-        first_q = quarter(g001, g101) if c_rel else quarter(g000, g100)
-        second_q = quarter(g011, g111) if c_rel else quarter(g010, g110)
-        wg = chosen(y, first_q, second_q)
-        wu = chosen(y, second_q, first_q)
         h = core ^ c_rel
-        wd = []
-        for i in range(hf):
-            for c in range(2):
-                wd.append(b_rows(i >> 1, h, i & 1, c, slice(0, ff_rows // 2)))
+        weights = []
+        for yy in range(2):
+            rows = [g_s[yy, h, f & 1, (f >> 1) & 1, f >> 2].astype(F32) for f in range(8)]
+            weights.append(jnp.concatenate(rows, axis=0).astype(BF))
+        wg, wu = weights
+        wd = [b_s[t, x, c, h, : ff_rows // 2, :] for x in range(2) for c in range(2)]
         wd = jnp.concatenate(wd, axis=0)
         gate = dot(second, wg, 1, 0)
         up = dot(second, wu, 1, 0)
         sig = jax.nn.sigmoid(gate)
         act = gate * sig
         product = (act * up).astype(BF)
-        part = dot(product, wd, 1, 0)
-        feed = part if feed is None else feed + part
-        down_s[...] = dot(product, feed_grad, 0, 0)
         pgrad = dot(feed_grad, wd, 1, 1)
         ggrad = (pgrad * up * (sig * (1.0 + gate * (1.0 - sig)))).astype(BF)
         ugrad = (pgrad * act).astype(BF)
-        part = dot(ggrad, wg, 1, 1) + dot(ugrad, wu, 1, 1)
-        back = part if back is None else back + part
-        for i in range(hf):
-            x, z0, z1 = rel(meta, hf * h + i)
-            for yy in range(2):
-                for c_to, to in ((0, dk_o), (1, dg_o)):
-                    at = pl.multiple_of(i * ff_rows + (yy * 2 + (core ^ c_to)) * part_d, 16)
-                    to[y ^ yy, x, z0, z1, :part_d, :] = down_s[pl.ds(at, part_d), :].astype(BF)
         to = gg_o if c_rel else gk_o
         for yy, grad in ((0, ggrad), (1, ugrad)):
             wgrad = dot(second, grad, 0, 0)
-            for f in range(n_f):
+            for f in range(8):
                 x, z0, z1 = rel(meta, f)
-                to[x, z0, z1, yy] = wgrad[d_rows * f : d_rows * (f + 1), :].astype(BF)
-    turned(out_o, middle + feed)
-    gain_o[...] = jnp.sum(back * normed, axis=0, keepdims=True)
-    middle_grad = out_grad + norm_back(back, g2, scale_two, normed)
-    mid_o[...] = middle_grad
+                to[x, y ^ yy, z0, z1] = wgrad[d_rows * f : d_rows * (f + 1), :].astype(BF)
+        down_s[...] = dot(product, feed_grad, 0, 0)
+        for x in range(2):
+            for yy in range(2):
+                for c_to in range(2):
+                    at = pl.multiple_of(x * ff_rows + (yy * 2 + (core ^ c_to)) * part_d, 16)
+                    value = down_s[pl.ds(at, part_d), :].astype(BF)
+                    put_down(c_to, y ^ yy, x ^ x_own, h ^ z1_own, value)
+        part = dot(product, wd, 1, 0)
+        feed = part if feed is None else feed + part
+        part = dot(ggrad, wg, 1, 1) + dot(ugrad, wu, 1, 1)
+        back = part if back is None else back + part
+    return feed, back
+
+
+def feed_forward_one(d_rows, ff_rows, meta, attended, source, gains, cot, weight, *refs):
+    mid_o, feed_o, back_o, wo_o, gk_o, gg_o, dk_o, dg_o, down_s, b_s, g_s, sems = refs[16:]
+    copies = fetch_pieces(0, meta, refs, b_s, g_s, sems)
+    cut = b_s.shape[4] - ff_rows // 2
+    for copy in copies[:8]:
+        copy.wait()
+    wo = []
+    for f in range(8):
+        for c in range(2):
+            rows = b_s[(f >> 1) & 1, f & 1, c, f >> 2, ff_rows // 2 :, :].astype(F32)
+            wo.append(rows if c == 0 else rows[: d_rows - cut])
+    wo = jnp.concatenate(wo, axis=0).astype(BF)
+    wo_o[...] = wo
+    middle = source[...].astype(F32) + dot(attended[...], wo, 1, 0)
+    mid_o[...] = middle
+    second = (norm_parts(middle)[1] * gains[1:2, :]).astype(BF)
+    feed_grad = (cot[...].astype(F32) * weight[...]).astype(BF)
+    for copy in copies[8:]:
+        copy.wait()
+
+    def put_down(c_to, y, x, z1, value):
+        (dg_o if c_to else dk_o)[y, x, z1] = value
+
+    feed_o[...], back_o[...] = hidden_block(
+        0, d_rows, ff_rows, meta, second, feed_grad, b_s, g_s, down_s, gk_o, gg_o, put_down
+    )
+
+
+def feed_forward_two(d_rows, ff_rows, meta, attended, gains, cot, weight, mid, feed, back, wo, dk_i, dg_i, *refs):
+    out_o, gk_o, gg_o, dk_o, dg_o, midg_o, attg_o, gain_o, down_s, wout_s, b_s, g_s, sems = refs[16:]
+    copies = fetch_pieces(1, meta, refs, b_s, g_s, sems)
+    core, y, z0_own = meta[0] & 1, (meta[0] >> 1) & 1, (meta[1] >> 1) & 1
+    part_d = ff_rows // 4
+    part_o = d_rows // 3
+    middle = mid[...]
+    scale_two, normed = norm_parts(middle)
+    g2 = gains[1:2, :]
+    second = (normed * g2).astype(BF)
+    out_grad = cot[...].astype(F32) * weight[...]
+    feed_grad = out_grad.astype(BF)
+    for first, to in ((dk_i, dk_o), (dg_i, dg_o)):
+        for i in range(8):
+            at = (i >> 2, (i >> 1) & 1, i & 1)
+            to[at[0], at[1], z0_own, at[2], :part_d, :] = first[at]
+    for copy in copies:
+        copy.wait()
+
+    def put_down(c_to, y, x, z1, value):
+        (dg_o if c_to else dk_o)[y, x, 1 ^ z0_own, z1, :part_d, :] = value
+
+    feed_part, back_part = hidden_block(
+        1, d_rows, ff_rows, meta, second, feed_grad, b_s, g_s, down_s, gk_o, gg_o, put_down
+    )
+    turned(out_o, middle + (feed[...] + feed_part))
+    back_all = back[...] + back_part
+    gain_o[...] = jnp.sum(back_all * normed, axis=0, keepdims=True)
+    middle_grad = out_grad + norm_back(back_all, g2, scale_two, normed)
+    midg_o[...] = middle_grad
     branch = middle_grad.astype(BF)
-    attg_o[...] = dot(branch, wo, 1, 1).astype(BF)
-    wout = dot(att, branch, 0, 0)
-    for f in range(n_f):
+    attg_o[...] = dot(branch, wo[...], 1, 1).astype(BF)
+    wout = dot(attended[...], branch, 0, 0)
+    for f in range(8):
         wout_s[f, :d_rows, :] = wout[d_rows * f : d_rows * (f + 1), :]
         wout_s[f, d_rows:, :] = jnp.zeros((part_o, wout.shape[1]), F32)
-    for f in range(n_f):
+    for f in range(8):
         x, z0, z1 = rel(meta, f)
         for yy in range(2):
             for c_to, to in ((0, dk_o), (1, dg_o)):
@@ -460,6 +491,12 @@
             out_o[:, pl.ds(at, n)] = pieces[yy].astype(F32)
 
 
+def place_quarters(meta, p00, p10, p01, p11, out_o):
+    n = p00.shape[1]
+    for piece, o in ((p00, 0), (p10, 2), (p01, 1), (p11, 3)):
+        out_o[:, pl.ds(pl.multiple_of((meta[0] ^ o) * n, 128), n)] = piece[...].astype(F32)
+
+
 def place_down(part_d, meta, p00, p10, p01, p11, out_o, wout_o):
     seq = meta[0]
     part_o = p00.shape[0] - part_d
@@ -485,9 +522,9 @@
     gains_o[1:2, :] = line[:, 256 : 256 + d_rows]
 
 
-def place_all(part_d, qk, v, meta, near, far, d0, d1, d2, d3, r_near, r_far,
+def place_all(part_d, qk, v, meta, g0, g1, g2, g3, d0, d1, d2, d3, r_near, r_far,
               gate_o, down_o, wout_o, w_o, bqk_o, bv_o, gains_o, all_s):
-    place_gate(meta, near, far, gate_o)
+    place_quarters(meta, g0, g1, g2, g3, gate_o)
     place_down(part_d, meta, d0, d1, d2, d3, down_o, wout_o)
     place_qkv(qk, v, meta, r_near, r_far, w_o, bqk_o, bv_o, gains_o, all_s)
 
@@ -818,6 +855,8 @@
     gu_c = net.swap(gu2, core)
     b1 = net.both(b0, zfar, 0, after(net.swap(b0, zfar), gu2))
     b_z = net.swap(b1, znear)
+    b_x = net.swap(b1, xbit)
+    b_c = net.swap(b1, core)
     a_xc = after(a_xc, b1)
 
     cos_t, sin_t = rope_tables(full_length, n_seq)
@@ -848,37 +887,63 @@
         20,
     )
     gu_y = after(gu_y, attended)
-    gu_x, b_z = after(gu_x, gu_y), after(b_z, gu_y)
+    gu_x, b_z, b_x = after(gu_x, gu_y), after(b_z, gu_y), after(b_x, gu_y)
     gu_xy = net.swap(gu_x, ybit)
-    b2 = net.both(b1, znear, 0, b_z)
-    b_x = net.swap(b2, xbit)
-    b_c = net.swap(b2, core)
+    b_zx = net.swap(b_z, xbit)
     gu_yc = net.swap(gu_y, core)
     gu_xc = net.swap(gu_x, core)
+    b_zc = net.swap(b_z, core)
     b_xc = net.swap(b_x, core)
+    b_zxc = net.swap(b_zx, core)
     gu_xyc = net.swap(gu_xy, core)
-    gate_up = [gu_c, gu_xc, gu_yc, gu_xyc, gu2, gu_x, gu_y, gu_xy]
+    pieces = [b1, b_c, b_x, b_xc, b_z, b_zc, b_zx, b_zxc]
+    pieces += [gu2, gu_c, gu_y, gu_yc, gu_x, gu_xc, gu_xy, gu_xyc]
 
     weight = tokens_micro / token_counts.astype(F32)
     weight = jnp.repeat(weight, batch * length)[:, None]
     lead = (2, 2, 2, 2)
-    block_out, gate_keep, gate_give, down_keep, down_give, middle_grad, attended_grad, gain_two = call(
-        functools.partial(feed_forward_pieces, d_rows, ff_rows),
+    cot = cotangent.reshape(rows, width)
+    part = units // 4
+    gate_lead = lead + (d_rows, part)
+    landing = [(2, 2, 2, 2) + b1.shape[1:], (2, 2, 2, 2, 2, d_rows, part)]
+    middle, feed_one, back_one, wf_out, keep_a, give_a, down_keep, down_give = call(
+        functools.partial(feed_forward_one, d_rows, ff_rows),
         [meta],
-        [attended, source, gains, cotangent.reshape(rows, width), weight],
+        [attended, source, gains, cot, weight],
+        [
+            sds((rows, width), F32),
+            sds((rows, width), F32),
+            sds((rows, width), F32),
+            sds((QW, width), BF),
+            sds(gate_lead, BF),
+            sds(gate_lead, BF),
+            sds((2, 2, 2, ff_rows // 4, width), BF),
+            sds((2, 2, 2, ff_rows // 4, width), BF),
+        ],
+        7e9,
+        [(2 * ff_rows, width)],
+        fetched=pieces,
+        landing=landing,
+    )
+    got_a = net.swap(give_a, core)
+    block_out, keep_b, give_b, down_keep, down_give, middle_grad, attended_grad, gain_two = call(
+        functools.partial(feed_forward_two, d_rows, ff_rows),
+        [meta],
+        [attended, gains, cot, weight, middle, feed_one, back_one, wf_out, down_keep, down_give],
         [
             sds((seqs, width, length), BF),
-            sds(lead + (d_rows, units // 2), BF),
-            sds(lead + (d_rows, units // 2), BF),
+            sds(gate_lead, BF),
+            sds(gate_lead, BF),
             sds(lead + (ff_rows // 4 + d_rows // 3, width), BF),
             sds(lead + (ff_rows // 4 + d_rows // 3, width), BF),
             sds((rows, width), F32),
             sds((rows, QW), BF),
             sds((1, width), F32),
         ],
-        1.4e10,
-        [(units // 2, width), (n_fsdp, d_rows + d_rows // 3, width)],
-        fetched=[b2, b_x, b_c, b_xc, *gate_up],
+        8e9,
+        [(2 * ff_rows, width), (n_fsdp, d_rows + d_rows // 3, width)],
+        fetched=pieces,
+        landing=landing,
     )
     block_out = block_out.reshape(micro, batch, width, length).swapaxes(2, 3)
 
@@ -888,12 +953,14 @@
     def halves(keep, got):
         return add(keep[0], got[0]), add(keep[1], got[1])
 
-    gate_got = net.swap(gate_give, core)
-    down_got = net.swap(after(down_give, gate_got), core)
-    gate, gate_give = halves(gate_keep, gate_got)
-    gate_got = net.swap(gate_give, xbit)
+    gate_a, give_a = halves(keep_a, after(got_a, attended_grad))
+    got_a = net.swap(give_a, xbit)
+    got_b = net.swap(after(give_b, give_a), core)
+    down_got = net.swap(after(down_give, got_b), core)
+    gate_b, give_b = halves(keep_b, got_b)
+    got_b = net.swap(give_b, xbit)
     down, down_give = halves(down_keep, down_got)
-    attended_grad = after(attended_grad, gate_give, down_give)
+    attended_grad = after(attended_grad, give_a, give_b, down_give)
     down_got = net.swap(down_give, ybit)
 
     dq, dkv_keep, dkv_give, rest_keep, rest_give = call(
@@ -910,8 +977,11 @@
         1.4e10,
         [(width, 1024), (1, qkv_w), (1, width), (n_fsdp, 8, 1024)],
     )
-    gate, gate_give = halves(gate, after(gate_got, dq, down_got))
-    gate_got = net.swap(gate_give, znear)
+    gate_a, give_a = halves(gate_a, after(got_a, dq))
+    gate_b, give_b = halves(gate_b, after(got_b, down_got))
+    gate_give = jnp.concatenate([give_a, give_b], axis=-1)
+    gate = jnp.concatenate([gate_a, gate_b], axis=-1)
+    gate_got = net.swap(gate_give, ybit)
     down, down_give = halves(down, after(down_got, gate_give))
     down_got = net.swap(down_give, xbit)
     rest, rest_give = halves(rest_keep, after(net.swap(rest_give, core), down_give))
@@ -927,33 +997,35 @@
         mib=16,
     )
     gate, gate_give = halves(gate, after(gate_got, hidden_grad))
-    gate_got = net.swap(gate_give, zfar)
+    gate_got = net.swap(gate_give, znear)
     hidden_grad = hidden_grad.reshape(micro, batch, width, length).swapaxes(2, 3)
     down, down_give = halves(down, after(down_got, gate_give))
     down_got = net.swap(down_give, znear)
     rest, rest_give = halves(rest, after(rest_got, down_give))
     rest_got = net.swap(rest_give, znear)
-    gate = add(gate, after(gate_got, rest_give))
-    gate_got = net.swap(gate, ybit)
-    down, down_give = halves(down, after(down_got, gate))
+    gate, gate_give = halves(gate, after(gate_got, rest_give))
+    gate_got = net.swap(gate_give, zfar)
+    down, down_give = halves(down, after(down_got, gate_give))
     down_got = net.swap(down_give, zfar)
     rest, rest_give = halves(rest, after(rest_got, down_give))
     rest_got = net.swap(rest_give, zfar)
     gate = add(gate, after(gate_got, rest_give))
-    gate_far = net.swap(gate, core)
+    gate_y = net.swap(gate, ybit)
+    gate_c = net.swap(gate, core)
     down = add(down, after(down_got, gate))
     down_y = net.swap(down, ybit)
     down_c = net.swap(down, core)
     rest = add(rest, after(rest_got, down))
     rest_got = net.swap(rest, ybit)
     down_yc = net.swap(down_y, core)
+    gate_yc = net.swap(gate_y, core)
     rest = add(rest, rest_got)
     rest_far = net.swap(rest, core)
     qk, v = (QW + KW) // n_fsdp, KW // n_fsdp
     out_gate, out_down, out_wout, out_qkv, b_qk, b_v, out_gains = call(
         functools.partial(place_all, ff_rows // 4, qk, v),
         [meta],
-        [gate, gate_far, down, down_y, down_c, down_yc, rest, rest_far],
+        [gate, gate_y, gate_c, gate_yc, down, down_y, down_c, down_yc, rest, rest_far],
         [
             sds((d_rows, 2 * units), F32),
             sds((ff_rows, width), F32),

time: 161 us -> 167 us (1.037)
  Pallas kernels: 39.2 us -> 46.3 us
  waiting for transfers between devices: 70.1 us -> 63.8 us
  starting transfers between devices: 36.1 us -> 40 us
  local copies, waits for them, and re-layouts: 8.17 us -> 12 us
  other arithmetic: 6.25 us -> 3.77 us
    pallas_call x5 -> x6, Pallas kernels: 38.3 us -> 45.5 us  [call(): pl.pallas_call(kernel, out_shape=outs, in_specs=specs, out_specs=whole(*o...]
    ppermute x44 -> x51, waiting for transfers between devices: 70.1 us -> 63.8 us  [swap(): return lax.ppermute(value, ('fsdp', 'seq'), pairs)]
    ppermute x44 -> x51, starting transfers between devices: 36.1 us -> 40 us  [swap(): return lax.ppermute(value, ('fsdp', 'seq'), pairs)]
    unnamed x50 -> x66, local copies, waits for them, and re-layouts: 7.11 us -> 11 us
    convert_element_type x16 -> x17, other arithmetic: 3.49 us -> 2.04 us  [add(): return (keep.astype(F32) + got.astype(F32)).astype(BF)]
  transfers between devices with their start and end apart: 44 -> 51, of which waited for: 22 -> 24; matrix products, arithmetic and copies ran while one was open for 5% -> 3% of each run, Pallas kernels for 14% -> 21%
where the time goes in v5:
time: 167 us
  waiting for transfers between devices  63.8 us (38%)
  Pallas kernels  46.3 us (28%)
  starting transfers between devices  40 us (24%)
  local copies, waits for them, and re-layouts  12 us (7%)
  other arithmetic  3.77 us (2%)
    ppermute x51, waiting for transfers between devices, swap(): return lax.ppermute(value, ('fsdp', 'seq'), pairs)  63.8 us
    pallas_call x6, Pallas kernels, call(): pl.pallas_call(kernel, out_shape=outs, in_specs=specs, out_specs=whole(*o...  45.5 us
    ppermute x51, starting transfers between devices, swap(): return lax.ppermute(value, ('fsdp', 'seq'), pairs)  40 us
    unnamed x66, local copies, waits for them, and re-layouts  11 us
  transfers between devices with their start and end apart: 51, of which 24 were waited for; matrix products, arithmetic and copies ran while one was open for 3% of the time, Pallas kernels for 21%

profile of v5, /device:TPU:0, one launch (start us, length us, event | category | flops | bytes accessed | tf_op | source)
XLA Modules:
  0.0 167.1 jit_solution(16078142829102741014)
XLA Ops:
  3.8 4.1 %collective-permute-start.3 = (bf16[40,960]{1,0:T(8,128)(2,1)S(1)}, bf16[40,960]{1,0:T(8,128)(2,1)S(1)}, u32[]{:S(2)}, u32[]{:S(2)}) collective-permute-start(bf16[40,960]{1,0:T(8,128)(2,1)S(1)} %shard_map.187), channel_id=1, source_target_pairs={{0,16},{1,17},{2,18},{3,19},{4,20},{5,21},{6,22},{7,23},{8,24},{9,... | collective-permute-start | bytes 230408 | tf_op jit(solution)/shard_map/ppermute | solution.py:543
  10.0 1.6 collective-permute-start
  12.6 1.6 collective-permute-start.4
  14.3 6.0 %collective-permute-done.9 = bf16[72,768]{1,0:T(8,128)(2,1)S(1)} collective-permute-done((bf16[72,768]{1,0:T(8,128)(2,1)S(1)}, bf16[72,768]{1,0:T(8,128)(2,1)S(1)}, u32[]{:S(2)}, u32[]{:S(2)}) %collective-permute-start.9) | collective-permute-done | bytes 110624 | tf_op jit(solution)/shard_map/ppermute | solution.py:543
  21.2 1.6 collective-permute-start.5
  22.8 4.1 %collective-permute-start.8 = (bf16[136,576]{1,0:T(8,128)(2,1)S(1)}, bf16[136,576]{1,0:T(8,128)(2,1)S(1)}, u32[]{:S(2)}, u32[]{:S(2)}) collective-permute-start(bf16[136,576]{1,0:T(8,128)(2,1)S(1)} %dynamic-slice_bitcast_fusion), channel_id=1, source_target_pairs={{0,16},{1,17},{2,18},{3,19},{4,20},{5,21},{6,22},{7,23},{8,24},{9,... | collective-permute-start | bytes 470024 | tf_op jit(solution)/shard_map/ppermute | solution.py:543
  27.3 6.7 %collective-permute-done.10 = bf16[2,72,768]{2,1,0:T(8,128)(2,1)S(1)} collective-permute-done((bf16[2,72,768]{2,1,0:T(8,128)(2,1)S(1)}, bf16[2,72,768]{2,1,0:T(8,128)(2,1)S(1)}, u32[]{:S(2)}, u32[]{:S(2)}) %collective-permute-start.10) | collective-permute-done | bytes 221216 | tf_op jit(solution)/shard_map/ppermute | solution.py:543
  34.3 2.2 %collective-permute-start.15 = (bf16[2,136,576]{2,1,0:T(8,128)(2,1)S(1)}, bf16[2,136,576]{2,1,0:T(8,128)(2,1)}, u32[]{:S(2)}, u32[]{:S(2)}) collective-permute-start(bf16[2,136,576]{2,1,0:T(8,128)(2,1)S(1)} %pad_maximum_fusion.3.refs_0_), channel_id=1, source_target_pairs={{0,8},{1,9},{2,10},{3,11},{4,12},{5,13},{6,14},{7,15},{8,0},{9,1},... | collective-permute-start | bytes 940040 | tf_op jit(solution)/shard_map/ppermute | solution.py:543
  37.0 1.5 collective-permute-start.21
  41.0 8.3 %shard_map.188 = (bf16[256,576]{1,0:T(8,128)(2,1)S(1)}, bf16[2,3,384,64]{3,2,1,0:T(8,128)(2,1)S(1)}, bf16[2,3,512,64]{3,2,1,0:T(8,128)(2,1)S(1)}, bf16[2,3,512,6...) custom-call(s32[2]{0:T(128)S(1)} %pad_add_fusion.meta, ...), custom_call_target="tpu_custom_call" | custom-call | flops 12000000000 | bytes 6084096 | tf_op jit(solution)/shard_map/pallas_call | solution.py:55
  58.4 8.9 %collective-permute-done.23.refs_14_ = bf16[2,2,72,768]{3,2,1,0:T(8,128)(2,1)} collective-permute-done((bf16[2,2,72,768]{3,2,1,0:T(8,128)(2,1)}, bf16[2,2,72,768]{3,2,1,0:T(8,128)(2,1)}, u32[]{:S(2)}, u32[]{:S(2)}) %collective-permute-start.23) | collective-permute-done | bytes 442400 | tf_op jit(solution)/shard_map/ppermute | solution.py:543
  68.4 1.5 collective-permute-done.16.refs_5_
  71.4 8.8 %shard_map.189 = (f32[256,576]{1,0:T(8,128)}, f32[256,576]{1,0:T(8,128)}, f32[256,576]{1,0:T(8,128)}, bf16[576,576]{1,0:T(8,128)(2,1)}, bf16[2,2,2,2,72,384]{5,4...) custom-call(s32[2]{0:T(128)S(1)} %pad_add_fusion.meta, ...), custom_call_target="tpu_custom_call" | custom-call | flops 7000000000 | bytes 12023296 | tf_op jit(solution)/shard_map/pallas_call | solution.py:55
  80.4 11.7 %shard_map.190 = (bf16[2,576,128]{2,1,0:T(8,128)(2,1)}, bf16[2,2,2,2,72,384]{5,4,3,2,1,0:T(8,128)(2,1)}, bf16[2,2,2,2,72,384]{5,4,3,2,1,0:T(8,128)(2,1)}, bf16[2...) custom-call(s32[2]{0:T(128)S(1)} %pad_add_fusion.meta, ...), custom_call_target="tpu_custom_call" | custom-call | flops 8000000000 | bytes 15564544 | tf_op jit(solution)/shard_map/pallas_call | solution.py:55
  92.9 2.3 %collective-permute-done.26 = bf16[2,2,2,2,72,384]{5,4,3,2,1,0:T(8,128)(2,1)S(1)} collective-permute-done((bf16[2,2,2,2,72,384]{5,4,3,2,1,0:T(8,128)(2,1)}, bf16[2,2,2,2,72,384]{5,4,3,2,1,0:T(8,128)(2,1)S(1)}, u32[]{:S(2)}, u32[]{:S(2)}) %collective-permute-start.26) | collective-permute-done | bytes 884768 | tf_op jit(solution)/shard_map/ppermute | solution.py:543
  96.4 1.5 collective-permute-start.32
  98.8 1.3 collective-permute-start.30
  100.2 12.7 %shard_map.191 = (bf16[256,640]{1,0:T(8,128)(2,1)S(1)}, bf16[2,256,384]{2,1,0:T(8,128)(2,1)}, bf16[2,256,384]{2,1,0:T(8,128)(2,1)}, bf16[2,2,2,2,80,256]{5,4,3,2...) custom-call(s32[2]{0:T(128)S(1)} %pad_add_fusion.meta, bf16[256,640]{1,0:T(8,128)(2,1)S(1)} %pad_maximum_fusion.4.b0, ...), custom_call_target="tpu_custom_call" | custom-call | flops 14000000000 | bytes 7282432 | tf_op jit(solution)/shard_map/pallas_call | solution.py:55
  113.4 3.8 %collective-permute-done.32 = bf16[2,2,2,72,384]{4,3,2,1,0:T(8,128)(2,1)S(1)} collective-permute-done((bf16[2,2,2,72,384]{4,3,2,1,0:T(8,128)(2,1)S(1)}, bf16[2,2,2,72,384]{4,3,2,1,0:T(8,128)(2,1)S(1)}, u32[]{:S(2)}, u32[]{:S(2)}) %collective-permute-start.32) | collective-permute-done | bytes 442400 | tf_op jit(solution)/shard_map/ppermute | solution.py:543
  119.3 1.3 collective-permute-start.33
  122.0 1.4 collective-permute-start.37
  123.4 3.8 %collective-permute-done.33.other = bf16[256,384]{1,0:T(8,128)(2,1)S(1)} collective-permute-done((bf16[256,384]{1,0:T(8,128)(2,1)S(1)}, bf16[256,384]{1,0:T(8,128)(2,1)S(1)}, u32[]{:S(2)}, u32[]{:S(2)}) %collective-permute-start.33) | collective-permute-done | bytes 196640 | tf_op jit(solution)/shard_map/ppermute | solution.py:543
  127.2 1.9 %shard_map.192 = f32[2,576,128]{2,1,0:T(8,128)} custom-call(bf16[256,640]{1,0:T(8,128)(2,1)S(1)} %get-tuple-element.110.dq, bf16[256,384]{1,0:T(8,128)(2,1)S(1)} %get-tuple-element.172.own, bf16[256,384]{1,0:T(8,128)(2,1)S(1)} %collective-permute-done.33.other, bf16[256,576]{1,0:T(8,128)(2,1)S(1)} %bitcast.188, f32[256,576]{1,0:T(8,128)S(1)} %copy-done.9, ...), custom_call_target="tpu_custom_call" | custom-call | flops 3000000000 | bytes 3305984 | tf_op jit(solution)/shard_map/pallas_call | solution.py:55
  129.1 6.1 %collective-permute-done.34 = bf16[2,2,72,768]{3,2,1,0:T(8,128)(2,1)S(1)} collective-permute-done((bf16[2,2,72,768]{3,2,1,0:T(8,128)(2,1)S(1)}, bf16[2,2,72,768]{3,2,1,0:T(8,128)(2,1)S(1)}, u32[]{:S(2)}, u32[]{:S(2)}) %collective-permute-start.34) | collective-permute-done | bytes 442400 | tf_op jit(solution)/shard_map/ppermute | solution.py:543
  135.5 2.4 %collective-permute-done.37 = bf16[2,2,72,576]{3,2,1,0:T(8,128)(2,1)S(1)} collective-permute-done((bf16[2,2,72,576]{3,2,1,0:T(8,128)(2,1)S(1)}, bf16[2,2,72,576]{3,2,1,0:T(8,128)(2,1)S(1)}, u32[]{:S(2)}, u32[]{:S(2)}) %collective-permute-start.37) | collective-permute-done | bytes 331808 | tf_op jit(solution)/shard_map/ppermute | solution.py:543
  138.2 2.0 %collective-permute-start.39 = (bf16[2,2,80,256]{3,2,1,0:T(8,128)(2,1)S(1)}, bf16[2,2,80,256]{3,2,1,0:T(8,128)(2,1)S(1)}, u32[]{:S(2)}, u32[]{:S(2)}) collective-permute-start(bf16[2,2,80,256]{3,2,1,0:T(8,128)(2,1)S(1)} %get-tuple-element.176), channel_id=1, source_target_pairs={{0,8},{1,9},{2,10},{3,11},{4,12},{5,13},{6,14},{7,15},{8,0},{9,1},... | collective-permute-start | bytes 491528 | tf_op jit(solution)/shard_map/ppermute | solution.py:543
  140.2 4.7 %collective-permute-done.35 = bf16[2,72,768]{2,1,0:T(8,128)(2,1)S(1)} collective-permute-done((bf16[2,72,768]{2,1,0:T(8,128)(2,1)S(1)}, bf16[2,72,768]{2,1,0:T(8,128)(2,1)S(1)}, u32[]{:S(2)}, u32[]{:S(2)}) %collective-permute-start.35) | collective-permute-done | bytes 221216 | tf_op jit(solution)/shard_map/ppermute | solution.py:543
  145.6 3.1 %collective-permute-done.40 = bf16[2,72,576]{2,1,0:T(8,128)(2,1)S(1)} collective-permute-done((bf16[2,72,576]{2,1,0:T(8,128)(2,1)S(1)}, bf16[2,72,576]{2,1,0:T(8,128)(2,1)S(1)}, u32[]{:S(2)}, u32[]{:S(2)}) %collective-permute-start.40) | collective-permute-done | bytes 165920 | tf_op jit(solution)/shard_map/ppermute | solution.py:543
  149.6 2.6 %collective-permute-done.39 = bf16[2,2,80,256]{3,2,1,0:T(8,128)(2,1)S(1)} collective-permute-done((bf16[2,2,80,256]{3,2,1,0:T(8,128)(2,1)S(1)}, bf16[2,2,80,256]{3,2,1,0:T(8,128)(2,1)S(1)}, u32[]{:S(2)}, u32[]{:S(2)}) %collective-permute-start.39) | collective-permute-done | bytes 163872 | tf_op jit(solution)/shard_map/ppermute | solution.py:543
  153.1 2.4 %collective-permute-done.38 = bf16[72,768]{1,0:T(8,128)(2,1)S(1)} collective-permute-done((bf16[72,768]{1,0:T(8,128)(2,1)S(1)}, bf16[72,768]{1,0:T(8,128)(2,1)S(1)}, u32[]{:S(2)}, u32[]{:S(2)}) %collective-permute-start.38) | collective-permute-done | bytes 110624 | tf_op jit(solution)/shard_map/ppermute | solution.py:543
  160.6 1.9 %collective-permute-done.45.d1 = bf16[72,576]{1,0:T(8,128)(2,1)S(1)} collective-permute-done((bf16[72,576]{1,0:T(8,128)(2,1)S(1)}, bf16[72,576]{1,0:T(8,128)(2,1)S(1)}, u32[]{:S(2)}, u32[]{:S(2)}) %collective-permute-start.45) | collective-permute-done | bytes 82976 | tf_op jit(solution)/shard_map/ppermute | solution.py:543
  165.2 1.9 %shard_map.193 = (f32[72,3072]{1,0:T(8,128)}, f32[192,576]{1,0:T(8,128)}, f32[72,576]{1,0:T(8,128)}, f32[72,960]{1,0:T(8,128)}, f32[1,96]{1,0:T(1,128)}, /*index=5*/f32[1,24]{1,0:T(1,128)}, f32[2,72]{1,0:T(2,128)}) custom-call(s32[2]{0:T(128)S(1)} %pad_add_fusion.meta, bf16[72,768]{1,0:T(8,128)(2,1)S(1)} %fusion.22.g0, ...), custom_call_target="tpu_custom_call" | custom-call | flops 3000000000 | bytes 2708512 | tf_op jit(solution)/shard_map/pallas_call | solution.py:55
  (192 shorter events, 40.1 us)
Async XLA Ops:
  3.8 8.8 %collective-permute-start.3 = (bf16[40,960]{1,0:T(8,128)(2,1)S(1)}, bf16[40,960]{1,0:T(8,128)(2,1)S(1)}, u32[]{:S(2)}, u32[]{:S(2)}) collective-permute-start(bf16[40,960]{1,0:T(8,128)(2,1)S(1)} %shard_map.187), channel_id=1, source_target_pairs={{0,16},{1,17},{2,18},{3,19},{4,20},{5,21},{6,22},{7,23},{8,24},{9,... | collective-permute-start | bytes 230408 | tf_op jit(solution)/shard_map/ppermute | solution.py:543
  10.0 17.1 %collective-permute-start.1 = (bf16[256,640]{1,0:T(8,128)(2,1)S(1)}, bf16[256,640]{1,0:T(8,128)(2,1)S(1)}, u32[]{:S(2)}, u32[]{:S(2)}) collective-permute-start(bf16[256,640]{1,0:T(8,128)(2,1)S(1)} %pad_maximum_fusion.4.b0), channel_id=1, source_target_pairs={{0,1},{1,0},{2,3},{3,2},{4,5},{5,4},{6,7},{7,6},{8,9},{9,8},{10,11... | collective-permute-start | bytes 983048 | tf_op jit(solution)/shard_map/ppermute | solution.py:543
  10.0 12.8 %collective-permute-start = (bf16[256,640]{1,0:T(8,128)(2,1)S(1)}, bf16[256,640]{1,0:T(8,128)(2,1)S(1)}, u32[]{:S(2)}, u32[]{:S(2)}) collective-permute-start(bf16[256,640]{1,0:T(8,128)(2,1)S(1)} %pad_maximum_fusion.4.b0), channel_id=1, source_target_pairs={{0,2},{1,3},{2,0},{3,1},{4,6},{5,7},{6,4},{7,5},{8,10},{9,11},{10,... | collective-permute-start | bytes 983048 | tf_op jit(solution)/shard_map/ppermute | solution.py:543
  11.6 8.6 %collective-permute-start.9 = (bf16[72,768]{1,0:T(8,128)(2,1)S(1)}, bf16[72,768]{1,0:T(8,128)(2,1)S(1)}, u32[]{:S(2)}, u32[]{:S(2)}) collective-permute-start(bf16[72,768]{1,0:T(8,128)(2,1)S(1)} %constant_dynamic-slice_fusion), channel_id=1, source_target_pairs={{0,16},{1,17},{2,18},{3,19},{4,20},{5,21},{6,22},{7,23},{8,24},{9,... | collective-permute-start | bytes 331784 | tf_op jit(solution)/shard_map/ppermute | solution.py:543
  12.6 8.4 %collective-permute-start.4 = (bf16[2,40,960]{2,1,0:T(8,128)(2,1)S(1)}, bf16[2,40,960]{2,1,0:T(8,128)(2,1)S(1)}, u32[]{:S(2)}, u32[]{:S(2)}) collective-permute-start(bf16[2,40,960]{2,1,0:T(8,128)(2,1)S(1)} %pad_maximum_fusion.8), channel_id=1, source_target_pairs={{0,8},{1,9},{2,10},{3,11},{4,12},{5,13},{6,14},{7,15},{8,0},{9,1},... | collective-permute-start | bytes 460808 | tf_op jit(solution)/shard_map/ppermute | solution.py:543
  21.1 19.1 %collective-permute-start.6 = (bf16[2,2,40,960]{3,2,1,0:T(8,128)(2,1)S(1)}, bf16[2,2,40,960]{3,2,1,0:T(8,128)(2,1)S(1)}, u32[]{:S(2)}, u32[]{:S(2)}) collective-permute-start(bf16[2,2,40,960]{3,2,1,0:T(8,128)(2,1)S(1)} %pad_maximum_fusion.5.a00), channel_id=1, source_target_pairs={{0,1},{1,0},{2,3},{3,2},{4,5},{5,4},{6,7},{7,6},{8,9},{9,8},{10,11... | collective-permute-start | bytes 921608 | tf_op jit(solution)/shard_map/ppermute | solution.py:543
  21.2 12.9 %collective-permute-start.5 = (bf16[2,2,40,960]{3,2,1,0:T(8,128)(2,1)S(1)}, bf16[2,2,40,960]{3,2,1,0:T(8,128)(2,1)S(1)}, u32[]{:S(2)}, u32[]{:S(2)}) collective-permute-start(bf16[2,2,40,960]{3,2,1,0:T(8,128)(2,1)S(1)} %pad_maximum_fusion.5.a00), channel_id=1, source_target_pairs={{0,4},{1,5},{2,6},{3,7},{4,0},{5,1},{6,2},{7,3},{8,12},{9,13},{10,... | collective-permute-start | bytes 921608 | tf_op jit(solution)/shard_map/ppermute | solution.py:543
  22.8 11.2 %collective-permute-start.10 = (bf16[2,72,768]{2,1,0:T(8,128)(2,1)S(1)}, bf16[2,72,768]{2,1,0:T(8,128)(2,1)S(1)}, u32[]{:S(2)}, u32[]{:S(2)}) collective-permute-start(bf16[2,72,768]{2,1,0:T(8,128)(2,1)S(1)} %pad_maximum_fusion.7), channel_id=1, source_target_pairs={{0,8},{1,9},{2,10},{3,11},{4,12},{5,13},{6,14},{7,15},{8,0},{9,1},... | collective-permute-start | bytes 663560 | tf_op jit(solution)/shard_map/ppermute | solution.py:543
  22.8 11.3 %collective-permute-start.8 = (bf16[136,576]{1,0:T(8,128)(2,1)S(1)}, bf16[136,576]{1,0:T(8,128)(2,1)S(1)}, u32[]{:S(2)}, u32[]{:S(2)}) collective-permute-start(bf16[136,576]{1,0:T(8,128)(2,1)S(1)} %dynamic-slice_bitcast_fusion), channel_id=1, source_target_pairs={{0,16},{1,17},{2,18},{3,19},{4,20},{5,21},{6,22},{7,23},{8,24},{9,... | collective-permute-start | bytes 470024 | tf_op jit(solution)/shard_map/ppermute | solution.py:543
  27.1 11.4 %collective-permute-start.2 = (bf16[256,640]{1,0:T(8,128)(2,1)S(1)}, bf16[256,640]{1,0:T(8,128)(2,1)S(1)}, u32[]{:S(2)}, u32[]{:S(2)}) collective-permute-start(bf16[256,640]{1,0:T(8,128)(2,1)S(1)} %collective-permute-done.b1), channel_id=1, source_target_pairs={{0,1},{1,0},{2,3},{3,2},{4,5},{5,4},{6,7},{7,6},{8,9},{9,8},{10,11... | collective-permute-start | bytes 983048 | tf_op jit(solution)/shard_map/ppermute | solution.py:543
  34.3 22.5 %collective-permute-start.15 = (bf16[2,136,576]{2,1,0:T(8,128)(2,1)S(1)}, bf16[2,136,576]{2,1,0:T(8,128)(2,1)}, u32[]{:S(2)}, u32[]{:S(2)}) collective-permute-start(bf16[2,136,576]{2,1,0:T(8,128)(2,1)S(1)} %pad_maximum_fusion.3.refs_0_), channel_id=1, source_target_pairs={{0,8},{1,9},{2,10},{3,11},{4,12},{5,13},{6,14},{7,15},{8,0},{9,1},... | collective-permute-start | bytes 940040 | tf_op jit(solution)/shard_map/ppermute | solution.py:543
  36.5 19.8 %collective-permute-start.12 = (bf16[2,136,576]{2,1,0:T(8,128)(2,1)S(1)}, bf16[2,136,576]{2,1,0:T(8,128)(2,1)S(1)}, u32[]{:S(2)}, u32[]{:S(2)}) collective-permute-start(bf16[2,136,576]{2,1,0:T(8,128)(2,1)S(1)} %pad_maximum_fusion.3.refs_0_), channel_id=1, source_target_pairs={{0,4},{1,5},{2,6},{3,7},{4,0},{5,1},{6,2},{7,3},{8,12},{9,13},{10,... | collective-permute-start | bytes 940040 | tf_op jit(solution)/shard_map/ppermute | solution.py:543
  37.0 18.5 %collective-permute-start.21 = (bf16[2,2,72,768]{3,2,1,0:T(8,128)(2,1)S(1)}, bf16[2,2,72,768]{3,2,1,0:T(8,128)(2,1)}, u32[]{:S(2)}, u32[]{:S(2)}) collective-permute-start(bf16[2,2,72,768]{3,2,1,0:T(8,128)(2,1)S(1)} %pad_maximum_fusion.refs_8_), channel_id=1, source_target_pairs={{0,4},{1,5},{2,6},{3,7},{4,0},{5,1},{6,2},{7,3},{8,12},{9,13},{10,... | collective-permute-start | bytes 1327112 | tf_op jit(solution)/shard_map/ppermute | solution.py:543
  40.1 17.9 %collective-permute-start.19 = (bf16[2,2,72,768]{3,2,1,0:T(8,128)(2,1)S(1)}, bf16[2,2,72,768]{3,2,1,0:T(8,128)(2,1)S(1)}, u32[]{:S(2)}, u32[]{:S(2)}) collective-permute-start(bf16[2,2,72,768]{3,2,1,0:T(8,128)(2,1)S(1)} %pad_maximum_fusion.refs_8_), channel_id=1, source_target_pairs={{0,1},{1,0},{2,3},{3,2},{4,5},{5,4},{6,7},{7,6},{8,9},{9,8},{10,11... | collective-permute-start | bytes 1327112 | tf_op jit(solution)/shard_map/ppermute | solution.py:543
  40.3 14.6 %collective-permute-start.13 = (bf16[2,2,72,768]{3,2,1,0:T(8,128)(2,1)S(1)}, bf16[2,2,72,768]{3,2,1,0:T(8,128)(2,1)}, u32[]{:S(2)}, u32[]{:S(2)}) collective-permute-start(bf16[2,2,72,768]{3,2,1,0:T(8,128)(2,1)S(1)} %pad_maximum_fusion.refs_8_), channel_id=1, source_target_pairs={{0,2},{1,3},{2,0},{3,1},{4,6},{5,7},{6,4},{7,5},{8,10},{9,11},{10,... | collective-permute-start | bytes 1327112 | tf_op jit(solution)/shard_map/ppermute | solution.py:543
  55.5 11.8 %collective-permute-start.23 = (bf16[2,2,72,768]{3,2,1,0:T(8,128)(2,1)}, bf16[2,2,72,768]{3,2,1,0:T(8,128)(2,1)}, u32[]{:S(2)}, u32[]{:S(2)}) collective-permute-start(bf16[2,2,72,768]{3,2,1,0:T(8,128)(2,1)} %collective-permute-done.21.refs_12_), channel_id=1, source_target_pairs={{0,2},{1,3},{2,0},{3,1},{4,6},{5,7},{6,4},{7,5},{8,10},{9,11},{10,... | collective-permute-start | bytes 1327112 | tf_op jit(solution)/shard_map/ppermute | solution.py:543
  56.3 11.1 %collective-permute-start.14 = (bf16[2,136,576]{2,1,0:T(8,128)(2,1)S(1)}, bf16[2,136,576]{2,1,0:T(8,128)(2,1)S(1)}, u32[]{:S(2)}, u32[]{:S(2)}) collective-permute-start(bf16[2,136,576]{2,1,0:T(8,128)(2,1)S(1)} %collective-permute-done.12.refs_2_), channel_id=1, source_target_pairs={{0,1},{1,0},{2,3},{3,2},{4,5},{5,4},{6,7},{7,6},{8,9},{9,8},{10,11... | collective-permute-start | bytes 940040 | tf_op jit(solution)/shard_map/ppermute | solution.py:543
  56.8 11.1 %collective-permute-start.17 = (bf16[2,136,576]{2,1,0:T(8,128)(2,1)}, bf16[2,136,576]{2,1,0:T(8,128)(2,1)}, u32[]{:S(2)}, u32[]{:S(2)}) collective-permute-start(bf16[2,136,576]{2,1,0:T(8,128)(2,1)} %collective-permute-done.15.refs_4_), channel_id=1, source_target_pairs={{0,4},{1,5},{2,6},{3,7},{4,0},{5,1},{6,2},{7,3},{8,12},{9,13},{10,... | collective-permute-start | bytes 940040 | tf_op jit(solution)/shard_map/ppermute | solution.py:543
  57.9 12.0 %collective-permute-start.22 = (bf16[2,2,72,768]{3,2,1,0:T(8,128)(2,1)}, bf16[2,2,72,768]{3,2,1,0:T(8,128)(2,1)}, u32[]{:S(2)}, u32[]{:S(2)}) collective-permute-start(bf16[2,2,72,768]{3,2,1,0:T(8,128)(2,1)} %collective-permute-done.21.refs_12_), channel_id=1, source_target_pairs={{0,1},{1,0},{2,3},{3,2},{4,5},{5,4},{6,7},{7,6},{8,9},{9,8},{10,11... | collective-permute-start | bytes 1327112 | tf_op jit(solution)/shard_map/ppermute | solution.py:543
  58.0 11.9 %collective-permute-start.20 = (bf16[2,2,72,768]{3,2,1,0:T(8,128)(2,1)}, bf16[2,2,72,768]{3,2,1,0:T(8,128)(2,1)}, u32[]{:S(2)}, u32[]{:S(2)}) collective-permute-start(bf16[2,2,72,768]{3,2,1,0:T(8,128)(2,1)} %collective-permute-done.13.refs_10_), channel_id=1, source_target_pairs={{0,1},{1,0},{2,3},{3,2},{4,5},{5,4},{6,7},{7,6},{8,9},{9,8},{10,11... | collective-permute-start | bytes 1327112 | tf_op jit(solution)/shard_map/ppermute | solution.py:543
  80.2 12.0 %collective-permute-start.25 = (bf16[2,2,2,2,72,384]{5,4,3,2,1,0:T(8,128)(2,1)}, bf16[2,2,2,2,72,384]{5,4,3,2,1,0:T(8,128)(2,1)S(1)}, u32[]{:S(2)}, u32[]{:S(2)}) collective-permute-start(bf16[2,2,2,2,72,384]{5,4,3,2,1,0:T(8,128)(2,1)} %get-tuple-element.100), channel_id=1, source_target_pairs={{0,1},{1,0},{2,3},{3,2},{4,5},{5,4},{6,7},{7,6},{8,9},{9,8},{10,11... | collective-permute-start | bytes 2654216 | tf_op jit(solution)/shard_map/ppermute | solution.py:543
  95.5 17.4 %collective-permute-start.31 = (bf16[2,2,2,72,384]{4,3,2,1,0:T(8,128)(2,1)S(1)}, bf16[2,2,2,72,384]{4,3,2,1,0:T(8,128)(2,1)S(1)}, u32[]{:S(2)}, u32[]{:S(2)}) collective-permute-start(bf16[2,2,2,72,384]{4,3,2,1,0:T(8,128)(2,1)S(1)} %get-tuple-element.158), channel_id=1, source_target_pairs={{0,4},{1,5},{2,6},{3,7},{4,0},{5,1},{6,2},{7,3},{8,12},{9,13},{10,... | collective-permute-start | bytes 1327112 | tf_op jit(solution)/shard_map/ppermute | solution.py:543
  96.4 20.9 %collective-permute-start.32 = (bf16[2,2,2,72,384]{4,3,2,1,0:T(8,128)(2,1)S(1)}, bf16[2,2,2,72,384]{4,3,2,1,0:T(8,128)(2,1)S(1)}, u32[]{:S(2)}, u32[]{:S(2)}) collective-permute-start(bf16[2,2,2,72,384]{4,3,2,1,0:T(8,128)(2,1)S(1)} %get-tuple-element.160), channel_id=1, source_target_pairs={{0,4},{1,5},{2,6},{3,7},{4,0},{5,1},{6,2},{7,3},{8,12},{9,13},{10,... | collective-permute-start | bytes 1327112 | tf_op jit(solution)/shard_map/ppermute | solution.py:543
  98.8 18.8 %collective-permute-start.30 = (bf16[2,2,2,72,576]{4,3,2,1,0:T(8,128)(2,1)S(1)}, bf16[2,2,2,72,576]{4,3,2,1,0:T(8,128)(2,1)S(1)}, u32[]{:S(2)}, u32[]{:S(2)}) collective-permute-start(bf16[2,2,2,72,576]{4,3,2,1,0:T(8,128)(2,1)S(1)} %get-tuple-element.156), channel_id=1, source_target_pairs={{0,2},{1,3},{2,0},{3,1},{4,6},{5,7},{6,4},{7,5},{8,10},{9,11},{10,... | collective-permute-start | bytes 1990664 | tf_op jit(solution)/shard_map/ppermute | solution.py:543
  120.6 14.6 %collective-permute-start.34 = (bf16[2,2,72,768]{3,2,1,0:T(8,128)(2,1)S(1)}, bf16[2,2,72,768]{3,2,1,0:T(8,128)(2,1)S(1)}, u32[]{:S(2)}, u32[]{:S(2)}) collective-permute-start(bf16[2,2,72,768]{3,2,1,0:T(8,128)(2,1)S(1)} %pad_maximum_fusion.1), channel_id=1, source_target_pairs={{0,2},{1,3},{2,0},{3,1},{4,6},{5,7},{6,4},{7,5},{8,10},{9,11},{10,... | collective-permute-start | bytes 1327112 | tf_op jit(solution)/shard_map/ppermute | solution.py:543
  121.4 16.8 %collective-permute-start.36 = (bf16[2,2,2,80,256]{4,3,2,1,0:T(8,128)(2,1)S(1)}, bf16[2,2,2,80,256]{4,3,2,1,0:T(8,128)(2,1)S(1)}, u32[]{:S(2)}, u32[]{:S(2)}) collective-permute-start(bf16[2,2,2,80,256]{4,3,2,1,0:T(8,128)(2,1)S(1)} %get-tuple-element.164), channel_id=1, source_target_pairs={{0,4},{1,5},{2,6},{3,7},{4,0},{5,1},{6,2},{7,3},{8,12},{9,13},{10,... | collective-permute-start | bytes 983048 | tf_op jit(solution)/shard_map/ppermute | solution.py:543
  122.0 15.9 %collective-permute-start.37 = (bf16[2,2,72,576]{3,2,1,0:T(8,128)(2,1)S(1)}, bf16[2,2,72,576]{3,2,1,0:T(8,128)(2,1)S(1)}, u32[]{:S(2)}, u32[]{:S(2)}) collective-permute-start(bf16[2,2,72,576]{3,2,1,0:T(8,128)(2,1)S(1)} %get-tuple-element.162), channel_id=1, source_target_pairs={{0,4},{1,5},{2,6},{3,7},{4,0},{5,1},{6,2},{7,3},{8,12},{9,13},{10,... | collective-permute-start | bytes 995336 | tf_op jit(solution)/shard_map/ppermute | solution.py:543
  135.3 9.6 %collective-permute-start.35 = (bf16[2,72,768]{2,1,0:T(8,128)(2,1)S(1)}, bf16[2,72,768]{2,1,0:T(8,128)(2,1)S(1)}, u32[]{:S(2)}, u32[]{:S(2)}) collective-permute-start(bf16[2,72,768]{2,1,0:T(8,128)(2,1)S(1)} %get-tuple-element.165), channel_id=1, source_target_pairs={{0,8},{1,9},{2,10},{3,11},{4,12},{5,13},{6,14},{7,15},{8,0},{9,1},... | collective-permute-start | bytes 663560 | tf_op jit(solution)/shard_map/ppermute | solution.py:543
  138.0 10.7 %collective-permute-start.40 = (bf16[2,72,576]{2,1,0:T(8,128)(2,1)S(1)}, bf16[2,72,576]{2,1,0:T(8,128)(2,1)S(1)}, u32[]{:S(2)}, u32[]{:S(2)}) collective-permute-start(bf16[2,72,576]{2,1,0:T(8,128)(2,1)S(1)} %get-tuple-element.174), channel_id=1, source_target_pairs={{0,8},{1,9},{2,10},{3,11},{4,12},{5,13},{6,14},{7,15},{8,0},{9,1},... | collective-permute-start | bytes 497672 | tf_op jit(solution)/shard_map/ppermute | solution.py:543
  138.2 14.0 %collective-permute-start.39 = (bf16[2,2,80,256]{3,2,1,0:T(8,128)(2,1)S(1)}, bf16[2,2,80,256]{3,2,1,0:T(8,128)(2,1)S(1)}, u32[]{:S(2)}, u32[]{:S(2)}) collective-permute-start(bf16[2,2,80,256]{3,2,1,0:T(8,128)(2,1)S(1)} %get-tuple-element.176), channel_id=1, source_target_pairs={{0,8},{1,9},{2,10},{3,11},{4,12},{5,13},{6,14},{7,15},{8,0},{9,1},... | collective-permute-start | bytes 491528 | tf_op jit(solution)/shard_map/ppermute | solution.py:543
  145.0 10.5 %collective-permute-start.38 = (bf16[72,768]{1,0:T(8,128)(2,1)S(1)}, bf16[72,768]{1,0:T(8,128)(2,1)S(1)}, u32[]{:S(2)}, u32[]{:S(2)}) collective-permute-start(bf16[72,768]{1,0:T(8,128)(2,1)S(1)} %fusion.35), channel_id=1, source_target_pairs={{0,16},{1,17},{2,18},{3,19},{4,20},{5,21},{6,22},{7,23},{8,24},{9,... | collective-permute-start | bytes 331784 | tf_op jit(solution)/shard_map/ppermute | solution.py:543
  148.7 9.1 %collective-permute-start.44 = (bf16[72,576]{1,0:T(8,128)(2,1)S(1)}, bf16[72,576]{1,0:T(8,128)(2,1)S(1)}, u32[]{:S(2)}, u32[]{:S(2)}) collective-permute-start(bf16[72,576]{1,0:T(8,128)(2,1)S(1)} %fusion.36), channel_id=1, source_target_pairs={{0,16},{1,17},{2,18},{3,19},{4,20},{5,21},{6,22},{7,23},{8,24},{9,... | collective-permute-start | bytes 248840 | tf_op jit(solution)/shard_map/ppermute | solution.py:543
  (51 other events, 289.2 us)

commit v6 on v4

--- a/solution.py
+++ b/solution.py
@@ -45,7 +45,7 @@
     return [pl.BlockSpec(memory_space=pltpu.VMEM) for _ in shape_dtypes]
 
 
-def call(kernel, scalars, arrays, outs, flops, scratch=(), mib=52, fetched=()):
+def call(kernel, scalars, arrays, outs, flops, scratch=(), mib=52, fetched=(), landing=()):
     specs = [pl.BlockSpec(memory_space=pltpu.SMEM)] * len(scalars) + whole(*arrays)
     specs += [pl.BlockSpec(memory_space=pl.ANY)] * len(fetched)
     arrays = [*arrays, *fetched]
@@ -59,7 +59,7 @@
         out_specs=whole(*outs),
         scratch_shapes=[
             *[pltpu.VMEM(shape, F32) for shape in scratch],
-            *[pltpu.VMEM(v.shape, v.dtype) for v in fetched],
+            *[pltpu.VMEM(shape, BF) for shape in landing],
             *([pltpu.SemaphoreType.DMA((len(fetched),))] if fetched else []),
         ],
         compiler_params=pltpu.CompilerParams(vmem_limit_bytes=mib * 1024 * 1024),
@@ -107,7 +107,7 @@
 
 
 def attention_forward(order, length, seq_ref, blocks, wq, wkv, bq, bkv, gain, cos, sin, mask,
-                      att_o, q_o, k_o, v_o, lse_o):
+                      att_o, q_o, k_o, v_o):
     seq = seq_ref[0]
     cosine, sine = tables(seq, order, cos, sin)
     width = gain.shape[1]
@@ -133,7 +133,6 @@
             top = jnp.max(scores, axis=-1, keepdims=True)
             e = jnp.exp(scores - top)
             total = jnp.sum(e, axis=-1, keepdims=True)
-            lse_o[b, g] = jnp.log(total) + top
             probs = (e * (1.0 / total)).astype(BF)
             parts.append(dot(probs, vg, 1, 0))
         att_o[b * length : (b + 1) * length, :] = rows_to_heads(parts, length).astype(BF)
@@ -181,7 +180,7 @@
 
 
 def attention_backward(order, length, seq_ref, blocks, wq, wkv, gain, cos, sin, mask, q_i, k_i, v_i,
-                       lse, attg, dq_o, dkv_o, wgrad_o, bias_o, gain_o):
+                       attg, dq_o, dkv_o, wgrad_o, bias_o, gain_o):
     seq = seq_ref[0]
     cosine, sine = tables(seq, order, cos, sin)
     width = gain.shape[1]
@@ -197,7 +196,9 @@
         for g in range(KV_HEADS):
             qg, kg, vg = q_i[b, g], k_i[b, g], v_i[b, g]
             agg = heads_to_rows(ag, g)
-            p = jnp.exp(jnp.where(allowed, dot(qg, kg, 1, 1), MASKED) - lse[b, g])
+            scores = jnp.where(allowed, dot(qg, kg, 1, 1), MASKED)
+            e = jnp.exp(scores - jnp.max(scores, axis=-1, keepdims=True))
+            p = e * (1.0 / jnp.sum(e, axis=-1, keepdims=True))
             dvs.append(dot(p.astype(BF), agg, 0, 0))
             pg = dot(agg, vg, 1, 1)
             inner = jnp.sum(p * pg, axis=-1, keepdims=True)
@@ -268,7 +269,7 @@
 
 
 def first_forward(order, length, d_rows, n_bias, meta, b0, b1, b2, b3, a00, a10, a01, a11, cos, sin, mask,
-                  att_o, q_o, k_o, v_o, lse_o, w_o, gain_o, w_s, b_s):
+                  att_o, q_o, k_o, v_o, w_o, gain_o, w_s, b_s):
     blocks = Blocks(b0, b1, b2, b3)
     core, x = meta[0] & 1, meta[1] & 1
     cut = a00.shape[2]
@@ -287,7 +288,7 @@
         gain_o[i : i + 1, :] = jnp.concatenate([line[:, at : at + d_rows] for line in lines], axis=1)
     wide = QW + 64
     attention_forward(order, length, meta, blocks, w_o[:, :wide], w_o[:, QW:], b_s[:, :wide], b_s[:, QW:],
-                      gain_o[0:1, :], cos, sin, mask, att_o, q_o, k_o, v_o, lse_o)
+                      gain_o[0:1, :], cos, sin, mask, att_o, q_o, k_o, v_o)
 
 
 def turned(out, value):
@@ -301,39 +302,35 @@
     return r & 1, (r >> 1) & 1, (r >> 2) & 1
 
 
-def feed_forward_pieces(d_rows, ff_rows, meta, attended, source, gains, cot, weight, *refs):
-    out_o, gk_o, gg_o, dk_o, dg_o, mid_o, attg_o, gain_o, down_s, wout_s = refs[12:22]
-    copies = [pltpu.make_async_copy(refs[i], refs[22 + i], refs[34].at[i]) for i in range(12)]
+def fetch_pieces(meta, refs, b_s, g_s, sems):
+    core, y, x, z0 = meta[0] & 1, (meta[0] >> 1) & 1, meta[1] & 1, (meta[1] >> 1) & 1
+    copies = []
+    for i in range(8):
+        at = (z0 ^ (i >> 2), x ^ ((i >> 1) & 1), core ^ (i & 1))
+        copies.append(pltpu.make_async_copy(refs[i], b_s.at[at], sems.at[i]))
+    for i in range(8):
+        at = (y ^ ((i >> 1) & 1), core ^ (i & 1), x ^ (i >> 2))
+        copies.append(pltpu.make_async_copy(refs[8 + i], g_s.at[at], sems.at[8 + i]))
     for copy in copies:
         copy.start()
-    b00, b10, b01, b11, g001, g101, g011, g111, g000, g100, g010, g110 = refs[22:34]
-    core, y, x_own = meta[0] & 1, (meta[0] >> 1) & 1, meta[1] & 1
-    n_f = 8
-    hf = n_f // 2
+    return copies
+
+
+def feed_forward_pieces(d_rows, ff_rows, meta, attended, source, gains, cot, weight, *refs):
+    out_o, ak_o, ag_o, bk_o, bg_o, dk_o, dg_o, mid_o, attg_o, gain_o, down_s, wout_s, b_s, g_s, sems = refs[16:]
+    copies = fetch_pieces(meta, refs, b_s, g_s, sems)
+    core, y = meta[0] & 1, (meta[0] >> 1) & 1
     part_d = ff_rows // 4
     part_o = d_rows // 3
-    cut = b00.shape[2] - ff_rows // 2
-    for copy in copies[:4]:
+    cut = b_s.shape[4] - ff_rows // 2
+    half = g_s.shape[-1] // 2
+    for copy in copies[:8]:
         copy.wait()
-
-    def b_rows(z0, z1, x, c, rows):
-        low = chosen(x_own ^ x, b00[z0, z1, rows, :], b10[z0, z1, rows, :])
-        high = chosen(x_own ^ x, b01[z0, z1, rows, :], b11[z0, z1, rows, :])
-        return chosen(core ^ c, low, high)
-
-    def quarter(near, far):
-        parts = []
-        for f in range(n_f):
-            z1, z0, x = f >> 2, (f >> 1) & 1, f & 1
-            mine, other = near[z0, z1].astype(F32), far[z0, z1].astype(F32)
-            parts.append(chosen(x_own ^ x, mine, other))
-        return jnp.concatenate(parts, axis=0).astype(BF)
-
     wo = []
-    for f in range(n_f):
-        z1, z0, x = f >> 2, (f >> 1) & 1, f & 1
-        wo.append(b_rows(z0, z1, x, 0, slice(ff_rows // 2, None)).astype(F32))
-        wo.append(b_rows(z0, z1, x, 1, slice(ff_rows // 2, None)).astype(F32)[: d_rows - cut])
+    for f in range(8):
+        for c in range(2):
+            rows = b_s[(f >> 1) & 1, f & 1, c, f >> 2, ff_rows // 2 :, :].astype(F32)
+            wo.append(rows if c == 0 else rows[: d_rows - cut])
     wo = jnp.concatenate(wo, axis=0).astype(BF)
     att = attended[...]
     middle = source[...].astype(F32) + dot(att, wo, 1, 0)
@@ -342,19 +339,17 @@
     second = (normed * g2).astype(BF)
     out_grad = cot[...].astype(F32) * weight[...]
     feed_grad = out_grad.astype(BF)
+    for copy in copies[8:]:
+        copy.wait()
     feed = back = None
     for c_rel in (1, 0):
-        for copy in copies[8 - 4 * c_rel : 12 - 4 * c_rel]:
-            copy.wait()
-        first_q = quarter(g001, g101) if c_rel else quarter(g000, g100)
-        second_q = quarter(g011, g111) if c_rel else quarter(g010, g110)
-        wg = chosen(y, first_q, second_q)
-        wu = chosen(y, second_q, first_q)
         h = core ^ c_rel
-        wd = []
-        for i in range(hf):
-            for c in range(2):
-                wd.append(b_rows(i >> 1, h, i & 1, c, slice(0, ff_rows // 2)))
+        weights = []
+        for yy in range(2):
+            rows = [g_s[yy, h, f & 1, (f >> 1) & 1, f >> 2].astype(F32) for f in range(8)]
+            weights.append(jnp.concatenate(rows, axis=0).astype(BF))
+        wg, wu = weights
+        wd = [b_s[i >> 1, i & 1, c, h, : ff_rows // 2, :] for i in range(4) for c in range(2)]
         wd = jnp.concatenate(wd, axis=0)
         gate = dot(second, wg, 1, 0)
         up = dot(second, wu, 1, 0)
@@ -369,18 +364,20 @@
         ugrad = (pgrad * act).astype(BF)
         part = dot(ggrad, wg, 1, 1) + dot(ugrad, wu, 1, 1)
         back = part if back is None else back + part
-        for i in range(hf):
-            x, z0, z1 = rel(meta, hf * h + i)
+        for i in range(4):
+            x, z0, z1 = rel(meta, 4 * h + i)
             for yy in range(2):
                 for c_to, to in ((0, dk_o), (1, dg_o)):
                     at = pl.multiple_of(i * ff_rows + (yy * 2 + (core ^ c_to)) * part_d, 16)
                     to[y ^ yy, x, z0, z1, :part_d, :] = down_s[pl.ds(at, part_d), :].astype(BF)
-        to = gg_o if c_rel else gk_o
+        to_a, to_b = (ag_o, bg_o) if c_rel else (ak_o, bk_o)
         for yy, grad in ((0, ggrad), (1, ugrad)):
             wgrad = dot(second, grad, 0, 0)
-            for f in range(n_f):
+            for f in range(8):
                 x, z0, z1 = rel(meta, f)
-                to[x, z0, z1, yy] = wgrad[d_rows * f : d_rows * (f + 1), :].astype(BF)
+                block = wgrad[d_rows * f : d_rows * (f + 1), :].astype(BF)
+                to_a[x, z0, z1, yy] = block[:, :half]
+                to_b[z0, z1, x, yy] = block[:, half:]
     turned(out_o, middle + feed)
     gain_o[...] = jnp.sum(back * normed, axis=0, keepdims=True)
     middle_grad = out_grad + norm_back(back, g2, scale_two, normed)
@@ -388,10 +385,10 @@
     branch = middle_grad.astype(BF)
     attg_o[...] = dot(branch, wo, 1, 1).astype(BF)
     wout = dot(att, branch, 0, 0)
-    for f in range(n_f):
+    for f in range(8):
         wout_s[f, :d_rows, :] = wout[d_rows * f : d_rows * (f + 1), :]
         wout_s[f, d_rows:, :] = jnp.zeros((part_o, wout.shape[1]), F32)
-    for f in range(n_f):
+    for f in range(8):
         x, z0, z1 = rel(meta, f)
         for yy in range(2):
             for c_to, to in ((0, dk_o), (1, dg_o)):
@@ -400,7 +397,7 @@
 
 
 def attention_backward_pieces(order, length, d_rows, meta, b0, b1, b2, b3, w, gains, cos, sin, mask, q_i, k_i, v_i,
-                              lse, attg, gain_two, dq_o, dk_o, dg_o, rk_o, rg_o, w_s, bias_s, gain_s, small_s):
+                              attg, gain_two, dq_o, dk_o, dg_o, rk_o, rg_o, w_s, bias_s, gain_s, small_s):
     blocks = Blocks(b0, b1, b2, b3)
     half = len(order) // 2
 
@@ -417,7 +414,7 @@
 
     wide = QW + 64
     attention_backward(order, length, meta, blocks, w[:, :wide], w[:, QW:], gains[0:1, :], cos, sin, mask,
-                       q_i, k_i, v_i, lse, attg, dq_o, Pieces(), Wgrad(), bias_s, gain_s)
+                       q_i, k_i, v_i, attg, dq_o, Pieces(), Wgrad(), bias_s, gain_s)
     n_f = small_s.shape[0]
     qk, v = (QW + KW) // n_f, KW // n_f
     bias, g1, g2 = bias_s[...], gain_s[...], gain_two[...]
@@ -451,12 +448,12 @@
     turned(out_o, mid[...] + norm_back(first_grad, gains[0:1, :], scale_one, normed))
 
 
-def place_gate(meta, near, far, out_o):
+def place_gate(meta, near, far, out_o, parts=1, part=0):
     core = meta[0] & 1
     n = near.shape[2]
     for pieces, c_rel in ((near, 0), (far, 1)):
         for yy in range(2):
-            at = pl.multiple_of((yy * 2 + (core ^ c_rel)) * n, 128)
+            at = pl.multiple_of(((yy * 2 + (core ^ c_rel)) * parts + part) * n, 128)
             out_o[:, pl.ds(at, n)] = pieces[yy].astype(F32)
 
 
@@ -485,9 +482,10 @@
     gains_o[1:2, :] = line[:, 256 : 256 + d_rows]
 
 
-def place_all(part_d, qk, v, meta, near, far, d0, d1, d2, d3, r_near, r_far,
+def place_all(part_d, qk, v, meta, a_near, a_far, b_near, b_far, d0, d1, d2, d3, r_near, r_far,
               gate_o, down_o, wout_o, w_o, bqk_o, bv_o, gains_o, all_s):
-    place_gate(meta, near, far, gate_o)
+    place_gate(meta, a_near, a_far, gate_o, 2, 0)
+    place_gate(meta, b_near, b_far, gate_o, 2, 1)
     place_down(part_d, meta, d0, d1, d2, d3, down_o, wout_o)
     place_qkv(qk, v, meta, r_near, r_far, w_o, bqk_o, bv_o, gains_o, all_s)
 
@@ -617,7 +615,7 @@
     gain_one, gain_two = gain_one[None], gain_two[None]
     source = hidden.reshape(rows, width)
     n_all = n_seq * rows
-    attended, q_s, k_s, v_s, lse = call(
+    attended, q_s, k_s, v_s = call(
         functools.partial(attention_forward, order, length),
         [seq_scalar],
         [blocks, wq, wkv, bias[None, : QW + 64], bias[None, QW:], gain_one, cos_t, sin_t, allowed],
@@ -626,7 +624,6 @@
             sds((seqs, KV_HEADS, GROUP * length, HEAD_DIM), BF),
             sds((seqs, KV_HEADS, full_length, HEAD_DIM), BF),
             sds((seqs, KV_HEADS, full_length, HEAD_DIM), BF),
-            sds((seqs, KV_HEADS, GROUP * length, 1), F32),
         ],
         2 * n_all * width * 2 * KW + 2 * rows * width * QW + 4 * rows * full_length * QW,
     )
@@ -673,7 +670,7 @@
     dq, dkv, qkv_wgrad, bias_grad, gain_one_grad = call(
         functools.partial(attention_backward, order, length),
         [seq_scalar],
-        [blocks, wq, wkv, gain_one, cos_t, sin_t, allowed, q_s, k_s, v_s, lse, attended_grad],
+        [blocks, wq, wkv, gain_one, cos_t, sin_t, allowed, q_s, k_s, v_s, attended_grad],
         [
             sds((rows, QW + 64), BF),
             sds((n_seq, rows, 2 * KW), BF),
@@ -805,20 +802,18 @@
         axis=1,
     )
     a2 = net.both(a1, znear, 0)
-    b0 = net.half(after(half_b, a2), core, 0)
+    b0 = net.half(after(half_b, a1), core, 0)
     a_x = net.swap(a2, xbit)
     a_c = net.swap(a2, core)
     gu1 = net.both(gu0, zfar, 0)
     gu2 = net.both(after(gu1, a2), znear, 0)
     block_yc = net.swap(block_y, core)
     a_xc = net.swap(a_x, core)
-    gu2 = after(gu2, a_x)
     gu_x = net.swap(gu2, xbit)
     gu_y = net.swap(gu2, ybit)
     gu_c = net.swap(gu2, core)
-    b1 = net.both(b0, zfar, 0, after(net.swap(b0, zfar), gu2))
-    b_z = net.swap(b1, znear)
-    a_xc = after(a_xc, b1)
+    b1 = net.swap(after(b0, gu2), zfar)
+    a_xc = after(a_xc, gu2)
 
     cos_t, sin_t = rope_tables(full_length, n_seq)
     block_ids = [seq_index ^ o for o in order]
@@ -830,7 +825,7 @@
         own_places[None, :, None] >= key_places.reshape(1, 1, -1)
     )
     allowed = allowed.astype(F32)
-    attended, q_s, k_s, v_s, lse, wf, gains = call(
+    attended, q_s, k_s, v_s, wf, gains = call(
         functools.partial(first_forward, order, length, d_rows, n_bias),
         [meta],
         [*blocks, a2, a_x, a_c, a_xc, cos_t, sin_t, allowed],
@@ -839,37 +834,44 @@
             sds((seqs, KV_HEADS, GROUP * length, HEAD_DIM), BF),
             sds((seqs, KV_HEADS, full_length, HEAD_DIM), BF),
             sds((seqs, KV_HEADS, full_length, HEAD_DIM), BF),
-            sds((seqs, KV_HEADS, GROUP * length, 1), F32),
             sds((width, qkv_w), BF),
             sds((2, width), F32),
         ],
         1.2e10,
         [(n_fsdp * (d_rows + 8), qkv_w), (1, qkv_w)],
-        20,
-    )
-    gu_y = after(gu_y, attended)
-    gu_x, b_z = after(gu_x, gu_y), after(b_z, gu_y)
+    )
+    b1 = net.both(b0, zfar, 0, after(b1, attended))
+    b_z = net.swap(b1, znear)
+    b_x = net.swap(b1, xbit)
+    b_c = net.swap(b1, core)
+    gu_y = after(gu_y, b1)
+    gu_x = after(gu_x, b1)
     gu_xy = net.swap(gu_x, ybit)
-    b2 = net.both(b1, znear, 0, b_z)
-    b_x = net.swap(b2, xbit)
-    b_c = net.swap(b2, core)
+    b_zx = net.swap(b_z, xbit)
     gu_yc = net.swap(gu_y, core)
     gu_xc = net.swap(gu_x, core)
+    b_zc = net.swap(b_z, core)
     b_xc = net.swap(b_x, core)
+    b_zxc = net.swap(b_zx, core)
     gu_xyc = net.swap(gu_xy, core)
-    gate_up = [gu_c, gu_xc, gu_yc, gu_xyc, gu2, gu_x, gu_y, gu_xy]
+    pieces = [b1, b_c, b_x, b_xc, b_z, b_zc, b_zx, b_zxc]
+    pieces += [gu2, gu_c, gu_y, gu_yc, gu_x, gu_xc, gu_xy, gu_xyc]
 
     weight = tokens_micro / token_counts.astype(F32)
     weight = jnp.repeat(weight, batch * length)[:, None]
     lead = (2, 2, 2, 2)
-    block_out, gate_keep, gate_give, down_keep, down_give, middle_grad, attended_grad, gain_two = call(
+    cot = cotangent.reshape(rows, width)
+    gate_lead = lead + (d_rows, units // 4)
+    block_out, a_keep, a_give, b_keep, b_give, down_keep, down_give, middle_grad, attended_grad, gain_two = call(
         functools.partial(feed_forward_pieces, d_rows, ff_rows),
         [meta],
-        [attended, source, gains, cotangent.reshape(rows, width), weight],
+        [attended, source, gains, cot, weight],
         [
             sds((seqs, width, length), BF),
-            sds(lead + (d_rows, units // 2), BF),
-            sds(lead + (d_rows, units // 2), BF),
+            sds(gate_lead, BF),
+            sds(gate_lead, BF),
+            sds(gate_lead, BF),
+            sds(gate_lead, BF),
             sds(lead + (ff_rows // 4 + d_rows // 3, width), BF),
             sds(lead + (ff_rows // 4 + d_rows // 3, width), BF),
             sds((rows, width), F32),
@@ -878,7 +880,8 @@
         ],
         1.4e10,
         [(units // 2, width), (n_fsdp, d_rows + d_rows // 3, width)],
-        fetched=[b2, b_x, b_c, b_xc, *gate_up],
+        fetched=pieces,
+        landing=[(2, 2, 2, 2) + b1.shape[1:], (2, 2, 2, 2, 2, d_rows, units // 2)],
     )
     block_out = block_out.reshape(micro, batch, width, length).swapaxes(2, 3)
 
@@ -888,18 +891,21 @@
     def halves(keep, got):
         return add(keep[0], got[0]), add(keep[1], got[1])
 
-    gate_got = net.swap(gate_give, core)
-    down_got = net.swap(after(down_give, gate_got), core)
-    gate, gate_give = halves(gate_keep, gate_got)
-    gate_got = net.swap(gate_give, xbit)
+    a_got = net.swap(a_give, core)
+    b_got = net.swap(after(b_give, a_got), core)
+    down_got = net.swap(after(down_give, a_got), core)
+    a, a_give = halves(a_keep, a_got)
+    a_got = net.swap(a_give, xbit)
+    b, b_give = halves(b_keep, b_got)
+    b_got = net.swap(b_give, znear)
     down, down_give = halves(down_keep, down_got)
-    attended_grad = after(attended_grad, gate_give, down_give)
+    attended_grad = after(attended_grad, a_give, b_give, down_give)
     down_got = net.swap(down_give, ybit)
 
     dq, dkv_keep, dkv_give, rest_keep, rest_give = call(
         functools.partial(attention_backward_pieces, order, length, d_rows),
         [meta],
-        [*blocks, wf, gains, cos_t, sin_t, allowed, q_s, k_s, v_s, lse, attended_grad, gain_two],
+        [*blocks, wf, gains, cos_t, sin_t, allowed, q_s, k_s, v_s, attended_grad, gain_two],
         [
             sds((rows, QW + 64), BF),
             sds((2, rows, 2 * KW), BF),
@@ -910,38 +916,46 @@
         1.4e10,
         [(width, 1024), (1, qkv_w), (1, width), (n_fsdp, 8, 1024)],
     )
-    gate, gate_give = halves(gate, after(gate_got, dq, down_got))
-    gate_got = net.swap(gate_give, znear)
-    down, down_give = halves(down, after(down_got, gate_give))
+    b, b_give = halves(b, after(b_got, dq))
+    a, a_give = halves(a, after(a_got, b_give))
+    b_got = net.swap(b_give, zfar)
+    a_got = net.swap(a_give, znear)
+    down, down_give = halves(down, after(down_got, a_give))
     down_got = net.swap(down_give, xbit)
     rest, rest_give = halves(rest_keep, after(net.swap(rest_give, core), down_give))
     rest_got = net.swap(rest_give, xbit)
     dkv, dkv_give = halves(dkv_keep, after(net.swap(dkv_give, core), rest_give))
     dkv_got = net.swap(dkv_give, ybit)
+    a, a_give = halves(a, after(a_got, dkv_give))
+    a_got = net.swap(a_give, zfar)
+    b, b_give = halves(b, after(b_got, a_give))
+    b_got = net.swap(b_give, xbit)
     (hidden_grad,) = call(
         input_gradient_two,
         [],
-        [dq, dkv, dkv_got, source, middle_grad, wf, gains],
+        [dq, dkv, after(dkv_got, b_give), source, middle_grad, wf, gains],
         [sds((seqs, width, length), F32)],
         3e9,
         mib=16,
     )
-    gate, gate_give = halves(gate, after(gate_got, hidden_grad))
-    gate_got = net.swap(gate_give, zfar)
+    down, down_give = halves(down, after(down_got, hidden_grad))
     hidden_grad = hidden_grad.reshape(micro, batch, width, length).swapaxes(2, 3)
-    down, down_give = halves(down, after(down_got, gate_give))
     down_got = net.swap(down_give, znear)
     rest, rest_give = halves(rest, after(rest_got, down_give))
     rest_got = net.swap(rest_give, znear)
-    gate = add(gate, after(gate_got, rest_give))
-    gate_got = net.swap(gate, ybit)
-    down, down_give = halves(down, after(down_got, gate))
+    a = add(a, after(a_got, rest_give))
+    a_got = net.swap(a, ybit)
+    b = add(b, after(b_got, a))
+    b_got = net.swap(b, ybit)
+    down, down_give = halves(down, after(down_got, b))
     down_got = net.swap(down_give, zfar)
     rest, rest_give = halves(rest, after(rest_got, down_give))
     rest_got = net.swap(rest_give, zfar)
-    gate = add(gate, after(gate_got, rest_give))
-    gate_far = net.swap(gate, core)
-    down = add(down, after(down_got, gate))
+    a = add(a, after(a_got, rest_give))
+    a_far = net.swap(a, core)
+    b = add(b, b_got)
+    b_far = net.swap(b, core)
+    down = add(down, after(down_got, a))
     down_y = net.swap(down, ybit)
     down_c = net.swap(down, core)
     rest = add(rest, after(rest_got, down))
@@ -953,7 +967,7 @@
     out_gate, out_down, out_wout, out_qkv, b_qk, b_v, out_gains = call(
         functools.partial(place_all, ff_rows // 4, qk, v),
         [meta],
-        [gate, gate_far, down, down_y, down_c, down_yc, rest, rest_far],
+        [a, a_far, b, b_far, down, down_y, down_c, down_yc, rest, rest_far],
         [
             sds((d_rows, 2 * units), F32),
             sds((ff_rows, width), F32),

time: 161 us -> 152 us (0.944)
  waiting for transfers between devices: 70.1 us -> 52.4 us
  starting transfers between devices: 36.1 us -> 43.9 us
  Pallas kernels: 39.2 us -> 42.6 us
  local copies, waits for them, and re-layouts: 8.17 us -> 5.48 us
    ppermute x44 -> x53, waiting for transfers between devices: 70.1 us -> 52.4 us  [swap(): return lax.ppermute(value, ('fsdp', 'seq'), pairs)]
    ppermute x44 -> x53, starting transfers between devices: 36.1 us -> 43.9 us  [swap(): return lax.ppermute(value, ('fsdp', 'seq'), pairs)]
    pallas_call x5, Pallas kernels: 38.3 us -> 41.7 us  [call(): pl.pallas_call(kernel, out_shape=outs, in_specs=specs, out_specs=whole(*o...]
    unnamed x50 -> x58, local copies, waits for them, and re-layouts: 7.11 us -> 4.43 us
    convert_element_type x16 -> x21, other arithmetic: 3.49 us -> 3.16 us  [add(): return (keep.astype(F32) + got.astype(F32)).astype(BF)]
  transfers between devices with their start and end apart: 44 -> 53, of which waited for: 22 -> 21; matrix products, arithmetic and copies ran while one was open for 5% -> 5% of each run, Pallas kernels for 14% -> 17%
where the time goes in v6:
time: 152 us; the launch traced here: 151 us
  waiting for transfers between devices  52.4 us (34%)
  starting transfers between devices  43.9 us (29%)
  Pallas kernels  42.6 us (28%)
  other arithmetic  5.65 us (4%)
  local copies, waits for them, and re-layouts  5.48 us (4%)
    ppermute x53, waiting for transfers between devices, swap(): return lax.ppermute(value, ('fsdp', 'seq'), pairs)  52.4 us
    ppermute x53, starting transfers between devices, swap(): return lax.ppermute(value, ('fsdp', 'seq'), pairs)  43.9 us
    pallas_call x5, Pallas kernels, call(): pl.pallas_call(kernel, out_shape=outs, in_specs=specs, out_specs=whole(*o...  41.7 us
    unnamed x58, local copies, waits for them, and re-layouts  4.43 us
    convert_element_type x21, other arithmetic, add(): return (keep.astype(F32) + got.astype(F32)).astype(BF)  3.16 us
  transfers between devices with their start and end apart: 53, of which 21 were waited for; matrix products, arithmetic and copies ran while one was open for 5% of the time, Pallas kernels for 17%

profile of v6, /device:TPU:0, one launch (start us, length us, event | category | flops | bytes accessed | tf_op | source)
XLA Modules:
  0.0 151.3 jit_solution(9965138787309267464)
XLA Ops:
  3.8 4.1 %collective-permute-start.3 = (bf16[40,960]{1,0:T(8,128)(2,1)S(1)}, bf16[40,960]{1,0:T(8,128)(2,1)S(1)}, u32[]{:S(2)}, u32[]{:S(2)}) collective-permute-start(bf16[40,960]{1,0:T(8,128)(2,1)S(1)} %shard_map.187), channel_id=1, source_target_pairs={{0,16},{1,17},{2,18},{3,19},{4,20},{5,21},{6,22},{7,23},{8,24},{9,... | collective-permute-start | bytes 230408 | tf_op jit(solution)/shard_map/ppermute | solution.py:504
  10.0 1.6 %collective-permute-start = (bf16[256,640]{1,0:T(8,128)(2,1)S(1)}, bf16[256,640]{1,0:T(8,128)(2,1)S(1)}, u32[]{:S(2)}, u32[]{:S(2)}) collective-permute-start(bf16[256,640]{1,0:T(8,128)(2,1)S(1)} %pad_maximum_fusion.3.b0), channel_id=1, source_target_pairs={{0,2},{1,3},{2,0},{3,1},{4,6},{5,7},{6,4},{7,5},{8,10},{9,11},{10,... | collective-permute-start | bytes 983048 | tf_op jit(solution)/shard_map/ppermute | solution.py:504
  12.6 1.6 %collective-permute-start.4 = (bf16[2,40,960]{2,1,0:T(8,128)(2,1)S(1)}, bf16[2,40,960]{2,1,0:T(8,128)(2,1)S(1)}, u32[]{:S(2)}, u32[]{:S(2)}) collective-permute-start(bf16[2,40,960]{2,1,0:T(8,128)(2,1)S(1)} %pad_maximum_fusion.6), channel_id=1, source_target_pairs={{0,8},{1,9},{2,10},{3,11},{4,12},{5,13},{6,14},{7,15},{8,0},{9,1},... | collective-permute-start | bytes 460808 | tf_op jit(solution)/shard_map/ppermute | solution.py:504
  14.3 6.0 %collective-permute-done.8 = bf16[72,768]{1,0:T(8,128)(2,1)S(1)} collective-permute-done((bf16[72,768]{1,0:T(8,128)(2,1)S(1)}, bf16[72,768]{1,0:T(8,128)(2,1)S(1)}, u32[]{:S(2)}, u32[]{:S(2)}) %collective-permute-start.8) | collective-permute-done | bytes 110624 | tf_op jit(solution)/shard_map/ppermute | solution.py:504
  21.3 1.6 %collective-permute-start.5 = (bf16[2,2,40,960]{3,2,1,0:T(8,128)(2,1)S(1)}, bf16[2,2,40,960]{3,2,1,0:T(8,128)(2,1)S(1)}, u32[]{:S(2)}, u32[]{:S(2)}) collective-permute-start(bf16[2,2,40,960]{3,2,1,0:T(8,128)(2,1)S(1)} %pad_maximum_fusion.4.a00), channel_id=1, source_target_pairs={{0,4},{1,5},{2,6},{3,7},{4,0},{5,1},{6,2},{7,3},{8,12},{9,13},{10,... | collective-permute-start | bytes 921608 | tf_op jit(solution)/shard_map/ppermute | solution.py:504
  23.4 7.0 %collective-permute-done.9 = bf16[2,72,768]{2,1,0:T(8,128)(2,1)S(1)} collective-permute-done((bf16[2,72,768]{2,1,0:T(8,128)(2,1)S(1)}, bf16[2,72,768]{2,1,0:T(8,128)(2,1)S(1)}, u32[]{:S(2)}, u32[]{:S(2)}) %collective-permute-start.9) | collective-permute-done | bytes 221216 | tf_op jit(solution)/shard_map/ppermute | solution.py:504
  33.8 2.6 %collective-permute-start.10 = (bf16[136,576]{1,0:T(8,128)(2,1)S(1)}, bf16[136,576]{1,0:T(8,128)(2,1)S(1)}, u32[]{:S(2)}, u32[]{:S(2)}) collective-permute-start(bf16[136,576]{1,0:T(8,128)(2,1)S(1)} %dynamic-slice_bitcast_fusion), channel_id=1, source_target_pairs={{0,16},{1,17},{2,18},{3,19},{4,20},{5,21},{6,22},{7,23},{8,24},{9,... | collective-permute-start | bytes 470024 | tf_op jit(solution)/shard_map/ppermute | solution.py:504
  37.2 10.7 %shard_map.188 = (bf16[256,576]{1,0:T(8,128)(2,1)S(1)}, bf16[2,3,384,64]{3,2,1,0:T(8,128)(2,1)}, bf16[2,3,512,64]{3,2,1,0:T(8,128)(2,1)}, bf16[2,3,512,64]{3,2,1...) custom-call(s32[2]{0:T(128)S(1)} %pad_add_fusion.meta, bf16[256,640]{1,0:T(8,128)(2,1)S(1)} %pad_maximum_fusion.3.b0, ...), custom_call_target="tpu_custom_call" | custom-call | flops 12000000000 | bytes 6074880 | tf_op jit(solution)/shard_map/pallas_call | solution.py:55
  48.0 1.8 %collective-permute-start.14 = (bf16[2,136,576]{2,1,0:T(8,128)(2,1)S(1)}, bf16[2,136,576]{2,1,0:T(8,128)(2,1)}, u32[]{:S(2)}, u32[]{:S(2)}) collective-permute-start(bf16[2,136,576]{2,1,0:T(8,128)(2,1)S(1)} %pad_maximum_fusion.2.refs_0_), channel_id=1, source_target_pairs={{0,8},{1,9},{2,10},{3,11},{4,12},{5,13},{6,14},{7,15},{8,0},{9,1},... | collective-permute-start | bytes 940040 | tf_op jit(solution)/shard_map/ppermute | solution.py:504
  51.0 1.5 collective-permute-start.12
  53.0 5.1 %collective-permute-done.14.refs_4_ = bf16[2,136,576]{2,1,0:T(8,128)(2,1)} collective-permute-done((bf16[2,136,576]{2,1,0:T(8,128)(2,1)S(1)}, bf16[2,136,576]{2,1,0:T(8,128)(2,1)}, u32[]{:S(2)}, u32[]{:S(2)}) %collective-permute-start.14) | collective-permute-done | bytes 313376 | tf_op jit(solution)/shard_map/ppermute | solution.py:504
  58.1 1.4 collective-permute-start.16
  59.5 1.3 collective-permute-done.12.refs_2_
  62.4 5.5 %collective-permute-done.16.refs_6_ = bf16[2,136,576]{2,1,0:T(8,128)(2,1)} collective-permute-done((bf16[2,136,576]{2,1,0:T(8,128)(2,1)}, bf16[2,136,576]{2,1,0:T(8,128)(2,1)}, u32[]{:S(2)}, u32[]{:S(2)}) %collective-permute-start.16) | collective-permute-done | bytes 313376 | tf_op jit(solution)/shard_map/ppermute | solution.py:504
  68.5 1.5 collective-permute-done.17.refs_7_
  69.9 13.4 %shard_map.189 = (bf16[2,576,128]{2,1,0:T(8,128)(2,1)}, bf16[2,2,2,2,72,384]{5,4,3,2,1,0:T(8,128)(2,1)}, bf16[2,2,2,2,72,384]{5,4,3,2,1,0:T(8,128)(2,1)}, bf16[2...) custom-call(s32[2]{0:T(128)S(1)} %pad_add_fusion.meta, ...), custom_call_target="tpu_custom_call" | custom-call | flops 14000000000 | bytes 14311168 | tf_op jit(solution)/shard_map/pallas_call | solution.py:55
  83.6 2.5 %collective-permute-done.25 = bf16[2,2,2,2,72,384]{5,4,3,2,1,0:T(8,128)(2,1)S(1)} collective-permute-done((bf16[2,2,2,2,72,384]{5,4,3,2,1,0:T(8,128)(2,1)}, bf16[2,2,2,2,72,384]{5,4,3,2,1,0:T(8,128)(2,1)S(1)}, u32[]{:S(2)}, u32[]{:S(2)}) %collective-permute-start.25) | collective-permute-done | bytes 884768 | tf_op jit(solution)/shard_map/ppermute | solution.py:504
  86.6 1.4 add_convert_fusion.3
  88.0 1.6 %collective-permute-start.31 = (bf16[2,2,2,72,384]{4,3,2,1,0:T(8,128)(2,1)S(1)}, bf16[2,2,2,72,384]{4,3,2,1,0:T(8,128)(2,1)S(1)}, u32[]{:S(2)}, u32[]{:S(2)}) collective-permute-start(bf16[2,2,2,72,384]{4,3,2,1,0:T(8,128)(2,1)S(1)} %get-tuple-element.146), channel_id=1, source_target_pairs={{0,4},{1,5},{2,6},{3,7},{4,0},{5,1},{6,2},{7,3},{8,12},{9,13},{10,... | collective-permute-start | bytes 1327112 | tf_op jit(solution)/shard_map/ppermute | solution.py:504
  94.1 13.7 %shard_map.190 = (bf16[256,640]{1,0:T(8,128)(2,1)S(1)}, bf16[2,256,384]{2,1,0:T(8,128)(2,1)}, bf16[2,256,384]{2,1,0:T(8,128)(2,1)}, bf16[2,2,2,2,80,256]{5,4,3,2...) custom-call(s32[2]{0:T(128)S(1)} %pad_add_fusion.meta, bf16[256,640]{1,0:T(8,128)(2,1)S(1)} %pad_maximum_fusion.3.b0, ...), custom_call_target="tpu_custom_call" | custom-call | flops 14000000000 | bytes 7273216 | tf_op jit(solution)/shard_map/pallas_call | solution.py:55
  108.0 1.4 collective-permute-start.34
  111.3 1.5 collective-permute-start.38
  115.0 6.7 %collective-permute-done.35 = bf16[2,2,72,384]{3,2,1,0:T(8,128)(2,1)S(1)} collective-permute-done((bf16[2,2,72,384]{3,2,1,0:T(8,128)(2,1)S(1)}, bf16[2,2,72,384]{3,2,1,0:T(8,128)(2,1)S(1)}, u32[]{:S(2)}, u32[]{:S(2)}) %collective-permute-start.35) | collective-permute-done | bytes 221216 | tf_op jit(solution)/shard_map/ppermute | solution.py:504
  122.1 1.5 collective-permute-start.42
  123.6 1.9 %shard_map.191 = f32[2,576,128]{2,1,0:T(8,128)} custom-call(bf16[256,640]{1,0:T(8,128)(2,1)S(1)} %get-tuple-element.93.dq, bf16[256,384]{1,0:T(8,128)(2,1)S(1)} %get-tuple-element.156.own, bf16[256,384]{1,0:T(8,128)(2,1)S(1)} %collective-permute-done.33.other, bf16[256,576]{1,0:T(8,128)(2,1)S(1)} %bitcast.199, f32[256,576]{1,0:T(8,128)S(1)} %copy-done.6, ...), custom_call_target="tpu_custom_call" | custom-call | flops 3000000000 | bytes 3305984 | tf_op jit(solution)/shard_map/pallas_call | solution.py:55
  125.8 3.5 %collective-permute-done.37 = bf16[2,2,2,80,256]{4,3,2,1,0:T(8,128)(2,1)S(1)} collective-permute-done((bf16[2,2,2,80,256]{4,3,2,1,0:T(8,128)(2,1)S(1)}, bf16[2,2,2,80,256]{4,3,2,1,0:T(8,128)(2,1)S(1)}, u32[]{:S(2)}, u32[]{:S(2)}) %collective-permute-start.37) | collective-permute-done | bytes 327712 | tf_op jit(solution)/shard_map/ppermute | solution.py:504
  129.4 1.4 collective-permute-start.40
  133.3 2.6 %collective-permute-start.46 = (bf16[72,576]{1,0:T(8,128)(2,1)S(1)}, bf16[72,576]{1,0:T(8,128)(2,1)S(1)}, u32[]{:S(2)}, u32[]{:S(2)}) collective-permute-start(bf16[72,576]{1,0:T(8,128)(2,1)S(1)} %fusion.37), channel_id=1, source_target_pairs={{0,16},{1,17},{2,18},{3,19},{4,20},{5,21},{6,22},{7,23},{8,24},{9,... | collective-permute-start | bytes 248840 | tf_op jit(solution)/shard_map/ppermute | solution.py:504
  136.8 2.4 %collective-permute-start.50 = (bf16[2,80,256]{2,1,0:T(8,128)(2,1)S(1)}, bf16[2,80,256]{2,1,0:T(8,128)(2,1)S(1)}, u32[]{:S(2)}, u32[]{:S(2)}) collective-permute-start(bf16[2,80,256]{2,1,0:T(8,128)(2,1)S(1)} %fusion.39), channel_id=1, source_target_pairs={{0,16},{1,17},{2,18},{3,19},{4,20},{5,21},{6,22},{7,23},{8,24},{9,... | collective-permute-start | bytes 245768 | tf_op jit(solution)/shard_map/ppermute | solution.py:504
  139.2 2.9 %collective-permute-done.46 = bf16[72,576]{1,0:T(8,128)(2,1)S(1)} collective-permute-done((bf16[72,576]{1,0:T(8,128)(2,1)S(1)}, bf16[72,576]{1,0:T(8,128)(2,1)S(1)}, u32[]{:S(2)}, u32[]{:S(2)}) %collective-permute-start.46) | collective-permute-done | bytes 82976 | tf_op jit(solution)/shard_map/ppermute | solution.py:504
  145.0 2.1 %collective-permute-done.47.d1 = bf16[72,576]{1,0:T(8,128)(2,1)S(1)} collective-permute-done((bf16[72,576]{1,0:T(8,128)(2,1)S(1)}, bf16[72,576]{1,0:T(8,128)(2,1)S(1)}, u32[]{:S(2)}, u32[]{:S(2)}) %collective-permute-start.47) | collective-permute-done | bytes 82976 | tf_op jit(solution)/shard_map/ppermute | solution.py:504
  149.4 1.9 %shard_map.192 = (f32[72,3072]{1,0:T(8,128)}, f32[192,576]{1,0:T(8,128)}, f32[72,576]{1,0:T(8,128)}, f32[72,960]{1,0:T(8,128)}, f32[1,96]{1,0:T(1,128)}, /*index=5*/f32[1,24]{1,0:T(1,128)}, f32[2,72]{1,0:T(2,128)}) custom-call(s32[2]{0:T(128)S(1)} %pad_add_fusion.meta, bf16[2,72,384]{2,1,0:T(8,128)(2,1)S(1)} %add_convert_fusion.11.a_near, ...), custom_call_target="tpu_custom_call" | custom-call | flops 3000000000 | bytes 2708512 | tf_op jit(solution)/shard_map/pallas_call | solution.py:55
  (190 shorter events, 34.4 us)
Async XLA Ops:
  3.8 8.8 %collective-permute-start.3 = (bf16[40,960]{1,0:T(8,128)(2,1)S(1)}, bf16[40,960]{1,0:T(8,128)(2,1)S(1)}, u32[]{:S(2)}, u32[]{:S(2)}) collective-permute-start(bf16[40,960]{1,0:T(8,128)(2,1)S(1)} %shard_map.187), channel_id=1, source_target_pairs={{0,16},{1,17},{2,18},{3,19},{4,20},{5,21},{6,22},{7,23},{8,24},{9,... | collective-permute-start | bytes 230408 | tf_op jit(solution)/shard_map/ppermute | solution.py:504
  10.0 13.2 %collective-permute-start.1 = (bf16[256,640]{1,0:T(8,128)(2,1)S(1)}, bf16[256,640]{1,0:T(8,128)(2,1)S(1)}, u32[]{:S(2)}, u32[]{:S(2)}) collective-permute-start(bf16[256,640]{1,0:T(8,128)(2,1)S(1)} %pad_maximum_fusion.3.b0), channel_id=1, source_target_pairs={{0,1},{1,0},{2,3},{3,2},{4,5},{5,4},{6,7},{7,6},{8,9},{9,8},{10,11... | collective-permute-start | bytes 983048 | tf_op jit(solution)/shard_map/ppermute | solution.py:504
  10.0 12.8 %collective-permute-start = (bf16[256,640]{1,0:T(8,128)(2,1)S(1)}, bf16[256,640]{1,0:T(8,128)(2,1)S(1)}, u32[]{:S(2)}, u32[]{:S(2)}) collective-permute-start(bf16[256,640]{1,0:T(8,128)(2,1)S(1)} %pad_maximum_fusion.3.b0), channel_id=1, source_target_pairs={{0,2},{1,3},{2,0},{3,1},{4,6},{5,7},{6,4},{7,5},{8,10},{9,11},{10,... | collective-permute-start | bytes 983048 | tf_op jit(solution)/shard_map/ppermute | solution.py:504
  11.6 8.6 %collective-permute-start.8 = (bf16[72,768]{1,0:T(8,128)(2,1)S(1)}, bf16[72,768]{1,0:T(8,128)(2,1)S(1)}, u32[]{:S(2)}, u32[]{:S(2)}) collective-permute-start(bf16[72,768]{1,0:T(8,128)(2,1)S(1)} %constant_dynamic-slice_fusion), channel_id=1, source_target_pairs={{0,16},{1,17},{2,18},{3,19},{4,20},{5,21},{6,22},{7,23},{8,24},{9,... | collective-permute-start | bytes 331784 | tf_op jit(solution)/shard_map/ppermute | solution.py:504
  12.6 8.4 %collective-permute-start.4 = (bf16[2,40,960]{2,1,0:T(8,128)(2,1)S(1)}, bf16[2,40,960]{2,1,0:T(8,128)(2,1)S(1)}, u32[]{:S(2)}, u32[]{:S(2)}) collective-permute-start(bf16[2,40,960]{2,1,0:T(8,128)(2,1)S(1)} %pad_maximum_fusion.6), channel_id=1, source_target_pairs={{0,8},{1,9},{2,10},{3,11},{4,12},{5,13},{6,14},{7,15},{8,0},{9,1},... | collective-permute-start | bytes 460808 | tf_op jit(solution)/shard_map/ppermute | solution.py:504
  21.2 15.2 %collective-permute-start.6 = (bf16[2,2,40,960]{3,2,1,0:T(8,128)(2,1)S(1)}, bf16[2,2,40,960]{3,2,1,0:T(8,128)(2,1)S(1)}, u32[]{:S(2)}, u32[]{:S(2)}) collective-permute-start(bf16[2,2,40,960]{3,2,1,0:T(8,128)(2,1)S(1)} %pad_maximum_fusion.4.a00), channel_id=1, source_target_pairs={{0,1},{1,0},{2,3},{3,2},{4,5},{5,4},{6,7},{7,6},{8,9},{9,8},{10,11... | collective-permute-start | bytes 921608 | tf_op jit(solution)/shard_map/ppermute | solution.py:504
  21.3 10.3 %collective-permute-start.5 = (bf16[2,2,40,960]{3,2,1,0:T(8,128)(2,1)S(1)}, bf16[2,2,40,960]{3,2,1,0:T(8,128)(2,1)S(1)}, u32[]{:S(2)}, u32[]{:S(2)}) collective-permute-start(bf16[2,2,40,960]{3,2,1,0:T(8,128)(2,1)S(1)} %pad_maximum_fusion.4.a00), channel_id=1, source_target_pairs={{0,4},{1,5},{2,6},{3,7},{4,0},{5,1},{6,2},{7,3},{8,12},{9,13},{10,... | collective-permute-start | bytes 921608 | tf_op jit(solution)/shard_map/ppermute | solution.py:504
  22.8 8.7 %collective-permute-start.2 = (bf16[256,640]{1,0:T(8,128)(2,1)S(1)}, bf16[256,640]{1,0:T(8,128)(2,1)S(1)}, u32[]{:S(2)}, u32[]{:S(2)}) collective-permute-start(bf16[256,640]{1,0:T(8,128)(2,1)S(1)} %collective-permute-done.b1), channel_id=1, source_target_pairs={{0,1},{1,0},{2,3},{3,2},{4,5},{5,4},{6,7},{7,6},{8,9},{9,8},{10,11... | collective-permute-start | bytes 983048 | tf_op jit(solution)/shard_map/ppermute | solution.py:504
  30.4 19.4 %collective-permute-start.21 = (bf16[2,2,72,768]{3,2,1,0:T(8,128)(2,1)S(1)}, bf16[2,2,72,768]{3,2,1,0:T(8,128)(2,1)}, u32[]{:S(2)}, u32[]{:S(2)}) collective-permute-start(bf16[2,2,72,768]{3,2,1,0:T(8,128)(2,1)S(1)} %pad_maximum_fusion.refs_8_), channel_id=1, source_target_pairs={{0,4},{1,5},{2,6},{3,7},{4,0},{5,1},{6,2},{7,3},{8,12},{9,13},{10,... | collective-permute-start | bytes 1327112 | tf_op jit(solution)/shard_map/ppermute | solution.py:504
  31.0 21.5 %collective-permute-start.19 = (bf16[2,2,72,768]{3,2,1,0:T(8,128)(2,1)S(1)}, bf16[2,2,72,768]{3,2,1,0:T(8,128)(2,1)S(1)}, u32[]{:S(2)}, u32[]{:S(2)}) collective-permute-start(bf16[2,2,72,768]{3,2,1,0:T(8,128)(2,1)S(1)} %pad_maximum_fusion.refs_8_), channel_id=1, source_target_pairs={{0,2},{1,3},{2,0},{3,1},{4,6},{5,7},{6,4},{7,5},{8,10},{9,11},{10,... | collective-permute-start | bytes 1327112 | tf_op jit(solution)/shard_map/ppermute | solution.py:504
  31.5 21.0 %collective-permute-start.18 = (bf16[2,2,72,768]{3,2,1,0:T(8,128)(2,1)S(1)}, bf16[2,2,72,768]{3,2,1,0:T(8,128)(2,1)S(1)}, u32[]{:S(2)}, u32[]{:S(2)}) collective-permute-start(bf16[2,2,72,768]{3,2,1,0:T(8,128)(2,1)S(1)} %pad_maximum_fusion.refs_8_), channel_id=1, source_target_pairs={{0,1},{1,0},{2,3},{3,2},{4,5},{5,4},{6,7},{7,6},{8,9},{9,8},{10,11... | collective-permute-start | bytes 1327112 | tf_op jit(solution)/shard_map/ppermute | solution.py:504
  33.8 14.1 %collective-permute-start.10 = (bf16[136,576]{1,0:T(8,128)(2,1)S(1)}, bf16[136,576]{1,0:T(8,128)(2,1)S(1)}, u32[]{:S(2)}, u32[]{:S(2)}) collective-permute-start(bf16[136,576]{1,0:T(8,128)(2,1)S(1)} %dynamic-slice_bitcast_fusion), channel_id=1, source_target_pairs={{0,16},{1,17},{2,18},{3,19},{4,20},{5,21},{6,22},{7,23},{8,24},{9,... | collective-permute-start | bytes 470024 | tf_op jit(solution)/shard_map/ppermute | solution.py:504
  48.0 10.1 %collective-permute-start.14 = (bf16[2,136,576]{2,1,0:T(8,128)(2,1)S(1)}, bf16[2,136,576]{2,1,0:T(8,128)(2,1)}, u32[]{:S(2)}, u32[]{:S(2)}) collective-permute-start(bf16[2,136,576]{2,1,0:T(8,128)(2,1)S(1)} %pad_maximum_fusion.2.refs_0_), channel_id=1, source_target_pairs={{0,8},{1,9},{2,10},{3,11},{4,12},{5,13},{6,14},{7,15},{8,0},{9,1},... | collective-permute-start | bytes 940040 | tf_op jit(solution)/shard_map/ppermute | solution.py:504
  49.8 12.0 %collective-permute-start.23 = (bf16[2,2,72,768]{3,2,1,0:T(8,128)(2,1)}, bf16[2,2,72,768]{3,2,1,0:T(8,128)(2,1)}, u32[]{:S(2)}, u32[]{:S(2)}) collective-permute-start(bf16[2,2,72,768]{3,2,1,0:T(8,128)(2,1)} %collective-permute-done.21.refs_12_), channel_id=1, source_target_pairs={{0,2},{1,3},{2,0},{3,1},{4,6},{5,7},{6,4},{7,5},{8,10},{9,11},{10,... | collective-permute-start | bytes 1327112 | tf_op jit(solution)/shard_map/ppermute | solution.py:504
  51.0 9.8 %collective-permute-start.12 = (bf16[2,136,576]{2,1,0:T(8,128)(2,1)S(1)}, bf16[2,136,576]{2,1,0:T(8,128)(2,1)}, u32[]{:S(2)}, u32[]{:S(2)}) collective-permute-start(bf16[2,136,576]{2,1,0:T(8,128)(2,1)S(1)} %pad_maximum_fusion.2.refs_0_), channel_id=1, source_target_pairs={{0,4},{1,5},{2,6},{3,7},{4,0},{5,1},{6,2},{7,3},{8,12},{9,13},{10,... | collective-permute-start | bytes 940040 | tf_op jit(solution)/shard_map/ppermute | solution.py:504
  52.5 9.8 %collective-permute-start.20 = (bf16[2,2,72,768]{3,2,1,0:T(8,128)(2,1)S(1)}, bf16[2,2,72,768]{3,2,1,0:T(8,128)(2,1)S(1)}, u32[]{:S(2)}, u32[]{:S(2)}) collective-permute-start(bf16[2,2,72,768]{3,2,1,0:T(8,128)(2,1)S(1)} %collective-permute-done.19.refs_10_), channel_id=1, source_target_pairs={{0,1},{1,0},{2,3},{3,2},{4,5},{5,4},{6,7},{7,6},{8,9},{9,8},{10,11... | collective-permute-start | bytes 1327112 | tf_op jit(solution)/shard_map/ppermute | solution.py:504
  52.6 9.3 %collective-permute-start.11 = (bf16[2,136,576]{2,1,0:T(8,128)(2,1)S(1)}, bf16[2,136,576]{2,1,0:T(8,128)(2,1)S(1)}, u32[]{:S(2)}, u32[]{:S(2)}) collective-permute-start(bf16[2,136,576]{2,1,0:T(8,128)(2,1)S(1)} %pad_maximum_fusion.2.refs_0_), channel_id=1, source_target_pairs={{0,1},{1,0},{2,3},{3,2},{4,5},{5,4},{6,7},{7,6},{8,9},{9,8},{10,11... | collective-permute-start | bytes 940040 | tf_op jit(solution)/shard_map/ppermute | solution.py:504
  58.1 9.8 %collective-permute-start.16 = (bf16[2,136,576]{2,1,0:T(8,128)(2,1)}, bf16[2,136,576]{2,1,0:T(8,128)(2,1)}, u32[]{:S(2)}, u32[]{:S(2)}) collective-permute-start(bf16[2,136,576]{2,1,0:T(8,128)(2,1)} %collective-permute-done.14.refs_4_), channel_id=1, source_target_pairs={{0,4},{1,5},{2,6},{3,7},{4,0},{5,1},{6,2},{7,3},{8,12},{9,13},{10,... | collective-permute-start | bytes 940040 | tf_op jit(solution)/shard_map/ppermute | solution.py:504
  88.0 21.3 %collective-permute-start.31 = (bf16[2,2,2,72,384]{4,3,2,1,0:T(8,128)(2,1)S(1)}, bf16[2,2,2,72,384]{4,3,2,1,0:T(8,128)(2,1)S(1)}, u32[]{:S(2)}, u32[]{:S(2)}) collective-permute-start(bf16[2,2,2,72,384]{4,3,2,1,0:T(8,128)(2,1)S(1)} %get-tuple-element.146), channel_id=1, source_target_pairs={{0,4},{1,5},{2,6},{3,7},{4,0},{5,1},{6,2},{7,3},{8,12},{9,13},{10,... | collective-permute-start | bytes 1327112 | tf_op jit(solution)/shard_map/ppermute | solution.py:504
  91.1 16.7 %collective-permute-start.32 = (bf16[2,2,2,72,384]{4,3,2,1,0:T(8,128)(2,1)S(1)}, bf16[2,2,2,72,384]{4,3,2,1,0:T(8,128)(2,1)S(1)}, u32[]{:S(2)}, u32[]{:S(2)}) collective-permute-start(bf16[2,2,2,72,384]{4,3,2,1,0:T(8,128)(2,1)S(1)} %get-tuple-element.144), channel_id=1, source_target_pairs={{0,8},{1,9},{2,10},{3,11},{4,12},{5,13},{6,14},{7,15},{8,0},{9,1},... | collective-permute-start | bytes 1327112 | tf_op jit(solution)/shard_map/ppermute | solution.py:504
  92.8 18.3 %collective-permute-start.30 = (bf16[2,2,2,72,576]{4,3,2,1,0:T(8,128)(2,1)S(1)}, bf16[2,2,2,72,576]{4,3,2,1,0:T(8,128)(2,1)S(1)}, u32[]{:S(2)}, u32[]{:S(2)}) collective-permute-start(bf16[2,2,2,72,576]{4,3,2,1,0:T(8,128)(2,1)S(1)} %get-tuple-element.142), channel_id=1, source_target_pairs={{0,2},{1,3},{2,0},{3,1},{4,6},{5,7},{6,4},{7,5},{8,10},{9,11},{10,... | collective-permute-start | bytes 1990664 | tf_op jit(solution)/shard_map/ppermute | solution.py:504
  108.0 14.1 %collective-permute-start.34 = (bf16[2,2,72,384]{3,2,1,0:T(8,128)(2,1)S(1)}, bf16[2,2,72,384]{3,2,1,0:T(8,128)(2,1)S(1)}, u32[]{:S(2)}, u32[]{:S(2)}) collective-permute-start(bf16[2,2,72,384]{3,2,1,0:T(8,128)(2,1)S(1)} %get-tuple-element.154), channel_id=1, source_target_pairs={{0,16},{1,17},{2,18},{3,19},{4,20},{5,21},{6,22},{7,23},{8,24},{9,... | collective-permute-start | bytes 663560 | tf_op jit(solution)/shard_map/ppermute | solution.py:504
  109.4 12.3 %collective-permute-start.35 = (bf16[2,2,72,384]{3,2,1,0:T(8,128)(2,1)S(1)}, bf16[2,2,72,384]{3,2,1,0:T(8,128)(2,1)S(1)}, u32[]{:S(2)}, u32[]{:S(2)}) collective-permute-start(bf16[2,2,72,384]{3,2,1,0:T(8,128)(2,1)S(1)} %get-tuple-element.152), channel_id=1, source_target_pairs={{0,8},{1,9},{2,10},{3,11},{4,12},{5,13},{6,14},{7,15},{8,0},{9,1},... | collective-permute-start | bytes 663560 | tf_op jit(solution)/shard_map/ppermute | solution.py:504
  111.3 14.2 %collective-permute-start.38 = (bf16[2,2,72,576]{3,2,1,0:T(8,128)(2,1)S(1)}, bf16[2,2,72,576]{3,2,1,0:T(8,128)(2,1)S(1)}, u32[]{:S(2)}, u32[]{:S(2)}) collective-permute-start(bf16[2,2,72,576]{3,2,1,0:T(8,128)(2,1)S(1)} %get-tuple-element.148), channel_id=1, source_target_pairs={{0,4},{1,5},{2,6},{3,7},{4,0},{5,1},{6,2},{7,3},{8,12},{9,13},{10,... | collective-permute-start | bytes 995336 | tf_op jit(solution)/shard_map/ppermute | solution.py:504
  113.0 16.3 %collective-permute-start.37 = (bf16[2,2,2,80,256]{4,3,2,1,0:T(8,128)(2,1)S(1)}, bf16[2,2,2,80,256]{4,3,2,1,0:T(8,128)(2,1)S(1)}, u32[]{:S(2)}, u32[]{:S(2)}) collective-permute-start(bf16[2,2,2,80,256]{4,3,2,1,0:T(8,128)(2,1)S(1)} %get-tuple-element.150), channel_id=1, source_target_pairs={{0,4},{1,5},{2,6},{3,7},{4,0},{5,1},{6,2},{7,3},{8,12},{9,13},{10,... | collective-permute-start | bytes 983048 | tf_op jit(solution)/shard_map/ppermute | solution.py:504
  113.8 9.8 %collective-permute-start.33 = (bf16[256,384]{1,0:T(8,128)(2,1)S(1)}, bf16[256,384]{1,0:T(8,128)(2,1)S(1)}, u32[]{:S(2)}, u32[]{:S(2)}) collective-permute-start(bf16[256,384]{1,0:T(8,128)(2,1)S(1)} %get-tuple-element.155), channel_id=1, source_target_pairs={{0,2},{1,3},{2,0},{3,1},{4,6},{5,7},{6,4},{7,5},{8,10},{9,11},{10,... | collective-permute-start | bytes 589832 | tf_op jit(solution)/shard_map/ppermute | solution.py:504
  121.8 9.0 %collective-permute-start.36 = (bf16[2,72,384]{2,1,0:T(8,128)(2,1)S(1)}, bf16[2,72,384]{2,1,0:T(8,128)(2,1)S(1)}, u32[]{:S(2)}, u32[]{:S(2)}) collective-permute-start(bf16[2,72,384]{2,1,0:T(8,128)(2,1)S(1)} %fusion.34), channel_id=1, source_target_pairs={{0,16},{1,17},{2,18},{3,19},{4,20},{5,21},{6,22},{7,23},{8,24},{9,... | collective-permute-start | bytes 331784 | tf_op jit(solution)/shard_map/ppermute | solution.py:504
  122.1 9.6 %collective-permute-start.42 = (bf16[2,72,384]{2,1,0:T(8,128)(2,1)S(1)}, bf16[2,72,384]{2,1,0:T(8,128)(2,1)S(1)}, u32[]{:S(2)}, u32[]{:S(2)}) collective-permute-start(bf16[2,72,384]{2,1,0:T(8,128)(2,1)S(1)} %fusion.33), channel_id=1, source_target_pairs={{0,4},{1,5},{2,6},{3,7},{4,0},{5,1},{6,2},{7,3},{8,12},{9,13},{10,... | collective-permute-start | bytes 331784 | tf_op jit(solution)/shard_map/ppermute | solution.py:504
  125.7 7.6 %collective-permute-start.41 = (bf16[2,72,576]{2,1,0:T(8,128)(2,1)S(1)}, bf16[2,72,576]{2,1,0:T(8,128)(2,1)S(1)}, u32[]{:S(2)}, u32[]{:S(2)}) collective-permute-start(bf16[2,72,576]{2,1,0:T(8,128)(2,1)S(1)} %get-tuple-element.158), channel_id=1, source_target_pairs={{0,8},{1,9},{2,10},{3,11},{4,12},{5,13},{6,14},{7,15},{8,0},{9,1},... | collective-permute-start | bytes 497672 | tf_op jit(solution)/shard_map/ppermute | solution.py:504
  130.8 8.4 %collective-permute-start.39 = (bf16[2,72,384]{2,1,0:T(8,128)(2,1)S(1)}, bf16[2,72,384]{2,1,0:T(8,128)(2,1)S(1)}, u32[]{:S(2)}, u32[]{:S(2)}) collective-permute-start(bf16[2,72,384]{2,1,0:T(8,128)(2,1)S(1)} %fusion.19), channel_id=1, source_target_pairs={{0,2},{1,3},{2,0},{3,1},{4,6},{5,7},{6,4},{7,5},{8,10},{9,11},{10,... | collective-permute-start | bytes 331784 | tf_op jit(solution)/shard_map/ppermute | solution.py:504
  131.8 12.6 %collective-permute-start.44 = (bf16[2,72,384]{2,1,0:T(8,128)(2,1)S(1)}, bf16[2,72,384]{2,1,0:T(8,128)(2,1)S(1)}, u32[]{:S(2)}, u32[]{:S(2)}) collective-permute-start(bf16[2,72,384]{2,1,0:T(8,128)(2,1)S(1)} %fusion.17), channel_id=1, source_target_pairs={{0,2},{1,3},{2,0},{3,1},{4,6},{5,7},{6,4},{7,5},{8,10},{9,11},{10,... | collective-permute-start | bytes 331784 | tf_op jit(solution)/shard_map/ppermute | solution.py:504
  133.3 8.8 %collective-permute-start.46 = (bf16[72,576]{1,0:T(8,128)(2,1)S(1)}, bf16[72,576]{1,0:T(8,128)(2,1)S(1)}, u32[]{:S(2)}, u32[]{:S(2)}) collective-permute-start(bf16[72,576]{1,0:T(8,128)(2,1)S(1)} %fusion.37), channel_id=1, source_target_pairs={{0,16},{1,17},{2,18},{3,19},{4,20},{5,21},{6,22},{7,23},{8,24},{9,... | collective-permute-start | bytes 248840 | tf_op jit(solution)/shard_map/ppermute | solution.py:504
  (49 other events, 353.5 us)

commit v7 on v6

--- a/solution.py
+++ b/solution.py
@@ -47,7 +47,7 @@
 
 def call(kernel, scalars, arrays, outs, flops, scratch=(), mib=52, fetched=(), landing=()):
     specs = [pl.BlockSpec(memory_space=pltpu.SMEM)] * len(scalars) + whole(*arrays)
-    specs += [pl.BlockSpec(memory_space=pl.ANY)] * len(fetched)
+    specs += [pl.BlockSpec(memory_space=pltpu.HBM)] * len(fetched)
     arrays = [*arrays, *fetched]
     moved = sum(a.size * a.dtype.itemsize for a in arrays) + sum(
         int(np.prod(o.shape)) * o.dtype.itemsize for o in outs
@@ -775,7 +775,7 @@
     a0 = pl.pallas_call(
         functools.partial(cut_qkv, core),
         out_shape=sds(((d_rows + 8) // 2, qkv_w), BF),
-        in_specs=[pl.BlockSpec(memory_space=pltpu.SMEM)] + [pl.BlockSpec(memory_space=pl.ANY)] * 3,
+        in_specs=[pl.BlockSpec(memory_space=pltpu.SMEM)] + [pl.BlockSpec(memory_space=pltpu.HBM)] * 3,
         out_specs=pl.BlockSpec(memory_space=pltpu.VMEM),
         scratch_shapes=[
             *[pltpu.VMEM(v.shape, BF) for v in small],
@@ -802,7 +802,7 @@
         axis=1,
     )
     a2 = net.both(a1, znear, 0)
-    b0 = net.half(after(half_b, a1), core, 0)
+    b0 = net.half(after(half_b, a2), core, 0)
     a_x = net.swap(a2, xbit)
     a_c = net.swap(a2, core)
     gu1 = net.both(gu0, zfar, 0)
@@ -812,8 +812,11 @@
     gu_x = net.swap(gu2, xbit)
     gu_y = net.swap(gu2, ybit)
     gu_c = net.swap(gu2, core)
-    b1 = net.swap(after(b0, gu2), zfar)
-    a_xc = after(a_xc, gu2)
+    b1 = net.both(b0, zfar, 0, after(net.swap(b0, zfar), gu2))
+    b_z = net.swap(b1, znear)
+    b_x = net.swap(b1, xbit)
+    b_c = net.swap(b1, core)
+    a_xc = after(a_xc, b1)
 
     cos_t, sin_t = rope_tables(full_length, n_seq)
     block_ids = [seq_index ^ o for o in order]
@@ -840,12 +843,8 @@
         1.2e10,
         [(n_fsdp * (d_rows + 8), qkv_w), (1, qkv_w)],
     )
-    b1 = net.both(b0, zfar, 0, after(b1, attended))
-    b_z = net.swap(b1, znear)
-    b_x = net.swap(b1, xbit)
-    b_c = net.swap(b1, core)
-    gu_y = after(gu_y, b1)
-    gu_x = after(gu_x, b1)
+    gu_y = after(gu_y, attended)
+    gu_x, b_z, b_x = after(gu_x, gu_y), after(b_z, gu_y), after(b_x, gu_y)
     gu_xy = net.swap(gu_x, ybit)
     b_zx = net.swap(b_z, xbit)
     gu_yc = net.swap(gu_y, core)
@@ -920,46 +919,47 @@
     a, a_give = halves(a, after(a_got, b_give))
     b_got = net.swap(b_give, zfar)
     a_got = net.swap(a_give, znear)
-    down, down_give = halves(down, after(down_got, a_give))
+    rest, rest_give = halves(rest_keep, after(net.swap(rest_give, core), b_give, down_got))
+    rest_got = net.swap(rest_give, xbit)
+    down, down_give = halves(down, after(down_got, rest_give))
     down_got = net.swap(down_give, xbit)
-    rest, rest_give = halves(rest_keep, after(net.swap(rest_give, core), down_give))
-    rest_got = net.swap(rest_give, xbit)
-    dkv, dkv_give = halves(dkv_keep, after(net.swap(dkv_give, core), rest_give))
+    dkv, dkv_give = halves(dkv_keep, after(net.swap(dkv_give, core), down_give))
     dkv_got = net.swap(dkv_give, ybit)
     a, a_give = halves(a, after(a_got, dkv_give))
     a_got = net.swap(a_give, zfar)
     b, b_give = halves(b, after(b_got, a_give))
     b_got = net.swap(b_give, xbit)
+    rest, rest_give = halves(rest, after(rest_got, b_give))
+    rest_got = net.swap(rest_give, znear)
+    down, down_give = halves(down, after(down_got, rest_give))
+    down_got = net.swap(down_give, znear)
     (hidden_grad,) = call(
         input_gradient_two,
         [],
-        [dq, dkv, after(dkv_got, b_give), source, middle_grad, wf, gains],
+        [dq, dkv, after(dkv_got, down_give), source, middle_grad, wf, gains],
         [sds((seqs, width, length), F32)],
         3e9,
         mib=16,
     )
-    down, down_give = halves(down, after(down_got, hidden_grad))
+    a_got = after(a_got, hidden_grad)
     hidden_grad = hidden_grad.reshape(micro, batch, width, length).swapaxes(2, 3)
-    down_got = net.swap(down_give, znear)
-    rest, rest_give = halves(rest, after(rest_got, down_give))
-    rest_got = net.swap(rest_give, znear)
-    a = add(a, after(a_got, rest_give))
+    a = add(a, a_got)
     a_got = net.swap(a, ybit)
     b = add(b, after(b_got, a))
     b_got = net.swap(b, ybit)
-    down, down_give = halves(down, after(down_got, b))
+    rest, rest_give = halves(rest, after(rest_got, b))
+    rest_got = net.swap(rest_give, zfar)
+    down, down_give = halves(down, after(down_got, rest_give))
     down_got = net.swap(down_give, zfar)
-    rest, rest_give = halves(rest, after(rest_got, down_give))
-    rest_got = net.swap(rest_give, zfar)
-    a = add(a, after(a_got, rest_give))
+    a = add(a, after(a_got, down_give))
     a_far = net.swap(a, core)
     b = add(b, b_got)
     b_far = net.swap(b, core)
-    down = add(down, after(down_got, a))
+    rest = add(rest, after(rest_got, a))
+    rest_got = net.swap(rest, ybit)
+    down = add(down, after(down_got, rest))
     down_y = net.swap(down, ybit)
     down_c = net.swap(down, core)
-    rest = add(rest, after(rest_got, down))
-    rest_got = net.swap(rest, ybit)
     down_yc = net.swap(down_y, core)
     rest = add(rest, rest_got)
     rest_far = net.swap(rest, core)

time: 152 us -> 151 us (level)
  starting transfers between devices: 43.9 us -> 45.6 us
    ppermute x53, starting transfers between devices: 43.9 us -> 45.6 us  [swap(): return lax.ppermute(value, ('fsdp', 'seq'), pairs)]
  transfers between devices with their start and end apart: 53 -> 53, of which waited for: 21 -> 20; matrix products, arithmetic and copies ran while one was open for 5% -> 5% of each run, Pallas kernels for 17% -> 17%
where the time goes in v7:
time: 151 us
  waiting for transfers between devices  51.1 us (34%)
  starting transfers between devices  45.6 us (30%)
  Pallas kernels  42.6 us (28%)
  other arithmetic  5.75 us (4%)
  local copies, waits for them, and re-layouts  4.74 us (3%)
    ppermute x53, waiting for transfers between devices, swap(): return lax.ppermute(value, ('fsdp', 'seq'), pairs)  51.1 us
    ppermute x53, starting transfers between devices, swap(): return lax.ppermute(value, ('fsdp', 'seq'), pairs)  45.6 us
    pallas_call x5, Pallas kernels, call(): pl.pallas_call(kernel, out_shape=outs, in_specs=specs, out_specs=whole(*o...  41.8 us
    unnamed x58, local copies, waits for them, and re-layouts  3.7 us
    convert_element_type x21, other arithmetic, add(): return (keep.astype(F32) + got.astype(F32)).astype(BF)  3.25 us
  transfers between devices with their start and end apart: 53, of which 20 were waited for; matrix products, arithmetic and copies ran while one was open for 5% of the time, Pallas kernels for 17%

profile of v7, /device:TPU:0, one launch (start us, length us, event | category | flops | bytes accessed | tf_op | source)
XLA Modules:
  0.0 150.9 jit_solution(3228926139068408436)
XLA Ops:
  3.8 4.1 %collective-permute-start.3 = (bf16[40,960]{1,0:T(8,128)(2,1)S(1)}, bf16[40,960]{1,0:T(8,128)(2,1)S(1)}, u32[]{:S(2)}, u32[]{:S(2)}) collective-permute-start(bf16[40,960]{1,0:T(8,128)(2,1)S(1)} %shard_map.187), channel_id=1, source_target_pairs={{0,16},{1,17},{2,18},{3,19},{4,20},{5,21},{6,22},{7,23},{8,24},{9,... | collective-permute-start | bytes 230408 | tf_op jit(solution)/shard_map/ppermute | solution.py:504
  10.0 1.6 %collective-permute-start = (bf16[256,640]{1,0:T(8,128)(2,1)S(1)}, bf16[256,640]{1,0:T(8,128)(2,1)S(1)}, u32[]{:S(2)}, u32[]{:S(2)}) collective-permute-start(bf16[256,640]{1,0:T(8,128)(2,1)S(1)} %pad_maximum_fusion.3.b0), channel_id=1, source_target_pairs={{0,2},{1,3},{2,0},{3,1},{4,6},{5,7},{6,4},{7,5},{8,10},{9,11},{10,... | collective-permute-start | bytes 983048 | tf_op jit(solution)/shard_map/ppermute | solution.py:504
  12.6 1.6 %collective-permute-start.4 = (bf16[2,40,960]{2,1,0:T(8,128)(2,1)S(1)}, bf16[2,40,960]{2,1,0:T(8,128)(2,1)S(1)}, u32[]{:S(2)}, u32[]{:S(2)}) collective-permute-start(bf16[2,40,960]{2,1,0:T(8,128)(2,1)S(1)} %pad_maximum_fusion.6), channel_id=1, source_target_pairs={{0,8},{1,9},{2,10},{3,11},{4,12},{5,13},{6,14},{7,15},{8,0},{9,1},... | collective-permute-start | bytes 460808 | tf_op jit(solution)/shard_map/ppermute | solution.py:504
  14.3 6.0 %collective-permute-done.9 = bf16[72,768]{1,0:T(8,128)(2,1)S(1)} collective-permute-done((bf16[72,768]{1,0:T(8,128)(2,1)S(1)}, bf16[72,768]{1,0:T(8,128)(2,1)S(1)}, u32[]{:S(2)}, u32[]{:S(2)}) %collective-permute-start.9) | collective-permute-done | bytes 110624 | tf_op jit(solution)/shard_map/ppermute | solution.py:504
  21.2 1.6 %collective-permute-start.5 = (bf16[2,2,40,960]{3,2,1,0:T(8,128)(2,1)S(1)}, bf16[2,2,40,960]{3,2,1,0:T(8,128)(2,1)S(1)}, u32[]{:S(2)}, u32[]{:S(2)}) collective-permute-start(bf16[2,2,40,960]{3,2,1,0:T(8,128)(2,1)S(1)} %pad_maximum_fusion.4.a00), channel_id=1, source_target_pairs={{0,4},{1,5},{2,6},{3,7},{4,0},{5,1},{6,2},{7,3},{8,12},{9,13},{10,... | collective-permute-start | bytes 921608 | tf_op jit(solution)/shard_map/ppermute | solution.py:504
  22.8 4.1 %collective-permute-start.8 = (bf16[136,576]{1,0:T(8,128)(2,1)S(1)}, bf16[136,576]{1,0:T(8,128)(2,1)S(1)}, u32[]{:S(2)}, u32[]{:S(2)}) collective-permute-start(bf16[136,576]{1,0:T(8,128)(2,1)S(1)} %dynamic-slice_bitcast_fusion), channel_id=1, source_target_pairs={{0,16},{1,17},{2,18},{3,19},{4,20},{5,21},{6,22},{7,23},{8,24},{9,... | collective-permute-start | bytes 470024 | tf_op jit(solution)/shard_map/ppermute | solution.py:504
  27.4 6.7 %collective-permute-done.10 = bf16[2,72,768]{2,1,0:T(8,128)(2,1)S(1)} collective-permute-done((bf16[2,72,768]{2,1,0:T(8,128)(2,1)S(1)}, bf16[2,72,768]{2,1,0:T(8,128)(2,1)S(1)}, u32[]{:S(2)}, u32[]{:S(2)}) %collective-permute-start.10) | collective-permute-done | bytes 221216 | tf_op jit(solution)/shard_map/ppermute | solution.py:504
  34.3 2.2 %collective-permute-start.15 = (bf16[2,136,576]{2,1,0:T(8,128)(2,1)S(1)}, bf16[2,136,576]{2,1,0:T(8,128)(2,1)}, u32[]{:S(2)}, u32[]{:S(2)}) collective-permute-start(bf16[2,136,576]{2,1,0:T(8,128)(2,1)S(1)} %pad_maximum_fusion.2.refs_0_), channel_id=1, source_target_pairs={{0,8},{1,9},{2,10},{3,11},{4,12},{5,13},{6,14},{7,15},{8,0},{9,1},... | collective-permute-start | bytes 940040 | tf_op jit(solution)/shard_map/ppermute | solution.py:504
  37.0 1.5 collective-permute-start.21
  41.1 10.7 %shard_map.188 = (bf16[256,576]{1,0:T(8,128)(2,1)S(1)}, bf16[2,3,384,64]{3,2,1,0:T(8,128)(2,1)}, bf16[2,3,512,64]{3,2,1,0:T(8,128)(2,1)}, bf16[2,3,512,64]{3,2,1...) custom-call(s32[2]{0:T(128)S(1)} %pad_add_fusion.meta, bf16[256,640]{1,0:T(8,128)(2,1)S(1)} %pad_maximum_fusion.3.b0, ...), custom_call_target="tpu_custom_call" | custom-call | flops 12000000000 | bytes 6074880 | tf_op jit(solution)/shard_map/pallas_call | solution.py:55
  52.8 2.6 %collective-permute-done.21.refs_12_ = bf16[2,2,72,768]{3,2,1,0:T(8,128)(2,1)} collective-permute-done((bf16[2,2,72,768]{3,2,1,0:T(8,128)(2,1)S(1)}, bf16[2,2,72,768]{3,2,1,0:T(8,128)(2,1)}, u32[]{:S(2)}, u32[]{:S(2)}) %collective-permute-start.21) | collective-permute-done | bytes 442400 | tf_op jit(solution)/shard_map/ppermute | solution.py:504
  58.4 7.9 %collective-permute-done.23.refs_14_ = bf16[2,2,72,768]{3,2,1,0:T(8,128)(2,1)} collective-permute-done((bf16[2,2,72,768]{3,2,1,0:T(8,128)(2,1)}, bf16[2,2,72,768]{3,2,1,0:T(8,128)(2,1)}, u32[]{:S(2)}, u32[]{:S(2)}) %collective-permute-start.23) | collective-permute-done | bytes 442400 | tf_op jit(solution)/shard_map/ppermute | solution.py:504
  67.7 1.3 collective-permute-done.16.refs_5_
  69.5 13.5 %shard_map.189 = (bf16[2,576,128]{2,1,0:T(8,128)(2,1)}, bf16[2,2,2,2,72,384]{5,4,3,2,1,0:T(8,128)(2,1)}, bf16[2,2,2,2,72,384]{5,4,3,2,1,0:T(8,128)(2,1)}, bf16[2...) custom-call(s32[2]{0:T(128)S(1)} %pad_add_fusion.meta, ...), custom_call_target="tpu_custom_call" | custom-call | flops 14000000000 | bytes 14311168 | tf_op jit(solution)/shard_map/pallas_call | solution.py:55
  83.2 2.5 %collective-permute-done.25 = bf16[2,2,2,2,72,384]{5,4,3,2,1,0:T(8,128)(2,1)S(1)} collective-permute-done((bf16[2,2,2,2,72,384]{5,4,3,2,1,0:T(8,128)(2,1)}, bf16[2,2,2,2,72,384]{5,4,3,2,1,0:T(8,128)(2,1)S(1)}, u32[]{:S(2)}, u32[]{:S(2)}) %collective-permute-start.25) | collective-permute-done | bytes 884768 | tf_op jit(solution)/shard_map/ppermute | solution.py:504
  86.2 1.4 add_convert_fusion.2
  88.1 2.3 %collective-permute-done.26 = bf16[2,2,2,2,72,384]{5,4,3,2,1,0:T(8,128)(2,1)S(1)} collective-permute-done((bf16[2,2,2,2,72,384]{5,4,3,2,1,0:T(8,128)(2,1)}, bf16[2,2,2,2,72,384]{5,4,3,2,1,0:T(8,128)(2,1)S(1)}, u32[]{:S(2)}, u32[]{:S(2)}) %collective-permute-start.26) | collective-permute-done | bytes 884768 | tf_op jit(solution)/shard_map/ppermute | solution.py:504
  92.6 13.7 %shard_map.190 = (bf16[256,640]{1,0:T(8,128)(2,1)S(1)}, bf16[2,256,384]{2,1,0:T(8,128)(2,1)}, bf16[2,256,384]{2,1,0:T(8,128)(2,1)}, bf16[2,2,2,2,80,256]{5,4,3,2...) custom-call(s32[2]{0:T(128)S(1)} %pad_add_fusion.meta, bf16[256,640]{1,0:T(8,128)(2,1)S(1)} %pad_maximum_fusion.3.b0, ...), custom_call_target="tpu_custom_call" | custom-call | flops 14000000000 | bytes 7273216 | tf_op jit(solution)/shard_map/pallas_call | solution.py:55
  106.5 1.5 collective-permute-start.35
  108.1 1.7 %collective-permute-start.37 = (bf16[2,2,72,384]{3,2,1,0:T(8,128)(2,1)S(1)}, bf16[2,2,72,384]{3,2,1,0:T(8,128)(2,1)S(1)}, u32[]{:S(2)}, u32[]{:S(2)}) collective-permute-start(bf16[2,2,72,384]{3,2,1,0:T(8,128)(2,1)S(1)} %get-tuple-element.153), channel_id=1, source_target_pairs={{0,8},{1,9},{2,10},{3,11},{4,12},{5,13},{6,14},{7,15},{8,0},{9,1},... | collective-permute-start | bytes 663560 | tf_op jit(solution)/shard_map/ppermute | solution.py:504
  111.1 1.6 %collective-permute-start.33 = (bf16[2,2,72,576]{3,2,1,0:T(8,128)(2,1)S(1)}, bf16[2,2,72,576]{3,2,1,0:T(8,128)(2,1)S(1)}, u32[]{:S(2)}, u32[]{:S(2)}) collective-permute-start(bf16[2,2,72,576]{3,2,1,0:T(8,128)(2,1)S(1)} %get-tuple-element.150), channel_id=1, source_target_pairs={{0,4},{1,5},{2,6},{3,7},{4,0},{5,1},{6,2},{7,3},{8,12},{9,13},{10,... | collective-permute-start | bytes 995336 | tf_op jit(solution)/shard_map/ppermute | solution.py:504
  113.6 4.5 %collective-permute-done.37 = bf16[2,2,72,384]{3,2,1,0:T(8,128)(2,1)S(1)} collective-permute-done((bf16[2,2,72,384]{3,2,1,0:T(8,128)(2,1)S(1)}, bf16[2,2,72,384]{3,2,1,0:T(8,128)(2,1)S(1)}, u32[]{:S(2)}, u32[]{:S(2)}) %collective-permute-start.37) | collective-permute-done | bytes 221216 | tf_op jit(solution)/shard_map/ppermute | solution.py:504
  118.2 3.7 %collective-permute-start.38 = (bf16[2,72,384]{2,1,0:T(8,128)(2,1)S(1)}, bf16[2,72,384]{2,1,0:T(8,128)(2,1)S(1)}, u32[]{:S(2)}, u32[]{:S(2)}) collective-permute-start(bf16[2,72,384]{2,1,0:T(8,128)(2,1)S(1)} %fusion.34), channel_id=1, source_target_pairs={{0,16},{1,17},{2,18},{3,19},{4,20},{5,21},{6,22},{7,23},{8,24},{9,... | collective-permute-start | bytes 331784 | tf_op jit(solution)/shard_map/ppermute | solution.py:504
  122.6 1.9 %collective-permute-start.41 = (bf16[2,2,80,256]{3,2,1,0:T(8,128)(2,1)S(1)}, bf16[2,2,80,256]{3,2,1,0:T(8,128)(2,1)S(1)}, u32[]{:S(2)}, u32[]{:S(2)}) collective-permute-start(bf16[2,2,80,256]{3,2,1,0:T(8,128)(2,1)S(1)} %get-tuple-element.162), channel_id=1, source_target_pairs={{0,8},{1,9},{2,10},{3,11},{4,12},{5,13},{6,14},{7,15},{8,0},{9,1},... | collective-permute-start | bytes 491528 | tf_op jit(solution)/shard_map/ppermute | solution.py:504
  124.5 4.4 %collective-permute-done.33 = bf16[2,2,72,576]{3,2,1,0:T(8,128)(2,1)S(1)} collective-permute-done((bf16[2,2,72,576]{3,2,1,0:T(8,128)(2,1)S(1)}, bf16[2,2,72,576]{3,2,1,0:T(8,128)(2,1)S(1)}, u32[]{:S(2)}, u32[]{:S(2)}) %collective-permute-start.33) | collective-permute-done | bytes 331808 | tf_op jit(solution)/shard_map/ppermute | solution.py:504
  129.9 1.9 %shard_map.191 = f32[2,576,128]{2,1,0:T(8,128)} custom-call(bf16[256,640]{1,0:T(8,128)(2,1)S(1)} %get-tuple-element.95.dq, bf16[256,384]{1,0:T(8,128)(2,1)S(1)} %get-tuple-element.158.own, bf16[256,384]{1,0:T(8,128)(2,1)S(1)} %collective-permute-done.32.other, bf16[256,576]{1,0:T(8,128)(2,1)S(1)} %bitcast.199, f32[256,576]{1,0:T(8,128)S(1)} %copy-done.6, ...), custom_call_target="tpu_custom_call" | custom-call | flops 3000000000 | bytes 3305984 | tf_op jit(solution)/shard_map/pallas_call | solution.py:55
  134.1 1.6 %collective-permute-start.47 = (bf16[2,80,256]{2,1,0:T(8,128)(2,1)S(1)}, bf16[2,80,256]{2,1,0:T(8,128)(2,1)S(1)}, u32[]{:S(2)}, u32[]{:S(2)}) collective-permute-start(bf16[2,80,256]{2,1,0:T(8,128)(2,1)S(1)} %fusion.39), channel_id=1, source_target_pairs={{0,16},{1,17},{2,18},{3,19},{4,20},{5,21},{6,22},{7,23},{8,24},{9,... | collective-permute-start | bytes 245768 | tf_op jit(solution)/shard_map/ppermute | solution.py:504
  135.8 1.5 collective-permute-start.46
  137.3 4.6 %collective-permute-done.47 = bf16[2,80,256]{2,1,0:T(8,128)(2,1)S(1)} collective-permute-done((bf16[2,80,256]{2,1,0:T(8,128)(2,1)S(1)}, bf16[2,80,256]{2,1,0:T(8,128)(2,1)S(1)}, u32[]{:S(2)}, u32[]{:S(2)}) %collective-permute-start.47) | collective-permute-done | bytes 81952 | tf_op jit(solution)/shard_map/ppermute | solution.py:504
  142.9 1.2 collective-permute-start.48
  144.8 2.7 %collective-permute-done.48.d1 = bf16[72,576]{1,0:T(8,128)(2,1)S(1)} collective-permute-done((bf16[72,576]{1,0:T(8,128)(2,1)S(1)}, bf16[72,576]{1,0:T(8,128)(2,1)S(1)}, u32[]{:S(2)}, u32[]{:S(2)}) %collective-permute-start.48) | collective-permute-done | bytes 82976 | tf_op jit(solution)/shard_map/ppermute | solution.py:504
  149.0 1.9 %shard_map.192 = (f32[72,3072]{1,0:T(8,128)}, f32[192,576]{1,0:T(8,128)}, f32[72,576]{1,0:T(8,128)}, f32[72,960]{1,0:T(8,128)}, f32[1,96]{1,0:T(1,128)}, /*index=5*/f32[1,24]{1,0:T(1,128)}, f32[2,72]{1,0:T(2,128)}) custom-call(s32[2]{0:T(128)S(1)} %pad_add_fusion.meta, bf16[2,72,384]{2,1,0:T(8,128)(2,1)S(1)} %add_convert_fusion.11.a_near, ...), custom_call_target="tpu_custom_call" | custom-call | flops 3000000000 | bytes 2708512 | tf_op jit(solution)/shard_map/pallas_call | solution.py:55
  (190 shorter events, 30.0 us)
Async XLA Ops:
  3.8 8.8 %collective-permute-start.3 = (bf16[40,960]{1,0:T(8,128)(2,1)S(1)}, bf16[40,960]{1,0:T(8,128)(2,1)S(1)}, u32[]{:S(2)}, u32[]{:S(2)}) collective-permute-start(bf16[40,960]{1,0:T(8,128)(2,1)S(1)} %shard_map.187), channel_id=1, source_target_pairs={{0,16},{1,17},{2,18},{3,19},{4,20},{5,21},{6,22},{7,23},{8,24},{9,... | collective-permute-start | bytes 230408 | tf_op jit(solution)/shard_map/ppermute | solution.py:504
  10.0 17.1 %collective-permute-start.1 = (bf16[256,640]{1,0:T(8,128)(2,1)S(1)}, bf16[256,640]{1,0:T(8,128)(2,1)S(1)}, u32[]{:S(2)}, u32[]{:S(2)}) collective-permute-start(bf16[256,640]{1,0:T(8,128)(2,1)S(1)} %pad_maximum_fusion.3.b0), channel_id=1, source_target_pairs={{0,1},{1,0},{2,3},{3,2},{4,5},{5,4},{6,7},{7,6},{8,9},{9,8},{10,11... | collective-permute-start | bytes 983048 | tf_op jit(solution)/shard_map/ppermute | solution.py:504
  10.0 12.8 %collective-permute-start = (bf16[256,640]{1,0:T(8,128)(2,1)S(1)}, bf16[256,640]{1,0:T(8,128)(2,1)S(1)}, u32[]{:S(2)}, u32[]{:S(2)}) collective-permute-start(bf16[256,640]{1,0:T(8,128)(2,1)S(1)} %pad_maximum_fusion.3.b0), channel_id=1, source_target_pairs={{0,2},{1,3},{2,0},{3,1},{4,6},{5,7},{6,4},{7,5},{8,10},{9,11},{10,... | collective-permute-start | bytes 983048 | tf_op jit(solution)/shard_map/ppermute | solution.py:504
  11.6 8.6 %collective-permute-start.9 = (bf16[72,768]{1,0:T(8,128)(2,1)S(1)}, bf16[72,768]{1,0:T(8,128)(2,1)S(1)}, u32[]{:S(2)}, u32[]{:S(2)}) collective-permute-start(bf16[72,768]{1,0:T(8,128)(2,1)S(1)} %constant_dynamic-slice_fusion), channel_id=1, source_target_pairs={{0,16},{1,17},{2,18},{3,19},{4,20},{5,21},{6,22},{7,23},{8,24},{9,... | collective-permute-start | bytes 331784 | tf_op jit(solution)/shard_map/ppermute | solution.py:504
  12.6 8.4 %collective-permute-start.4 = (bf16[2,40,960]{2,1,0:T(8,128)(2,1)S(1)}, bf16[2,40,960]{2,1,0:T(8,128)(2,1)S(1)}, u32[]{:S(2)}, u32[]{:S(2)}) collective-permute-start(bf16[2,40,960]{2,1,0:T(8,128)(2,1)S(1)} %pad_maximum_fusion.6), channel_id=1, source_target_pairs={{0,8},{1,9},{2,10},{3,11},{4,12},{5,13},{6,14},{7,15},{8,0},{9,1},... | collective-permute-start | bytes 460808 | tf_op jit(solution)/shard_map/ppermute | solution.py:504
  21.2 19.1 %collective-permute-start.6 = (bf16[2,2,40,960]{3,2,1,0:T(8,128)(2,1)S(1)}, bf16[2,2,40,960]{3,2,1,0:T(8,128)(2,1)S(1)}, u32[]{:S(2)}, u32[]{:S(2)}) collective-permute-start(bf16[2,2,40,960]{3,2,1,0:T(8,128)(2,1)S(1)} %pad_maximum_fusion.4.a00), channel_id=1, source_target_pairs={{0,1},{1,0},{2,3},{3,2},{4,5},{5,4},{6,7},{7,6},{8,9},{9,8},{10,11... | collective-permute-start | bytes 921608 | tf_op jit(solution)/shard_map/ppermute | solution.py:504
  21.2 15.8 %collective-permute-start.5 = (bf16[2,2,40,960]{3,2,1,0:T(8,128)(2,1)S(1)}, bf16[2,2,40,960]{3,2,1,0:T(8,128)(2,1)S(1)}, u32[]{:S(2)}, u32[]{:S(2)}) collective-permute-start(bf16[2,2,40,960]{3,2,1,0:T(8,128)(2,1)S(1)} %pad_maximum_fusion.4.a00), channel_id=1, source_target_pairs={{0,4},{1,5},{2,6},{3,7},{4,0},{5,1},{6,2},{7,3},{8,12},{9,13},{10,... | collective-permute-start | bytes 921608 | tf_op jit(solution)/shard_map/ppermute | solution.py:504
  22.8 11.2 %collective-permute-start.10 = (bf16[2,72,768]{2,1,0:T(8,128)(2,1)S(1)}, bf16[2,72,768]{2,1,0:T(8,128)(2,1)S(1)}, u32[]{:S(2)}, u32[]{:S(2)}) collective-permute-start(bf16[2,72,768]{2,1,0:T(8,128)(2,1)S(1)} %pad_maximum_fusion.5), channel_id=1, source_target_pairs={{0,8},{1,9},{2,10},{3,11},{4,12},{5,13},{6,14},{7,15},{8,0},{9,1},... | collective-permute-start | bytes 663560 | tf_op jit(solution)/shard_map/ppermute | solution.py:504
  22.8 11.3 %collective-permute-start.8 = (bf16[136,576]{1,0:T(8,128)(2,1)S(1)}, bf16[136,576]{1,0:T(8,128)(2,1)S(1)}, u32[]{:S(2)}, u32[]{:S(2)}) collective-permute-start(bf16[136,576]{1,0:T(8,128)(2,1)S(1)} %dynamic-slice_bitcast_fusion), channel_id=1, source_target_pairs={{0,16},{1,17},{2,18},{3,19},{4,20},{5,21},{6,22},{7,23},{8,24},{9,... | collective-permute-start | bytes 470024 | tf_op jit(solution)/shard_map/ppermute | solution.py:504
  27.1 11.4 %collective-permute-start.2 = (bf16[256,640]{1,0:T(8,128)(2,1)S(1)}, bf16[256,640]{1,0:T(8,128)(2,1)S(1)}, u32[]{:S(2)}, u32[]{:S(2)}) collective-permute-start(bf16[256,640]{1,0:T(8,128)(2,1)S(1)} %collective-permute-done.b1), channel_id=1, source_target_pairs={{0,1},{1,0},{2,3},{3,2},{4,5},{5,4},{6,7},{7,6},{8,9},{9,8},{10,11... | collective-permute-start | bytes 983048 | tf_op jit(solution)/shard_map/ppermute | solution.py:504
  34.3 22.5 %collective-permute-start.15 = (bf16[2,136,576]{2,1,0:T(8,128)(2,1)S(1)}, bf16[2,136,576]{2,1,0:T(8,128)(2,1)}, u32[]{:S(2)}, u32[]{:S(2)}) collective-permute-start(bf16[2,136,576]{2,1,0:T(8,128)(2,1)S(1)} %pad_maximum_fusion.2.refs_0_), channel_id=1, source_target_pairs={{0,8},{1,9},{2,10},{3,11},{4,12},{5,13},{6,14},{7,15},{8,0},{9,1},... | collective-permute-start | bytes 940040 | tf_op jit(solution)/shard_map/ppermute | solution.py:504
  36.5 19.8 %collective-permute-start.12 = (bf16[2,136,576]{2,1,0:T(8,128)(2,1)S(1)}, bf16[2,136,576]{2,1,0:T(8,128)(2,1)S(1)}, u32[]{:S(2)}, u32[]{:S(2)}) collective-permute-start(bf16[2,136,576]{2,1,0:T(8,128)(2,1)S(1)} %pad_maximum_fusion.2.refs_0_), channel_id=1, source_target_pairs={{0,4},{1,5},{2,6},{3,7},{4,0},{5,1},{6,2},{7,3},{8,12},{9,13},{10,... | collective-permute-start | bytes 940040 | tf_op jit(solution)/shard_map/ppermute | solution.py:504
  37.0 18.5 %collective-permute-start.21 = (bf16[2,2,72,768]{3,2,1,0:T(8,128)(2,1)S(1)}, bf16[2,2,72,768]{3,2,1,0:T(8,128)(2,1)}, u32[]{:S(2)}, u32[]{:S(2)}) collective-permute-start(bf16[2,2,72,768]{3,2,1,0:T(8,128)(2,1)S(1)} %pad_maximum_fusion.refs_8_), channel_id=1, source_target_pairs={{0,4},{1,5},{2,6},{3,7},{4,0},{5,1},{6,2},{7,3},{8,12},{9,13},{10,... | collective-permute-start | bytes 1327112 | tf_op jit(solution)/shard_map/ppermute | solution.py:504
  40.2 17.9 %collective-permute-start.19 = (bf16[2,2,72,768]{3,2,1,0:T(8,128)(2,1)S(1)}, bf16[2,2,72,768]{3,2,1,0:T(8,128)(2,1)S(1)}, u32[]{:S(2)}, u32[]{:S(2)}) collective-permute-start(bf16[2,2,72,768]{3,2,1,0:T(8,128)(2,1)S(1)} %pad_maximum_fusion.refs_8_), channel_id=1, source_target_pairs={{0,1},{1,0},{2,3},{3,2},{4,5},{5,4},{6,7},{7,6},{8,9},{9,8},{10,11... | collective-permute-start | bytes 1327112 | tf_op jit(solution)/shard_map/ppermute | solution.py:504
  40.3 12.6 %collective-permute-start.13 = (bf16[2,2,72,768]{3,2,1,0:T(8,128)(2,1)S(1)}, bf16[2,2,72,768]{3,2,1,0:T(8,128)(2,1)}, u32[]{:S(2)}, u32[]{:S(2)}) collective-permute-start(bf16[2,2,72,768]{3,2,1,0:T(8,128)(2,1)S(1)} %pad_maximum_fusion.refs_8_), channel_id=1, source_target_pairs={{0,2},{1,3},{2,0},{3,1},{4,6},{5,7},{6,4},{7,5},{8,10},{9,11},{10,... | collective-permute-start | bytes 1327112 | tf_op jit(solution)/shard_map/ppermute | solution.py:504
  55.5 10.8 %collective-permute-start.23 = (bf16[2,2,72,768]{3,2,1,0:T(8,128)(2,1)}, bf16[2,2,72,768]{3,2,1,0:T(8,128)(2,1)}, u32[]{:S(2)}, u32[]{:S(2)}) collective-permute-start(bf16[2,2,72,768]{3,2,1,0:T(8,128)(2,1)} %collective-permute-done.21.refs_12_), channel_id=1, source_target_pairs={{0,2},{1,3},{2,0},{3,1},{4,6},{5,7},{6,4},{7,5},{8,10},{9,11},{10,... | collective-permute-start | bytes 1327112 | tf_op jit(solution)/shard_map/ppermute | solution.py:504
  56.3 10.1 %collective-permute-start.14 = (bf16[2,136,576]{2,1,0:T(8,128)(2,1)S(1)}, bf16[2,136,576]{2,1,0:T(8,128)(2,1)S(1)}, u32[]{:S(2)}, u32[]{:S(2)}) collective-permute-start(bf16[2,136,576]{2,1,0:T(8,128)(2,1)S(1)} %collective-permute-done.12.refs_2_), channel_id=1, source_target_pairs={{0,1},{1,0},{2,3},{3,2},{4,5},{5,4},{6,7},{7,6},{8,9},{9,8},{10,11... | collective-permute-start | bytes 940040 | tf_op jit(solution)/shard_map/ppermute | solution.py:504
  56.8 10.4 %collective-permute-start.17 = (bf16[2,136,576]{2,1,0:T(8,128)(2,1)}, bf16[2,136,576]{2,1,0:T(8,128)(2,1)}, u32[]{:S(2)}, u32[]{:S(2)}) collective-permute-start(bf16[2,136,576]{2,1,0:T(8,128)(2,1)} %collective-permute-done.15.refs_4_), channel_id=1, source_target_pairs={{0,4},{1,5},{2,6},{3,7},{4,0},{5,1},{6,2},{7,3},{8,12},{9,13},{10,... | collective-permute-start | bytes 940040 | tf_op jit(solution)/shard_map/ppermute | solution.py:504
  57.9 11.1 %collective-permute-start.22 = (bf16[2,2,72,768]{3,2,1,0:T(8,128)(2,1)}, bf16[2,2,72,768]{3,2,1,0:T(8,128)(2,1)}, u32[]{:S(2)}, u32[]{:S(2)}) collective-permute-start(bf16[2,2,72,768]{3,2,1,0:T(8,128)(2,1)} %collective-permute-done.21.refs_12_), channel_id=1, source_target_pairs={{0,1},{1,0},{2,3},{3,2},{4,5},{5,4},{6,7},{7,6},{8,9},{9,8},{10,11... | collective-permute-start | bytes 1327112 | tf_op jit(solution)/shard_map/ppermute | solution.py:504
  58.1 10.9 %collective-permute-start.20 = (bf16[2,2,72,768]{3,2,1,0:T(8,128)(2,1)}, bf16[2,2,72,768]{3,2,1,0:T(8,128)(2,1)}, u32[]{:S(2)}, u32[]{:S(2)}) collective-permute-start(bf16[2,2,72,768]{3,2,1,0:T(8,128)(2,1)} %collective-permute-done.13.refs_10_), channel_id=1, source_target_pairs={{0,1},{1,0},{2,3},{3,2},{4,5},{5,4},{6,7},{7,6},{8,9},{9,8},{10,11... | collective-permute-start | bytes 1327112 | tf_op jit(solution)/shard_map/ppermute | solution.py:504
  87.5 20.5 %collective-permute-start.36 = (bf16[2,2,2,72,384]{4,3,2,1,0:T(8,128)(2,1)S(1)}, bf16[2,2,2,72,384]{4,3,2,1,0:T(8,128)(2,1)S(1)}, u32[]{:S(2)}, u32[]{:S(2)}) collective-permute-start(bf16[2,2,2,72,384]{4,3,2,1,0:T(8,128)(2,1)S(1)} %get-tuple-element.146), channel_id=1, source_target_pairs={{0,4},{1,5},{2,6},{3,7},{4,0},{5,1},{6,2},{7,3},{8,12},{9,13},{10,... | collective-permute-start | bytes 1327112 | tf_op jit(solution)/shard_map/ppermute | solution.py:504
  90.7 15.7 %collective-permute-start.31 = (bf16[2,2,2,72,384]{4,3,2,1,0:T(8,128)(2,1)S(1)}, bf16[2,2,2,72,384]{4,3,2,1,0:T(8,128)(2,1)S(1)}, u32[]{:S(2)}, u32[]{:S(2)}) collective-permute-start(bf16[2,2,2,72,384]{4,3,2,1,0:T(8,128)(2,1)S(1)} %get-tuple-element.148), channel_id=1, source_target_pairs={{0,8},{1,9},{2,10},{3,11},{4,12},{5,13},{6,14},{7,15},{8,0},{9,1},... | collective-permute-start | bytes 1327112 | tf_op jit(solution)/shard_map/ppermute | solution.py:504
  91.8 18.3 %collective-permute-start.29 = (bf16[2,2,2,72,576]{4,3,2,1,0:T(8,128)(2,1)S(1)}, bf16[2,2,2,72,576]{4,3,2,1,0:T(8,128)(2,1)S(1)}, u32[]{:S(2)}, u32[]{:S(2)}) collective-permute-start(bf16[2,2,2,72,576]{4,3,2,1,0:T(8,128)(2,1)S(1)} %get-tuple-element.144), channel_id=1, source_target_pairs={{0,2},{1,3},{2,0},{3,1},{4,6},{5,7},{6,4},{7,5},{8,10},{9,11},{10,... | collective-permute-start | bytes 1990664 | tf_op jit(solution)/shard_map/ppermute | solution.py:504
  106.5 15.3 %collective-permute-start.35 = (bf16[2,2,72,384]{3,2,1,0:T(8,128)(2,1)S(1)}, bf16[2,2,72,384]{3,2,1,0:T(8,128)(2,1)S(1)}, u32[]{:S(2)}, u32[]{:S(2)}) collective-permute-start(bf16[2,2,72,384]{3,2,1,0:T(8,128)(2,1)S(1)} %get-tuple-element.156), channel_id=1, source_target_pairs={{0,16},{1,17},{2,18},{3,19},{4,20},{5,21},{6,22},{7,23},{8,24},{9,... | collective-permute-start | bytes 663560 | tf_op jit(solution)/shard_map/ppermute | solution.py:504
  108.1 10.0 %collective-permute-start.37 = (bf16[2,2,72,384]{3,2,1,0:T(8,128)(2,1)S(1)}, bf16[2,2,72,384]{3,2,1,0:T(8,128)(2,1)S(1)}, u32[]{:S(2)}, u32[]{:S(2)}) collective-permute-start(bf16[2,2,72,384]{3,2,1,0:T(8,128)(2,1)S(1)} %get-tuple-element.153), channel_id=1, source_target_pairs={{0,8},{1,9},{2,10},{3,11},{4,12},{5,13},{6,14},{7,15},{8,0},{9,1},... | collective-permute-start | bytes 663560 | tf_op jit(solution)/shard_map/ppermute | solution.py:504
  110.3 12.2 %collective-permute-start.34 = (bf16[2,2,2,80,256]{4,3,2,1,0:T(8,128)(2,1)S(1)}, bf16[2,2,2,80,256]{4,3,2,1,0:T(8,128)(2,1)S(1)}, u32[]{:S(2)}, u32[]{:S(2)}) collective-permute-start(bf16[2,2,2,80,256]{4,3,2,1,0:T(8,128)(2,1)S(1)} %get-tuple-element.152), channel_id=1, source_target_pairs={{0,4},{1,5},{2,6},{3,7},{4,0},{5,1},{6,2},{7,3},{8,12},{9,13},{10,... | collective-permute-start | bytes 983048 | tf_op jit(solution)/shard_map/ppermute | solution.py:504
  111.1 17.7 %collective-permute-start.33 = (bf16[2,2,72,576]{3,2,1,0:T(8,128)(2,1)S(1)}, bf16[2,2,72,576]{3,2,1,0:T(8,128)(2,1)S(1)}, u32[]{:S(2)}, u32[]{:S(2)}) collective-permute-start(bf16[2,2,72,576]{3,2,1,0:T(8,128)(2,1)S(1)} %get-tuple-element.150), channel_id=1, source_target_pairs={{0,4},{1,5},{2,6},{3,7},{4,0},{5,1},{6,2},{7,3},{8,12},{9,13},{10,... | collective-permute-start | bytes 995336 | tf_op jit(solution)/shard_map/ppermute | solution.py:504
  112.8 17.1 %collective-permute-start.32 = (bf16[256,384]{1,0:T(8,128)(2,1)S(1)}, bf16[256,384]{1,0:T(8,128)(2,1)S(1)}, u32[]{:S(2)}, u32[]{:S(2)}) collective-permute-start(bf16[256,384]{1,0:T(8,128)(2,1)S(1)} %get-tuple-element.157), channel_id=1, source_target_pairs={{0,2},{1,3},{2,0},{3,1},{4,6},{5,7},{6,4},{7,5},{8,10},{9,11},{10,... | collective-permute-start | bytes 589832 | tf_op jit(solution)/shard_map/ppermute | solution.py:504
  118.2 13.7 %collective-permute-start.38 = (bf16[2,72,384]{2,1,0:T(8,128)(2,1)S(1)}, bf16[2,72,384]{2,1,0:T(8,128)(2,1)S(1)}, u32[]{:S(2)}, u32[]{:S(2)}) collective-permute-start(bf16[2,72,384]{2,1,0:T(8,128)(2,1)S(1)} %fusion.34), channel_id=1, source_target_pairs={{0,16},{1,17},{2,18},{3,19},{4,20},{5,21},{6,22},{7,23},{8,24},{9,... | collective-permute-start | bytes 331784 | tf_op jit(solution)/shard_map/ppermute | solution.py:504
  121.9 11.1 %collective-permute-start.42 = (bf16[2,72,384]{2,1,0:T(8,128)(2,1)S(1)}, bf16[2,72,384]{2,1,0:T(8,128)(2,1)S(1)}, u32[]{:S(2)}, u32[]{:S(2)}) collective-permute-start(bf16[2,72,384]{2,1,0:T(8,128)(2,1)S(1)} %fusion.33), channel_id=1, source_target_pairs={{0,4},{1,5},{2,6},{3,7},{4,0},{5,1},{6,2},{7,3},{8,12},{9,13},{10,... | collective-permute-start | bytes 331784 | tf_op jit(solution)/shard_map/ppermute | solution.py:504
  122.6 11.6 %collective-permute-start.41 = (bf16[2,2,80,256]{3,2,1,0:T(8,128)(2,1)S(1)}, bf16[2,2,80,256]{3,2,1,0:T(8,128)(2,1)S(1)}, u32[]{:S(2)}, u32[]{:S(2)}) collective-permute-start(bf16[2,2,80,256]{3,2,1,0:T(8,128)(2,1)S(1)} %get-tuple-element.162), channel_id=1, source_target_pairs={{0,8},{1,9},{2,10},{3,11},{4,12},{5,13},{6,14},{7,15},{8,0},{9,1},... | collective-permute-start | bytes 491528 | tf_op jit(solution)/shard_map/ppermute | solution.py:504
  133.0 11.1 %collective-permute-start.44 = (bf16[2,72,384]{2,1,0:T(8,128)(2,1)S(1)}, bf16[2,72,384]{2,1,0:T(8,128)(2,1)S(1)}, u32[]{:S(2)}, u32[]{:S(2)}) collective-permute-start(bf16[2,72,384]{2,1,0:T(8,128)(2,1)S(1)} %fusion.17), channel_id=1, source_target_pairs={{0,2},{1,3},{2,0},{3,1},{4,6},{5,7},{6,4},{7,5},{8,10},{9,11},{10,... | collective-permute-start | bytes 331784 | tf_op jit(solution)/shard_map/ppermute | solution.py:504
  (49 other events, 313.8 us)

commit v8 on v7

--- a/solution.py
+++ b/solution.py
@@ -438,7 +438,7 @@
             for c_to, to in ((0, rk_o), (1, rg_o)):
                 at = pl.multiple_of((yy * 2 + (core ^ c_to)) * 256, 256)
                 block = [w_s[d_rows * f : d_rows * (f + 1), pl.ds(at, 256)], small_s[f, :, pl.ds(at, 256)]]
-                to[x, z0, z1, yy] = jnp.concatenate(block, axis=0).astype(BF)
+                to[y ^ yy, x, z0, z1] = jnp.concatenate(block, axis=0).astype(BF)
 
 
 def input_gradient_two(dq, own, other, source, mid, w, gains, out_o):
@@ -470,8 +470,10 @@
             wout_o[pl.ds(pl.multiple_of(to * part_o, 8), part_o), :] = piece[part_d:]
 
 
-def place_qkv(qk, v, meta, near, far, w_o, bqk_o, bv_o, gains_o, all_s):
-    place_gate(meta, near, far, all_s)
+def place_qkv(qk, v, meta, p00, p10, p01, p11, w_o, bqk_o, bv_o, gains_o, all_s):
+    n = p00.shape[1]
+    for piece, o in ((p00, 0), (p10, 2), (p01, 1), (p11, 3)):
+        all_s[:, pl.ds(pl.multiple_of((meta[0] ^ o) * n, 128), n)] = piece[...].astype(F32)
     d_rows = w_o.shape[0]
     w_o[:, :QW] = all_s[:d_rows, 2 * KW : 2 * KW + QW]
     w_o[:, QW:] = all_s[:d_rows, : 2 * KW]
@@ -482,12 +484,12 @@
     gains_o[1:2, :] = line[:, 256 : 256 + d_rows]
 
 
-def place_all(part_d, qk, v, meta, a_near, a_far, b_near, b_far, d0, d1, d2, d3, r_near, r_far,
+def place_all(part_d, qk, v, meta, a_near, a_far, b_near, b_far, d0, d1, d2, d3, r0, r1, r2, r3,
               gate_o, down_o, wout_o, w_o, bqk_o, bv_o, gains_o, all_s):
     place_gate(meta, a_near, a_far, gate_o, 2, 0)
     place_gate(meta, b_near, b_far, gate_o, 2, 1)
     place_down(part_d, meta, d0, d1, d2, d3, down_o, wout_o)
-    place_qkv(qk, v, meta, r_near, r_far, w_o, bqk_o, bv_o, gains_o, all_s)
+    place_qkv(qk, v, meta, r0, r1, r2, r3, w_o, bqk_o, bv_o, gains_o, all_s)
 
 
 class Net:
@@ -802,7 +804,6 @@
         axis=1,
     )
     a2 = net.both(a1, znear, 0)
-    b0 = net.half(after(half_b, a2), core, 0)
     a_x = net.swap(a2, xbit)
     a_c = net.swap(a2, core)
     gu1 = net.both(gu0, zfar, 0)
@@ -812,7 +813,8 @@
     gu_x = net.swap(gu2, xbit)
     gu_y = net.swap(gu2, ybit)
     gu_c = net.swap(gu2, core)
-    b1 = net.both(b0, zfar, 0, after(net.swap(b0, zfar), gu2))
+    b0 = net.half(after(half_b, gu2), core, 0)
+    b1 = net.both(b0, zfar, 0)
     b_z = net.swap(b1, znear)
     b_x = net.swap(b1, xbit)
     b_c = net.swap(b1, core)
@@ -920,18 +922,18 @@
     b_got = net.swap(b_give, zfar)
     a_got = net.swap(a_give, znear)
     rest, rest_give = halves(rest_keep, after(net.swap(rest_give, core), b_give, down_got))
-    rest_got = net.swap(rest_give, xbit)
+    rest_got = net.swap(rest_give, ybit)
     down, down_give = halves(down, after(down_got, rest_give))
     down_got = net.swap(down_give, xbit)
     dkv, dkv_give = halves(dkv_keep, after(net.swap(dkv_give, core), down_give))
     dkv_got = net.swap(dkv_give, ybit)
     a, a_give = halves(a, after(a_got, dkv_give))
     a_got = net.swap(a_give, zfar)
-    b, b_give = halves(b, after(b_got, a_give))
+    rest, rest_give = halves(rest, after(rest_got, a_give))
+    rest_got = net.swap(rest_give, xbit)
+    b, b_give = halves(b, after(b_got, rest_give))
     b_got = net.swap(b_give, xbit)
-    rest, rest_give = halves(rest, after(rest_got, b_give))
-    rest_got = net.swap(rest_give, znear)
-    down, down_give = halves(down, after(down_got, rest_give))
+    down, down_give = halves(down, after(down_got, b_give))
     down_got = net.swap(down_give, znear)
     (hidden_grad,) = call(
         input_gradient_two,
@@ -941,33 +943,34 @@
         3e9,
         mib=16,
     )
-    a_got = after(a_got, hidden_grad)
+    rest, rest_give = halves(rest, after(rest_got, hidden_grad))
     hidden_grad = hidden_grad.reshape(micro, batch, width, length).swapaxes(2, 3)
-    a = add(a, a_got)
+    rest_got = net.swap(rest_give, znear)
+    a = add(a, after(a_got, rest_give))
     a_got = net.swap(a, ybit)
     b = add(b, after(b_got, a))
     b_got = net.swap(b, ybit)
-    rest, rest_give = halves(rest, after(rest_got, b))
+    down, down_give = halves(down, after(down_got, b))
+    down_got = net.swap(down_give, zfar)
+    rest, rest_give = halves(rest, after(rest_got, down_give))
     rest_got = net.swap(rest_give, zfar)
-    down, down_give = halves(down, after(down_got, rest_give))
-    down_got = net.swap(down_give, zfar)
-    a = add(a, after(a_got, down_give))
+    a = add(a, after(a_got, rest_give))
     a_far = net.swap(a, core)
     b = add(b, b_got)
     b_far = net.swap(b, core)
-    rest = add(rest, after(rest_got, a))
-    rest_got = net.swap(rest, ybit)
-    down = add(down, after(down_got, rest))
+    down = add(down, after(down_got, a))
     down_y = net.swap(down, ybit)
     down_c = net.swap(down, core)
+    rest = add(rest, after(rest_got, down))
+    rest_y = net.swap(rest, ybit)
+    rest_c = net.swap(after(rest, rest_y), core)
     down_yc = net.swap(down_y, core)
-    rest = add(rest, rest_got)
-    rest_far = net.swap(rest, core)
+    rest_yc = net.swap(rest_y, core)
     qk, v = (QW + KW) // n_fsdp, KW // n_fsdp
     out_gate, out_down, out_wout, out_qkv, b_qk, b_v, out_gains = call(
         functools.partial(place_all, ff_rows // 4, qk, v),
         [meta],
-        [a, a_far, b, b_far, down, down_y, down_c, down_yc, rest, rest_far],
+        [a, a_far, b, b_far, down, down_y, down_c, down_yc, rest, rest_y, rest_c, rest_yc],
         [
             sds((d_rows, 2 * units), F32),
             sds((ff_rows, width), F32),

time: 151 us -> 151 us (level)
  waiting for transfers between devices: 51.1 us -> 53.2 us
  starting transfers between devices: 45.6 us -> 43.7 us
    ppermute x53 -> x55, waiting for transfers between devices: 51.1 us -> 53.2 us  [swap(): return lax.ppermute(value, ('fsdp', 'seq'), pairs)]
    ppermute x53 -> x55, starting transfers between devices: 45.6 us -> 43.7 us  [swap(): return lax.ppermute(value, ('fsdp', 'seq'), pairs)]
  transfers between devices with their start and end apart: 53 -> 55, of which waited for: 20 -> 20; matrix products, arithmetic and copies ran while one was open for 5% -> 5% of each run, Pallas kernels for 17% -> 17%
where the time goes in v8:
time: 151 us
  waiting for transfers between devices  53.2 us (35%)
  starting transfers between devices  43.7 us (29%)
  Pallas kernels  42.6 us (28%)
  other arithmetic  5.67 us (4%)
  local copies, waits for them, and re-layouts  4.81 us (3%)
    ppermute x55, waiting for transfers between devices, swap(): return lax.ppermute(value, ('fsdp', 'seq'), pairs)  53.2 us
    ppermute x55, starting transfers between devices, swap(): return lax.ppermute(value, ('fsdp', 'seq'), pairs)  43.7 us
    pallas_call x5, Pallas kernels, call(): pl.pallas_call(kernel, out_shape=outs, in_specs=specs, out_specs=whole(*o...  41.7 us
    unnamed x58, local copies, waits for them, and re-layouts  3.76 us
    convert_element_type x21, other arithmetic, add(): return (keep.astype(F32) + got.astype(F32)).astype(BF)  3.18 us
  transfers between devices with their start and end apart: 55, of which 20 were waited for; matrix products, arithmetic and copies ran while one was open for 5% of the time, Pallas kernels for 17%

profile of v8, /device:TPU:0, one launch (start us, length us, event | category | flops | bytes accessed | tf_op | source)
XLA Modules:
  0.0 151.1 jit_solution(17485929952216826141)
XLA Ops:
  3.8 4.1 %collective-permute-start.3 = (bf16[40,960]{1,0:T(8,128)(2,1)S(1)}, bf16[40,960]{1,0:T(8,128)(2,1)S(1)}, u32[]{:S(2)}, u32[]{:S(2)}) collective-permute-start(bf16[40,960]{1,0:T(8,128)(2,1)S(1)} %shard_map.187), channel_id=1, source_target_pairs={{0,16},{1,17},{2,18},{3,19},{4,20},{5,21},{6,22},{7,23},{8,24},{9,... | collective-permute-start | bytes 230408 | tf_op jit(solution)/shard_map/ppermute | solution.py:506
  10.0 1.6 %collective-permute-start = (bf16[256,640]{1,0:T(8,128)(2,1)S(1)}, bf16[256,640]{1,0:T(8,128)(2,1)S(1)}, u32[]{:S(2)}, u32[]{:S(2)}) collective-permute-start(bf16[256,640]{1,0:T(8,128)(2,1)S(1)} %pad_maximum_fusion.3.b0), channel_id=1, source_target_pairs={{0,2},{1,3},{2,0},{3,1},{4,6},{5,7},{6,4},{7,5},{8,10},{9,11},{10,... | collective-permute-start | bytes 983048 | tf_op jit(solution)/shard_map/ppermute | solution.py:506
  12.5 1.6 %collective-permute-start.4 = (bf16[2,40,960]{2,1,0:T(8,128)(2,1)S(1)}, bf16[2,40,960]{2,1,0:T(8,128)(2,1)S(1)}, u32[]{:S(2)}, u32[]{:S(2)}) collective-permute-start(bf16[2,40,960]{2,1,0:T(8,128)(2,1)S(1)} %pad_maximum_fusion.6), channel_id=1, source_target_pairs={{0,8},{1,9},{2,10},{3,11},{4,12},{5,13},{6,14},{7,15},{8,0},{9,1},... | collective-permute-start | bytes 460808 | tf_op jit(solution)/shard_map/ppermute | solution.py:506
  14.2 6.1 %collective-permute-done.8 = bf16[72,768]{1,0:T(8,128)(2,1)S(1)} collective-permute-done((bf16[72,768]{1,0:T(8,128)(2,1)S(1)}, bf16[72,768]{1,0:T(8,128)(2,1)S(1)}, u32[]{:S(2)}, u32[]{:S(2)}) %collective-permute-start.8) | collective-permute-done | bytes 110624 | tf_op jit(solution)/shard_map/ppermute | solution.py:506
  21.3 1.6 %collective-permute-start.5 = (bf16[2,2,40,960]{3,2,1,0:T(8,128)(2,1)S(1)}, bf16[2,2,40,960]{3,2,1,0:T(8,128)(2,1)S(1)}, u32[]{:S(2)}, u32[]{:S(2)}) collective-permute-start(bf16[2,2,40,960]{3,2,1,0:T(8,128)(2,1)S(1)} %pad_maximum_fusion.4.a00), channel_id=1, source_target_pairs={{0,4},{1,5},{2,6},{3,7},{4,0},{5,1},{6,2},{7,3},{8,12},{9,13},{10,... | collective-permute-start | bytes 921608 | tf_op jit(solution)/shard_map/ppermute | solution.py:506
  22.9 5.3 %collective-permute-done.9 = bf16[2,72,768]{2,1,0:T(8,128)(2,1)S(1)} collective-permute-done((bf16[2,72,768]{2,1,0:T(8,128)(2,1)S(1)}, bf16[2,72,768]{2,1,0:T(8,128)(2,1)S(1)}, u32[]{:S(2)}, u32[]{:S(2)}) %collective-permute-start.9) | collective-permute-done | bytes 221216 | tf_op jit(solution)/shard_map/ppermute | solution.py:506
  28.3 2.2 %collective-permute-start.10 = (bf16[136,576]{1,0:T(8,128)(2,1)S(1)}, bf16[136,576]{1,0:T(8,128)(2,1)S(1)}, u32[]{:S(2)}, u32[]{:S(2)}) collective-permute-start(bf16[136,576]{1,0:T(8,128)(2,1)S(1)} %dynamic-slice_bitcast_fusion), channel_id=1, source_target_pairs={{0,16},{1,17},{2,18},{3,19},{4,20},{5,21},{6,22},{7,23},{8,24},{9,... | collective-permute-start | bytes 470024 | tf_op jit(solution)/shard_map/ppermute | solution.py:506
  31.0 1.6 %collective-permute-start.21 = (bf16[2,2,72,768]{3,2,1,0:T(8,128)(2,1)S(1)}, bf16[2,2,72,768]{3,2,1,0:T(8,128)(2,1)}, u32[]{:S(2)}, u32[]{:S(2)}) collective-permute-start(bf16[2,2,72,768]{3,2,1,0:T(8,128)(2,1)S(1)} %pad_maximum_fusion.refs_8_), channel_id=1, source_target_pairs={{0,4},{1,5},{2,6},{3,7},{4,0},{5,1},{6,2},{7,3},{8,12},{9,13},{10,... | collective-permute-start | bytes 1327112 | tf_op jit(solution)/shard_map/ppermute | solution.py:506
  32.6 5.6 %collective-permute-done.10 = bf16[136,576]{1,0:T(8,128)(2,1)S(1)} collective-permute-done((bf16[136,576]{1,0:T(8,128)(2,1)S(1)}, bf16[136,576]{1,0:T(8,128)(2,1)S(1)}, u32[]{:S(2)}, u32[]{:S(2)}) %collective-permute-start.10) | collective-permute-done | bytes 156704 | tf_op jit(solution)/shard_map/ppermute | solution.py:506
  38.3 1.3 collective-permute-start.13
  43.3 10.7 %shard_map.188 = (bf16[256,576]{1,0:T(8,128)(2,1)S(1)}, bf16[2,3,384,64]{3,2,1,0:T(8,128)(2,1)}, bf16[2,3,512,64]{3,2,1,0:T(8,128)(2,1)}, bf16[2,3,512,64]{3,2,1...) custom-call(s32[2]{0:T(128)S(1)} %pad_add_fusion.meta, bf16[256,640]{1,0:T(8,128)(2,1)S(1)} %pad_maximum_fusion.3.b0, ...), custom_call_target="tpu_custom_call" | custom-call | flops 12000000000 | bytes 6074880 | tf_op jit(solution)/shard_map/pallas_call | solution.py:55
  56.5 9.6 %collective-permute-done.23.refs_14_ = bf16[2,2,72,768]{3,2,1,0:T(8,128)(2,1)} collective-permute-done((bf16[2,2,72,768]{3,2,1,0:T(8,128)(2,1)}, bf16[2,2,72,768]{3,2,1,0:T(8,128)(2,1)}, u32[]{:S(2)}, u32[]{:S(2)}) %collective-permute-start.23) | collective-permute-done | bytes 442400 | tf_op jit(solution)/shard_map/ppermute | solution.py:506
  67.3 1.5 %collective-permute-done.16.refs_5_ = bf16[2,136,576]{2,1,0:T(8,128)(2,1)} collective-permute-done((bf16[2,136,576]{2,1,0:T(8,128)(2,1)}, bf16[2,136,576]{2,1,0:T(8,128)(2,1)}, u32[]{:S(2)}, u32[]{:S(2)}) %collective-permute-start.16) | collective-permute-done | bytes 313376 | tf_op jit(solution)/shard_map/ppermute | solution.py:506
  69.3 13.4 %shard_map.189 = (bf16[2,576,128]{2,1,0:T(8,128)(2,1)}, bf16[2,2,2,2,72,384]{5,4,3,2,1,0:T(8,128)(2,1)}, bf16[2,2,2,2,72,384]{5,4,3,2,1,0:T(8,128)(2,1)}, bf16[2...) custom-call(s32[2]{0:T(128)S(1)} %pad_add_fusion.meta, ...), custom_call_target="tpu_custom_call" | custom-call | flops 14000000000 | bytes 14311168 | tf_op jit(solution)/shard_map/pallas_call | solution.py:55
  82.9 2.5 %collective-permute-done.25 = bf16[2,2,2,2,72,384]{5,4,3,2,1,0:T(8,128)(2,1)S(1)} collective-permute-done((bf16[2,2,2,2,72,384]{5,4,3,2,1,0:T(8,128)(2,1)}, bf16[2,2,2,2,72,384]{5,4,3,2,1,0:T(8,128)(2,1)S(1)}, u32[]{:S(2)}, u32[]{:S(2)}) %collective-permute-start.25) | collective-permute-done | bytes 884768 | tf_op jit(solution)/shard_map/ppermute | solution.py:506
  85.9 1.4 add_convert_fusion.2
  88.3 1.8 %collective-permute-done.26 = bf16[2,2,2,2,72,384]{5,4,3,2,1,0:T(8,128)(2,1)S(1)} collective-permute-done((bf16[2,2,2,2,72,384]{5,4,3,2,1,0:T(8,128)(2,1)}, bf16[2,2,2,2,72,384]{5,4,3,2,1,0:T(8,128)(2,1)S(1)}, u32[]{:S(2)}, u32[]{:S(2)}) %collective-permute-start.26) | collective-permute-done | bytes 884768 | tf_op jit(solution)/shard_map/ppermute | solution.py:506
  90.4 1.4 collective-permute-start.31
  93.3 13.7 %shard_map.190 = (bf16[256,640]{1,0:T(8,128)(2,1)S(1)}, bf16[2,256,384]{2,1,0:T(8,128)(2,1)}, bf16[2,256,384]{2,1,0:T(8,128)(2,1)}, bf16[2,2,2,2,80,256]{5,4,3,2...) custom-call(s32[2]{0:T(128)S(1)} %pad_add_fusion.meta, bf16[256,640]{1,0:T(8,128)(2,1)S(1)} %pad_maximum_fusion.3.b0, ...), custom_call_target="tpu_custom_call" | custom-call | flops 14000000000 | bytes 7273216 | tf_op jit(solution)/shard_map/pallas_call | solution.py:55
  107.2 2.1 %collective-permute-start.34 = (bf16[2,2,72,384]{3,2,1,0:T(8,128)(2,1)S(1)}, bf16[2,2,72,384]{3,2,1,0:T(8,128)(2,1)S(1)}, u32[]{:S(2)}, u32[]{:S(2)}) collective-permute-start(bf16[2,2,72,384]{3,2,1,0:T(8,128)(2,1)S(1)} %get-tuple-element.158), channel_id=1, source_target_pairs={{0,16},{1,17},{2,18},{3,19},{4,20},{5,21},{6,22},{7,23},{8,24},{9,... | collective-permute-start | bytes 663560 | tf_op jit(solution)/shard_map/ppermute | solution.py:506
  109.4 1.7 %collective-permute-start.37 = (bf16[2,2,72,384]{3,2,1,0:T(8,128)(2,1)S(1)}, bf16[2,2,72,384]{3,2,1,0:T(8,128)(2,1)S(1)}, u32[]{:S(2)}, u32[]{:S(2)}) collective-permute-start(bf16[2,2,72,384]{3,2,1,0:T(8,128)(2,1)S(1)} %get-tuple-element.155), channel_id=1, source_target_pairs={{0,8},{1,9},{2,10},{3,11},{4,12},{5,13},{6,14},{7,15},{8,0},{9,1},... | collective-permute-start | bytes 663560 | tf_op jit(solution)/shard_map/ppermute | solution.py:506
  111.3 1.4 collective-permute-start.35
  114.9 6.3 %collective-permute-done.37 = bf16[2,2,72,384]{3,2,1,0:T(8,128)(2,1)S(1)} collective-permute-done((bf16[2,2,72,384]{3,2,1,0:T(8,128)(2,1)S(1)}, bf16[2,2,72,384]{3,2,1,0:T(8,128)(2,1)S(1)}, u32[]{:S(2)}, u32[]{:S(2)}) %collective-permute-start.37) | collective-permute-done | bytes 221216 | tf_op jit(solution)/shard_map/ppermute | solution.py:506
  125.7 1.9 %shard_map.191 = f32[2,576,128]{2,1,0:T(8,128)} custom-call(bf16[256,640]{1,0:T(8,128)(2,1)S(1)} %get-tuple-element.95.dq, bf16[256,384]{1,0:T(8,128)(2,1)S(1)} %get-tuple-element.160.own, bf16[256,384]{1,0:T(8,128)(2,1)S(1)} %collective-permute-done.32.other, bf16[256,576]{1,0:T(8,128)(2,1)S(1)} %bitcast.211, f32[256,576]{1,0:T(8,128)S(1)} %copy-done.6, ...), custom_call_target="tpu_custom_call" | custom-call | flops 3000000000 | bytes 3305984 | tf_op jit(solution)/shard_map/pallas_call | solution.py:55
  129.3 1.4 collective-permute-start.40
  132.0 2.3 %collective-permute-start.47 = (bf16[72,576]{1,0:T(8,128)(2,1)S(1)}, bf16[72,576]{1,0:T(8,128)(2,1)S(1)}, u32[]{:S(2)}, u32[]{:S(2)}) collective-permute-start(bf16[72,576]{1,0:T(8,128)(2,1)S(1)} %fusion.36), channel_id=1, source_target_pairs={{0,16},{1,17},{2,18},{3,19},{4,20},{5,21},{6,22},{7,23},{8,24},{9,... | collective-permute-start | bytes 248840 | tf_op jit(solution)/shard_map/ppermute | solution.py:506
  135.1 3.4 %collective-permute-done.47 = bf16[72,576]{1,0:T(8,128)(2,1)S(1)} collective-permute-done((bf16[72,576]{1,0:T(8,128)(2,1)S(1)}, bf16[72,576]{1,0:T(8,128)(2,1)S(1)}, u32[]{:S(2)}, u32[]{:S(2)}) %collective-permute-start.47) | collective-permute-done | bytes 82976 | tf_op jit(solution)/shard_map/ppermute | solution.py:506
  138.6 1.4 collective-permute-start.48
  140.6 3.0 %collective-permute-done.48.d1 = bf16[72,576]{1,0:T(8,128)(2,1)S(1)} collective-permute-done((bf16[72,576]{1,0:T(8,128)(2,1)S(1)}, bf16[72,576]{1,0:T(8,128)(2,1)S(1)}, u32[]{:S(2)}, u32[]{:S(2)}) %collective-permute-start.48) | collective-permute-done | bytes 82976 | tf_op jit(solution)/shard_map/ppermute | solution.py:506
  143.7 1.4 collective-permute-start.52
  145.1 2.7 %collective-permute-done.52.r1 = bf16[80,256]{1,0:T(8,128)(2,1)S(1)} collective-permute-done((bf16[80,256]{1,0:T(8,128)(2,1)S(1)}, bf16[80,256]{1,0:T(8,128)(2,1)S(1)}, u32[]{:S(2)}, u32[]{:S(2)}) %collective-permute-start.52) | collective-permute-done | bytes 40992 | tf_op jit(solution)/shard_map/ppermute | solution.py:506
  149.2 1.9 %shard_map.192 = (f32[72,3072]{1,0:T(8,128)}, f32[192,576]{1,0:T(8,128)}, f32[72,576]{1,0:T(8,128)}, f32[72,960]{1,0:T(8,128)}, f32[1,96]{1,0:T(1,128)}, /*index=5*/f32[1,24]{1,0:T(1,128)}, f32[2,72]{1,0:T(2,128)}) custom-call(s32[2]{0:T(128)S(1)} %pad_add_fusion.meta, bf16[2,72,384]{2,1,0:T(8,128)(2,1)S(1)} %add_convert_fusion.11.a_near, ...), custom_call_target="tpu_custom_call" | custom-call | flops 3000000000 | bytes 2708512 | tf_op jit(solution)/shard_map/pallas_call | solution.py:55
  (194 shorter events, 31.8 us)
Async XLA Ops:
  3.8 8.7 %collective-permute-start.3 = (bf16[40,960]{1,0:T(8,128)(2,1)S(1)}, bf16[40,960]{1,0:T(8,128)(2,1)S(1)}, u32[]{:S(2)}, u32[]{:S(2)}) collective-permute-start(bf16[40,960]{1,0:T(8,128)(2,1)S(1)} %shard_map.187), channel_id=1, source_target_pairs={{0,16},{1,17},{2,18},{3,19},{4,20},{5,21},{6,22},{7,23},{8,24},{9,... | collective-permute-start | bytes 230408 | tf_op jit(solution)/shard_map/ppermute | solution.py:506
  10.0 20.8 %collective-permute-start.1 = (bf16[256,640]{1,0:T(8,128)(2,1)S(1)}, bf16[256,640]{1,0:T(8,128)(2,1)S(1)}, u32[]{:S(2)}, u32[]{:S(2)}) collective-permute-start(bf16[256,640]{1,0:T(8,128)(2,1)S(1)} %pad_maximum_fusion.3.b0), channel_id=1, source_target_pairs={{0,1},{1,0},{2,3},{3,2},{4,5},{5,4},{6,7},{7,6},{8,9},{9,8},{10,11... | collective-permute-start | bytes 983048 | tf_op jit(solution)/shard_map/ppermute | solution.py:506
  10.0 20.5 %collective-permute-start = (bf16[256,640]{1,0:T(8,128)(2,1)S(1)}, bf16[256,640]{1,0:T(8,128)(2,1)S(1)}, u32[]{:S(2)}, u32[]{:S(2)}) collective-permute-start(bf16[256,640]{1,0:T(8,128)(2,1)S(1)} %pad_maximum_fusion.3.b0), channel_id=1, source_target_pairs={{0,2},{1,3},{2,0},{3,1},{4,6},{5,7},{6,4},{7,5},{8,10},{9,11},{10,... | collective-permute-start | bytes 983048 | tf_op jit(solution)/shard_map/ppermute | solution.py:506
  11.6 8.6 %collective-permute-start.8 = (bf16[72,768]{1,0:T(8,128)(2,1)S(1)}, bf16[72,768]{1,0:T(8,128)(2,1)S(1)}, u32[]{:S(2)}, u32[]{:S(2)}) collective-permute-start(bf16[72,768]{1,0:T(8,128)(2,1)S(1)} %constant_dynamic-slice_fusion), channel_id=1, source_target_pairs={{0,16},{1,17},{2,18},{3,19},{4,20},{5,21},{6,22},{7,23},{8,24},{9,... | collective-permute-start | bytes 331784 | tf_op jit(solution)/shard_map/ppermute | solution.py:506
  12.5 8.4 %collective-permute-start.4 = (bf16[2,40,960]{2,1,0:T(8,128)(2,1)S(1)}, bf16[2,40,960]{2,1,0:T(8,128)(2,1)S(1)}, u32[]{:S(2)}, u32[]{:S(2)}) collective-permute-start(bf16[2,40,960]{2,1,0:T(8,128)(2,1)S(1)} %pad_maximum_fusion.6), channel_id=1, source_target_pairs={{0,8},{1,9},{2,10},{3,11},{4,12},{5,13},{6,14},{7,15},{8,0},{9,1},... | collective-permute-start | bytes 460808 | tf_op jit(solution)/shard_map/ppermute | solution.py:506
  21.2 20.7 %collective-permute-start.6 = (bf16[2,2,40,960]{3,2,1,0:T(8,128)(2,1)S(1)}, bf16[2,2,40,960]{3,2,1,0:T(8,128)(2,1)S(1)}, u32[]{:S(2)}, u32[]{:S(2)}) collective-permute-start(bf16[2,2,40,960]{3,2,1,0:T(8,128)(2,1)S(1)} %pad_maximum_fusion.4.a00), channel_id=1, source_target_pairs={{0,1},{1,0},{2,3},{3,2},{4,5},{5,4},{6,7},{7,6},{8,9},{9,8},{10,11... | collective-permute-start | bytes 921608 | tf_op jit(solution)/shard_map/ppermute | solution.py:506
  21.3 17.0 %collective-permute-start.5 = (bf16[2,2,40,960]{3,2,1,0:T(8,128)(2,1)S(1)}, bf16[2,2,40,960]{3,2,1,0:T(8,128)(2,1)S(1)}, u32[]{:S(2)}, u32[]{:S(2)}) collective-permute-start(bf16[2,2,40,960]{3,2,1,0:T(8,128)(2,1)S(1)} %pad_maximum_fusion.4.a00), channel_id=1, source_target_pairs={{0,4},{1,5},{2,6},{3,7},{4,0},{5,1},{6,2},{7,3},{8,12},{9,13},{10,... | collective-permute-start | bytes 921608 | tf_op jit(solution)/shard_map/ppermute | solution.py:506
  28.3 9.8 %collective-permute-start.10 = (bf16[136,576]{1,0:T(8,128)(2,1)S(1)}, bf16[136,576]{1,0:T(8,128)(2,1)S(1)}, u32[]{:S(2)}, u32[]{:S(2)}) collective-permute-start(bf16[136,576]{1,0:T(8,128)(2,1)S(1)} %dynamic-slice_bitcast_fusion), channel_id=1, source_target_pairs={{0,16},{1,17},{2,18},{3,19},{4,20},{5,21},{6,22},{7,23},{8,24},{9,... | collective-permute-start | bytes 470024 | tf_op jit(solution)/shard_map/ppermute | solution.py:506
  30.7 8.9 %collective-permute-start.2 = (bf16[256,640]{1,0:T(8,128)(2,1)S(1)}, bf16[256,640]{1,0:T(8,128)(2,1)S(1)}, u32[]{:S(2)}, u32[]{:S(2)}) collective-permute-start(bf16[256,640]{1,0:T(8,128)(2,1)S(1)} %collective-permute-done.b1), channel_id=1, source_target_pairs={{0,1},{1,0},{2,3},{3,2},{4,5},{5,4},{6,7},{7,6},{8,9},{9,8},{10,11... | collective-permute-start | bytes 983048 | tf_op jit(solution)/shard_map/ppermute | solution.py:506
  31.0 23.0 %collective-permute-start.21 = (bf16[2,2,72,768]{3,2,1,0:T(8,128)(2,1)S(1)}, bf16[2,2,72,768]{3,2,1,0:T(8,128)(2,1)}, u32[]{:S(2)}, u32[]{:S(2)}) collective-permute-start(bf16[2,2,72,768]{3,2,1,0:T(8,128)(2,1)S(1)} %pad_maximum_fusion.refs_8_), channel_id=1, source_target_pairs={{0,4},{1,5},{2,6},{3,7},{4,0},{5,1},{6,2},{7,3},{8,12},{9,13},{10,... | collective-permute-start | bytes 1327112 | tf_op jit(solution)/shard_map/ppermute | solution.py:506
  38.2 17.8 %collective-permute-start.19 = (bf16[2,2,72,768]{3,2,1,0:T(8,128)(2,1)S(1)}, bf16[2,2,72,768]{3,2,1,0:T(8,128)(2,1)S(1)}, u32[]{:S(2)}, u32[]{:S(2)}) collective-permute-start(bf16[2,2,72,768]{3,2,1,0:T(8,128)(2,1)S(1)} %pad_maximum_fusion.refs_8_), channel_id=1, source_target_pairs={{0,1},{1,0},{2,3},{3,2},{4,5},{5,4},{6,7},{7,6},{8,9},{9,8},{10,11... | collective-permute-start | bytes 1327112 | tf_op jit(solution)/shard_map/ppermute | solution.py:506
  38.3 15.7 %collective-permute-start.13 = (bf16[2,2,72,768]{3,2,1,0:T(8,128)(2,1)S(1)}, bf16[2,2,72,768]{3,2,1,0:T(8,128)(2,1)}, u32[]{:S(2)}, u32[]{:S(2)}) collective-permute-start(bf16[2,2,72,768]{3,2,1,0:T(8,128)(2,1)S(1)} %pad_maximum_fusion.refs_8_), channel_id=1, source_target_pairs={{0,2},{1,3},{2,0},{3,1},{4,6},{5,7},{6,4},{7,5},{8,10},{9,11},{10,... | collective-permute-start | bytes 1327112 | tf_op jit(solution)/shard_map/ppermute | solution.py:506
  41.3 14.0 %collective-permute-start.15 = (bf16[2,136,576]{2,1,0:T(8,128)(2,1)S(1)}, bf16[2,136,576]{2,1,0:T(8,128)(2,1)}, u32[]{:S(2)}, u32[]{:S(2)}) collective-permute-start(bf16[2,136,576]{2,1,0:T(8,128)(2,1)S(1)} %pad_maximum_fusion.2.refs_0_), channel_id=1, source_target_pairs={{0,8},{1,9},{2,10},{3,11},{4,12},{5,13},{6,14},{7,15},{8,0},{9,1},... | collective-permute-start | bytes 940040 | tf_op jit(solution)/shard_map/ppermute | solution.py:506
  41.9 12.8 %collective-permute-start.12 = (bf16[2,136,576]{2,1,0:T(8,128)(2,1)S(1)}, bf16[2,136,576]{2,1,0:T(8,128)(2,1)S(1)}, u32[]{:S(2)}, u32[]{:S(2)}) collective-permute-start(bf16[2,136,576]{2,1,0:T(8,128)(2,1)S(1)} %pad_maximum_fusion.2.refs_0_), channel_id=1, source_target_pairs={{0,4},{1,5},{2,6},{3,7},{4,0},{5,1},{6,2},{7,3},{8,12},{9,13},{10,... | collective-permute-start | bytes 940040 | tf_op jit(solution)/shard_map/ppermute | solution.py:506
  54.0 12.1 %collective-permute-start.23 = (bf16[2,2,72,768]{3,2,1,0:T(8,128)(2,1)}, bf16[2,2,72,768]{3,2,1,0:T(8,128)(2,1)}, u32[]{:S(2)}, u32[]{:S(2)}) collective-permute-start(bf16[2,2,72,768]{3,2,1,0:T(8,128)(2,1)} %collective-permute-done.21.refs_12_), channel_id=1, source_target_pairs={{0,2},{1,3},{2,0},{3,1},{4,6},{5,7},{6,4},{7,5},{8,10},{9,11},{10,... | collective-permute-start | bytes 1327112 | tf_op jit(solution)/shard_map/ppermute | solution.py:506
  54.7 11.4 %collective-permute-start.14 = (bf16[2,136,576]{2,1,0:T(8,128)(2,1)S(1)}, bf16[2,136,576]{2,1,0:T(8,128)(2,1)S(1)}, u32[]{:S(2)}, u32[]{:S(2)}) collective-permute-start(bf16[2,136,576]{2,1,0:T(8,128)(2,1)S(1)} %collective-permute-done.12.refs_2_), channel_id=1, source_target_pairs={{0,1},{1,0},{2,3},{3,2},{4,5},{5,4},{6,7},{7,6},{8,9},{9,8},{10,11... | collective-permute-start | bytes 940040 | tf_op jit(solution)/shard_map/ppermute | solution.py:506
  55.3 11.4 %collective-permute-start.17 = (bf16[2,136,576]{2,1,0:T(8,128)(2,1)}, bf16[2,136,576]{2,1,0:T(8,128)(2,1)}, u32[]{:S(2)}, u32[]{:S(2)}) collective-permute-start(bf16[2,136,576]{2,1,0:T(8,128)(2,1)} %collective-permute-done.15.refs_4_), channel_id=1, source_target_pairs={{0,4},{1,5},{2,6},{3,7},{4,0},{5,1},{6,2},{7,3},{8,12},{9,13},{10,... | collective-permute-start | bytes 940040 | tf_op jit(solution)/shard_map/ppermute | solution.py:506
  56.0 12.8 %collective-permute-start.22 = (bf16[2,2,72,768]{3,2,1,0:T(8,128)(2,1)}, bf16[2,2,72,768]{3,2,1,0:T(8,128)(2,1)}, u32[]{:S(2)}, u32[]{:S(2)}) collective-permute-start(bf16[2,2,72,768]{3,2,1,0:T(8,128)(2,1)} %collective-permute-done.21.refs_12_), channel_id=1, source_target_pairs={{0,1},{1,0},{2,3},{3,2},{4,5},{5,4},{6,7},{7,6},{8,9},{9,8},{10,11... | collective-permute-start | bytes 1327112 | tf_op jit(solution)/shard_map/ppermute | solution.py:506
  56.4 12.4 %collective-permute-start.20 = (bf16[2,2,72,768]{3,2,1,0:T(8,128)(2,1)}, bf16[2,2,72,768]{3,2,1,0:T(8,128)(2,1)}, u32[]{:S(2)}, u32[]{:S(2)}) collective-permute-start(bf16[2,2,72,768]{3,2,1,0:T(8,128)(2,1)} %collective-permute-done.13.refs_10_), channel_id=1, source_target_pairs={{0,1},{1,0},{2,3},{3,2},{4,5},{5,4},{6,7},{7,6},{8,9},{9,8},{10,11... | collective-permute-start | bytes 1327112 | tf_op jit(solution)/shard_map/ppermute | solution.py:506
  87.3 22.0 %collective-permute-start.36 = (bf16[2,2,2,72,384]{4,3,2,1,0:T(8,128)(2,1)S(1)}, bf16[2,2,2,72,384]{4,3,2,1,0:T(8,128)(2,1)S(1)}, u32[]{:S(2)}, u32[]{:S(2)}) collective-permute-start(bf16[2,2,2,72,384]{4,3,2,1,0:T(8,128)(2,1)S(1)} %get-tuple-element.148), channel_id=1, source_target_pairs={{0,4},{1,5},{2,6},{3,7},{4,0},{5,1},{6,2},{7,3},{8,12},{9,13},{10,... | collective-permute-start | bytes 1327112 | tf_op jit(solution)/shard_map/ppermute | solution.py:506
  90.4 16.6 %collective-permute-start.31 = (bf16[2,2,2,72,384]{4,3,2,1,0:T(8,128)(2,1)S(1)}, bf16[2,2,2,72,384]{4,3,2,1,0:T(8,128)(2,1)S(1)}, u32[]{:S(2)}, u32[]{:S(2)}) collective-permute-start(bf16[2,2,2,72,384]{4,3,2,1,0:T(8,128)(2,1)S(1)} %get-tuple-element.150), channel_id=1, source_target_pairs={{0,8},{1,9},{2,10},{3,11},{4,12},{5,13},{6,14},{7,15},{8,0},{9,1},... | collective-permute-start | bytes 1327112 | tf_op jit(solution)/shard_map/ppermute | solution.py:506
  92.2 18.9 %collective-permute-start.29 = (bf16[2,2,2,72,576]{4,3,2,1,0:T(8,128)(2,1)S(1)}, bf16[2,2,2,72,576]{4,3,2,1,0:T(8,128)(2,1)S(1)}, u32[]{:S(2)}, u32[]{:S(2)}) collective-permute-start(bf16[2,2,2,72,576]{4,3,2,1,0:T(8,128)(2,1)S(1)} %get-tuple-element.146), channel_id=1, source_target_pairs={{0,2},{1,3},{2,0},{3,1},{4,6},{5,7},{6,4},{7,5},{8,10},{9,11},{10,... | collective-permute-start | bytes 1990664 | tf_op jit(solution)/shard_map/ppermute | solution.py:506
  107.2 15.9 %collective-permute-start.34 = (bf16[2,2,72,384]{3,2,1,0:T(8,128)(2,1)S(1)}, bf16[2,2,72,384]{3,2,1,0:T(8,128)(2,1)S(1)}, u32[]{:S(2)}, u32[]{:S(2)}) collective-permute-start(bf16[2,2,72,384]{3,2,1,0:T(8,128)(2,1)S(1)} %get-tuple-element.158), channel_id=1, source_target_pairs={{0,16},{1,17},{2,18},{3,19},{4,20},{5,21},{6,22},{7,23},{8,24},{9,... | collective-permute-start | bytes 663560 | tf_op jit(solution)/shard_map/ppermute | solution.py:506
  109.4 11.7 %collective-permute-start.37 = (bf16[2,2,72,384]{3,2,1,0:T(8,128)(2,1)S(1)}, bf16[2,2,72,384]{3,2,1,0:T(8,128)(2,1)S(1)}, u32[]{:S(2)}, u32[]{:S(2)}) collective-permute-start(bf16[2,2,72,384]{3,2,1,0:T(8,128)(2,1)S(1)} %get-tuple-element.155), channel_id=1, source_target_pairs={{0,8},{1,9},{2,10},{3,11},{4,12},{5,13},{6,14},{7,15},{8,0},{9,1},... | collective-permute-start | bytes 663560 | tf_op jit(solution)/shard_map/ppermute | solution.py:506
  111.3 10.6 %collective-permute-start.35 = (bf16[2,2,2,80,256]{4,3,2,1,0:T(8,128)(2,1)S(1)}, bf16[2,2,2,80,256]{4,3,2,1,0:T(8,128)(2,1)S(1)}, u32[]{:S(2)}, u32[]{:S(2)}) collective-permute-start(bf16[2,2,2,80,256]{4,3,2,1,0:T(8,128)(2,1)S(1)} %get-tuple-element.154), channel_id=1, source_target_pairs={{0,2},{1,3},{2,0},{3,1},{4,6},{5,7},{6,4},{7,5},{8,10},{9,11},{10,... | collective-permute-start | bytes 983048 | tf_op jit(solution)/shard_map/ppermute | solution.py:506
  113.0 11.2 %collective-permute-start.33 = (bf16[2,2,72,576]{3,2,1,0:T(8,128)(2,1)S(1)}, bf16[2,2,72,576]{3,2,1,0:T(8,128)(2,1)S(1)}, u32[]{:S(2)}, u32[]{:S(2)}) collective-permute-start(bf16[2,2,72,576]{3,2,1,0:T(8,128)(2,1)S(1)} %get-tuple-element.152), channel_id=1, source_target_pairs={{0,4},{1,5},{2,6},{3,7},{4,0},{5,1},{6,2},{7,3},{8,12},{9,13},{10,... | collective-permute-start | bytes 995336 | tf_op jit(solution)/shard_map/ppermute | solution.py:506
  114.2 11.6 %collective-permute-start.32 = (bf16[256,384]{1,0:T(8,128)(2,1)S(1)}, bf16[256,384]{1,0:T(8,128)(2,1)S(1)}, u32[]{:S(2)}, u32[]{:S(2)}) collective-permute-start(bf16[256,384]{1,0:T(8,128)(2,1)S(1)} %get-tuple-element.159), channel_id=1, source_target_pairs={{0,2},{1,3},{2,0},{3,1},{4,6},{5,7},{6,4},{7,5},{8,10},{9,11},{10,... | collective-permute-start | bytes 589832 | tf_op jit(solution)/shard_map/ppermute | solution.py:506
  121.1 8.1 %collective-permute-start.38 = (bf16[2,72,384]{2,1,0:T(8,128)(2,1)S(1)}, bf16[2,72,384]{2,1,0:T(8,128)(2,1)S(1)}, u32[]{:S(2)}, u32[]{:S(2)}) collective-permute-start(bf16[2,72,384]{2,1,0:T(8,128)(2,1)S(1)} %fusion.33), channel_id=1, source_target_pairs={{0,16},{1,17},{2,18},{3,19},{4,20},{5,21},{6,22},{7,23},{8,24},{9,... | collective-permute-start | bytes 331784 | tf_op jit(solution)/shard_map/ppermute | solution.py:506
  130.8 9.4 %collective-permute-start.45 = (bf16[2,72,384]{2,1,0:T(8,128)(2,1)S(1)}, bf16[2,72,384]{2,1,0:T(8,128)(2,1)S(1)}, u32[]{:S(2)}, u32[]{:S(2)}) collective-permute-start(bf16[2,72,384]{2,1,0:T(8,128)(2,1)S(1)} %fusion.17), channel_id=1, source_target_pairs={{0,2},{1,3},{2,0},{3,1},{4,6},{5,7},{6,4},{7,5},{8,10},{9,11},{10,... | collective-permute-start | bytes 331784 | tf_op jit(solution)/shard_map/ppermute | solution.py:506
  138.5 9.3 %collective-permute-start.49 = (bf16[72,576]{1,0:T(8,128)(2,1)S(1)}, bf16[72,576]{1,0:T(8,128)(2,1)S(1)}, u32[]{:S(2)}, u32[]{:S(2)}) collective-permute-start(bf16[72,576]{1,0:T(8,128)(2,1)S(1)} %fusion.26.d0), channel_id=1, source_target_pairs={{0,1},{1,0},{2,3},{3,2},{4,5},{5,4},{6,7},{7,6},{8,9},{9,8},{10,11... | collective-permute-start | bytes 248840 | tf_op jit(solution)/shard_map/ppermute | solution.py:506
  140.0 9.2 %collective-permute-start.44 = (bf16[2,72,384]{2,1,0:T(8,128)(2,1)S(1)}, bf16[2,72,384]{2,1,0:T(8,128)(2,1)S(1)}, u32[]{:S(2)}, u32[]{:S(2)}) collective-permute-start(bf16[2,72,384]{2,1,0:T(8,128)(2,1)S(1)} %add_convert_fusion.11.a_near), channel_id=1, source_target_pairs={{0,1},{1,0},{2,3},{3,2},{4,5},{5,4},{6,7},{7,6},{8,9},{9,8},{10,11... | collective-permute-start | bytes 331784 | tf_op jit(solution)/shard_map/ppermute | solution.py:506
  140.2 8.9 %collective-permute-start.46 = (bf16[2,72,384]{2,1,0:T(8,128)(2,1)S(1)}, bf16[2,72,384]{2,1,0:T(8,128)(2,1)S(1)}, u32[]{:S(2)}, u32[]{:S(2)}) collective-permute-start(bf16[2,72,384]{2,1,0:T(8,128)(2,1)S(1)} %add_convert_fusion.10.b_near), channel_id=1, source_target_pairs={{0,1},{1,0},{2,3},{3,2},{4,5},{5,4},{6,7},{7,6},{8,9},{9,8},{10,11... | collective-permute-start | bytes 331784 | tf_op jit(solution)/shard_map/ppermute | solution.py:506
  (51 other events, 357.1 us)

commit v9 on v8

--- a/solution.py
+++ b/solution.py
@@ -813,12 +813,12 @@
     gu_x = net.swap(gu2, xbit)
     gu_y = net.swap(gu2, ybit)
     gu_c = net.swap(gu2, core)
-    b0 = net.half(after(half_b, gu2), core, 0)
-    b1 = net.both(b0, zfar, 0)
-    b_z = net.swap(b1, znear)
+    b0 = net.half(after(half_b, a0), core, 0)
+    b1 = net.both(b0, zfar, 0, after(net.swap(b0, zfar), a2))
     b_x = net.swap(b1, xbit)
+    b_z = net.swap(after(b1, gu2), znear)
     b_c = net.swap(b1, core)
-    a_xc = after(a_xc, b1)
+    a_xc = after(a_xc, b_x)
 
     cos_t, sin_t = rope_tables(full_length, n_seq)
     block_ids = [seq_index ^ o for o in order]
@@ -916,6 +916,7 @@
         ],
         1.4e10,
         [(width, 1024), (1, qkv_w), (1, width), (n_fsdp, 8, 1024)],
+        24,
     )
     b, b_give = halves(b, after(b_got, dq))
     a, a_give = halves(a, after(a_got, b_give))
@@ -960,11 +961,11 @@
     b_far = net.swap(b, core)
     down = add(down, after(down_got, a))
     down_y = net.swap(down, ybit)
-    down_c = net.swap(down, core)
+    down_c = net.swap(after(down, down_y), core)
     rest = add(rest, after(rest_got, down))
     rest_y = net.swap(rest, ybit)
     rest_c = net.swap(after(rest, rest_y), core)
-    down_yc = net.swap(down_y, core)
+    down_yc = net.swap(after(down_y, rest_y), core)
     rest_yc = net.swap(rest_y, core)
     qk, v = (QW + KW) // n_fsdp, KW // n_fsdp
     out_gate, out_down, out_wout, out_qkv, b_qk, b_v, out_gains = call(

time: 151 us -> 148 us (0.980)
  waiting for transfers between devices: 53.2 us -> 49.3 us
  Pallas kernels: 42.6 us -> 40.1 us
  local copies, waits for them, and re-layouts: 4.81 us -> 6.58 us
    ppermute x55, waiting for transfers between devices: 53.2 us -> 49.3 us  [swap(): return lax.ppermute(value, ('fsdp', 'seq'), pairs)]
    pallas_call x5, Pallas kernels: 41.7 us -> 39.2 us  [call(): pl.pallas_call(kernel, out_shape=outs, in_specs=specs, out_specs=whole(*o...]
    unnamed x58 -> x60, local copies, waits for them, and re-layouts: 3.76 us -> 5.53 us
  transfers between devices with their start and end apart: 55 -> 55, of which waited for: 20 -> 18; matrix products, arithmetic and copies ran while one was open for 5% -> 5% of each run, Pallas kernels for 17% -> 16%
where the time goes in v9:
time: 148 us
  waiting for transfers between devices  49.3 us (33%)
  starting transfers between devices  45.2 us (31%)
  Pallas kernels  40.1 us (27%)
  local copies, waits for them, and re-layouts  6.58 us (4%)
  other arithmetic  5.73 us (4%)
    ppermute x55, waiting for transfers between devices, swap(): return lax.ppermute(value, ('fsdp', 'seq'), pairs)  49.3 us
    ppermute x55, starting transfers between devices, swap(): return lax.ppermute(value, ('fsdp', 'seq'), pairs)  45.2 us
    pallas_call x5, Pallas kernels, call(): pl.pallas_call(kernel, out_shape=outs, in_specs=specs, out_specs=whole(*o...  39.2 us
    unnamed x60, local copies, waits for them, and re-layouts  5.53 us
    convert_element_type x21, other arithmetic, add(): return (keep.astype(F32) + got.astype(F32)).astype(BF)  3.25 us
  transfers between devices with their start and end apart: 55, of which 18 were waited for; matrix products, arithmetic and copies ran while one was open for 5% of the time, Pallas kernels for 16%

profile of v9, /device:TPU:0, one launch (start us, length us, event | category | flops | bytes accessed | tf_op | source)
XLA Modules:
  0.0 148.1 jit_solution(941075371033438826)
XLA Ops:
  3.8 4.1 %collective-permute-start.3 = (bf16[40,960]{1,0:T(8,128)(2,1)S(1)}, bf16[40,960]{1,0:T(8,128)(2,1)S(1)}, u32[]{:S(2)}, u32[]{:S(2)}) collective-permute-start(bf16[40,960]{1,0:T(8,128)(2,1)S(1)} %shard_map.187), channel_id=1, source_target_pairs={{0,16},{1,17},{2,18},{3,19},{4,20},{5,21},{6,22},{7,23},{8,24},{9,... | collective-permute-start | bytes 230408 | tf_op jit(solution)/shard_map/ppermute | solution.py:506
  10.0 1.6 %collective-permute-start = (bf16[256,640]{1,0:T(8,128)(2,1)S(1)}, bf16[256,640]{1,0:T(8,128)(2,1)S(1)}, u32[]{:S(2)}, u32[]{:S(2)}) collective-permute-start(bf16[256,640]{1,0:T(8,128)(2,1)S(1)} %pad_maximum_fusion.3.b0), channel_id=1, source_target_pairs={{0,2},{1,3},{2,0},{3,1},{4,6},{5,7},{6,4},{7,5},{8,10},{9,11},{10,... | collective-permute-start | bytes 983048 | tf_op jit(solution)/shard_map/ppermute | solution.py:506
  12.2 2.7 %collective-permute-start.8 = (bf16[136,576]{1,0:T(8,128)(2,1)S(1)}, bf16[136,576]{1,0:T(8,128)(2,1)S(1)}, u32[]{:S(2)}, u32[]{:S(2)}) collective-permute-start(bf16[136,576]{1,0:T(8,128)(2,1)S(1)} %dynamic-slice_bitcast_fusion), channel_id=1, source_target_pairs={{0,16},{1,17},{2,18},{3,19},{4,20},{5,21},{6,22},{7,23},{8,24},{9,... | collective-permute-start | bytes 470024 | tf_op jit(solution)/shard_map/ppermute | solution.py:506
  15.3 1.6 %collective-permute-start.4 = (bf16[2,40,960]{2,1,0:T(8,128)(2,1)S(1)}, bf16[2,40,960]{2,1,0:T(8,128)(2,1)S(1)}, u32[]{:S(2)}, u32[]{:S(2)}) collective-permute-start(bf16[2,40,960]{2,1,0:T(8,128)(2,1)S(1)} %pad_maximum_fusion.6), channel_id=1, source_target_pairs={{0,8},{1,9},{2,10},{3,11},{4,12},{5,13},{6,14},{7,15},{8,0},{9,1},... | collective-permute-start | bytes 460808 | tf_op jit(solution)/shard_map/ppermute | solution.py:506
  17.0 7.6 %collective-permute-done.11 = bf16[72,768]{1,0:T(8,128)(2,1)S(1)} collective-permute-done((bf16[72,768]{1,0:T(8,128)(2,1)S(1)}, bf16[72,768]{1,0:T(8,128)(2,1)S(1)}, u32[]{:S(2)}, u32[]{:S(2)}) %collective-permute-start.11) | collective-permute-done | bytes 110624 | tf_op jit(solution)/shard_map/ppermute | solution.py:506
  24.9 1.6 %collective-permute-start.5 = (bf16[2,2,40,960]{3,2,1,0:T(8,128)(2,1)S(1)}, bf16[2,2,40,960]{3,2,1,0:T(8,128)(2,1)S(1)}, u32[]{:S(2)}, u32[]{:S(2)}) collective-permute-start(bf16[2,2,40,960]{3,2,1,0:T(8,128)(2,1)S(1)} %pad_maximum_fusion.4.a00), channel_id=1, source_target_pairs={{0,4},{1,5},{2,6},{3,7},{4,0},{5,1},{6,2},{7,3},{8,12},{9,13},{10,... | collective-permute-start | bytes 921608 | tf_op jit(solution)/shard_map/ppermute | solution.py:506
  27.7 1.6 %collective-permute-start.9 = (bf16[2,136,576]{2,1,0:T(8,128)(2,1)S(1)}, bf16[2,136,576]{2,1,0:T(8,128)(2,1)S(1)}, u32[]{:S(2)}, u32[]{:S(2)}) collective-permute-start(bf16[2,136,576]{2,1,0:T(8,128)(2,1)S(1)} %pad_maximum_fusion.2.refs_0_), channel_id=1, source_target_pairs={{0,4},{1,5},{2,6},{3,7},{4,0},{5,1},{6,2},{7,3},{8,12},{9,13},{10,... | collective-permute-start | bytes 940040 | tf_op jit(solution)/shard_map/ppermute | solution.py:506
  29.7 4.5 %collective-permute-done.12 = bf16[2,72,768]{2,1,0:T(8,128)(2,1)S(1)} collective-permute-done((bf16[2,72,768]{2,1,0:T(8,128)(2,1)S(1)}, bf16[2,72,768]{2,1,0:T(8,128)(2,1)S(1)}, u32[]{:S(2)}, u32[]{:S(2)}) %collective-permute-start.12) | collective-permute-done | bytes 221216 | tf_op jit(solution)/shard_map/ppermute | solution.py:506
  34.3 1.6 %collective-permute-start.21 = (bf16[2,2,72,768]{3,2,1,0:T(8,128)(2,1)S(1)}, bf16[2,2,72,768]{3,2,1,0:T(8,128)(2,1)}, u32[]{:S(2)}, u32[]{:S(2)}) collective-permute-start(bf16[2,2,72,768]{3,2,1,0:T(8,128)(2,1)S(1)} %pad_maximum_fusion.refs_8_), channel_id=1, source_target_pairs={{0,4},{1,5},{2,6},{3,7},{4,0},{5,1},{6,2},{7,3},{8,12},{9,13},{10,... | collective-permute-start | bytes 1327112 | tf_op jit(solution)/shard_map/ppermute | solution.py:506
  37.6 5.4 %collective-permute-done.9.refs_2_ = bf16[2,136,576]{2,1,0:T(8,128)(2,1)S(1)} collective-permute-done((bf16[2,136,576]{2,1,0:T(8,128)(2,1)S(1)}, bf16[2,136,576]{2,1,0:T(8,128)(2,1)S(1)}, u32[]{:S(2)}, u32[]{:S(2)}) %collective-permute-start.9) | collective-permute-done | bytes 313376 | tf_op jit(solution)/shard_map/ppermute | solution.py:506
  44.9 10.7 %shard_map.188 = (bf16[256,576]{1,0:T(8,128)(2,1)S(1)}, bf16[2,3,384,64]{3,2,1,0:T(8,128)(2,1)}, bf16[2,3,512,64]{3,2,1,0:T(8,128)(2,1)}, bf16[2,3,512,64]{3,2,1...) custom-call(s32[2]{0:T(128)S(1)} %pad_add_fusion.meta, bf16[256,640]{1,0:T(8,128)(2,1)S(1)} %pad_maximum_fusion.3.b0, ...), custom_call_target="tpu_custom_call" | custom-call | flops 12000000000 | bytes 6074880 | tf_op jit(solution)/shard_map/pallas_call | solution.py:55
  55.6 1.6 %collective-permute-start.23 = (bf16[2,2,72,768]{3,2,1,0:T(8,128)(2,1)}, bf16[2,2,72,768]{3,2,1,0:T(8,128)(2,1)}, u32[]{:S(2)}, u32[]{:S(2)}) collective-permute-start(bf16[2,2,72,768]{3,2,1,0:T(8,128)(2,1)} %collective-permute-done.21.refs_12_), channel_id=1, source_target_pairs={{0,2},{1,3},{2,0},{3,1},{4,6},{5,7},{6,4},{7,5},{8,10},{9,11},{10,... | collective-permute-start | bytes 1327112 | tf_op jit(solution)/shard_map/ppermute | solution.py:506
  57.7 1.5 %collective-permute-start.17 = (bf16[2,136,576]{2,1,0:T(8,128)(2,1)}, bf16[2,136,576]{2,1,0:T(8,128)(2,1)}, u32[]{:S(2)}, u32[]{:S(2)}) collective-permute-start(bf16[2,136,576]{2,1,0:T(8,128)(2,1)} %collective-permute-done.15.refs_4_), channel_id=1, source_target_pairs={{0,4},{1,5},{2,6},{3,7},{4,0},{5,1},{6,2},{7,3},{8,12},{9,13},{10,... | collective-permute-start | bytes 940040 | tf_op jit(solution)/shard_map/ppermute | solution.py:506
  59.8 7.3 %collective-permute-done.23.refs_14_ = bf16[2,2,72,768]{3,2,1,0:T(8,128)(2,1)} collective-permute-done((bf16[2,2,72,768]{3,2,1,0:T(8,128)(2,1)}, bf16[2,2,72,768]{3,2,1,0:T(8,128)(2,1)}, u32[]{:S(2)}, u32[]{:S(2)}) %collective-permute-start.23) | collective-permute-done | bytes 442400 | tf_op jit(solution)/shard_map/ppermute | solution.py:506
  70.2 13.4 %shard_map.189 = (bf16[2,576,128]{2,1,0:T(8,128)(2,1)}, bf16[2,2,2,2,72,384]{5,4,3,2,1,0:T(8,128)(2,1)}, bf16[2,2,2,2,72,384]{5,4,3,2,1,0:T(8,128)(2,1)}, bf16[2...) custom-call(s32[2]{0:T(128)S(1)} %pad_add_fusion.meta, ...), custom_call_target="tpu_custom_call" | custom-call | flops 14000000000 | bytes 14311168 | tf_op jit(solution)/shard_map/pallas_call | solution.py:55
  83.8 2.5 %collective-permute-done.25 = bf16[2,2,2,2,72,384]{5,4,3,2,1,0:T(8,128)(2,1)S(1)} collective-permute-done((bf16[2,2,2,2,72,384]{5,4,3,2,1,0:T(8,128)(2,1)}, bf16[2,2,2,2,72,384]{5,4,3,2,1,0:T(8,128)(2,1)S(1)}, u32[]{:S(2)}, u32[]{:S(2)}) %collective-permute-start.25) | collective-permute-done | bytes 884768 | tf_op jit(solution)/shard_map/ppermute | solution.py:506
  86.8 1.4 add_convert_fusion.2
  88.3 1.6 %collective-permute-start.36 = (bf16[2,2,2,72,384]{4,3,2,1,0:T(8,128)(2,1)S(1)}, bf16[2,2,2,72,384]{4,3,2,1,0:T(8,128)(2,1)S(1)}, u32[]{:S(2)}, u32[]{:S(2)}) collective-permute-start(bf16[2,2,2,72,384]{4,3,2,1,0:T(8,128)(2,1)S(1)} %get-tuple-element.156), channel_id=1, source_target_pairs={{0,4},{1,5},{2,6},{3,7},{4,0},{5,1},{6,2},{7,3},{8,12},{9,13},{10,... | collective-permute-start | bytes 1327112 | tf_op jit(solution)/shard_map/ppermute | solution.py:506
  91.3 1.4 collective-permute-start.31
  94.8 11.2 %shard_map.190 = (bf16[256,640]{1,0:T(8,128)(2,1)S(1)}, bf16[2,256,384]{2,1,0:T(8,128)(2,1)S(1)}, bf16[2,256,384]{2,1,0:T(8,128)(2,1)S(1)}, bf16[2,2,2,2,80,256]...) custom-call(s32[2]{0:T(128)S(1)} %pad_add_fusion.meta, bf16[256,640]{1,0:T(8,128)(2,1)S(1)} %pad_maximum_fusion.3.b0, ...), custom_call_target="tpu_custom_call" | custom-call | flops 14000000000 | bytes 7273216 | tf_op jit(solution)/shard_map/pallas_call | solution.py:55
  106.3 1.9 %collective-permute-start.34 = (bf16[2,2,72,384]{3,2,1,0:T(8,128)(2,1)S(1)}, bf16[2,2,72,384]{3,2,1,0:T(8,128)(2,1)S(1)}, u32[]{:S(2)}, u32[]{:S(2)}) collective-permute-start(bf16[2,2,72,384]{3,2,1,0:T(8,128)(2,1)S(1)} %get-tuple-element.166), channel_id=1, source_target_pairs={{0,16},{1,17},{2,18},{3,19},{4,20},{5,21},{6,22},{7,23},{8,24},{9,... | collective-permute-start | bytes 663560 | tf_op jit(solution)/shard_map/ppermute | solution.py:506
  109.1 2.4 %collective-permute-done.29 = bf16[2,2,2,72,576]{4,3,2,1,0:T(8,128)(2,1)S(1)} collective-permute-done((bf16[2,2,2,72,576]{4,3,2,1,0:T(8,128)(2,1)S(1)}, bf16[2,2,2,72,576]{4,3,2,1,0:T(8,128)(2,1)S(1)}, u32[]{:S(2)}, u32[]{:S(2)}) %collective-permute-start.29) | collective-permute-done | bytes 663584 | tf_op jit(solution)/shard_map/ppermute | solution.py:506
  113.1 1.6 %collective-permute-start.33 = (bf16[2,2,72,576]{3,2,1,0:T(8,128)(2,1)S(1)}, bf16[2,2,72,576]{3,2,1,0:T(8,128)(2,1)S(1)}, u32[]{:S(2)}, u32[]{:S(2)}) collective-permute-start(bf16[2,2,72,576]{3,2,1,0:T(8,128)(2,1)S(1)} %get-tuple-element.160), channel_id=1, source_target_pairs={{0,4},{1,5},{2,6},{3,7},{4,0},{5,1},{6,2},{7,3},{8,12},{9,13},{10,... | collective-permute-start | bytes 995336 | tf_op jit(solution)/shard_map/ppermute | solution.py:506
  115.6 4.8 %collective-permute-done.37 = bf16[2,2,72,384]{3,2,1,0:T(8,128)(2,1)S(1)} collective-permute-done((bf16[2,2,72,384]{3,2,1,0:T(8,128)(2,1)S(1)}, bf16[2,2,72,384]{3,2,1,0:T(8,128)(2,1)S(1)}, u32[]{:S(2)}, u32[]{:S(2)}) %collective-permute-start.37) | collective-permute-done | bytes 221216 | tf_op jit(solution)/shard_map/ppermute | solution.py:506
  120.6 1.7 %collective-permute-done.35 = bf16[2,2,2,80,256]{4,3,2,1,0:T(8,128)(2,1)S(1)} collective-permute-done((bf16[2,2,2,80,256]{4,3,2,1,0:T(8,128)(2,1)S(1)}, bf16[2,2,2,80,256]{4,3,2,1,0:T(8,128)(2,1)S(1)}, u32[]{:S(2)}, u32[]{:S(2)}) %collective-permute-start.35) | collective-permute-done | bytes 327712 | tf_op jit(solution)/shard_map/ppermute | solution.py:506
  122.4 1.6 %collective-permute-start.39 = (bf16[2,2,80,256]{3,2,1,0:T(8,128)(2,1)S(1)}, bf16[2,2,80,256]{3,2,1,0:T(8,128)(2,1)S(1)}, u32[]{:S(2)}, u32[]{:S(2)}) collective-permute-start(bf16[2,2,80,256]{3,2,1,0:T(8,128)(2,1)S(1)} %get-tuple-element.172), channel_id=1, source_target_pairs={{0,4},{1,5},{2,6},{3,7},{4,0},{5,1},{6,2},{7,3},{8,12},{9,13},{10,... | collective-permute-start | bytes 491528 | tf_op jit(solution)/shard_map/ppermute | solution.py:506
  125.5 1.9 %shard_map.191 = f32[2,576,128]{2,1,0:T(8,128)} custom-call(bf16[256,640]{1,0:T(8,128)(2,1)S(1)} %get-tuple-element.101.dq, bf16[256,384]{1,0:T(8,128)(2,1)S(1)} %get-tuple-element.168.own, bf16[256,384]{1,0:T(8,128)(2,1)S(1)} %collective-permute-done.32.other, bf16[256,576]{1,0:T(8,128)(2,1)S(1)} %bitcast.211, f32[256,576]{1,0:T(8,128)S(1)} %copy-done.9, ...), custom_call_target="tpu_custom_call" | custom-call | flops 3000000000 | bytes 3305984 | tf_op jit(solution)/shard_map/pallas_call | solution.py:55
  128.9 1.3 collective-permute-start.40
  131.2 2.0 %collective-permute-start.47 = (bf16[72,576]{1,0:T(8,128)(2,1)S(1)}, bf16[72,576]{1,0:T(8,128)(2,1)S(1)}, u32[]{:S(2)}, u32[]{:S(2)}) collective-permute-start(bf16[72,576]{1,0:T(8,128)(2,1)S(1)} %fusion.36), channel_id=1, source_target_pairs={{0,16},{1,17},{2,18},{3,19},{4,20},{5,21},{6,22},{7,23},{8,24},{9,... | collective-permute-start | bytes 248840 | tf_op jit(solution)/shard_map/ppermute | solution.py:506
  134.4 3.3 %collective-permute-done.47 = bf16[72,576]{1,0:T(8,128)(2,1)S(1)} collective-permute-done((bf16[72,576]{1,0:T(8,128)(2,1)S(1)}, bf16[72,576]{1,0:T(8,128)(2,1)S(1)}, u32[]{:S(2)}, u32[]{:S(2)}) %collective-permute-start.47) | collective-permute-done | bytes 82976 | tf_op jit(solution)/shard_map/ppermute | solution.py:506
  140.5 2.6 %collective-permute-done.51.r1 = bf16[80,256]{1,0:T(8,128)(2,1)S(1)} collective-permute-done((bf16[80,256]{1,0:T(8,128)(2,1)S(1)}, bf16[80,256]{1,0:T(8,128)(2,1)S(1)}, u32[]{:S(2)}, u32[]{:S(2)}) %collective-permute-start.51) | collective-permute-done | bytes 40992 | tf_op jit(solution)/shard_map/ppermute | solution.py:506
  146.1 1.9 %shard_map.192 = (f32[72,3072]{1,0:T(8,128)}, f32[192,576]{1,0:T(8,128)}, f32[72,576]{1,0:T(8,128)}, f32[72,960]{1,0:T(8,128)}, f32[1,96]{1,0:T(1,128)}, /*index=5*/f32[1,24]{1,0:T(1,128)}, f32[2,72]{1,0:T(2,128)}) custom-call(s32[2]{0:T(128)S(1)} %pad_add_fusion.meta, bf16[2,72,384]{2,1,0:T(8,128)(2,1)S(1)} %add_convert_fusion.11.a_near, ...), custom_call_target="tpu_custom_call" | custom-call | flops 3000000000 | bytes 2708512 | tf_op jit(solution)/shard_map/pallas_call | solution.py:55
  (196 shorter events, 35.1 us)
Async XLA Ops:
  3.8 11.5 %collective-permute-start.3 = (bf16[40,960]{1,0:T(8,128)(2,1)S(1)}, bf16[40,960]{1,0:T(8,128)(2,1)S(1)}, u32[]{:S(2)}, u32[]{:S(2)}) collective-permute-start(bf16[40,960]{1,0:T(8,128)(2,1)S(1)} %shard_map.187), channel_id=1, source_target_pairs={{0,16},{1,17},{2,18},{3,19},{4,20},{5,21},{6,22},{7,23},{8,24},{9,... | collective-permute-start | bytes 230408 | tf_op jit(solution)/shard_map/ppermute | solution.py:506
  10.0 19.5 %collective-permute-start.1 = (bf16[256,640]{1,0:T(8,128)(2,1)S(1)}, bf16[256,640]{1,0:T(8,128)(2,1)S(1)}, u32[]{:S(2)}, u32[]{:S(2)}) collective-permute-start(bf16[256,640]{1,0:T(8,128)(2,1)S(1)} %pad_maximum_fusion.3.b0), channel_id=1, source_target_pairs={{0,1},{1,0},{2,3},{3,2},{4,5},{5,4},{6,7},{7,6},{8,9},{9,8},{10,11... | collective-permute-start | bytes 983048 | tf_op jit(solution)/shard_map/ppermute | solution.py:506
  10.0 17.7 %collective-permute-start = (bf16[256,640]{1,0:T(8,128)(2,1)S(1)}, bf16[256,640]{1,0:T(8,128)(2,1)S(1)}, u32[]{:S(2)}, u32[]{:S(2)}) collective-permute-start(bf16[256,640]{1,0:T(8,128)(2,1)S(1)} %pad_maximum_fusion.3.b0), channel_id=1, source_target_pairs={{0,2},{1,3},{2,0},{3,1},{4,6},{5,7},{6,4},{7,5},{8,10},{9,11},{10,... | collective-permute-start | bytes 983048 | tf_op jit(solution)/shard_map/ppermute | solution.py:506
  11.6 13.0 %collective-permute-start.11 = (bf16[72,768]{1,0:T(8,128)(2,1)S(1)}, bf16[72,768]{1,0:T(8,128)(2,1)S(1)}, u32[]{:S(2)}, u32[]{:S(2)}) collective-permute-start(bf16[72,768]{1,0:T(8,128)(2,1)S(1)} %constant_dynamic-slice_fusion), channel_id=1, source_target_pairs={{0,16},{1,17},{2,18},{3,19},{4,20},{5,21},{6,22},{7,23},{8,24},{9,... | collective-permute-start | bytes 331784 | tf_op jit(solution)/shard_map/ppermute | solution.py:506
  12.2 15.4 %collective-permute-start.8 = (bf16[136,576]{1,0:T(8,128)(2,1)S(1)}, bf16[136,576]{1,0:T(8,128)(2,1)S(1)}, u32[]{:S(2)}, u32[]{:S(2)}) collective-permute-start(bf16[136,576]{1,0:T(8,128)(2,1)S(1)} %dynamic-slice_bitcast_fusion), channel_id=1, source_target_pairs={{0,16},{1,17},{2,18},{3,19},{4,20},{5,21},{6,22},{7,23},{8,24},{9,... | collective-permute-start | bytes 470024 | tf_op jit(solution)/shard_map/ppermute | solution.py:506
  15.3 9.4 %collective-permute-start.4 = (bf16[2,40,960]{2,1,0:T(8,128)(2,1)S(1)}, bf16[2,40,960]{2,1,0:T(8,128)(2,1)S(1)}, u32[]{:S(2)}, u32[]{:S(2)}) collective-permute-start(bf16[2,40,960]{2,1,0:T(8,128)(2,1)S(1)} %pad_maximum_fusion.6), channel_id=1, source_target_pairs={{0,8},{1,9},{2,10},{3,11},{4,12},{5,13},{6,14},{7,15},{8,0},{9,1},... | collective-permute-start | bytes 460808 | tf_op jit(solution)/shard_map/ppermute | solution.py:506
  24.8 18.6 %collective-permute-start.6 = (bf16[2,2,40,960]{3,2,1,0:T(8,128)(2,1)S(1)}, bf16[2,2,40,960]{3,2,1,0:T(8,128)(2,1)S(1)}, u32[]{:S(2)}, u32[]{:S(2)}) collective-permute-start(bf16[2,2,40,960]{3,2,1,0:T(8,128)(2,1)S(1)} %pad_maximum_fusion.4.a00), channel_id=1, source_target_pairs={{0,1},{1,0},{2,3},{3,2},{4,5},{5,4},{6,7},{7,6},{8,9},{9,8},{10,11... | collective-permute-start | bytes 921608 | tf_op jit(solution)/shard_map/ppermute | solution.py:506
  24.9 11.0 %collective-permute-start.5 = (bf16[2,2,40,960]{3,2,1,0:T(8,128)(2,1)S(1)}, bf16[2,2,40,960]{3,2,1,0:T(8,128)(2,1)S(1)}, u32[]{:S(2)}, u32[]{:S(2)}) collective-permute-start(bf16[2,2,40,960]{3,2,1,0:T(8,128)(2,1)S(1)} %pad_maximum_fusion.4.a00), channel_id=1, source_target_pairs={{0,4},{1,5},{2,6},{3,7},{4,0},{5,1},{6,2},{7,3},{8,12},{9,13},{10,... | collective-permute-start | bytes 921608 | tf_op jit(solution)/shard_map/ppermute | solution.py:506
  27.6 6.6 %collective-permute-start.12 = (bf16[2,72,768]{2,1,0:T(8,128)(2,1)S(1)}, bf16[2,72,768]{2,1,0:T(8,128)(2,1)S(1)}, u32[]{:S(2)}, u32[]{:S(2)}) collective-permute-start(bf16[2,72,768]{2,1,0:T(8,128)(2,1)S(1)} %pad_maximum_fusion.5), channel_id=1, source_target_pairs={{0,8},{1,9},{2,10},{3,11},{4,12},{5,13},{6,14},{7,15},{8,0},{9,1},... | collective-permute-start | bytes 663560 | tf_op jit(solution)/shard_map/ppermute | solution.py:506
  27.7 15.2 %collective-permute-start.9 = (bf16[2,136,576]{2,1,0:T(8,128)(2,1)S(1)}, bf16[2,136,576]{2,1,0:T(8,128)(2,1)S(1)}, u32[]{:S(2)}, u32[]{:S(2)}) collective-permute-start(bf16[2,136,576]{2,1,0:T(8,128)(2,1)S(1)} %pad_maximum_fusion.2.refs_0_), channel_id=1, source_target_pairs={{0,4},{1,5},{2,6},{3,7},{4,0},{5,1},{6,2},{7,3},{8,12},{9,13},{10,... | collective-permute-start | bytes 940040 | tf_op jit(solution)/shard_map/ppermute | solution.py:506
  29.5 6.4 %collective-permute-start.2 = (bf16[256,640]{1,0:T(8,128)(2,1)S(1)}, bf16[256,640]{1,0:T(8,128)(2,1)S(1)}, u32[]{:S(2)}, u32[]{:S(2)}) collective-permute-start(bf16[256,640]{1,0:T(8,128)(2,1)S(1)} %collective-permute-done.b1), channel_id=1, source_target_pairs={{0,1},{1,0},{2,3},{3,2},{4,5},{5,4},{6,7},{7,6},{8,9},{9,8},{10,11... | collective-permute-start | bytes 983048 | tf_op jit(solution)/shard_map/ppermute | solution.py:506
  34.3 21.3 %collective-permute-start.21 = (bf16[2,2,72,768]{3,2,1,0:T(8,128)(2,1)S(1)}, bf16[2,2,72,768]{3,2,1,0:T(8,128)(2,1)}, u32[]{:S(2)}, u32[]{:S(2)}) collective-permute-start(bf16[2,2,72,768]{3,2,1,0:T(8,128)(2,1)S(1)} %pad_maximum_fusion.refs_8_), channel_id=1, source_target_pairs={{0,4},{1,5},{2,6},{3,7},{4,0},{5,1},{6,2},{7,3},{8,12},{9,13},{10,... | collective-permute-start | bytes 1327112 | tf_op jit(solution)/shard_map/ppermute | solution.py:506
  35.9 23.4 %collective-permute-start.19 = (bf16[2,2,72,768]{3,2,1,0:T(8,128)(2,1)S(1)}, bf16[2,2,72,768]{3,2,1,0:T(8,128)(2,1)S(1)}, u32[]{:S(2)}, u32[]{:S(2)}) collective-permute-start(bf16[2,2,72,768]{3,2,1,0:T(8,128)(2,1)S(1)} %pad_maximum_fusion.refs_8_), channel_id=1, source_target_pairs={{0,1},{1,0},{2,3},{3,2},{4,5},{5,4},{6,7},{7,6},{8,9},{9,8},{10,11... | collective-permute-start | bytes 1327112 | tf_op jit(solution)/shard_map/ppermute | solution.py:506
  35.9 7.5 %collective-permute-start.7 = (bf16[2,2,40,960]{3,2,1,0:T(8,128)(2,1)S(1)}, bf16[2,2,40,960]{3,2,1,0:T(8,128)(2,1)S(1)}, u32[]{:S(2)}, u32[]{:S(2)}) collective-permute-start(bf16[2,2,40,960]{3,2,1,0:T(8,128)(2,1)S(1)} %collective-permute-done.5.a10), channel_id=1, source_target_pairs={{0,1},{1,0},{2,3},{3,2},{4,5},{5,4},{6,7},{7,6},{8,9},{9,8},{10,11... | collective-permute-start | bytes 921608 | tf_op jit(solution)/shard_map/ppermute | solution.py:506
  42.9 12.7 %collective-permute-start.13 = (bf16[2,2,72,768]{3,2,1,0:T(8,128)(2,1)S(1)}, bf16[2,2,72,768]{3,2,1,0:T(8,128)(2,1)}, u32[]{:S(2)}, u32[]{:S(2)}) collective-permute-start(bf16[2,2,72,768]{3,2,1,0:T(8,128)(2,1)S(1)} %pad_maximum_fusion.refs_8_), channel_id=1, source_target_pairs={{0,2},{1,3},{2,0},{3,1},{4,6},{5,7},{6,4},{7,5},{8,10},{9,11},{10,... | collective-permute-start | bytes 1327112 | tf_op jit(solution)/shard_map/ppermute | solution.py:506
  43.4 14.3 %collective-permute-start.15 = (bf16[2,136,576]{2,1,0:T(8,128)(2,1)S(1)}, bf16[2,136,576]{2,1,0:T(8,128)(2,1)}, u32[]{:S(2)}, u32[]{:S(2)}) collective-permute-start(bf16[2,136,576]{2,1,0:T(8,128)(2,1)S(1)} %pad_maximum_fusion.2.refs_0_), channel_id=1, source_target_pairs={{0,8},{1,9},{2,10},{3,11},{4,12},{5,13},{6,14},{7,15},{8,0},{9,1},... | collective-permute-start | bytes 940040 | tf_op jit(solution)/shard_map/ppermute | solution.py:506
  55.6 11.4 %collective-permute-start.23 = (bf16[2,2,72,768]{3,2,1,0:T(8,128)(2,1)}, bf16[2,2,72,768]{3,2,1,0:T(8,128)(2,1)}, u32[]{:S(2)}, u32[]{:S(2)}) collective-permute-start(bf16[2,2,72,768]{3,2,1,0:T(8,128)(2,1)} %collective-permute-done.21.refs_12_), channel_id=1, source_target_pairs={{0,2},{1,3},{2,0},{3,1},{4,6},{5,7},{6,4},{7,5},{8,10},{9,11},{10,... | collective-permute-start | bytes 1327112 | tf_op jit(solution)/shard_map/ppermute | solution.py:506
  57.2 9.8 %collective-permute-start.14 = (bf16[2,136,576]{2,1,0:T(8,128)(2,1)S(1)}, bf16[2,136,576]{2,1,0:T(8,128)(2,1)S(1)}, u32[]{:S(2)}, u32[]{:S(2)}) collective-permute-start(bf16[2,136,576]{2,1,0:T(8,128)(2,1)S(1)} %collective-permute-done.9.refs_2_), channel_id=1, source_target_pairs={{0,1},{1,0},{2,3},{3,2},{4,5},{5,4},{6,7},{7,6},{8,9},{9,8},{10,11... | collective-permute-start | bytes 940040 | tf_op jit(solution)/shard_map/ppermute | solution.py:506
  57.7 10.4 %collective-permute-start.17 = (bf16[2,136,576]{2,1,0:T(8,128)(2,1)}, bf16[2,136,576]{2,1,0:T(8,128)(2,1)}, u32[]{:S(2)}, u32[]{:S(2)}) collective-permute-start(bf16[2,136,576]{2,1,0:T(8,128)(2,1)} %collective-permute-done.15.refs_4_), channel_id=1, source_target_pairs={{0,4},{1,5},{2,6},{3,7},{4,0},{5,1},{6,2},{7,3},{8,12},{9,13},{10,... | collective-permute-start | bytes 940040 | tf_op jit(solution)/shard_map/ppermute | solution.py:506
  59.3 10.4 %collective-permute-start.22 = (bf16[2,2,72,768]{3,2,1,0:T(8,128)(2,1)}, bf16[2,2,72,768]{3,2,1,0:T(8,128)(2,1)}, u32[]{:S(2)}, u32[]{:S(2)}) collective-permute-start(bf16[2,2,72,768]{3,2,1,0:T(8,128)(2,1)} %collective-permute-done.21.refs_12_), channel_id=1, source_target_pairs={{0,1},{1,0},{2,3},{3,2},{4,5},{5,4},{6,7},{7,6},{8,9},{9,8},{10,11... | collective-permute-start | bytes 1327112 | tf_op jit(solution)/shard_map/ppermute | solution.py:506
  59.3 10.4 %collective-permute-start.20 = (bf16[2,2,72,768]{3,2,1,0:T(8,128)(2,1)}, bf16[2,2,72,768]{3,2,1,0:T(8,128)(2,1)}, u32[]{:S(2)}, u32[]{:S(2)}) collective-permute-start(bf16[2,2,72,768]{3,2,1,0:T(8,128)(2,1)} %collective-permute-done.13.refs_10_), channel_id=1, source_target_pairs={{0,1},{1,0},{2,3},{3,2},{4,5},{5,4},{6,7},{7,6},{8,9},{9,8},{10,11... | collective-permute-start | bytes 1327112 | tf_op jit(solution)/shard_map/ppermute | solution.py:506
  88.3 19.9 %collective-permute-start.36 = (bf16[2,2,2,72,384]{4,3,2,1,0:T(8,128)(2,1)S(1)}, bf16[2,2,2,72,384]{4,3,2,1,0:T(8,128)(2,1)S(1)}, u32[]{:S(2)}, u32[]{:S(2)}) collective-permute-start(bf16[2,2,2,72,384]{4,3,2,1,0:T(8,128)(2,1)S(1)} %get-tuple-element.156), channel_id=1, source_target_pairs={{0,4},{1,5},{2,6},{3,7},{4,0},{5,1},{6,2},{7,3},{8,12},{9,13},{10,... | collective-permute-start | bytes 1327112 | tf_op jit(solution)/shard_map/ppermute | solution.py:506
  91.3 14.8 %collective-permute-start.31 = (bf16[2,2,2,72,384]{4,3,2,1,0:T(8,128)(2,1)S(1)}, bf16[2,2,2,72,384]{4,3,2,1,0:T(8,128)(2,1)S(1)}, u32[]{:S(2)}, u32[]{:S(2)}) collective-permute-start(bf16[2,2,2,72,384]{4,3,2,1,0:T(8,128)(2,1)S(1)} %get-tuple-element.158), channel_id=1, source_target_pairs={{0,8},{1,9},{2,10},{3,11},{4,12},{5,13},{6,14},{7,15},{8,0},{9,1},... | collective-permute-start | bytes 1327112 | tf_op jit(solution)/shard_map/ppermute | solution.py:506
  93.1 18.3 %collective-permute-start.29 = (bf16[2,2,2,72,576]{4,3,2,1,0:T(8,128)(2,1)S(1)}, bf16[2,2,2,72,576]{4,3,2,1,0:T(8,128)(2,1)S(1)}, u32[]{:S(2)}, u32[]{:S(2)}) collective-permute-start(bf16[2,2,2,72,576]{4,3,2,1,0:T(8,128)(2,1)S(1)} %get-tuple-element.154), channel_id=1, source_target_pairs={{0,2},{1,3},{2,0},{3,1},{4,6},{5,7},{6,4},{7,5},{8,10},{9,11},{10,... | collective-permute-start | bytes 1990664 | tf_op jit(solution)/shard_map/ppermute | solution.py:506
  106.3 17.7 %collective-permute-start.34 = (bf16[2,2,72,384]{3,2,1,0:T(8,128)(2,1)S(1)}, bf16[2,2,72,384]{3,2,1,0:T(8,128)(2,1)S(1)}, u32[]{:S(2)}, u32[]{:S(2)}) collective-permute-start(bf16[2,2,72,384]{3,2,1,0:T(8,128)(2,1)S(1)} %get-tuple-element.166), channel_id=1, source_target_pairs={{0,16},{1,17},{2,18},{3,19},{4,20},{5,21},{6,22},{7,23},{8,24},{9,... | collective-permute-start | bytes 663560 | tf_op jit(solution)/shard_map/ppermute | solution.py:506
  108.3 12.1 %collective-permute-start.37 = (bf16[2,2,72,384]{3,2,1,0:T(8,128)(2,1)S(1)}, bf16[2,2,72,384]{3,2,1,0:T(8,128)(2,1)S(1)}, u32[]{:S(2)}, u32[]{:S(2)}) collective-permute-start(bf16[2,2,72,384]{3,2,1,0:T(8,128)(2,1)S(1)} %get-tuple-element.163), channel_id=1, source_target_pairs={{0,8},{1,9},{2,10},{3,11},{4,12},{5,13},{6,14},{7,15},{8,0},{9,1},... | collective-permute-start | bytes 663560 | tf_op jit(solution)/shard_map/ppermute | solution.py:506
  111.6 10.7 %collective-permute-start.35 = (bf16[2,2,2,80,256]{4,3,2,1,0:T(8,128)(2,1)S(1)}, bf16[2,2,2,80,256]{4,3,2,1,0:T(8,128)(2,1)S(1)}, u32[]{:S(2)}, u32[]{:S(2)}) collective-permute-start(bf16[2,2,2,80,256]{4,3,2,1,0:T(8,128)(2,1)S(1)} %get-tuple-element.162), channel_id=1, source_target_pairs={{0,2},{1,3},{2,0},{3,1},{4,6},{5,7},{6,4},{7,5},{8,10},{9,11},{10,... | collective-permute-start | bytes 983048 | tf_op jit(solution)/shard_map/ppermute | solution.py:506
  113.1 11.5 %collective-permute-start.33 = (bf16[2,2,72,576]{3,2,1,0:T(8,128)(2,1)S(1)}, bf16[2,2,72,576]{3,2,1,0:T(8,128)(2,1)S(1)}, u32[]{:S(2)}, u32[]{:S(2)}) collective-permute-start(bf16[2,2,72,576]{3,2,1,0:T(8,128)(2,1)S(1)} %get-tuple-element.160), channel_id=1, source_target_pairs={{0,4},{1,5},{2,6},{3,7},{4,0},{5,1},{6,2},{7,3},{8,12},{9,13},{10,... | collective-permute-start | bytes 995336 | tf_op jit(solution)/shard_map/ppermute | solution.py:506
  114.8 10.7 %collective-permute-start.32 = (bf16[256,384]{1,0:T(8,128)(2,1)S(1)}, bf16[256,384]{1,0:T(8,128)(2,1)S(1)}, u32[]{:S(2)}, u32[]{:S(2)}) collective-permute-start(bf16[256,384]{1,0:T(8,128)(2,1)S(1)} %get-tuple-element.167), channel_id=1, source_target_pairs={{0,2},{1,3},{2,0},{3,1},{4,6},{5,7},{6,4},{7,5},{8,10},{9,11},{10,... | collective-permute-start | bytes 589832 | tf_op jit(solution)/shard_map/ppermute | solution.py:506
  120.4 8.4 %collective-permute-start.38 = (bf16[2,72,384]{2,1,0:T(8,128)(2,1)S(1)}, bf16[2,72,384]{2,1,0:T(8,128)(2,1)S(1)}, u32[]{:S(2)}, u32[]{:S(2)}) collective-permute-start(bf16[2,72,384]{2,1,0:T(8,128)(2,1)S(1)} %fusion.33), channel_id=1, source_target_pairs={{0,16},{1,17},{2,18},{3,19},{4,20},{5,21},{6,22},{7,23},{8,24},{9,... | collective-permute-start | bytes 331784 | tf_op jit(solution)/shard_map/ppermute | solution.py:506
  130.3 9.6 %collective-permute-start.45 = (bf16[2,72,384]{2,1,0:T(8,128)(2,1)S(1)}, bf16[2,72,384]{2,1,0:T(8,128)(2,1)S(1)}, u32[]{:S(2)}, u32[]{:S(2)}) collective-permute-start(bf16[2,72,384]{2,1,0:T(8,128)(2,1)S(1)} %fusion.17), channel_id=1, source_target_pairs={{0,2},{1,3},{2,0},{3,1},{4,6},{5,7},{6,4},{7,5},{8,10},{9,11},{10,... | collective-permute-start | bytes 331784 | tf_op jit(solution)/shard_map/ppermute | solution.py:506
  131.2 6.5 %collective-permute-start.47 = (bf16[72,576]{1,0:T(8,128)(2,1)S(1)}, bf16[72,576]{1,0:T(8,128)(2,1)S(1)}, u32[]{:S(2)}, u32[]{:S(2)}) collective-permute-start(bf16[72,576]{1,0:T(8,128)(2,1)S(1)} %fusion.36), channel_id=1, source_target_pairs={{0,16},{1,17},{2,18},{3,19},{4,20},{5,21},{6,22},{7,23},{8,24},{9,... | collective-permute-start | bytes 248840 | tf_op jit(solution)/shard_map/ppermute | solution.py:506
  (52 other events, 336.5 us)

commit v10 on v9

--- a/solution.py
+++ b/solution.py
@@ -484,12 +484,15 @@
     gains_o[1:2, :] = line[:, 256 : 256 + d_rows]
 
 
-def place_all(part_d, qk, v, meta, a_near, a_far, b_near, b_far, d0, d1, d2, d3, r0, r1, r2, r3,
-              gate_o, down_o, wout_o, w_o, bqk_o, bv_o, gains_o, all_s):
-    place_gate(meta, a_near, a_far, gate_o, 2, 0)
-    place_gate(meta, b_near, b_far, gate_o, 2, 1)
+def place_rest(part_d, qk, v, meta, d0, d1, d2, d3, r0, r1, far,
+               down_o, wout_o, w_o, bqk_o, bv_o, gains_o, all_s):
     place_down(part_d, meta, d0, d1, d2, d3, down_o, wout_o)
-    place_qkv(qk, v, meta, r0, r1, r2, r3, w_o, bqk_o, bv_o, gains_o, all_s)
+    place_qkv(qk, v, meta, r0, r1, far.at[0], far.at[1], w_o, bqk_o, bv_o, gains_o, all_s)
+
+
+def place_halves(meta, a_near, a_far, b_near, b_far, out_o):
+    place_gate(meta, a_near, a_far, out_o, 2, 0)
+    place_gate(meta, b_near, b_far, out_o, 2, 1)
 
 
 class Net:
@@ -810,12 +813,12 @@
     gu2 = net.both(after(gu1, a2), znear, 0)
     block_yc = net.swap(block_y, core)
     a_xc = net.swap(a_x, core)
-    gu_x = net.swap(gu2, xbit)
     gu_y = net.swap(gu2, ybit)
     gu_c = net.swap(gu2, core)
     b0 = net.half(after(half_b, a0), core, 0)
     b1 = net.both(b0, zfar, 0, after(net.swap(b0, zfar), a2))
     b_x = net.swap(b1, xbit)
+    gu_x = net.swap(after(gu2, b_x), xbit)
     b_z = net.swap(after(b1, gu2), znear)
     b_c = net.swap(b1, core)
     a_xc = after(a_xc, b_x)
@@ -964,16 +967,23 @@
     down_c = net.swap(after(down, down_y), core)
     rest = add(rest, after(rest_got, down))
     rest_y = net.swap(rest, ybit)
-    rest_c = net.swap(after(rest, rest_y), core)
+    (out_gate,) = call(
+        place_halves,
+        [meta],
+        [a, a_far, b, b_far],
+        [sds((d_rows, 2 * units), F32)],
+        1e9,
+        mib=16,
+    )
+    rest_y = after(rest_y, out_gate)
+    rest_far = net.swap(jnp.stack([rest, rest_y]), core)
     down_yc = net.swap(after(down_y, rest_y), core)
-    rest_yc = net.swap(rest_y, core)
     qk, v = (QW + KW) // n_fsdp, KW // n_fsdp
-    out_gate, out_down, out_wout, out_qkv, b_qk, b_v, out_gains = call(
-        functools.partial(place_all, ff_rows // 4, qk, v),
+    out_down, out_wout, out_qkv, b_qk, b_v, out_gains = call(
+        functools.partial(place_rest, ff_rows // 4, qk, v),
         [meta],
-        [a, a_far, b, b_far, down, down_y, down_c, down_yc, rest, rest_y, rest_c, rest_yc],
+        [down, down_y, down_c, down_yc, rest, rest_y, rest_far],
         [
-            sds((d_rows, 2 * units), F32),
             sds((ff_rows, width), F32),
             sds((d_rows, width), F32),
             sds((d_rows, qkv_w), F32),

time: 148 us -> 152 us (1.027)
  waiting for transfers between devices: 49.3 us -> 54.5 us
  starting transfers between devices: 45.2 us -> 43 us
    ppermute x55 -> x54, waiting for transfers between devices: 49.3 us -> 54.5 us  [swap(): return lax.ppermute(value, ('fsdp', 'seq'), pairs)]
    ppermute x55 -> x54, starting transfers between devices: 45.2 us -> 43 us  [swap(): return lax.ppermute(value, ('fsdp', 'seq'), pairs)]
    pallas_call x5 -> x6, Pallas kernels: 39.2 us -> 40.4 us  [call(): pl.pallas_call(kernel, out_shape=outs, in_specs=specs, out_specs=whole(*o...]
  transfers between devices with their start and end apart: 55 -> 54, of which waited for: 18 -> 20; matrix products, arithmetic and copies ran while one was open for 5% -> 5% of each run, Pallas kernels for 16% -> 17%
where the time goes in v10:
time: 152 us; the launch traced here: 151 us
  waiting for transfers between devices  54.5 us (36%)
  starting transfers between devices  43 us (28%)
  Pallas kernels  41.2 us (27%)
  other arithmetic  5.75 us (4%)
  local copies, waits for them, and re-layouts  5.63 us (4%)
    ppermute x54, waiting for transfers between devices, swap(): return lax.ppermute(value, ('fsdp', 'seq'), pairs)  54.5 us
    ppermute x54, starting transfers between devices, swap(): return lax.ppermute(value, ('fsdp', 'seq'), pairs)  43 us
    pallas_call x6, Pallas kernels, call(): pl.pallas_call(kernel, out_shape=outs, in_specs=specs, out_specs=whole(*o...  40.4 us
    unnamed x60, local copies, waits for them, and re-layouts  4.58 us
    convert_element_type x21, other arithmetic, add(): return (keep.astype(F32) + got.astype(F32)).astype(BF)  3.25 us
  transfers between devices with their start and end apart: 54, of which 20 were waited for; matrix products, arithmetic and copies ran while one was open for 5% of the time, Pallas kernels for 17%

profile of v10, /device:TPU:0, one launch (start us, length us, event | category | flops | bytes accessed | tf_op | source)
XLA Modules:
  0.0 151.4 jit_solution(9643689536395999560)
XLA Ops:
  3.8 4.1 %collective-permute-start.3 = (bf16[40,960]{1,0:T(8,128)(2,1)S(1)}, bf16[40,960]{1,0:T(8,128)(2,1)S(1)}, u32[]{:S(2)}, u32[]{:S(2)}) collective-permute-start(bf16[40,960]{1,0:T(8,128)(2,1)S(1)} %shard_map.187), channel_id=1, source_target_pairs={{0,16},{1,17},{2,18},{3,19},{4,20},{5,21},{6,22},{7,23},{8,24},{9,... | collective-permute-start | bytes 230408 | tf_op jit(solution)/shard_map/ppermute | solution.py:509
  10.0 1.6 %collective-permute-start = (bf16[256,640]{1,0:T(8,128)(2,1)S(1)}, bf16[256,640]{1,0:T(8,128)(2,1)S(1)}, u32[]{:S(2)}, u32[]{:S(2)}) collective-permute-start(bf16[256,640]{1,0:T(8,128)(2,1)S(1)} %pad_maximum_fusion.3.b0), channel_id=1, source_target_pairs={{0,2},{1,3},{2,0},{3,1},{4,6},{5,7},{6,4},{7,5},{8,10},{9,11},{10,... | collective-permute-start | bytes 983048 | tf_op jit(solution)/shard_map/ppermute | solution.py:509
  12.2 2.7 %collective-permute-start.8 = (bf16[136,576]{1,0:T(8,128)(2,1)S(1)}, bf16[136,576]{1,0:T(8,128)(2,1)S(1)}, u32[]{:S(2)}, u32[]{:S(2)}) collective-permute-start(bf16[136,576]{1,0:T(8,128)(2,1)S(1)} %dynamic-slice_bitcast_fusion), channel_id=1, source_target_pairs={{0,16},{1,17},{2,18},{3,19},{4,20},{5,21},{6,22},{7,23},{8,24},{9,... | collective-permute-start | bytes 470024 | tf_op jit(solution)/shard_map/ppermute | solution.py:509
  15.3 1.6 %collective-permute-start.4 = (bf16[2,40,960]{2,1,0:T(8,128)(2,1)S(1)}, bf16[2,40,960]{2,1,0:T(8,128)(2,1)S(1)}, u32[]{:S(2)}, u32[]{:S(2)}) collective-permute-start(bf16[2,40,960]{2,1,0:T(8,128)(2,1)S(1)} %pad_maximum_fusion.6), channel_id=1, source_target_pairs={{0,8},{1,9},{2,10},{3,11},{4,12},{5,13},{6,14},{7,15},{8,0},{9,1},... | collective-permute-start | bytes 460808 | tf_op jit(solution)/shard_map/ppermute | solution.py:509
  17.0 7.6 %collective-permute-done.11 = bf16[72,768]{1,0:T(8,128)(2,1)S(1)} collective-permute-done((bf16[72,768]{1,0:T(8,128)(2,1)S(1)}, bf16[72,768]{1,0:T(8,128)(2,1)S(1)}, u32[]{:S(2)}, u32[]{:S(2)}) %collective-permute-start.11) | collective-permute-done | bytes 110624 | tf_op jit(solution)/shard_map/ppermute | solution.py:509
  24.9 1.6 %collective-permute-start.5 = (bf16[2,2,40,960]{3,2,1,0:T(8,128)(2,1)S(1)}, bf16[2,2,40,960]{3,2,1,0:T(8,128)(2,1)S(1)}, u32[]{:S(2)}, u32[]{:S(2)}) collective-permute-start(bf16[2,2,40,960]{3,2,1,0:T(8,128)(2,1)S(1)} %pad_maximum_fusion.4.a00), channel_id=1, source_target_pairs={{0,4},{1,5},{2,6},{3,7},{4,0},{5,1},{6,2},{7,3},{8,12},{9,13},{10,... | collective-permute-start | bytes 921608 | tf_op jit(solution)/shard_map/ppermute | solution.py:509
  27.7 1.6 %collective-permute-start.9 = (bf16[2,136,576]{2,1,0:T(8,128)(2,1)S(1)}, bf16[2,136,576]{2,1,0:T(8,128)(2,1)S(1)}, u32[]{:S(2)}, u32[]{:S(2)}) collective-permute-start(bf16[2,136,576]{2,1,0:T(8,128)(2,1)S(1)} %pad_maximum_fusion.2.refs_0_), channel_id=1, source_target_pairs={{0,4},{1,5},{2,6},{3,7},{4,0},{5,1},{6,2},{7,3},{8,12},{9,13},{10,... | collective-permute-start | bytes 940040 | tf_op jit(solution)/shard_map/ppermute | solution.py:509
  29.7 4.5 %collective-permute-done.12 = bf16[2,72,768]{2,1,0:T(8,128)(2,1)S(1)} collective-permute-done((bf16[2,72,768]{2,1,0:T(8,128)(2,1)S(1)}, bf16[2,72,768]{2,1,0:T(8,128)(2,1)S(1)}, u32[]{:S(2)}, u32[]{:S(2)}) %collective-permute-start.12) | collective-permute-done | bytes 221216 | tf_op jit(solution)/shard_map/ppermute | solution.py:509
  34.4 8.1 %collective-permute-done.9.refs_2_ = bf16[2,136,576]{2,1,0:T(8,128)(2,1)S(1)} collective-permute-done((bf16[2,136,576]{2,1,0:T(8,128)(2,1)S(1)}, bf16[2,136,576]{2,1,0:T(8,128)(2,1)S(1)}, u32[]{:S(2)}, u32[]{:S(2)}) %collective-permute-start.9) | collective-permute-done | bytes 313376 | tf_op jit(solution)/shard_map/ppermute | solution.py:509
  47.0 10.7 %shard_map.188 = (bf16[256,576]{1,0:T(8,128)(2,1)S(1)}, bf16[2,3,384,64]{3,2,1,0:T(8,128)(2,1)}, bf16[2,3,512,64]{3,2,1,0:T(8,128)(2,1)}, bf16[2,3,512,64]{3,2,1...) custom-call(s32[2]{0:T(128)S(1)} %pad_add_fusion.meta, bf16[256,640]{1,0:T(8,128)(2,1)S(1)} %pad_maximum_fusion.3.b0, ...), custom_call_target="tpu_custom_call" | custom-call | flops 12000000000 | bytes 6074880 | tf_op jit(solution)/shard_map/pallas_call | solution.py:55
  57.7 1.6 %collective-permute-start.23 = (bf16[2,2,72,768]{3,2,1,0:T(8,128)(2,1)}, bf16[2,2,72,768]{3,2,1,0:T(8,128)(2,1)}, u32[]{:S(2)}, u32[]{:S(2)}) collective-permute-start(bf16[2,2,72,768]{3,2,1,0:T(8,128)(2,1)} %collective-permute-done.21.refs_12_), channel_id=1, source_target_pairs={{0,2},{1,3},{2,0},{3,1},{4,6},{5,7},{6,4},{7,5},{8,10},{9,11},{10,... | collective-permute-start | bytes 1327112 | tf_op jit(solution)/shard_map/ppermute | solution.py:509
  61.5 8.6 %collective-permute-done.23.refs_14_ = bf16[2,2,72,768]{3,2,1,0:T(8,128)(2,1)} collective-permute-done((bf16[2,2,72,768]{3,2,1,0:T(8,128)(2,1)}, bf16[2,2,72,768]{3,2,1,0:T(8,128)(2,1)}, u32[]{:S(2)}, u32[]{:S(2)}) %collective-permute-start.23) | collective-permute-done | bytes 442400 | tf_op jit(solution)/shard_map/ppermute | solution.py:509
  71.1 1.5 %collective-permute-done.16.refs_5_ = bf16[2,136,576]{2,1,0:T(8,128)(2,1)} collective-permute-done((bf16[2,136,576]{2,1,0:T(8,128)(2,1)}, bf16[2,136,576]{2,1,0:T(8,128)(2,1)}, u32[]{:S(2)}, u32[]{:S(2)}) %collective-permute-start.16) | collective-permute-done | bytes 313376 | tf_op jit(solution)/shard_map/ppermute | solution.py:509
  73.2 13.4 %shard_map.189 = (bf16[2,576,128]{2,1,0:T(8,128)(2,1)}, bf16[2,2,2,2,72,384]{5,4,3,2,1,0:T(8,128)(2,1)}, bf16[2,2,2,2,72,384]{5,4,3,2,1,0:T(8,128)(2,1)}, bf16[2...) custom-call(s32[2]{0:T(128)S(1)} %pad_add_fusion.meta, ...), custom_call_target="tpu_custom_call" | custom-call | flops 14000000000 | bytes 14311168 | tf_op jit(solution)/shard_map/pallas_call | solution.py:55
  86.8 2.5 %collective-permute-done.25 = bf16[2,2,2,2,72,384]{5,4,3,2,1,0:T(8,128)(2,1)S(1)} collective-permute-done((bf16[2,2,2,2,72,384]{5,4,3,2,1,0:T(8,128)(2,1)}, bf16[2,2,2,2,72,384]{5,4,3,2,1,0:T(8,128)(2,1)S(1)}, u32[]{:S(2)}, u32[]{:S(2)}) %collective-permute-start.25) | collective-permute-done | bytes 884768 | tf_op jit(solution)/shard_map/ppermute | solution.py:509
  92.3 1.7 %collective-permute-done.26 = bf16[2,2,2,2,72,384]{5,4,3,2,1,0:T(8,128)(2,1)S(1)} collective-permute-done((bf16[2,2,2,2,72,384]{5,4,3,2,1,0:T(8,128)(2,1)}, bf16[2,2,2,2,72,384]{5,4,3,2,1,0:T(8,128)(2,1)S(1)}, u32[]{:S(2)}, u32[]{:S(2)}) %collective-permute-start.26) | collective-permute-done | bytes 884768 | tf_op jit(solution)/shard_map/ppermute | solution.py:509
  94.2 2.0 %collective-permute-start.31 = (bf16[2,2,2,72,384]{4,3,2,1,0:T(8,128)(2,1)S(1)}, bf16[2,2,2,72,384]{4,3,2,1,0:T(8,128)(2,1)S(1)}, u32[]{:S(2)}, u32[]{:S(2)}) collective-permute-start(bf16[2,2,2,72,384]{4,3,2,1,0:T(8,128)(2,1)S(1)} %get-tuple-element.158), channel_id=1, source_target_pairs={{0,8},{1,9},{2,10},{3,11},{4,12},{5,13},{6,14},{7,15},{8,0},{9,1},... | collective-permute-start | bytes 1327112 | tf_op jit(solution)/shard_map/ppermute | solution.py:509
  96.7 1.6 %collective-permute-start.29 = (bf16[2,2,2,72,576]{4,3,2,1,0:T(8,128)(2,1)S(1)}, bf16[2,2,2,72,576]{4,3,2,1,0:T(8,128)(2,1)S(1)}, u32[]{:S(2)}, u32[]{:S(2)}) collective-permute-start(bf16[2,2,2,72,576]{4,3,2,1,0:T(8,128)(2,1)S(1)} %get-tuple-element.154), channel_id=1, source_target_pairs={{0,2},{1,3},{2,0},{3,1},{4,6},{5,7},{6,4},{7,5},{8,10},{9,11},{10,... | collective-permute-start | bytes 1990664 | tf_op jit(solution)/shard_map/ppermute | solution.py:509
  98.4 11.2 %shard_map.190 = (bf16[256,640]{1,0:T(8,128)(2,1)S(1)}, bf16[2,256,384]{2,1,0:T(8,128)(2,1)S(1)}, bf16[2,256,384]{2,1,0:T(8,128)(2,1)S(1)}, bf16[2,2,2,2,80,256]...) custom-call(s32[2]{0:T(128)S(1)} %pad_add_fusion.meta, bf16[256,640]{1,0:T(8,128)(2,1)S(1)} %pad_maximum_fusion.3.b0, ...), custom_call_target="tpu_custom_call" | custom-call | flops 14000000000 | bytes 7273216 | tf_op jit(solution)/shard_map/pallas_call | solution.py:55
  109.8 1.9 %collective-permute-start.34 = (bf16[2,2,72,384]{3,2,1,0:T(8,128)(2,1)S(1)}, bf16[2,2,72,384]{3,2,1,0:T(8,128)(2,1)S(1)}, u32[]{:S(2)}, u32[]{:S(2)}) collective-permute-start(bf16[2,2,72,384]{3,2,1,0:T(8,128)(2,1)S(1)} %get-tuple-element.166), channel_id=1, source_target_pairs={{0,16},{1,17},{2,18},{3,19},{4,20},{5,21},{6,22},{7,23},{8,24},{9,... | collective-permute-start | bytes 663560 | tf_op jit(solution)/shard_map/ppermute | solution.py:509
  112.2 2.8 %collective-permute-done.29 = bf16[2,2,2,72,576]{4,3,2,1,0:T(8,128)(2,1)S(1)} collective-permute-done((bf16[2,2,2,72,576]{4,3,2,1,0:T(8,128)(2,1)S(1)}, bf16[2,2,2,72,576]{4,3,2,1,0:T(8,128)(2,1)S(1)}, u32[]{:S(2)}, u32[]{:S(2)}) %collective-permute-start.29) | collective-permute-done | bytes 663584 | tf_op jit(solution)/shard_map/ppermute | solution.py:509
  115.2 1.6 %collective-permute-start.35 = (bf16[2,2,2,80,256]{4,3,2,1,0:T(8,128)(2,1)S(1)}, bf16[2,2,2,80,256]{4,3,2,1,0:T(8,128)(2,1)S(1)}, u32[]{:S(2)}, u32[]{:S(2)}) collective-permute-start(bf16[2,2,2,80,256]{4,3,2,1,0:T(8,128)(2,1)S(1)} %get-tuple-element.162), channel_id=1, source_target_pairs={{0,2},{1,3},{2,0},{3,1},{4,6},{5,7},{6,4},{7,5},{8,10},{9,11},{10,... | collective-permute-start | bytes 983048 | tf_op jit(solution)/shard_map/ppermute | solution.py:509
  118.7 5.4 %collective-permute-done.37 = bf16[2,2,72,384]{3,2,1,0:T(8,128)(2,1)S(1)} collective-permute-done((bf16[2,2,72,384]{3,2,1,0:T(8,128)(2,1)S(1)}, bf16[2,2,72,384]{3,2,1,0:T(8,128)(2,1)S(1)}, u32[]{:S(2)}, u32[]{:S(2)}) %collective-permute-start.37) | collective-permute-done | bytes 221216 | tf_op jit(solution)/shard_map/ppermute | solution.py:509
  124.2 1.7 %collective-permute-done.35 = bf16[2,2,2,80,256]{4,3,2,1,0:T(8,128)(2,1)S(1)} collective-permute-done((bf16[2,2,2,80,256]{4,3,2,1,0:T(8,128)(2,1)S(1)}, bf16[2,2,2,80,256]{4,3,2,1,0:T(8,128)(2,1)S(1)}, u32[]{:S(2)}, u32[]{:S(2)}) %collective-permute-start.35) | collective-permute-done | bytes 327712 | tf_op jit(solution)/shard_map/ppermute | solution.py:509
  128.7 1.9 %shard_map.191 = f32[2,576,128]{2,1,0:T(8,128)} custom-call(bf16[256,640]{1,0:T(8,128)(2,1)S(1)} %get-tuple-element.102.dq, bf16[256,384]{1,0:T(8,128)(2,1)S(1)} %get-tuple-element.168.own, bf16[256,384]{1,0:T(8,128)(2,1)S(1)} %collective-permute-done.32.other, bf16[256,576]{1,0:T(8,128)(2,1)S(1)} %bitcast.213, f32[256,576]{1,0:T(8,128)S(1)} %copy-done.9, ...), custom_call_target="tpu_custom_call" | custom-call | flops 3000000000 | bytes 3305984 | tf_op jit(solution)/shard_map/pallas_call | solution.py:55
  132.5 1.6 %collective-permute-start.43 = (bf16[2,72,384]{2,1,0:T(8,128)(2,1)S(1)}, bf16[2,72,384]{2,1,0:T(8,128)(2,1)S(1)}, u32[]{:S(2)}, u32[]{:S(2)}) collective-permute-start(bf16[2,72,384]{2,1,0:T(8,128)(2,1)S(1)} %fusion.17), channel_id=1, source_target_pairs={{0,2},{1,3},{2,0},{3,1},{4,6},{5,7},{6,4},{7,5},{8,10},{9,11},{10,... | collective-permute-start | bytes 331784 | tf_op jit(solution)/shard_map/ppermute | solution.py:509
  136.7 1.7 %collective-permute-start.47 = (bf16[80,256]{1,0:T(8,128)(2,1)S(1)}, bf16[80,256]{1,0:T(8,128)(2,1)S(1)}, u32[]{:S(2)}, u32[]{:S(2)}) collective-permute-start(bf16[80,256]{1,0:T(8,128)(2,1)S(1)} %fusion.42), channel_id=1, source_target_pairs={{0,16},{1,17},{2,18},{3,19},{4,20},{5,21},{6,22},{7,23},{8,24},{9,... | collective-permute-start | bytes 122888 | tf_op jit(solution)/shard_map/ppermute | solution.py:509
  140.2 1.5 %collective-permute-done.42 = bf16[72,576]{1,0:T(8,128)(2,1)S(1)} collective-permute-done((bf16[72,576]{1,0:T(8,128)(2,1)S(1)}, bf16[72,576]{1,0:T(8,128)(2,1)S(1)}, u32[]{:S(2)}, u32[]{:S(2)}) %collective-permute-start.42) | collective-permute-done | bytes 82976 | tf_op jit(solution)/shard_map/ppermute | solution.py:509
  141.8 1.6 %collective-permute-start.45 = (bf16[72,576]{1,0:T(8,128)(2,1)S(1)}, bf16[72,576]{1,0:T(8,128)(2,1)S(1)}, u32[]{:S(2)}, u32[]{:S(2)}) collective-permute-start(bf16[72,576]{1,0:T(8,128)(2,1)S(1)} %fusion.27.d0), channel_id=1, source_target_pairs={{0,2},{1,3},{2,0},{3,1},{4,6},{5,7},{6,4},{7,5},{8,10},{9,11},{10,... | collective-permute-start | bytes 248840 | tf_op jit(solution)/shard_map/ppermute | solution.py:509
  144.0 2.4 %collective-permute-done.45.d1 = bf16[72,576]{1,0:T(8,128)(2,1)S(1)} collective-permute-done((bf16[72,576]{1,0:T(8,128)(2,1)S(1)}, bf16[72,576]{1,0:T(8,128)(2,1)S(1)}, u32[]{:S(2)}, u32[]{:S(2)}) %collective-permute-start.45) | collective-permute-done | bytes 82976 | tf_op jit(solution)/shard_map/ppermute | solution.py:509
  146.4 1.5 %shard_map.192 = f32[72,3072]{1,0:T(8,128)} custom-call(s32[2]{0:T(128)S(1)} %pad_add_fusion.meta, bf16[2,72,384]{2,1,0:T(8,128)(2,1)S(1)} %add_convert_fusion.11.a_near, bf16[2,72,384]{2,1,0:T(8,128)(2,1)S(1)} %collective-permute-done.49.a_far, bf16[2,72,384]{2,1,0:T(8,128)(2,1)S(1)} %add_convert_fusion.10.b_near, ...), custom_call_target="tpu_custom_call" | custom-call | flops 1000000000 | bytes 1327104 | tf_op jit(solution)/shard_map/pallas_call | solution.py:55
  149.8 1.6 %shard_map.193 = (f32[192,576]{1,0:T(8,128)}, f32[72,576]{1,0:T(8,128)}, f32[72,960]{1,0:T(8,128)}, f32[1,96]{1,0:T(1,128)}, f32[1,24]{1,0:T(1,128)}, /*index=5*/f32[2,72]{1,0:T(2,128)}) custom-call(s32[2]{0:T(128)S(1)} %pad_add_fusion.meta, bf16[72,576]{1,0:T(8,128)(2,1)S(1)} %fusion.27.d0, bf16[72,576]{1,0:T(8,128)(2,1)S(1)} %collective-permute-done.45.d1, ...), custom_call_target="tpu_custom_call" | custom-call | flops 3000000000 | bytes 1381408 | tf_op jit(solution)/shard_map/pallas_call | solution.py:55
  (196 shorter events, 34.7 us)
Async XLA Ops:
  3.8 11.5 %collective-permute-start.3 = (bf16[40,960]{1,0:T(8,128)(2,1)S(1)}, bf16[40,960]{1,0:T(8,128)(2,1)S(1)}, u32[]{:S(2)}, u32[]{:S(2)}) collective-permute-start(bf16[40,960]{1,0:T(8,128)(2,1)S(1)} %shard_map.187), channel_id=1, source_target_pairs={{0,16},{1,17},{2,18},{3,19},{4,20},{5,21},{6,22},{7,23},{8,24},{9,... | collective-permute-start | bytes 230408 | tf_op jit(solution)/shard_map/ppermute | solution.py:509
  10.0 19.5 %collective-permute-start.1 = (bf16[256,640]{1,0:T(8,128)(2,1)S(1)}, bf16[256,640]{1,0:T(8,128)(2,1)S(1)}, u32[]{:S(2)}, u32[]{:S(2)}) collective-permute-start(bf16[256,640]{1,0:T(8,128)(2,1)S(1)} %pad_maximum_fusion.3.b0), channel_id=1, source_target_pairs={{0,1},{1,0},{2,3},{3,2},{4,5},{5,4},{6,7},{7,6},{8,9},{9,8},{10,11... | collective-permute-start | bytes 983048 | tf_op jit(solution)/shard_map/ppermute | solution.py:509
  10.0 17.7 %collective-permute-start = (bf16[256,640]{1,0:T(8,128)(2,1)S(1)}, bf16[256,640]{1,0:T(8,128)(2,1)S(1)}, u32[]{:S(2)}, u32[]{:S(2)}) collective-permute-start(bf16[256,640]{1,0:T(8,128)(2,1)S(1)} %pad_maximum_fusion.3.b0), channel_id=1, source_target_pairs={{0,2},{1,3},{2,0},{3,1},{4,6},{5,7},{6,4},{7,5},{8,10},{9,11},{10,... | collective-permute-start | bytes 983048 | tf_op jit(solution)/shard_map/ppermute | solution.py:509
  11.6 13.0 %collective-permute-start.11 = (bf16[72,768]{1,0:T(8,128)(2,1)S(1)}, bf16[72,768]{1,0:T(8,128)(2,1)S(1)}, u32[]{:S(2)}, u32[]{:S(2)}) collective-permute-start(bf16[72,768]{1,0:T(8,128)(2,1)S(1)} %constant_dynamic-slice_fusion), channel_id=1, source_target_pairs={{0,16},{1,17},{2,18},{3,19},{4,20},{5,21},{6,22},{7,23},{8,24},{9,... | collective-permute-start | bytes 331784 | tf_op jit(solution)/shard_map/ppermute | solution.py:509
  12.2 15.4 %collective-permute-start.8 = (bf16[136,576]{1,0:T(8,128)(2,1)S(1)}, bf16[136,576]{1,0:T(8,128)(2,1)S(1)}, u32[]{:S(2)}, u32[]{:S(2)}) collective-permute-start(bf16[136,576]{1,0:T(8,128)(2,1)S(1)} %dynamic-slice_bitcast_fusion), channel_id=1, source_target_pairs={{0,16},{1,17},{2,18},{3,19},{4,20},{5,21},{6,22},{7,23},{8,24},{9,... | collective-permute-start | bytes 470024 | tf_op jit(solution)/shard_map/ppermute | solution.py:509
  15.3 9.4 %collective-permute-start.4 = (bf16[2,40,960]{2,1,0:T(8,128)(2,1)S(1)}, bf16[2,40,960]{2,1,0:T(8,128)(2,1)S(1)}, u32[]{:S(2)}, u32[]{:S(2)}) collective-permute-start(bf16[2,40,960]{2,1,0:T(8,128)(2,1)S(1)} %pad_maximum_fusion.6), channel_id=1, source_target_pairs={{0,8},{1,9},{2,10},{3,11},{4,12},{5,13},{6,14},{7,15},{8,0},{9,1},... | collective-permute-start | bytes 460808 | tf_op jit(solution)/shard_map/ppermute | solution.py:509
  24.8 21.4 %collective-permute-start.6 = (bf16[2,2,40,960]{3,2,1,0:T(8,128)(2,1)S(1)}, bf16[2,2,40,960]{3,2,1,0:T(8,128)(2,1)S(1)}, u32[]{:S(2)}, u32[]{:S(2)}) collective-permute-start(bf16[2,2,40,960]{3,2,1,0:T(8,128)(2,1)S(1)} %pad_maximum_fusion.4.a00), channel_id=1, source_target_pairs={{0,1},{1,0},{2,3},{3,2},{4,5},{5,4},{6,7},{7,6},{8,9},{9,8},{10,11... | collective-permute-start | bytes 921608 | tf_op jit(solution)/shard_map/ppermute | solution.py:509
  24.9 18.1 %collective-permute-start.5 = (bf16[2,2,40,960]{3,2,1,0:T(8,128)(2,1)S(1)}, bf16[2,2,40,960]{3,2,1,0:T(8,128)(2,1)S(1)}, u32[]{:S(2)}, u32[]{:S(2)}) collective-permute-start(bf16[2,2,40,960]{3,2,1,0:T(8,128)(2,1)S(1)} %pad_maximum_fusion.4.a00), channel_id=1, source_target_pairs={{0,4},{1,5},{2,6},{3,7},{4,0},{5,1},{6,2},{7,3},{8,12},{9,13},{10,... | collective-permute-start | bytes 921608 | tf_op jit(solution)/shard_map/ppermute | solution.py:509
  27.7 14.8 %collective-permute-start.9 = (bf16[2,136,576]{2,1,0:T(8,128)(2,1)S(1)}, bf16[2,136,576]{2,1,0:T(8,128)(2,1)S(1)}, u32[]{:S(2)}, u32[]{:S(2)}) collective-permute-start(bf16[2,136,576]{2,1,0:T(8,128)(2,1)S(1)} %pad_maximum_fusion.2.refs_0_), channel_id=1, source_target_pairs={{0,4},{1,5},{2,6},{3,7},{4,0},{5,1},{6,2},{7,3},{8,12},{9,13},{10,... | collective-permute-start | bytes 940040 | tf_op jit(solution)/shard_map/ppermute | solution.py:509
  29.5 13.5 %collective-permute-start.2 = (bf16[256,640]{1,0:T(8,128)(2,1)S(1)}, bf16[256,640]{1,0:T(8,128)(2,1)S(1)}, u32[]{:S(2)}, u32[]{:S(2)}) collective-permute-start(bf16[256,640]{1,0:T(8,128)(2,1)S(1)} %collective-permute-done.b1), channel_id=1, source_target_pairs={{0,1},{1,0},{2,3},{3,2},{4,5},{5,4},{6,7},{7,6},{8,9},{9,8},{10,11... | collective-permute-start | bytes 983048 | tf_op jit(solution)/shard_map/ppermute | solution.py:509
  34.3 26.8 %collective-permute-start.19 = (bf16[2,2,72,768]{3,2,1,0:T(8,128)(2,1)S(1)}, bf16[2,2,72,768]{3,2,1,0:T(8,128)(2,1)S(1)}, u32[]{:S(2)}, u32[]{:S(2)}) collective-permute-start(bf16[2,2,72,768]{3,2,1,0:T(8,128)(2,1)S(1)} %pad_maximum_fusion.refs_8_), channel_id=1, source_target_pairs={{0,1},{1,0},{2,3},{3,2},{4,5},{5,4},{6,7},{7,6},{8,9},{9,8},{10,11... | collective-permute-start | bytes 1327112 | tf_op jit(solution)/shard_map/ppermute | solution.py:509
  42.5 15.2 %collective-permute-start.13 = (bf16[2,2,72,768]{3,2,1,0:T(8,128)(2,1)S(1)}, bf16[2,2,72,768]{3,2,1,0:T(8,128)(2,1)}, u32[]{:S(2)}, u32[]{:S(2)}) collective-permute-start(bf16[2,2,72,768]{3,2,1,0:T(8,128)(2,1)S(1)} %pad_maximum_fusion.refs_8_), channel_id=1, source_target_pairs={{0,2},{1,3},{2,0},{3,1},{4,6},{5,7},{6,4},{7,5},{8,10},{9,11},{10,... | collective-permute-start | bytes 1327112 | tf_op jit(solution)/shard_map/ppermute | solution.py:509
  43.0 16.8 %collective-permute-start.15 = (bf16[2,136,576]{2,1,0:T(8,128)(2,1)S(1)}, bf16[2,136,576]{2,1,0:T(8,128)(2,1)}, u32[]{:S(2)}, u32[]{:S(2)}) collective-permute-start(bf16[2,136,576]{2,1,0:T(8,128)(2,1)S(1)} %pad_maximum_fusion.2.refs_0_), channel_id=1, source_target_pairs={{0,8},{1,9},{2,10},{3,11},{4,12},{5,13},{6,14},{7,15},{8,0},{9,1},... | collective-permute-start | bytes 940040 | tf_op jit(solution)/shard_map/ppermute | solution.py:509
  44.7 13.0 %collective-permute-start.21 = (bf16[2,2,72,768]{3,2,1,0:T(8,128)(2,1)S(1)}, bf16[2,2,72,768]{3,2,1,0:T(8,128)(2,1)}, u32[]{:S(2)}, u32[]{:S(2)}) collective-permute-start(bf16[2,2,72,768]{3,2,1,0:T(8,128)(2,1)S(1)} %pad_maximum_fusion.refs_8_), channel_id=1, source_target_pairs={{0,4},{1,5},{2,6},{3,7},{4,0},{5,1},{6,2},{7,3},{8,12},{9,13},{10,... | collective-permute-start | bytes 1327112 | tf_op jit(solution)/shard_map/ppermute | solution.py:509
  57.7 12.3 %collective-permute-start.23 = (bf16[2,2,72,768]{3,2,1,0:T(8,128)(2,1)}, bf16[2,2,72,768]{3,2,1,0:T(8,128)(2,1)}, u32[]{:S(2)}, u32[]{:S(2)}) collective-permute-start(bf16[2,2,72,768]{3,2,1,0:T(8,128)(2,1)} %collective-permute-done.21.refs_12_), channel_id=1, source_target_pairs={{0,2},{1,3},{2,0},{3,1},{4,6},{5,7},{6,4},{7,5},{8,10},{9,11},{10,... | collective-permute-start | bytes 1327112 | tf_op jit(solution)/shard_map/ppermute | solution.py:509
  59.3 10.7 %collective-permute-start.14 = (bf16[2,136,576]{2,1,0:T(8,128)(2,1)S(1)}, bf16[2,136,576]{2,1,0:T(8,128)(2,1)S(1)}, u32[]{:S(2)}, u32[]{:S(2)}) collective-permute-start(bf16[2,136,576]{2,1,0:T(8,128)(2,1)S(1)} %collective-permute-done.9.refs_2_), channel_id=1, source_target_pairs={{0,1},{1,0},{2,3},{3,2},{4,5},{5,4},{6,7},{7,6},{8,9},{9,8},{10,11... | collective-permute-start | bytes 940040 | tf_op jit(solution)/shard_map/ppermute | solution.py:509
  59.8 10.7 %collective-permute-start.17 = (bf16[2,136,576]{2,1,0:T(8,128)(2,1)}, bf16[2,136,576]{2,1,0:T(8,128)(2,1)}, u32[]{:S(2)}, u32[]{:S(2)}) collective-permute-start(bf16[2,136,576]{2,1,0:T(8,128)(2,1)} %collective-permute-done.15.refs_4_), channel_id=1, source_target_pairs={{0,4},{1,5},{2,6},{3,7},{4,0},{5,1},{6,2},{7,3},{8,12},{9,13},{10,... | collective-permute-start | bytes 940040 | tf_op jit(solution)/shard_map/ppermute | solution.py:509
  61.0 11.7 %collective-permute-start.20 = (bf16[2,2,72,768]{3,2,1,0:T(8,128)(2,1)}, bf16[2,2,72,768]{3,2,1,0:T(8,128)(2,1)}, u32[]{:S(2)}, u32[]{:S(2)}) collective-permute-start(bf16[2,2,72,768]{3,2,1,0:T(8,128)(2,1)} %collective-permute-done.13.refs_10_), channel_id=1, source_target_pairs={{0,1},{1,0},{2,3},{3,2},{4,5},{5,4},{6,7},{7,6},{8,9},{9,8},{10,11... | collective-permute-start | bytes 1327112 | tf_op jit(solution)/shard_map/ppermute | solution.py:509
  61.1 11.6 %collective-permute-start.22 = (bf16[2,2,72,768]{3,2,1,0:T(8,128)(2,1)}, bf16[2,2,72,768]{3,2,1,0:T(8,128)(2,1)}, u32[]{:S(2)}, u32[]{:S(2)}) collective-permute-start(bf16[2,2,72,768]{3,2,1,0:T(8,128)(2,1)} %collective-permute-done.21.refs_12_), channel_id=1, source_target_pairs={{0,1},{1,0},{2,3},{3,2},{4,5},{5,4},{6,7},{7,6},{8,9},{9,8},{10,11... | collective-permute-start | bytes 1327112 | tf_op jit(solution)/shard_map/ppermute | solution.py:509
  89.3 7.0 %collective-permute-start.27 = (bf16[2,2,2,2,72,576]{5,4,3,2,1,0:T(8,128)(2,1)}, bf16[2,2,2,2,72,576]{5,4,3,2,1,0:T(8,128)(2,1)S(1)}, u32[]{:S(2)}, u32[]{:S(2)}) collective-permute-start(bf16[2,2,2,2,72,576]{5,4,3,2,1,0:T(8,128)(2,1)} %get-tuple-element.99), channel_id=1, source_target_pairs={{0,1},{1,0},{2,3},{3,2},{4,5},{5,4},{6,7},{7,6},{8,9},{9,8},{10,11... | collective-permute-start | bytes 3981320 | tf_op jit(solution)/shard_map/ppermute | solution.py:509
  91.2 20.5 %collective-permute-start.36 = (bf16[2,2,2,72,384]{4,3,2,1,0:T(8,128)(2,1)S(1)}, bf16[2,2,2,72,384]{4,3,2,1,0:T(8,128)(2,1)S(1)}, u32[]{:S(2)}, u32[]{:S(2)}) collective-permute-start(bf16[2,2,2,72,384]{4,3,2,1,0:T(8,128)(2,1)S(1)} %get-tuple-element.156), channel_id=1, source_target_pairs={{0,4},{1,5},{2,6},{3,7},{4,0},{5,1},{6,2},{7,3},{8,12},{9,13},{10,... | collective-permute-start | bytes 1327112 | tf_op jit(solution)/shard_map/ppermute | solution.py:509
  94.2 15.5 %collective-permute-start.31 = (bf16[2,2,2,72,384]{4,3,2,1,0:T(8,128)(2,1)S(1)}, bf16[2,2,2,72,384]{4,3,2,1,0:T(8,128)(2,1)S(1)}, u32[]{:S(2)}, u32[]{:S(2)}) collective-permute-start(bf16[2,2,2,72,384]{4,3,2,1,0:T(8,128)(2,1)S(1)} %get-tuple-element.158), channel_id=1, source_target_pairs={{0,8},{1,9},{2,10},{3,11},{4,12},{5,13},{6,14},{7,15},{8,0},{9,1},... | collective-permute-start | bytes 1327112 | tf_op jit(solution)/shard_map/ppermute | solution.py:509
  96.7 18.3 %collective-permute-start.29 = (bf16[2,2,2,72,576]{4,3,2,1,0:T(8,128)(2,1)S(1)}, bf16[2,2,2,72,576]{4,3,2,1,0:T(8,128)(2,1)S(1)}, u32[]{:S(2)}, u32[]{:S(2)}) collective-permute-start(bf16[2,2,2,72,576]{4,3,2,1,0:T(8,128)(2,1)S(1)} %get-tuple-element.154), channel_id=1, source_target_pairs={{0,2},{1,3},{2,0},{3,1},{4,6},{5,7},{6,4},{7,5},{8,10},{9,11},{10,... | collective-permute-start | bytes 1990664 | tf_op jit(solution)/shard_map/ppermute | solution.py:509
  109.8 17.2 %collective-permute-start.34 = (bf16[2,2,72,384]{3,2,1,0:T(8,128)(2,1)S(1)}, bf16[2,2,72,384]{3,2,1,0:T(8,128)(2,1)S(1)}, u32[]{:S(2)}, u32[]{:S(2)}) collective-permute-start(bf16[2,2,72,384]{3,2,1,0:T(8,128)(2,1)S(1)} %get-tuple-element.166), channel_id=1, source_target_pairs={{0,16},{1,17},{2,18},{3,19},{4,20},{5,21},{6,22},{7,23},{8,24},{9,... | collective-permute-start | bytes 663560 | tf_op jit(solution)/shard_map/ppermute | solution.py:509
  111.9 12.3 %collective-permute-start.37 = (bf16[2,2,72,384]{3,2,1,0:T(8,128)(2,1)S(1)}, bf16[2,2,72,384]{3,2,1,0:T(8,128)(2,1)S(1)}, u32[]{:S(2)}, u32[]{:S(2)}) collective-permute-start(bf16[2,2,72,384]{3,2,1,0:T(8,128)(2,1)S(1)} %get-tuple-element.163), channel_id=1, source_target_pairs={{0,8},{1,9},{2,10},{3,11},{4,12},{5,13},{6,14},{7,15},{8,0},{9,1},... | collective-permute-start | bytes 663560 | tf_op jit(solution)/shard_map/ppermute | solution.py:509
  115.2 10.7 %collective-permute-start.35 = (bf16[2,2,2,80,256]{4,3,2,1,0:T(8,128)(2,1)S(1)}, bf16[2,2,2,80,256]{4,3,2,1,0:T(8,128)(2,1)S(1)}, u32[]{:S(2)}, u32[]{:S(2)}) collective-permute-start(bf16[2,2,2,80,256]{4,3,2,1,0:T(8,128)(2,1)S(1)} %get-tuple-element.162), channel_id=1, source_target_pairs={{0,2},{1,3},{2,0},{3,1},{4,6},{5,7},{6,4},{7,5},{8,10},{9,11},{10,... | collective-permute-start | bytes 983048 | tf_op jit(solution)/shard_map/ppermute | solution.py:509
  117.0 11.2 %collective-permute-start.33 = (bf16[2,2,72,576]{3,2,1,0:T(8,128)(2,1)S(1)}, bf16[2,2,72,576]{3,2,1,0:T(8,128)(2,1)S(1)}, u32[]{:S(2)}, u32[]{:S(2)}) collective-permute-start(bf16[2,2,72,576]{3,2,1,0:T(8,128)(2,1)S(1)} %get-tuple-element.160), channel_id=1, source_target_pairs={{0,4},{1,5},{2,6},{3,7},{4,0},{5,1},{6,2},{7,3},{8,12},{9,13},{10,... | collective-permute-start | bytes 995336 | tf_op jit(solution)/shard_map/ppermute | solution.py:509
  118.1 10.6 %collective-permute-start.32 = (bf16[256,384]{1,0:T(8,128)(2,1)S(1)}, bf16[256,384]{1,0:T(8,128)(2,1)S(1)}, u32[]{:S(2)}, u32[]{:S(2)}) collective-permute-start(bf16[256,384]{1,0:T(8,128)(2,1)S(1)} %get-tuple-element.167), channel_id=1, source_target_pairs={{0,2},{1,3},{2,0},{3,1},{4,6},{5,7},{6,4},{7,5},{8,10},{9,11},{10,... | collective-permute-start | bytes 589832 | tf_op jit(solution)/shard_map/ppermute | solution.py:509
  124.2 8.3 %collective-permute-start.40 = (bf16[2,72,384]{2,1,0:T(8,128)(2,1)S(1)}, bf16[2,72,384]{2,1,0:T(8,128)(2,1)S(1)}, u32[]{:S(2)}, u32[]{:S(2)}) collective-permute-start(bf16[2,72,384]{2,1,0:T(8,128)(2,1)S(1)} %fusion.33), channel_id=1, source_target_pairs={{0,16},{1,17},{2,18},{3,19},{4,20},{5,21},{6,22},{7,23},{8,24},{9,... | collective-permute-start | bytes 331784 | tf_op jit(solution)/shard_map/ppermute | solution.py:509
  127.1 7.0 %collective-permute-start.39 = (bf16[2,72,384]{2,1,0:T(8,128)(2,1)S(1)}, bf16[2,72,384]{2,1,0:T(8,128)(2,1)S(1)}, u32[]{:S(2)}, u32[]{:S(2)}) collective-permute-start(bf16[2,72,384]{2,1,0:T(8,128)(2,1)S(1)} %fusion.32), channel_id=1, source_target_pairs={{0,4},{1,5},{2,6},{3,7},{4,0},{5,1},{6,2},{7,3},{8,12},{9,13},{10,... | collective-permute-start | bytes 331784 | tf_op jit(solution)/shard_map/ppermute | solution.py:509
  128.3 6.9 %collective-permute-start.38 = (bf16[2,72,576]{2,1,0:T(8,128)(2,1)S(1)}, bf16[2,72,576]{2,1,0:T(8,128)(2,1)S(1)}, u32[]{:S(2)}, u32[]{:S(2)}) collective-permute-start(bf16[2,72,576]{2,1,0:T(8,128)(2,1)S(1)} %get-tuple-element.170), channel_id=1, source_target_pairs={{0,8},{1,9},{2,10},{3,11},{4,12},{5,13},{6,14},{7,15},{8,0},{9,1},... | collective-permute-start | bytes 497672 | tf_op jit(solution)/shard_map/ppermute | solution.py:509
  132.5 7.1 %collective-permute-start.43 = (bf16[2,72,384]{2,1,0:T(8,128)(2,1)S(1)}, bf16[2,72,384]{2,1,0:T(8,128)(2,1)S(1)}, u32[]{:S(2)}, u32[]{:S(2)}) collective-permute-start(bf16[2,72,384]{2,1,0:T(8,128)(2,1)S(1)} %fusion.17), channel_id=1, source_target_pairs={{0,2},{1,3},{2,0},{3,1},{4,6},{5,7},{6,4},{7,5},{8,10},{9,11},{10,... | collective-permute-start | bytes 331784 | tf_op jit(solution)/shard_map/ppermute | solution.py:509
  (51 other events, 326.1 us)

commit v11 on v9

--- a/solution.py
+++ b/solution.py
@@ -818,7 +818,7 @@
     b_x = net.swap(b1, xbit)
     b_z = net.swap(after(b1, gu2), znear)
     b_c = net.swap(b1, core)
-    a_xc = after(a_xc, b_x)
+    a_xc = after(a_xc, gu2, b1)
 
     cos_t, sin_t = rope_tables(full_length, n_seq)
     block_ids = [seq_index ^ o for o in order]
@@ -892,9 +892,9 @@
     def halves(keep, got):
         return add(keep[0], got[0]), add(keep[1], got[1])
 
-    a_got = net.swap(a_give, core)
-    b_got = net.swap(after(b_give, a_got), core)
-    down_got = net.swap(after(down_give, a_got), core)
+    down_got = net.swap(down_give, core)
+    a_got = net.swap(after(a_give, down_got), core)
+    b_got = net.swap(after(b_give, down_got), core)
     a, a_give = halves(a_keep, a_got)
     a_got = net.swap(a_give, xbit)
     b, b_give = halves(b_keep, b_got)

time: 148 us -> 144 us (0.973)
  waiting for transfers between devices: 49.3 us -> 43 us
  starting transfers between devices: 45.2 us -> 47.8 us
    ppermute x55, waiting for transfers between devices: 49.3 us -> 43 us  [swap(): return lax.ppermute(value, ('fsdp', 'seq'), pairs)]
    ppermute x55, starting transfers between devices: 45.2 us -> 47.8 us  [swap(): return lax.ppermute(value, ('fsdp', 'seq'), pairs)]
  transfers between devices with their start and end apart: 55 -> 55, of which waited for: 18 -> 17; matrix products, arithmetic and copies ran while one was open for 5% -> 6% of each run, Pallas kernels for 16% -> 17%
where the time goes in v11:
time: 144 us; the launch traced here: 143 us
  starting transfers between devices  47.8 us (33%)
  waiting for transfers between devices  43 us (30%)
  Pallas kernels  40.1 us (28%)
  other arithmetic  5.91 us (4%)
  local copies, waits for them, and re-layouts  5.31 us (4%)
    ppermute x55, starting transfers between devices, swap(): return lax.ppermute(value, ('fsdp', 'seq'), pairs)  47.8 us
    ppermute x55, waiting for transfers between devices, swap(): return lax.ppermute(value, ('fsdp', 'seq'), pairs)  43 us
    pallas_call x5, Pallas kernels, call(): pl.pallas_call(kernel, out_shape=outs, in_specs=specs, out_specs=whole(*o...  39.2 us
    unnamed x60, local copies, waits for them, and re-layouts  4.25 us
    convert_element_type x21, other arithmetic, add(): return (keep.astype(F32) + got.astype(F32)).astype(BF)  3.43 us
  transfers between devices with their start and end apart: 55, of which 17 were waited for; matrix products, arithmetic and copies ran while one was open for 6% of the time, Pallas kernels for 17%

profile of v11, /device:TPU:0, one launch (start us, length us, event | category | flops | bytes accessed | tf_op | source)
XLA Modules:
  0.0 143.4 jit_solution(9910146481466351073)
XLA Ops:
  3.8 4.1 %collective-permute-start.3 = (bf16[40,960]{1,0:T(8,128)(2,1)S(1)}, bf16[40,960]{1,0:T(8,128)(2,1)S(1)}, u32[]{:S(2)}, u32[]{:S(2)}) collective-permute-start(bf16[40,960]{1,0:T(8,128)(2,1)S(1)} %shard_map.187), channel_id=1, source_target_pairs={{0,16},{1,17},{2,18},{3,19},{4,20},{5,21},{6,22},{7,23},{8,24},{9,... | collective-permute-start | bytes 230408 | tf_op jit(solution)/shard_map/ppermute | solution.py:506
  10.0 1.6 %collective-permute-start = (bf16[256,640]{1,0:T(8,128)(2,1)S(1)}, bf16[256,640]{1,0:T(8,128)(2,1)S(1)}, u32[]{:S(2)}, u32[]{:S(2)}) collective-permute-start(bf16[256,640]{1,0:T(8,128)(2,1)S(1)} %pad_maximum_fusion.3.b0), channel_id=1, source_target_pairs={{0,2},{1,3},{2,0},{3,1},{4,6},{5,7},{6,4},{7,5},{8,10},{9,11},{10,... | collective-permute-start | bytes 983048 | tf_op jit(solution)/shard_map/ppermute | solution.py:506
  12.2 2.7 %collective-permute-start.10 = (bf16[136,576]{1,0:T(8,128)(2,1)S(1)}, bf16[136,576]{1,0:T(8,128)(2,1)S(1)}, u32[]{:S(2)}, u32[]{:S(2)}) collective-permute-start(bf16[136,576]{1,0:T(8,128)(2,1)S(1)} %dynamic-slice_bitcast_fusion), channel_id=1, source_target_pairs={{0,16},{1,17},{2,18},{3,19},{4,20},{5,21},{6,22},{7,23},{8,24},{9,... | collective-permute-start | bytes 470024 | tf_op jit(solution)/shard_map/ppermute | solution.py:506
  15.3 1.6 %collective-permute-start.4 = (bf16[2,40,960]{2,1,0:T(8,128)(2,1)S(1)}, bf16[2,40,960]{2,1,0:T(8,128)(2,1)S(1)}, u32[]{:S(2)}, u32[]{:S(2)}) collective-permute-start(bf16[2,40,960]{2,1,0:T(8,128)(2,1)S(1)} %pad_maximum_fusion.6), channel_id=1, source_target_pairs={{0,8},{1,9},{2,10},{3,11},{4,12},{5,13},{6,14},{7,15},{8,0},{9,1},... | collective-permute-start | bytes 460808 | tf_op jit(solution)/shard_map/ppermute | solution.py:506
  17.0 7.6 %collective-permute-done.8 = bf16[72,768]{1,0:T(8,128)(2,1)S(1)} collective-permute-done((bf16[72,768]{1,0:T(8,128)(2,1)S(1)}, bf16[72,768]{1,0:T(8,128)(2,1)S(1)}, u32[]{:S(2)}, u32[]{:S(2)}) %collective-permute-start.8) | collective-permute-done | bytes 110624 | tf_op jit(solution)/shard_map/ppermute | solution.py:506
  24.9 1.6 %collective-permute-start.5 = (bf16[2,2,40,960]{3,2,1,0:T(8,128)(2,1)S(1)}, bf16[2,2,40,960]{3,2,1,0:T(8,128)(2,1)S(1)}, u32[]{:S(2)}, u32[]{:S(2)}) collective-permute-start(bf16[2,2,40,960]{3,2,1,0:T(8,128)(2,1)S(1)} %pad_maximum_fusion.4.a00), channel_id=1, source_target_pairs={{0,4},{1,5},{2,6},{3,7},{4,0},{5,1},{6,2},{7,3},{8,12},{9,13},{10,... | collective-permute-start | bytes 921608 | tf_op jit(solution)/shard_map/ppermute | solution.py:506
  27.7 1.6 %collective-permute-start.12 = (bf16[2,136,576]{2,1,0:T(8,128)(2,1)S(1)}, bf16[2,136,576]{2,1,0:T(8,128)(2,1)S(1)}, u32[]{:S(2)}, u32[]{:S(2)}) collective-permute-start(bf16[2,136,576]{2,1,0:T(8,128)(2,1)S(1)} %pad_maximum_fusion.2.refs_0_), channel_id=1, source_target_pairs={{0,4},{1,5},{2,6},{3,7},{4,0},{5,1},{6,2},{7,3},{8,12},{9,13},{10,... | collective-permute-start | bytes 940040 | tf_op jit(solution)/shard_map/ppermute | solution.py:506
  29.7 4.5 %collective-permute-done.9 = bf16[2,72,768]{2,1,0:T(8,128)(2,1)S(1)} collective-permute-done((bf16[2,72,768]{2,1,0:T(8,128)(2,1)S(1)}, bf16[2,72,768]{2,1,0:T(8,128)(2,1)S(1)}, u32[]{:S(2)}, u32[]{:S(2)}) %collective-permute-start.9) | collective-permute-done | bytes 221216 | tf_op jit(solution)/shard_map/ppermute | solution.py:506
  34.3 1.6 %collective-permute-start.21 = (bf16[2,2,72,768]{3,2,1,0:T(8,128)(2,1)S(1)}, bf16[2,2,72,768]{3,2,1,0:T(8,128)(2,1)}, u32[]{:S(2)}, u32[]{:S(2)}) collective-permute-start(bf16[2,2,72,768]{3,2,1,0:T(8,128)(2,1)S(1)} %pad_maximum_fusion.refs_8_), channel_id=1, source_target_pairs={{0,4},{1,5},{2,6},{3,7},{4,0},{5,1},{6,2},{7,3},{8,12},{9,13},{10,... | collective-permute-start | bytes 1327112 | tf_op jit(solution)/shard_map/ppermute | solution.py:506
  39.4 10.7 %shard_map.188 = (bf16[256,576]{1,0:T(8,128)(2,1)S(1)}, bf16[2,3,384,64]{3,2,1,0:T(8,128)(2,1)}, bf16[2,3,512,64]{3,2,1,0:T(8,128)(2,1)}, bf16[2,3,512,64]{3,2,1...) custom-call(s32[2]{0:T(128)S(1)} %pad_add_fusion.meta, bf16[256,640]{1,0:T(8,128)(2,1)S(1)} %pad_maximum_fusion.3.b0, ...), custom_call_target="tpu_custom_call" | custom-call | flops 12000000000 | bytes 6074880 | tf_op jit(solution)/shard_map/pallas_call | solution.py:55
  50.5 1.6 %collective-permute-done.21.refs_12_ = bf16[2,2,72,768]{3,2,1,0:T(8,128)(2,1)} collective-permute-done((bf16[2,2,72,768]{3,2,1,0:T(8,128)(2,1)S(1)}, bf16[2,2,72,768]{3,2,1,0:T(8,128)(2,1)}, u32[]{:S(2)}, u32[]{:S(2)}) %collective-permute-start.21) | collective-permute-done | bytes 442400 | tf_op jit(solution)/shard_map/ppermute | solution.py:506
  53.1 1.5 %collective-permute-start.17 = (bf16[2,136,576]{2,1,0:T(8,128)(2,1)}, bf16[2,136,576]{2,1,0:T(8,128)(2,1)}, u32[]{:S(2)}, u32[]{:S(2)}) collective-permute-start(bf16[2,136,576]{2,1,0:T(8,128)(2,1)} %collective-permute-done.15.refs_4_), channel_id=1, source_target_pairs={{0,4},{1,5},{2,6},{3,7},{4,0},{5,1},{6,2},{7,3},{8,12},{9,13},{10,... | collective-permute-start | bytes 940040 | tf_op jit(solution)/shard_map/ppermute | solution.py:506
  55.1 9.0 %collective-permute-done.23.refs_14_ = bf16[2,2,72,768]{3,2,1,0:T(8,128)(2,1)} collective-permute-done((bf16[2,2,72,768]{3,2,1,0:T(8,128)(2,1)}, bf16[2,2,72,768]{3,2,1,0:T(8,128)(2,1)}, u32[]{:S(2)}, u32[]{:S(2)}) %collective-permute-start.23) | collective-permute-done | bytes 442400 | tf_op jit(solution)/shard_map/ppermute | solution.py:506
  65.2 1.5 %collective-permute-done.16.refs_5_ = bf16[2,136,576]{2,1,0:T(8,128)(2,1)} collective-permute-done((bf16[2,136,576]{2,1,0:T(8,128)(2,1)}, bf16[2,136,576]{2,1,0:T(8,128)(2,1)}, u32[]{:S(2)}, u32[]{:S(2)}) %collective-permute-start.16) | collective-permute-done | bytes 313376 | tf_op jit(solution)/shard_map/ppermute | solution.py:506
  67.3 13.4 %shard_map.189 = (bf16[2,576,128]{2,1,0:T(8,128)(2,1)}, bf16[2,2,2,2,72,384]{5,4,3,2,1,0:T(8,128)(2,1)}, bf16[2,2,2,2,72,384]{5,4,3,2,1,0:T(8,128)(2,1)}, bf16[2...) custom-call(s32[2]{0:T(128)S(1)} %pad_add_fusion.meta, ...), custom_call_target="tpu_custom_call" | custom-call | flops 14000000000 | bytes 14311168 | tf_op jit(solution)/shard_map/pallas_call | solution.py:55
  80.9 3.4 %collective-permute-done.25 = bf16[2,2,2,2,72,576]{5,4,3,2,1,0:T(8,128)(2,1)S(1)} collective-permute-done((bf16[2,2,2,2,72,576]{5,4,3,2,1,0:T(8,128)(2,1)}, bf16[2,2,2,2,72,576]{5,4,3,2,1,0:T(8,128)(2,1)S(1)}, u32[]{:S(2)}, u32[]{:S(2)}) %collective-permute-start.25) | collective-permute-done | bytes 1327136 | tf_op jit(solution)/shard_map/ppermute | solution.py:506
  84.7 1.8 %add_convert_fusion = (bf16[1,2,2,2,72,576]{5,4,3,2,1,0:T(8,128)(2,1)S(1)}, bf16[2,2,2,72,576]{4,3,2,1,0:T(8,128)(2,1)S(1)}) fusion(bf16[2,2,2,2,72,576]{5,4,3,2,1,0:T(8,128)(2,1)S(1)} %collective-permute-done.25, bf16[2,2,2,2,72,576]{5,4,3,2,1,0:T(8,128)(2,1)} %get-tuple-element.98), kind=kLoop, calls=%fused_computation | loop fusion | flops 2654208 | bytes 3981312 | tf_op jit(solution)/shard_map/convert_element_type | solution.py:890
  87.4 1.6 %collective-permute-start.36 = (bf16[2,2,2,72,384]{4,3,2,1,0:T(8,128)(2,1)S(1)}, bf16[2,2,2,72,384]{4,3,2,1,0:T(8,128)(2,1)S(1)}, u32[]{:S(2)}, u32[]{:S(2)}) collective-permute-start(bf16[2,2,2,72,384]{4,3,2,1,0:T(8,128)(2,1)S(1)} %get-tuple-element.156), channel_id=1, source_target_pairs={{0,4},{1,5},{2,6},{3,7},{4,0},{5,1},{6,2},{7,3},{8,12},{9,13},{10,... | collective-permute-start | bytes 1327112 | tf_op jit(solution)/shard_map/ppermute | solution.py:506
  89.4 11.2 %shard_map.190 = (bf16[256,640]{1,0:T(8,128)(2,1)S(1)}, bf16[2,256,384]{2,1,0:T(8,128)(2,1)S(1)}, bf16[2,256,384]{2,1,0:T(8,128)(2,1)S(1)}, bf16[2,2,2,2,80,256]...) custom-call(s32[2]{0:T(128)S(1)} %pad_add_fusion.meta, bf16[256,640]{1,0:T(8,128)(2,1)S(1)} %pad_maximum_fusion.3.b0, ...), custom_call_target="tpu_custom_call" | custom-call | flops 14000000000 | bytes 7273216 | tf_op jit(solution)/shard_map/pallas_call | solution.py:55
  101.3 1.9 %collective-permute-start.34 = (bf16[2,2,72,384]{3,2,1,0:T(8,128)(2,1)S(1)}, bf16[2,2,72,384]{3,2,1,0:T(8,128)(2,1)S(1)}, u32[]{:S(2)}, u32[]{:S(2)}) collective-permute-start(bf16[2,2,72,384]{3,2,1,0:T(8,128)(2,1)S(1)} %get-tuple-element.166), channel_id=1, source_target_pairs={{0,16},{1,17},{2,18},{3,19},{4,20},{5,21},{6,22},{7,23},{8,24},{9,... | collective-permute-start | bytes 663560 | tf_op jit(solution)/shard_map/ppermute | solution.py:506
  103.3 2.0 %collective-permute-start.37 = (bf16[2,2,72,384]{3,2,1,0:T(8,128)(2,1)S(1)}, bf16[2,2,72,384]{3,2,1,0:T(8,128)(2,1)S(1)}, u32[]{:S(2)}, u32[]{:S(2)}) collective-permute-start(bf16[2,2,72,384]{3,2,1,0:T(8,128)(2,1)S(1)} %get-tuple-element.163), channel_id=1, source_target_pairs={{0,8},{1,9},{2,10},{3,11},{4,12},{5,13},{6,14},{7,15},{8,0},{9,1},... | collective-permute-start | bytes 663560 | tf_op jit(solution)/shard_map/ppermute | solution.py:506
  105.5 1.6 %collective-permute-start.35 = (bf16[2,2,2,80,256]{4,3,2,1,0:T(8,128)(2,1)S(1)}, bf16[2,2,2,80,256]{4,3,2,1,0:T(8,128)(2,1)S(1)}, u32[]{:S(2)}, u32[]{:S(2)}) collective-permute-start(bf16[2,2,2,80,256]{4,3,2,1,0:T(8,128)(2,1)S(1)} %get-tuple-element.162), channel_id=1, source_target_pairs={{0,2},{1,3},{2,0},{3,1},{4,6},{5,7},{6,4},{7,5},{8,10},{9,11},{10,... | collective-permute-start | bytes 983048 | tf_op jit(solution)/shard_map/ppermute | solution.py:506
  108.0 1.4 collective-permute-start.32
  109.3 3.6 %collective-permute-done.37 = bf16[2,2,72,384]{3,2,1,0:T(8,128)(2,1)S(1)} collective-permute-done((bf16[2,2,72,384]{3,2,1,0:T(8,128)(2,1)S(1)}, bf16[2,2,72,384]{3,2,1,0:T(8,128)(2,1)S(1)}, u32[]{:S(2)}, u32[]{:S(2)}) %collective-permute-start.37) | collective-permute-done | bytes 221216 | tf_op jit(solution)/shard_map/ppermute | solution.py:506
  112.9 3.5 %collective-permute-start.38 = (bf16[2,72,384]{2,1,0:T(8,128)(2,1)S(1)}, bf16[2,72,384]{2,1,0:T(8,128)(2,1)S(1)}, u32[]{:S(2)}, u32[]{:S(2)}) collective-permute-start(bf16[2,72,384]{2,1,0:T(8,128)(2,1)S(1)} %fusion.33), channel_id=1, source_target_pairs={{0,16},{1,17},{2,18},{3,19},{4,20},{5,21},{6,22},{7,23},{8,24},{9,... | collective-permute-start | bytes 331784 | tf_op jit(solution)/shard_map/ppermute | solution.py:506
  118.9 1.9 %collective-permute-start.42 = (bf16[2,72,576]{2,1,0:T(8,128)(2,1)S(1)}, bf16[2,72,576]{2,1,0:T(8,128)(2,1)S(1)}, u32[]{:S(2)}, u32[]{:S(2)}) collective-permute-start(bf16[2,72,576]{2,1,0:T(8,128)(2,1)S(1)} %get-tuple-element.170), channel_id=1, source_target_pairs={{0,8},{1,9},{2,10},{3,11},{4,12},{5,13},{6,14},{7,15},{8,0},{9,1},... | collective-permute-start | bytes 497672 | tf_op jit(solution)/shard_map/ppermute | solution.py:506
  120.8 1.9 %shard_map.191 = f32[2,576,128]{2,1,0:T(8,128)} custom-call(bf16[256,640]{1,0:T(8,128)(2,1)S(1)} %get-tuple-element.101.dq, bf16[256,384]{1,0:T(8,128)(2,1)S(1)} %get-tuple-element.168.own, bf16[256,384]{1,0:T(8,128)(2,1)S(1)} %collective-permute-done.32.other, bf16[256,576]{1,0:T(8,128)(2,1)S(1)} %bitcast.211, f32[256,576]{1,0:T(8,128)S(1)} %copy-done.9, ...), custom_call_target="tpu_custom_call" | custom-call | flops 3000000000 | bytes 3305984 | tf_op jit(solution)/shard_map/pallas_call | solution.py:55
  124.0 1.6 %collective-permute-start.40 = (bf16[2,72,384]{2,1,0:T(8,128)(2,1)S(1)}, bf16[2,72,384]{2,1,0:T(8,128)(2,1)S(1)}, u32[]{:S(2)}, u32[]{:S(2)}) collective-permute-start(bf16[2,72,384]{2,1,0:T(8,128)(2,1)S(1)} %fusion.19), channel_id=1, source_target_pairs={{0,2},{1,3},{2,0},{3,1},{4,6},{5,7},{6,4},{7,5},{8,10},{9,11},{10,... | collective-permute-start | bytes 331784 | tf_op jit(solution)/shard_map/ppermute | solution.py:506
  127.8 1.5 %collective-permute-start.50 = (bf16[80,256]{1,0:T(8,128)(2,1)S(1)}, bf16[80,256]{1,0:T(8,128)(2,1)S(1)}, u32[]{:S(2)}, u32[]{:S(2)}) collective-permute-start(bf16[80,256]{1,0:T(8,128)(2,1)S(1)} %fusion.42), channel_id=1, source_target_pairs={{0,16},{1,17},{2,18},{3,19},{4,20},{5,21},{6,22},{7,23},{8,24},{9,... | collective-permute-start | bytes 122888 | tf_op jit(solution)/shard_map/ppermute | solution.py:506
  129.3 3.8 %collective-permute-done.47 = bf16[72,576]{1,0:T(8,128)(2,1)S(1)} collective-permute-done((bf16[72,576]{1,0:T(8,128)(2,1)S(1)}, bf16[72,576]{1,0:T(8,128)(2,1)S(1)}, u32[]{:S(2)}, u32[]{:S(2)}) %collective-permute-start.47) | collective-permute-done | bytes 82976 | tf_op jit(solution)/shard_map/ppermute | solution.py:506
  136.0 2.4 %collective-permute-done.51.r1 = bf16[80,256]{1,0:T(8,128)(2,1)S(1)} collective-permute-done((bf16[80,256]{1,0:T(8,128)(2,1)S(1)}, bf16[80,256]{1,0:T(8,128)(2,1)S(1)}, u32[]{:S(2)}, u32[]{:S(2)}) %collective-permute-start.51) | collective-permute-done | bytes 40992 | tf_op jit(solution)/shard_map/ppermute | solution.py:506
  141.4 1.9 %shard_map.192 = (f32[72,3072]{1,0:T(8,128)}, f32[192,576]{1,0:T(8,128)}, f32[72,576]{1,0:T(8,128)}, f32[72,960]{1,0:T(8,128)}, f32[1,96]{1,0:T(1,128)}, /*index=5*/f32[1,24]{1,0:T(1,128)}, f32[2,72]{1,0:T(2,128)}) custom-call(s32[2]{0:T(128)S(1)} %pad_add_fusion.meta, bf16[2,72,384]{2,1,0:T(8,128)(2,1)S(1)} %add_convert_fusion.11.a_near, ...), custom_call_target="tpu_custom_call" | custom-call | flops 3000000000 | bytes 2708512 | tf_op jit(solution)/shard_map/pallas_call | solution.py:55
  (196 shorter events, 30.5 us)
Async XLA Ops:
  3.8 11.5 %collective-permute-start.3 = (bf16[40,960]{1,0:T(8,128)(2,1)S(1)}, bf16[40,960]{1,0:T(8,128)(2,1)S(1)}, u32[]{:S(2)}, u32[]{:S(2)}) collective-permute-start(bf16[40,960]{1,0:T(8,128)(2,1)S(1)} %shard_map.187), channel_id=1, source_target_pairs={{0,16},{1,17},{2,18},{3,19},{4,20},{5,21},{6,22},{7,23},{8,24},{9,... | collective-permute-start | bytes 230408 | tf_op jit(solution)/shard_map/ppermute | solution.py:506
  10.0 19.5 %collective-permute-start.1 = (bf16[256,640]{1,0:T(8,128)(2,1)S(1)}, bf16[256,640]{1,0:T(8,128)(2,1)S(1)}, u32[]{:S(2)}, u32[]{:S(2)}) collective-permute-start(bf16[256,640]{1,0:T(8,128)(2,1)S(1)} %pad_maximum_fusion.3.b0), channel_id=1, source_target_pairs={{0,1},{1,0},{2,3},{3,2},{4,5},{5,4},{6,7},{7,6},{8,9},{9,8},{10,11... | collective-permute-start | bytes 983048 | tf_op jit(solution)/shard_map/ppermute | solution.py:506
  10.0 17.7 %collective-permute-start = (bf16[256,640]{1,0:T(8,128)(2,1)S(1)}, bf16[256,640]{1,0:T(8,128)(2,1)S(1)}, u32[]{:S(2)}, u32[]{:S(2)}) collective-permute-start(bf16[256,640]{1,0:T(8,128)(2,1)S(1)} %pad_maximum_fusion.3.b0), channel_id=1, source_target_pairs={{0,2},{1,3},{2,0},{3,1},{4,6},{5,7},{6,4},{7,5},{8,10},{9,11},{10,... | collective-permute-start | bytes 983048 | tf_op jit(solution)/shard_map/ppermute | solution.py:506
  11.6 13.0 %collective-permute-start.8 = (bf16[72,768]{1,0:T(8,128)(2,1)S(1)}, bf16[72,768]{1,0:T(8,128)(2,1)S(1)}, u32[]{:S(2)}, u32[]{:S(2)}) collective-permute-start(bf16[72,768]{1,0:T(8,128)(2,1)S(1)} %constant_dynamic-slice_fusion), channel_id=1, source_target_pairs={{0,16},{1,17},{2,18},{3,19},{4,20},{5,21},{6,22},{7,23},{8,24},{9,... | collective-permute-start | bytes 331784 | tf_op jit(solution)/shard_map/ppermute | solution.py:506
  12.2 15.4 %collective-permute-start.10 = (bf16[136,576]{1,0:T(8,128)(2,1)S(1)}, bf16[136,576]{1,0:T(8,128)(2,1)S(1)}, u32[]{:S(2)}, u32[]{:S(2)}) collective-permute-start(bf16[136,576]{1,0:T(8,128)(2,1)S(1)} %dynamic-slice_bitcast_fusion), channel_id=1, source_target_pairs={{0,16},{1,17},{2,18},{3,19},{4,20},{5,21},{6,22},{7,23},{8,24},{9,... | collective-permute-start | bytes 470024 | tf_op jit(solution)/shard_map/ppermute | solution.py:506
  15.3 9.4 %collective-permute-start.4 = (bf16[2,40,960]{2,1,0:T(8,128)(2,1)S(1)}, bf16[2,40,960]{2,1,0:T(8,128)(2,1)S(1)}, u32[]{:S(2)}, u32[]{:S(2)}) collective-permute-start(bf16[2,40,960]{2,1,0:T(8,128)(2,1)S(1)} %pad_maximum_fusion.6), channel_id=1, source_target_pairs={{0,8},{1,9},{2,10},{3,11},{4,12},{5,13},{6,14},{7,15},{8,0},{9,1},... | collective-permute-start | bytes 460808 | tf_op jit(solution)/shard_map/ppermute | solution.py:506
  24.8 13.8 %collective-permute-start.6 = (bf16[2,2,40,960]{3,2,1,0:T(8,128)(2,1)S(1)}, bf16[2,2,40,960]{3,2,1,0:T(8,128)(2,1)S(1)}, u32[]{:S(2)}, u32[]{:S(2)}) collective-permute-start(bf16[2,2,40,960]{3,2,1,0:T(8,128)(2,1)S(1)} %pad_maximum_fusion.4.a00), channel_id=1, source_target_pairs={{0,1},{1,0},{2,3},{3,2},{4,5},{5,4},{6,7},{7,6},{8,9},{9,8},{10,11... | collective-permute-start | bytes 921608 | tf_op jit(solution)/shard_map/ppermute | solution.py:506
  24.9 11.0 %collective-permute-start.5 = (bf16[2,2,40,960]{3,2,1,0:T(8,128)(2,1)S(1)}, bf16[2,2,40,960]{3,2,1,0:T(8,128)(2,1)S(1)}, u32[]{:S(2)}, u32[]{:S(2)}) collective-permute-start(bf16[2,2,40,960]{3,2,1,0:T(8,128)(2,1)S(1)} %pad_maximum_fusion.4.a00), channel_id=1, source_target_pairs={{0,4},{1,5},{2,6},{3,7},{4,0},{5,1},{6,2},{7,3},{8,12},{9,13},{10,... | collective-permute-start | bytes 921608 | tf_op jit(solution)/shard_map/ppermute | solution.py:506
  27.7 24.9 %collective-permute-start.12 = (bf16[2,136,576]{2,1,0:T(8,128)(2,1)S(1)}, bf16[2,136,576]{2,1,0:T(8,128)(2,1)S(1)}, u32[]{:S(2)}, u32[]{:S(2)}) collective-permute-start(bf16[2,136,576]{2,1,0:T(8,128)(2,1)S(1)} %pad_maximum_fusion.2.refs_0_), channel_id=1, source_target_pairs={{0,4},{1,5},{2,6},{3,7},{4,0},{5,1},{6,2},{7,3},{8,12},{9,13},{10,... | collective-permute-start | bytes 940040 | tf_op jit(solution)/shard_map/ppermute | solution.py:506
  34.3 17.8 %collective-permute-start.21 = (bf16[2,2,72,768]{3,2,1,0:T(8,128)(2,1)S(1)}, bf16[2,2,72,768]{3,2,1,0:T(8,128)(2,1)}, u32[]{:S(2)}, u32[]{:S(2)}) collective-permute-start(bf16[2,2,72,768]{3,2,1,0:T(8,128)(2,1)S(1)} %pad_maximum_fusion.refs_8_), channel_id=1, source_target_pairs={{0,4},{1,5},{2,6},{3,7},{4,0},{5,1},{6,2},{7,3},{8,12},{9,13},{10,... | collective-permute-start | bytes 1327112 | tf_op jit(solution)/shard_map/ppermute | solution.py:506
  35.9 18.7 %collective-permute-start.19 = (bf16[2,2,72,768]{3,2,1,0:T(8,128)(2,1)S(1)}, bf16[2,2,72,768]{3,2,1,0:T(8,128)(2,1)S(1)}, u32[]{:S(2)}, u32[]{:S(2)}) collective-permute-start(bf16[2,2,72,768]{3,2,1,0:T(8,128)(2,1)S(1)} %pad_maximum_fusion.refs_8_), channel_id=1, source_target_pairs={{0,1},{1,0},{2,3},{3,2},{4,5},{5,4},{6,7},{7,6},{8,9},{9,8},{10,11... | collective-permute-start | bytes 1327112 | tf_op jit(solution)/shard_map/ppermute | solution.py:506
  38.2 12.3 %collective-permute-start.13 = (bf16[2,2,72,768]{3,2,1,0:T(8,128)(2,1)S(1)}, bf16[2,2,72,768]{3,2,1,0:T(8,128)(2,1)}, u32[]{:S(2)}, u32[]{:S(2)}) collective-permute-start(bf16[2,2,72,768]{3,2,1,0:T(8,128)(2,1)S(1)} %pad_maximum_fusion.refs_8_), channel_id=1, source_target_pairs={{0,2},{1,3},{2,0},{3,1},{4,6},{5,7},{6,4},{7,5},{8,10},{9,11},{10,... | collective-permute-start | bytes 1327112 | tf_op jit(solution)/shard_map/ppermute | solution.py:506
  38.7 14.4 %collective-permute-start.15 = (bf16[2,136,576]{2,1,0:T(8,128)(2,1)S(1)}, bf16[2,136,576]{2,1,0:T(8,128)(2,1)}, u32[]{:S(2)}, u32[]{:S(2)}) collective-permute-start(bf16[2,136,576]{2,1,0:T(8,128)(2,1)S(1)} %pad_maximum_fusion.2.refs_0_), channel_id=1, source_target_pairs={{0,8},{1,9},{2,10},{3,11},{4,12},{5,13},{6,14},{7,15},{8,0},{9,1},... | collective-permute-start | bytes 940040 | tf_op jit(solution)/shard_map/ppermute | solution.py:506
  52.1 12.0 %collective-permute-start.23 = (bf16[2,2,72,768]{3,2,1,0:T(8,128)(2,1)}, bf16[2,2,72,768]{3,2,1,0:T(8,128)(2,1)}, u32[]{:S(2)}, u32[]{:S(2)}) collective-permute-start(bf16[2,2,72,768]{3,2,1,0:T(8,128)(2,1)} %collective-permute-done.21.refs_12_), channel_id=1, source_target_pairs={{0,2},{1,3},{2,0},{3,1},{4,6},{5,7},{6,4},{7,5},{8,10},{9,11},{10,... | collective-permute-start | bytes 1327112 | tf_op jit(solution)/shard_map/ppermute | solution.py:506
  52.6 11.5 %collective-permute-start.14 = (bf16[2,136,576]{2,1,0:T(8,128)(2,1)S(1)}, bf16[2,136,576]{2,1,0:T(8,128)(2,1)S(1)}, u32[]{:S(2)}, u32[]{:S(2)}) collective-permute-start(bf16[2,136,576]{2,1,0:T(8,128)(2,1)S(1)} %collective-permute-done.12.refs_2_), channel_id=1, source_target_pairs={{0,1},{1,0},{2,3},{3,2},{4,5},{5,4},{6,7},{7,6},{8,9},{9,8},{10,11... | collective-permute-start | bytes 940040 | tf_op jit(solution)/shard_map/ppermute | solution.py:506
  53.1 11.6 %collective-permute-start.17 = (bf16[2,136,576]{2,1,0:T(8,128)(2,1)}, bf16[2,136,576]{2,1,0:T(8,128)(2,1)}, u32[]{:S(2)}, u32[]{:S(2)}) collective-permute-start(bf16[2,136,576]{2,1,0:T(8,128)(2,1)} %collective-permute-done.15.refs_4_), channel_id=1, source_target_pairs={{0,4},{1,5},{2,6},{3,7},{4,0},{5,1},{6,2},{7,3},{8,12},{9,13},{10,... | collective-permute-start | bytes 940040 | tf_op jit(solution)/shard_map/ppermute | solution.py:506
  54.6 12.2 %collective-permute-start.22 = (bf16[2,2,72,768]{3,2,1,0:T(8,128)(2,1)}, bf16[2,2,72,768]{3,2,1,0:T(8,128)(2,1)}, u32[]{:S(2)}, u32[]{:S(2)}) collective-permute-start(bf16[2,2,72,768]{3,2,1,0:T(8,128)(2,1)} %collective-permute-done.21.refs_12_), channel_id=1, source_target_pairs={{0,1},{1,0},{2,3},{3,2},{4,5},{5,4},{6,7},{7,6},{8,9},{9,8},{10,11... | collective-permute-start | bytes 1327112 | tf_op jit(solution)/shard_map/ppermute | solution.py:506
  54.6 12.1 %collective-permute-start.20 = (bf16[2,2,72,768]{3,2,1,0:T(8,128)(2,1)}, bf16[2,2,72,768]{3,2,1,0:T(8,128)(2,1)}, u32[]{:S(2)}, u32[]{:S(2)}) collective-permute-start(bf16[2,2,72,768]{3,2,1,0:T(8,128)(2,1)} %collective-permute-done.13.refs_10_), channel_id=1, source_target_pairs={{0,1},{1,0},{2,3},{3,2},{4,5},{5,4},{6,7},{7,6},{8,9},{9,8},{10,11... | collective-permute-start | bytes 1327112 | tf_op jit(solution)/shard_map/ppermute | solution.py:506
  86.5 18.8 %collective-permute-start.29 = (bf16[2,2,2,72,576]{4,3,2,1,0:T(8,128)(2,1)S(1)}, bf16[2,2,2,72,576]{4,3,2,1,0:T(8,128)(2,1)S(1)}, u32[]{:S(2)}, u32[]{:S(2)}) collective-permute-start(bf16[2,2,2,72,576]{4,3,2,1,0:T(8,128)(2,1)S(1)} %get-tuple-element.154), channel_id=1, source_target_pairs={{0,2},{1,3},{2,0},{3,1},{4,6},{5,7},{6,4},{7,5},{8,10},{9,11},{10,... | collective-permute-start | bytes 1990664 | tf_op jit(solution)/shard_map/ppermute | solution.py:506
  87.4 15.8 %collective-permute-start.36 = (bf16[2,2,2,72,384]{4,3,2,1,0:T(8,128)(2,1)S(1)}, bf16[2,2,2,72,384]{4,3,2,1,0:T(8,128)(2,1)S(1)}, u32[]{:S(2)}, u32[]{:S(2)}) collective-permute-start(bf16[2,2,2,72,384]{4,3,2,1,0:T(8,128)(2,1)S(1)} %get-tuple-element.156), channel_id=1, source_target_pairs={{0,4},{1,5},{2,6},{3,7},{4,0},{5,1},{6,2},{7,3},{8,12},{9,13},{10,... | collective-permute-start | bytes 1327112 | tf_op jit(solution)/shard_map/ppermute | solution.py:506
  89.2 12.0 %collective-permute-start.31 = (bf16[2,2,2,72,384]{4,3,2,1,0:T(8,128)(2,1)S(1)}, bf16[2,2,2,72,384]{4,3,2,1,0:T(8,128)(2,1)S(1)}, u32[]{:S(2)}, u32[]{:S(2)}) collective-permute-start(bf16[2,2,2,72,384]{4,3,2,1,0:T(8,128)(2,1)S(1)} %get-tuple-element.158), channel_id=1, source_target_pairs={{0,8},{1,9},{2,10},{3,11},{4,12},{5,13},{6,14},{7,15},{8,0},{9,1},... | collective-permute-start | bytes 1327112 | tf_op jit(solution)/shard_map/ppermute | solution.py:506
  100.7 7.2 %collective-permute-start.28 = (bf16[2,256,384]{2,1,0:T(8,128)(2,1)S(1)}, bf16[2,256,384]{2,1,0:T(8,128)(2,1)S(1)}, u32[]{:S(2)}, u32[]{:S(2)}) collective-permute-start(bf16[2,256,384]{2,1,0:T(8,128)(2,1)S(1)} %get-tuple-element.103), channel_id=1, source_target_pairs={{0,1},{1,0},{2,3},{3,2},{4,5},{5,4},{6,7},{7,6},{8,9},{9,8},{10,11... | collective-permute-start | bytes 1179656 | tf_op jit(solution)/shard_map/ppermute | solution.py:506
  101.3 16.4 %collective-permute-start.34 = (bf16[2,2,72,384]{3,2,1,0:T(8,128)(2,1)S(1)}, bf16[2,2,72,384]{3,2,1,0:T(8,128)(2,1)S(1)}, u32[]{:S(2)}, u32[]{:S(2)}) collective-permute-start(bf16[2,2,72,384]{3,2,1,0:T(8,128)(2,1)S(1)} %get-tuple-element.166), channel_id=1, source_target_pairs={{0,16},{1,17},{2,18},{3,19},{4,20},{5,21},{6,22},{7,23},{8,24},{9,... | collective-permute-start | bytes 663560 | tf_op jit(solution)/shard_map/ppermute | solution.py:506
  103.3 9.6 %collective-permute-start.37 = (bf16[2,2,72,384]{3,2,1,0:T(8,128)(2,1)S(1)}, bf16[2,2,72,384]{3,2,1,0:T(8,128)(2,1)S(1)}, u32[]{:S(2)}, u32[]{:S(2)}) collective-permute-start(bf16[2,2,72,384]{3,2,1,0:T(8,128)(2,1)S(1)} %get-tuple-element.163), channel_id=1, source_target_pairs={{0,8},{1,9},{2,10},{3,11},{4,12},{5,13},{6,14},{7,15},{8,0},{9,1},... | collective-permute-start | bytes 663560 | tf_op jit(solution)/shard_map/ppermute | solution.py:506
  105.5 11.0 %collective-permute-start.35 = (bf16[2,2,2,80,256]{4,3,2,1,0:T(8,128)(2,1)S(1)}, bf16[2,2,2,80,256]{4,3,2,1,0:T(8,128)(2,1)S(1)}, u32[]{:S(2)}, u32[]{:S(2)}) collective-permute-start(bf16[2,2,2,80,256]{4,3,2,1,0:T(8,128)(2,1)S(1)} %get-tuple-element.162), channel_id=1, source_target_pairs={{0,2},{1,3},{2,0},{3,1},{4,6},{5,7},{6,4},{7,5},{8,10},{9,11},{10,... | collective-permute-start | bytes 983048 | tf_op jit(solution)/shard_map/ppermute | solution.py:506
  107.3 11.5 %collective-permute-start.33 = (bf16[2,2,72,576]{3,2,1,0:T(8,128)(2,1)S(1)}, bf16[2,2,72,576]{3,2,1,0:T(8,128)(2,1)S(1)}, u32[]{:S(2)}, u32[]{:S(2)}) collective-permute-start(bf16[2,2,72,576]{3,2,1,0:T(8,128)(2,1)S(1)} %get-tuple-element.160), channel_id=1, source_target_pairs={{0,4},{1,5},{2,6},{3,7},{4,0},{5,1},{6,2},{7,3},{8,12},{9,13},{10,... | collective-permute-start | bytes 995336 | tf_op jit(solution)/shard_map/ppermute | solution.py:506
  108.0 12.8 %collective-permute-start.32 = (bf16[256,384]{1,0:T(8,128)(2,1)S(1)}, bf16[256,384]{1,0:T(8,128)(2,1)S(1)}, u32[]{:S(2)}, u32[]{:S(2)}) collective-permute-start(bf16[256,384]{1,0:T(8,128)(2,1)S(1)} %get-tuple-element.167), channel_id=1, source_target_pairs={{0,2},{1,3},{2,0},{3,1},{4,6},{5,7},{6,4},{7,5},{8,10},{9,11},{10,... | collective-permute-start | bytes 589832 | tf_op jit(solution)/shard_map/ppermute | solution.py:506
  112.9 11.0 %collective-permute-start.38 = (bf16[2,72,384]{2,1,0:T(8,128)(2,1)S(1)}, bf16[2,72,384]{2,1,0:T(8,128)(2,1)S(1)}, u32[]{:S(2)}, u32[]{:S(2)}) collective-permute-start(bf16[2,72,384]{2,1,0:T(8,128)(2,1)S(1)} %fusion.33), channel_id=1, source_target_pairs={{0,16},{1,17},{2,18},{3,19},{4,20},{5,21},{6,22},{7,23},{8,24},{9,... | collective-permute-start | bytes 331784 | tf_op jit(solution)/shard_map/ppermute | solution.py:506
  117.7 7.9 %collective-permute-start.43 = (bf16[2,72,384]{2,1,0:T(8,128)(2,1)S(1)}, bf16[2,72,384]{2,1,0:T(8,128)(2,1)S(1)}, u32[]{:S(2)}, u32[]{:S(2)}) collective-permute-start(bf16[2,72,384]{2,1,0:T(8,128)(2,1)S(1)} %fusion.32), channel_id=1, source_target_pairs={{0,4},{1,5},{2,6},{3,7},{4,0},{5,1},{6,2},{7,3},{8,12},{9,13},{10,... | collective-permute-start | bytes 331784 | tf_op jit(solution)/shard_map/ppermute | solution.py:506
  118.9 7.3 %collective-permute-start.42 = (bf16[2,72,576]{2,1,0:T(8,128)(2,1)S(1)}, bf16[2,72,576]{2,1,0:T(8,128)(2,1)S(1)}, u32[]{:S(2)}, u32[]{:S(2)}) collective-permute-start(bf16[2,72,576]{2,1,0:T(8,128)(2,1)S(1)} %get-tuple-element.170), channel_id=1, source_target_pairs={{0,8},{1,9},{2,10},{3,11},{4,12},{5,13},{6,14},{7,15},{8,0},{9,1},... | collective-permute-start | bytes 497672 | tf_op jit(solution)/shard_map/ppermute | solution.py:506
  125.6 9.8 %collective-permute-start.45 = (bf16[2,72,384]{2,1,0:T(8,128)(2,1)S(1)}, bf16[2,72,384]{2,1,0:T(8,128)(2,1)S(1)}, u32[]{:S(2)}, u32[]{:S(2)}) collective-permute-start(bf16[2,72,384]{2,1,0:T(8,128)(2,1)S(1)} %fusion.17), channel_id=1, source_target_pairs={{0,2},{1,3},{2,0},{3,1},{4,6},{5,7},{6,4},{7,5},{8,10},{9,11},{10,... | collective-permute-start | bytes 331784 | tf_op jit(solution)/shard_map/ppermute | solution.py:506
  126.2 6.9 %collective-permute-start.47 = (bf16[72,576]{1,0:T(8,128)(2,1)S(1)}, bf16[72,576]{1,0:T(8,128)(2,1)S(1)}, u32[]{:S(2)}, u32[]{:S(2)}) collective-permute-start(bf16[72,576]{1,0:T(8,128)(2,1)S(1)} %fusion.36), channel_id=1, source_target_pairs={{0,16},{1,17},{2,18},{3,19},{4,20},{5,21},{6,22},{7,23},{8,24},{9,... | collective-permute-start | bytes 248840 | tf_op jit(solution)/shard_map/ppermute | solution.py:506
  (52 other events, 297.3 us)

commit v12 on v11

--- a/solution.py
+++ b/solution.py
@@ -484,12 +484,12 @@
     gains_o[1:2, :] = line[:, 256 : 256 + d_rows]
 
 
-def place_all(part_d, qk, v, meta, a_near, a_far, b_near, b_far, d0, d1, d2, d3, r0, r1, r2, r3,
+def place_all(part_d, qk, v, meta, a_near, a_far, b_near, b_far, d0, d1, d2, d3, r0, r1, far,
               gate_o, down_o, wout_o, w_o, bqk_o, bv_o, gains_o, all_s):
     place_gate(meta, a_near, a_far, gate_o, 2, 0)
     place_gate(meta, b_near, b_far, gate_o, 2, 1)
     place_down(part_d, meta, d0, d1, d2, d3, down_o, wout_o)
-    place_qkv(qk, v, meta, r0, r1, r2, r3, w_o, bqk_o, bv_o, gains_o, all_s)
+    place_qkv(qk, v, meta, r0, r1, far.at[0], far.at[1], w_o, bqk_o, bv_o, gains_o, all_s)
 
 
 class Net:
@@ -813,7 +813,7 @@
     gu_x = net.swap(gu2, xbit)
     gu_y = net.swap(gu2, ybit)
     gu_c = net.swap(gu2, core)
-    b0 = net.half(after(half_b, a0), core, 0)
+    b0 = net.half(after(half_b, a1), core, 0)
     b1 = net.both(b0, zfar, 0, after(net.swap(b0, zfar), a2))
     b_x = net.swap(b1, xbit)
     b_z = net.swap(after(b1, gu2), znear)
@@ -936,18 +936,19 @@
     b_got = net.swap(b_give, xbit)
     down, down_give = halves(down, after(down_got, b_give))
     down_got = net.swap(down_give, znear)
+    rest, rest_give = halves(rest, after(rest_got, down_give))
+    rest_got = net.swap(rest_give, znear)
     (hidden_grad,) = call(
         input_gradient_two,
         [],
-        [dq, dkv, after(dkv_got, down_give), source, middle_grad, wf, gains],
+        [dq, dkv, after(dkv_got, rest_give), source, middle_grad, wf, gains],
         [sds((seqs, width, length), F32)],
         3e9,
         mib=16,
     )
-    rest, rest_give = halves(rest, after(rest_got, hidden_grad))
+    a_got = after(a_got, hidden_grad)
     hidden_grad = hidden_grad.reshape(micro, batch, width, length).swapaxes(2, 3)
-    rest_got = net.swap(rest_give, znear)
-    a = add(a, after(a_got, rest_give))
+    a = add(a, a_got)
     a_got = net.swap(a, ybit)
     b = add(b, after(b_got, a))
     b_got = net.swap(b, ybit)
@@ -964,14 +965,13 @@
     down_c = net.swap(after(down, down_y), core)
     rest = add(rest, after(rest_got, down))
     rest_y = net.swap(rest, ybit)
-    rest_c = net.swap(after(rest, rest_y), core)
     down_yc = net.swap(after(down_y, rest_y), core)
-    rest_yc = net.swap(rest_y, core)
+    rest_far = net.swap(jnp.stack([rest, rest_y]), core)
     qk, v = (QW + KW) // n_fsdp, KW // n_fsdp
     out_gate, out_down, out_wout, out_qkv, b_qk, b_v, out_gains = call(
         functools.partial(place_all, ff_rows // 4, qk, v),
         [meta],
-        [a, a_far, b, b_far, down, down_y, down_c, down_yc, rest, rest_y, rest_c, rest_yc],
+        [a, a_far, b, b_far, down, down_y, down_c, down_yc, rest, rest_y, rest_far],
         [
             sds((d_rows, 2 * units), F32),
             sds((ff_rows, width), F32),

time: 144 us -> 143 us (level)
  starting transfers between devices: 47.8 us -> 42.8 us
  waiting for transfers between devices: 43 us -> 47 us
    ppermute x55 -> x54, starting transfers between devices: 47.8 us -> 42.8 us  [swap(): return lax.ppermute(value, ('fsdp', 'seq'), pairs)]
    ppermute x55 -> x54, waiting for transfers between devices: 43 us -> 47 us  [swap(): return lax.ppermute(value, ('fsdp', 'seq'), pairs)]
  transfers between devices with their start and end apart: 55 -> 54, of which waited for: 17 -> 18; matrix products, arithmetic and copies ran while one was open for 6% -> 6% of each run, Pallas kernels for 17% -> 17%
where the time goes in v12:
time: 143 us; the launch traced here: 142 us
  waiting for transfers between devices  47 us (33%)
  starting transfers between devices  42.8 us (30%)
  Pallas kernels  40.1 us (28%)
  other arithmetic  5.99 us (4%)
  local copies, waits for them, and re-layouts  5.24 us (4%)
    ppermute x54, waiting for transfers between devices, swap(): return lax.ppermute(value, ('fsdp', 'seq'), pairs)  47 us
    ppermute x54, starting transfers between devices, swap(): return lax.ppermute(value, ('fsdp', 'seq'), pairs)  42.8 us
    pallas_call x5, Pallas kernels, call(): pl.pallas_call(kernel, out_shape=outs, in_specs=specs, out_specs=whole(*o...  39.2 us
    unnamed x60, local copies, waits for them, and re-layouts  4.2 us
    convert_element_type x21, other arithmetic, add(): return (keep.astype(F32) + got.astype(F32)).astype(BF)  3.49 us
  transfers between devices with their start and end apart: 54, of which 18 were waited for; matrix products, arithmetic and copies ran while one was open for 6% of the time, Pallas kernels for 17%

profile of v12, /device:TPU:0, one launch (start us, length us, event | category | flops | bytes accessed | tf_op | source)
XLA Modules:
  0.0 142.4 jit_solution(17373844127589851512)
XLA Ops:
  3.8 4.1 %collective-permute-start.3 = (bf16[40,960]{1,0:T(8,128)(2,1)S(1)}, bf16[40,960]{1,0:T(8,128)(2,1)S(1)}, u32[]{:S(2)}, u32[]{:S(2)}) collective-permute-start(bf16[40,960]{1,0:T(8,128)(2,1)S(1)} %shard_map.187), channel_id=1, source_target_pairs={{0,16},{1,17},{2,18},{3,19},{4,20},{5,21},{6,22},{7,23},{8,24},{9,... | collective-permute-start | bytes 230408 | tf_op jit(solution)/shard_map/ppermute | solution.py:506
  10.0 1.6 %collective-permute-start = (bf16[256,640]{1,0:T(8,128)(2,1)S(1)}, bf16[256,640]{1,0:T(8,128)(2,1)S(1)}, u32[]{:S(2)}, u32[]{:S(2)}) collective-permute-start(bf16[256,640]{1,0:T(8,128)(2,1)S(1)} %pad_maximum_fusion.3.b0), channel_id=1, source_target_pairs={{0,2},{1,3},{2,0},{3,1},{4,6},{5,7},{6,4},{7,5},{8,10},{9,11},{10,... | collective-permute-start | bytes 983048 | tf_op jit(solution)/shard_map/ppermute | solution.py:506
  12.6 1.6 %collective-permute-start.4 = (bf16[2,40,960]{2,1,0:T(8,128)(2,1)S(1)}, bf16[2,40,960]{2,1,0:T(8,128)(2,1)S(1)}, u32[]{:S(2)}, u32[]{:S(2)}) collective-permute-start(bf16[2,40,960]{2,1,0:T(8,128)(2,1)S(1)} %pad_maximum_fusion.6), channel_id=1, source_target_pairs={{0,8},{1,9},{2,10},{3,11},{4,12},{5,13},{6,14},{7,15},{8,0},{9,1},... | collective-permute-start | bytes 460808 | tf_op jit(solution)/shard_map/ppermute | solution.py:506
  14.3 2.7 %collective-permute-start.10 = (bf16[136,576]{1,0:T(8,128)(2,1)S(1)}, bf16[136,576]{1,0:T(8,128)(2,1)S(1)}, u32[]{:S(2)}, u32[]{:S(2)}) collective-permute-start(bf16[136,576]{1,0:T(8,128)(2,1)S(1)} %dynamic-slice_bitcast_fusion), channel_id=1, source_target_pairs={{0,16},{1,17},{2,18},{3,19},{4,20},{5,21},{6,22},{7,23},{8,24},{9,... | collective-permute-start | bytes 470024 | tf_op jit(solution)/shard_map/ppermute | solution.py:506
  17.0 4.1 %collective-permute-done.8 = bf16[72,768]{1,0:T(8,128)(2,1)S(1)} collective-permute-done((bf16[72,768]{1,0:T(8,128)(2,1)S(1)}, bf16[72,768]{1,0:T(8,128)(2,1)S(1)}, u32[]{:S(2)}, u32[]{:S(2)}) %collective-permute-start.8) | collective-permute-done | bytes 110624 | tf_op jit(solution)/shard_map/ppermute | solution.py:506
  21.1 2.2 %collective-permute-done.4 = bf16[2,40,960]{2,1,0:T(8,128)(2,1)S(1)} collective-permute-done((bf16[2,40,960]{2,1,0:T(8,128)(2,1)S(1)}, bf16[2,40,960]{2,1,0:T(8,128)(2,1)S(1)}, u32[]{:S(2)}, u32[]{:S(2)}) %collective-permute-start.4) | collective-permute-done | bytes 153632 | tf_op jit(solution)/shard_map/ppermute | solution.py:506
  23.4 1.6 %collective-permute-start.5 = (bf16[2,2,40,960]{3,2,1,0:T(8,128)(2,1)S(1)}, bf16[2,2,40,960]{3,2,1,0:T(8,128)(2,1)S(1)}, u32[]{:S(2)}, u32[]{:S(2)}) collective-permute-start(bf16[2,2,40,960]{3,2,1,0:T(8,128)(2,1)S(1)} %pad_maximum_fusion.4.a00), channel_id=1, source_target_pairs={{0,4},{1,5},{2,6},{3,7},{4,0},{5,1},{6,2},{7,3},{8,12},{9,13},{10,... | collective-permute-start | bytes 921608 | tf_op jit(solution)/shard_map/ppermute | solution.py:506
  25.0 2.7 %collective-permute-done.10 = bf16[136,576]{1,0:T(8,128)(2,1)S(1)} collective-permute-done((bf16[136,576]{1,0:T(8,128)(2,1)S(1)}, bf16[136,576]{1,0:T(8,128)(2,1)S(1)}, u32[]{:S(2)}, u32[]{:S(2)}) %collective-permute-start.10) | collective-permute-done | bytes 156704 | tf_op jit(solution)/shard_map/ppermute | solution.py:506
  27.8 1.6 %collective-permute-start.12 = (bf16[2,136,576]{2,1,0:T(8,128)(2,1)S(1)}, bf16[2,136,576]{2,1,0:T(8,128)(2,1)S(1)}, u32[]{:S(2)}, u32[]{:S(2)}) collective-permute-start(bf16[2,136,576]{2,1,0:T(8,128)(2,1)S(1)} %pad_maximum_fusion.2.refs_0_), channel_id=1, source_target_pairs={{0,4},{1,5},{2,6},{3,7},{4,0},{5,1},{6,2},{7,3},{8,12},{9,13},{10,... | collective-permute-start | bytes 940040 | tf_op jit(solution)/shard_map/ppermute | solution.py:506
  29.8 4.5 %collective-permute-done.9 = bf16[2,72,768]{2,1,0:T(8,128)(2,1)S(1)} collective-permute-done((bf16[2,72,768]{2,1,0:T(8,128)(2,1)S(1)}, bf16[2,72,768]{2,1,0:T(8,128)(2,1)S(1)}, u32[]{:S(2)}, u32[]{:S(2)}) %collective-permute-start.9) | collective-permute-done | bytes 221216 | tf_op jit(solution)/shard_map/ppermute | solution.py:506
  34.4 1.6 %collective-permute-start.21 = (bf16[2,2,72,768]{3,2,1,0:T(8,128)(2,1)S(1)}, bf16[2,2,72,768]{3,2,1,0:T(8,128)(2,1)}, u32[]{:S(2)}, u32[]{:S(2)}) collective-permute-start(bf16[2,2,72,768]{3,2,1,0:T(8,128)(2,1)S(1)} %pad_maximum_fusion.refs_8_), channel_id=1, source_target_pairs={{0,4},{1,5},{2,6},{3,7},{4,0},{5,1},{6,2},{7,3},{8,12},{9,13},{10,... | collective-permute-start | bytes 1327112 | tf_op jit(solution)/shard_map/ppermute | solution.py:506
  39.5 10.7 %shard_map.188 = (bf16[256,576]{1,0:T(8,128)(2,1)S(1)}, bf16[2,3,384,64]{3,2,1,0:T(8,128)(2,1)}, bf16[2,3,512,64]{3,2,1,0:T(8,128)(2,1)}, bf16[2,3,512,64]{3,2,1...) custom-call(s32[2]{0:T(128)S(1)} %pad_add_fusion.meta, bf16[256,640]{1,0:T(8,128)(2,1)S(1)} %pad_maximum_fusion.3.b0, ...), custom_call_target="tpu_custom_call" | custom-call | flops 12000000000 | bytes 6074880 | tf_op jit(solution)/shard_map/pallas_call | solution.py:55
  50.6 1.2 collective-permute-start.23
  54.0 8.6 %collective-permute-done.23.refs_14_ = bf16[2,2,72,768]{3,2,1,0:T(8,128)(2,1)} collective-permute-done((bf16[2,2,72,768]{3,2,1,0:T(8,128)(2,1)}, bf16[2,2,72,768]{3,2,1,0:T(8,128)(2,1)}, u32[]{:S(2)}, u32[]{:S(2)}) %collective-permute-start.23) | collective-permute-done | bytes 442400 | tf_op jit(solution)/shard_map/ppermute | solution.py:506
  63.8 1.5 %collective-permute-done.16.refs_5_ = bf16[2,136,576]{2,1,0:T(8,128)(2,1)} collective-permute-done((bf16[2,136,576]{2,1,0:T(8,128)(2,1)}, bf16[2,136,576]{2,1,0:T(8,128)(2,1)}, u32[]{:S(2)}, u32[]{:S(2)}) %collective-permute-start.16) | collective-permute-done | bytes 313376 | tf_op jit(solution)/shard_map/ppermute | solution.py:506
  65.8 13.4 %shard_map.189 = (bf16[2,576,128]{2,1,0:T(8,128)(2,1)}, bf16[2,2,2,2,72,384]{5,4,3,2,1,0:T(8,128)(2,1)}, bf16[2,2,2,2,72,384]{5,4,3,2,1,0:T(8,128)(2,1)}, bf16[2...) custom-call(s32[2]{0:T(128)S(1)} %pad_add_fusion.meta, ...), custom_call_target="tpu_custom_call" | custom-call | flops 14000000000 | bytes 14311168 | tf_op jit(solution)/shard_map/pallas_call | solution.py:55
  79.4 3.4 %collective-permute-done.25 = bf16[2,2,2,2,72,576]{5,4,3,2,1,0:T(8,128)(2,1)S(1)} collective-permute-done((bf16[2,2,2,2,72,576]{5,4,3,2,1,0:T(8,128)(2,1)}, bf16[2,2,2,2,72,576]{5,4,3,2,1,0:T(8,128)(2,1)S(1)}, u32[]{:S(2)}, u32[]{:S(2)}) %collective-permute-start.25) | collective-permute-done | bytes 1327136 | tf_op jit(solution)/shard_map/ppermute | solution.py:506
  83.3 1.9 %add_convert_fusion = (bf16[1,2,2,2,72,576]{5,4,3,2,1,0:T(8,128)(2,1)S(1)}, bf16[2,2,2,72,576]{4,3,2,1,0:T(8,128)(2,1)S(1)}) fusion(bf16[2,2,2,2,72,576]{5,4,3,2,1,0:T(8,128)(2,1)S(1)} %collective-permute-done.25, bf16[2,2,2,2,72,576]{5,4,3,2,1,0:T(8,128)(2,1)} %get-tuple-element.97), kind=kLoop, calls=%fused_computation | loop fusion | flops 2654208 | bytes 3981312 | tf_op jit(solution)/shard_map/convert_element_type | solution.py:890
  85.2 1.5 %collective-permute-start.29 = (bf16[2,2,2,72,576]{4,3,2,1,0:T(8,128)(2,1)S(1)}, bf16[2,2,2,72,576]{4,3,2,1,0:T(8,128)(2,1)S(1)}, u32[]{:S(2)}, u32[]{:S(2)}) collective-permute-start(bf16[2,2,2,72,576]{4,3,2,1,0:T(8,128)(2,1)S(1)} %get-tuple-element.152), channel_id=1, source_target_pairs={{0,2},{1,3},{2,0},{3,1},{4,6},{5,7},{6,4},{7,5},{8,10},{9,11},{10,... | collective-permute-start | bytes 1990664 | tf_op jit(solution)/shard_map/ppermute | solution.py:506
  88.9 11.2 %shard_map.190 = (bf16[256,640]{1,0:T(8,128)(2,1)S(1)}, bf16[2,256,384]{2,1,0:T(8,128)(2,1)S(1)}, bf16[2,256,384]{2,1,0:T(8,128)(2,1)S(1)}, bf16[2,2,2,2,80,256]...) custom-call(s32[2]{0:T(128)S(1)} %pad_add_fusion.meta, bf16[256,640]{1,0:T(8,128)(2,1)S(1)} %pad_maximum_fusion.3.b0, ...), custom_call_target="tpu_custom_call" | custom-call | flops 14000000000 | bytes 7273216 | tf_op jit(solution)/shard_map/pallas_call | solution.py:55
  100.8 2.3 %collective-permute-start.38 = (bf16[2,2,72,384]{3,2,1,0:T(8,128)(2,1)S(1)}, bf16[2,2,72,384]{3,2,1,0:T(8,128)(2,1)S(1)}, u32[]{:S(2)}, u32[]{:S(2)}) collective-permute-start(bf16[2,2,72,384]{3,2,1,0:T(8,128)(2,1)S(1)} %get-tuple-element.162), channel_id=1, source_target_pairs={{0,16},{1,17},{2,18},{3,19},{4,20},{5,21},{6,22},{7,23},{8,24},{9,... | collective-permute-start | bytes 663560 | tf_op jit(solution)/shard_map/ppermute | solution.py:506
  103.9 1.5 %collective-permute-start.33 = (bf16[2,2,2,80,256]{4,3,2,1,0:T(8,128)(2,1)S(1)}, bf16[2,2,2,80,256]{4,3,2,1,0:T(8,128)(2,1)S(1)}, u32[]{:S(2)}, u32[]{:S(2)}) collective-permute-start(bf16[2,2,2,80,256]{4,3,2,1,0:T(8,128)(2,1)S(1)} %get-tuple-element.160), channel_id=1, source_target_pairs={{0,2},{1,3},{2,0},{3,1},{4,6},{5,7},{6,4},{7,5},{8,10},{9,11},{10,... | collective-permute-start | bytes 983048 | tf_op jit(solution)/shard_map/ppermute | solution.py:506
  107.9 6.7 %collective-permute-done.35 = bf16[2,2,72,384]{3,2,1,0:T(8,128)(2,1)S(1)} collective-permute-done((bf16[2,2,72,384]{3,2,1,0:T(8,128)(2,1)S(1)}, bf16[2,2,72,384]{3,2,1,0:T(8,128)(2,1)S(1)}, u32[]{:S(2)}, u32[]{:S(2)}) %collective-permute-start.35) | collective-permute-done | bytes 221216 | tf_op jit(solution)/shard_map/ppermute | solution.py:506
  115.2 1.5 %collective-permute-start.36 = (bf16[2,2,80,256]{3,2,1,0:T(8,128)(2,1)S(1)}, bf16[2,2,80,256]{3,2,1,0:T(8,128)(2,1)S(1)}, u32[]{:S(2)}, u32[]{:S(2)}) collective-permute-start(bf16[2,2,80,256]{3,2,1,0:T(8,128)(2,1)S(1)} %get-tuple-element.169), channel_id=1, source_target_pairs={{0,4},{1,5},{2,6},{3,7},{4,0},{5,1},{6,2},{7,3},{8,12},{9,13},{10,... | collective-permute-start | bytes 491528 | tf_op jit(solution)/shard_map/ppermute | solution.py:506
  118.7 2.8 %collective-permute-done.36 = bf16[2,2,80,256]{3,2,1,0:T(8,128)(2,1)S(1)} collective-permute-done((bf16[2,2,80,256]{3,2,1,0:T(8,128)(2,1)S(1)}, bf16[2,2,80,256]{3,2,1,0:T(8,128)(2,1)S(1)}, u32[]{:S(2)}, u32[]{:S(2)}) %collective-permute-start.36) | collective-permute-done | bytes 163872 | tf_op jit(solution)/shard_map/ppermute | solution.py:506
  122.3 1.9 %shard_map.191 = f32[2,576,128]{2,1,0:T(8,128)} custom-call(bf16[256,640]{1,0:T(8,128)(2,1)S(1)} %get-tuple-element.100.dq, bf16[256,384]{1,0:T(8,128)(2,1)S(1)} %get-tuple-element.166.own, bf16[256,384]{1,0:T(8,128)(2,1)S(1)} %collective-permute-done.32.other, bf16[256,576]{1,0:T(8,128)(2,1)S(1)} %bitcast.213, f32[256,576]{1,0:T(8,128)S(1)} %copy-done.9, ...), custom_call_target="tpu_custom_call" | custom-call | flops 3000000000 | bytes 3305984 | tf_op jit(solution)/shard_map/pallas_call | solution.py:55
  124.3 1.4 collective-permute-start.40
  126.5 2.7 %collective-permute-start.47 = (bf16[72,576]{1,0:T(8,128)(2,1)S(1)}, bf16[72,576]{1,0:T(8,128)(2,1)S(1)}, u32[]{:S(2)}, u32[]{:S(2)}) collective-permute-start(bf16[72,576]{1,0:T(8,128)(2,1)S(1)} %fusion.36), channel_id=1, source_target_pairs={{0,16},{1,17},{2,18},{3,19},{4,20},{5,21},{6,22},{7,23},{8,24},{9,... | collective-permute-start | bytes 248840 | tf_op jit(solution)/shard_map/ppermute | solution.py:506
  129.7 3.3 %collective-permute-done.47 = bf16[72,576]{1,0:T(8,128)(2,1)S(1)} collective-permute-done((bf16[72,576]{1,0:T(8,128)(2,1)S(1)}, bf16[72,576]{1,0:T(8,128)(2,1)S(1)}, u32[]{:S(2)}, u32[]{:S(2)}) %collective-permute-start.47) | collective-permute-done | bytes 82976 | tf_op jit(solution)/shard_map/ppermute | solution.py:506
  135.7 2.8 %collective-permute-done.51.r1 = bf16[80,256]{1,0:T(8,128)(2,1)S(1)} collective-permute-done((bf16[80,256]{1,0:T(8,128)(2,1)S(1)}, bf16[80,256]{1,0:T(8,128)(2,1)S(1)}, u32[]{:S(2)}, u32[]{:S(2)}) %collective-permute-start.51) | collective-permute-done | bytes 40992 | tf_op jit(solution)/shard_map/ppermute | solution.py:506
  139.2 1.2 collective-permute-done.53.far
  140.4 1.9 %shard_map.192 = (f32[72,3072]{1,0:T(8,128)}, f32[192,576]{1,0:T(8,128)}, f32[72,576]{1,0:T(8,128)}, f32[72,960]{1,0:T(8,128)}, f32[1,96]{1,0:T(1,128)}, /*index=5*/f32[1,24]{1,0:T(1,128)}, f32[2,72]{1,0:T(2,128)}) custom-call(s32[2]{0:T(128)S(1)} %pad_add_fusion.meta, bf16[2,72,384]{2,1,0:T(8,128)(2,1)S(1)} %add_convert_fusion.11.a_near, ...), custom_call_target="tpu_custom_call" | custom-call | flops 3000000000 | bytes 2708512 | tf_op jit(solution)/shard_map/pallas_call | solution.py:55
  (195 shorter events, 29.4 us)
Async XLA Ops:
  3.8 8.8 %collective-permute-start.3 = (bf16[40,960]{1,0:T(8,128)(2,1)S(1)}, bf16[40,960]{1,0:T(8,128)(2,1)S(1)}, u32[]{:S(2)}, u32[]{:S(2)}) collective-permute-start(bf16[40,960]{1,0:T(8,128)(2,1)S(1)} %shard_map.187), channel_id=1, source_target_pairs={{0,16},{1,17},{2,18},{3,19},{4,20},{5,21},{6,22},{7,23},{8,24},{9,... | collective-permute-start | bytes 230408 | tf_op jit(solution)/shard_map/ppermute | solution.py:506
  10.0 19.6 %collective-permute-start.1 = (bf16[256,640]{1,0:T(8,128)(2,1)S(1)}, bf16[256,640]{1,0:T(8,128)(2,1)S(1)}, u32[]{:S(2)}, u32[]{:S(2)}) collective-permute-start(bf16[256,640]{1,0:T(8,128)(2,1)S(1)} %pad_maximum_fusion.3.b0), channel_id=1, source_target_pairs={{0,1},{1,0},{2,3},{3,2},{4,5},{5,4},{6,7},{7,6},{8,9},{9,8},{10,11... | collective-permute-start | bytes 983048 | tf_op jit(solution)/shard_map/ppermute | solution.py:506
  10.0 17.7 %collective-permute-start = (bf16[256,640]{1,0:T(8,128)(2,1)S(1)}, bf16[256,640]{1,0:T(8,128)(2,1)S(1)}, u32[]{:S(2)}, u32[]{:S(2)}) collective-permute-start(bf16[256,640]{1,0:T(8,128)(2,1)S(1)} %pad_maximum_fusion.3.b0), channel_id=1, source_target_pairs={{0,2},{1,3},{2,0},{3,1},{4,6},{5,7},{6,4},{7,5},{8,10},{9,11},{10,... | collective-permute-start | bytes 983048 | tf_op jit(solution)/shard_map/ppermute | solution.py:506
  11.6 9.4 %collective-permute-start.8 = (bf16[72,768]{1,0:T(8,128)(2,1)S(1)}, bf16[72,768]{1,0:T(8,128)(2,1)S(1)}, u32[]{:S(2)}, u32[]{:S(2)}) collective-permute-start(bf16[72,768]{1,0:T(8,128)(2,1)S(1)} %constant_dynamic-slice_fusion), channel_id=1, source_target_pairs={{0,16},{1,17},{2,18},{3,19},{4,20},{5,21},{6,22},{7,23},{8,24},{9,... | collective-permute-start | bytes 331784 | tf_op jit(solution)/shard_map/ppermute | solution.py:506
  12.6 10.6 %collective-permute-start.4 = (bf16[2,40,960]{2,1,0:T(8,128)(2,1)S(1)}, bf16[2,40,960]{2,1,0:T(8,128)(2,1)S(1)}, u32[]{:S(2)}, u32[]{:S(2)}) collective-permute-start(bf16[2,40,960]{2,1,0:T(8,128)(2,1)S(1)} %pad_maximum_fusion.6), channel_id=1, source_target_pairs={{0,8},{1,9},{2,10},{3,11},{4,12},{5,13},{6,14},{7,15},{8,0},{9,1},... | collective-permute-start | bytes 460808 | tf_op jit(solution)/shard_map/ppermute | solution.py:506
  14.3 13.4 %collective-permute-start.10 = (bf16[136,576]{1,0:T(8,128)(2,1)S(1)}, bf16[136,576]{1,0:T(8,128)(2,1)S(1)}, u32[]{:S(2)}, u32[]{:S(2)}) collective-permute-start(bf16[136,576]{1,0:T(8,128)(2,1)S(1)} %dynamic-slice_bitcast_fusion), channel_id=1, source_target_pairs={{0,16},{1,17},{2,18},{3,19},{4,20},{5,21},{6,22},{7,23},{8,24},{9,... | collective-permute-start | bytes 470024 | tf_op jit(solution)/shard_map/ppermute | solution.py:506
  23.4 15.4 %collective-permute-start.6 = (bf16[2,2,40,960]{3,2,1,0:T(8,128)(2,1)S(1)}, bf16[2,2,40,960]{3,2,1,0:T(8,128)(2,1)S(1)}, u32[]{:S(2)}, u32[]{:S(2)}) collective-permute-start(bf16[2,2,40,960]{3,2,1,0:T(8,128)(2,1)S(1)} %pad_maximum_fusion.4.a00), channel_id=1, source_target_pairs={{0,1},{1,0},{2,3},{3,2},{4,5},{5,4},{6,7},{7,6},{8,9},{9,8},{10,11... | collective-permute-start | bytes 921608 | tf_op jit(solution)/shard_map/ppermute | solution.py:506
  23.4 12.6 %collective-permute-start.5 = (bf16[2,2,40,960]{3,2,1,0:T(8,128)(2,1)S(1)}, bf16[2,2,40,960]{3,2,1,0:T(8,128)(2,1)S(1)}, u32[]{:S(2)}, u32[]{:S(2)}) collective-permute-start(bf16[2,2,40,960]{3,2,1,0:T(8,128)(2,1)S(1)} %pad_maximum_fusion.4.a00), channel_id=1, source_target_pairs={{0,4},{1,5},{2,6},{3,7},{4,0},{5,1},{6,2},{7,3},{8,12},{9,13},{10,... | collective-permute-start | bytes 921608 | tf_op jit(solution)/shard_map/ppermute | solution.py:506
  27.8 24.0 %collective-permute-start.12 = (bf16[2,136,576]{2,1,0:T(8,128)(2,1)S(1)}, bf16[2,136,576]{2,1,0:T(8,128)(2,1)S(1)}, u32[]{:S(2)}, u32[]{:S(2)}) collective-permute-start(bf16[2,136,576]{2,1,0:T(8,128)(2,1)S(1)} %pad_maximum_fusion.2.refs_0_), channel_id=1, source_target_pairs={{0,4},{1,5},{2,6},{3,7},{4,0},{5,1},{6,2},{7,3},{8,12},{9,13},{10,... | collective-permute-start | bytes 940040 | tf_op jit(solution)/shard_map/ppermute | solution.py:506
  34.4 16.2 %collective-permute-start.21 = (bf16[2,2,72,768]{3,2,1,0:T(8,128)(2,1)S(1)}, bf16[2,2,72,768]{3,2,1,0:T(8,128)(2,1)}, u32[]{:S(2)}, u32[]{:S(2)}) collective-permute-start(bf16[2,2,72,768]{3,2,1,0:T(8,128)(2,1)S(1)} %pad_maximum_fusion.refs_8_), channel_id=1, source_target_pairs={{0,4},{1,5},{2,6},{3,7},{4,0},{5,1},{6,2},{7,3},{8,12},{9,13},{10,... | collective-permute-start | bytes 1327112 | tf_op jit(solution)/shard_map/ppermute | solution.py:506
  36.0 17.6 %collective-permute-start.19 = (bf16[2,2,72,768]{3,2,1,0:T(8,128)(2,1)S(1)}, bf16[2,2,72,768]{3,2,1,0:T(8,128)(2,1)S(1)}, u32[]{:S(2)}, u32[]{:S(2)}) collective-permute-start(bf16[2,2,72,768]{3,2,1,0:T(8,128)(2,1)S(1)} %pad_maximum_fusion.refs_8_), channel_id=1, source_target_pairs={{0,1},{1,0},{2,3},{3,2},{4,5},{5,4},{6,7},{7,6},{8,9},{9,8},{10,11... | collective-permute-start | bytes 1327112 | tf_op jit(solution)/shard_map/ppermute | solution.py:506
  38.3 12.3 %collective-permute-start.13 = (bf16[2,2,72,768]{3,2,1,0:T(8,128)(2,1)S(1)}, bf16[2,2,72,768]{3,2,1,0:T(8,128)(2,1)}, u32[]{:S(2)}, u32[]{:S(2)}) collective-permute-start(bf16[2,2,72,768]{3,2,1,0:T(8,128)(2,1)S(1)} %pad_maximum_fusion.refs_8_), channel_id=1, source_target_pairs={{0,2},{1,3},{2,0},{3,1},{4,6},{5,7},{6,4},{7,5},{8,10},{9,11},{10,... | collective-permute-start | bytes 1327112 | tf_op jit(solution)/shard_map/ppermute | solution.py:506
  38.8 13.6 %collective-permute-start.15 = (bf16[2,136,576]{2,1,0:T(8,128)(2,1)S(1)}, bf16[2,136,576]{2,1,0:T(8,128)(2,1)}, u32[]{:S(2)}, u32[]{:S(2)}) collective-permute-start(bf16[2,136,576]{2,1,0:T(8,128)(2,1)S(1)} %pad_maximum_fusion.2.refs_0_), channel_id=1, source_target_pairs={{0,8},{1,9},{2,10},{3,11},{4,12},{5,13},{6,14},{7,15},{8,0},{9,1},... | collective-permute-start | bytes 940040 | tf_op jit(solution)/shard_map/ppermute | solution.py:506
  50.6 12.0 %collective-permute-start.23 = (bf16[2,2,72,768]{3,2,1,0:T(8,128)(2,1)}, bf16[2,2,72,768]{3,2,1,0:T(8,128)(2,1)}, u32[]{:S(2)}, u32[]{:S(2)}) collective-permute-start(bf16[2,2,72,768]{3,2,1,0:T(8,128)(2,1)} %collective-permute-done.21.refs_12_), channel_id=1, source_target_pairs={{0,2},{1,3},{2,0},{3,1},{4,6},{5,7},{6,4},{7,5},{8,10},{9,11},{10,... | collective-permute-start | bytes 1327112 | tf_op jit(solution)/shard_map/ppermute | solution.py:506
  51.9 10.8 %collective-permute-start.14 = (bf16[2,136,576]{2,1,0:T(8,128)(2,1)S(1)}, bf16[2,136,576]{2,1,0:T(8,128)(2,1)S(1)}, u32[]{:S(2)}, u32[]{:S(2)}) collective-permute-start(bf16[2,136,576]{2,1,0:T(8,128)(2,1)S(1)} %collective-permute-done.12.refs_2_), channel_id=1, source_target_pairs={{0,1},{1,0},{2,3},{3,2},{4,5},{5,4},{6,7},{7,6},{8,9},{9,8},{10,11... | collective-permute-start | bytes 940040 | tf_op jit(solution)/shard_map/ppermute | solution.py:506
  52.4 10.8 %collective-permute-start.17 = (bf16[2,136,576]{2,1,0:T(8,128)(2,1)}, bf16[2,136,576]{2,1,0:T(8,128)(2,1)}, u32[]{:S(2)}, u32[]{:S(2)}) collective-permute-start(bf16[2,136,576]{2,1,0:T(8,128)(2,1)} %collective-permute-done.15.refs_4_), channel_id=1, source_target_pairs={{0,4},{1,5},{2,6},{3,7},{4,0},{5,1},{6,2},{7,3},{8,12},{9,13},{10,... | collective-permute-start | bytes 940040 | tf_op jit(solution)/shard_map/ppermute | solution.py:506
  53.5 11.8 %collective-permute-start.22 = (bf16[2,2,72,768]{3,2,1,0:T(8,128)(2,1)}, bf16[2,2,72,768]{3,2,1,0:T(8,128)(2,1)}, u32[]{:S(2)}, u32[]{:S(2)}) collective-permute-start(bf16[2,2,72,768]{3,2,1,0:T(8,128)(2,1)} %collective-permute-done.21.refs_12_), channel_id=1, source_target_pairs={{0,1},{1,0},{2,3},{3,2},{4,5},{5,4},{6,7},{7,6},{8,9},{9,8},{10,11... | collective-permute-start | bytes 1327112 | tf_op jit(solution)/shard_map/ppermute | solution.py:506
  53.6 11.7 %collective-permute-start.20 = (bf16[2,2,72,768]{3,2,1,0:T(8,128)(2,1)}, bf16[2,2,72,768]{3,2,1,0:T(8,128)(2,1)}, u32[]{:S(2)}, u32[]{:S(2)}) collective-permute-start(bf16[2,2,72,768]{3,2,1,0:T(8,128)(2,1)} %collective-permute-done.13.refs_10_), channel_id=1, source_target_pairs={{0,1},{1,0},{2,3},{3,2},{4,5},{5,4},{6,7},{7,6},{8,9},{9,8},{10,11... | collective-permute-start | bytes 1327112 | tf_op jit(solution)/shard_map/ppermute | solution.py:506
  85.2 18.6 %collective-permute-start.29 = (bf16[2,2,2,72,576]{4,3,2,1,0:T(8,128)(2,1)S(1)}, bf16[2,2,2,72,576]{4,3,2,1,0:T(8,128)(2,1)S(1)}, u32[]{:S(2)}, u32[]{:S(2)}) collective-permute-start(bf16[2,2,2,72,576]{4,3,2,1,0:T(8,128)(2,1)S(1)} %get-tuple-element.152), channel_id=1, source_target_pairs={{0,2},{1,3},{2,0},{3,1},{4,6},{5,7},{6,4},{7,5},{8,10},{9,11},{10,... | collective-permute-start | bytes 1990664 | tf_op jit(solution)/shard_map/ppermute | solution.py:506
  86.9 16.2 %collective-permute-start.34 = (bf16[2,2,2,72,384]{4,3,2,1,0:T(8,128)(2,1)S(1)}, bf16[2,2,2,72,384]{4,3,2,1,0:T(8,128)(2,1)S(1)}, u32[]{:S(2)}, u32[]{:S(2)}) collective-permute-start(bf16[2,2,2,72,384]{4,3,2,1,0:T(8,128)(2,1)S(1)} %get-tuple-element.154), channel_id=1, source_target_pairs={{0,4},{1,5},{2,6},{3,7},{4,0},{5,1},{6,2},{7,3},{8,12},{9,13},{10,... | collective-permute-start | bytes 1327112 | tf_op jit(solution)/shard_map/ppermute | solution.py:506
  87.8 12.9 %collective-permute-start.31 = (bf16[2,2,2,72,384]{4,3,2,1,0:T(8,128)(2,1)S(1)}, bf16[2,2,2,72,384]{4,3,2,1,0:T(8,128)(2,1)S(1)}, u32[]{:S(2)}, u32[]{:S(2)}) collective-permute-start(bf16[2,2,2,72,384]{4,3,2,1,0:T(8,128)(2,1)S(1)} %get-tuple-element.156), channel_id=1, source_target_pairs={{0,8},{1,9},{2,10},{3,11},{4,12},{5,13},{6,14},{7,15},{8,0},{9,1},... | collective-permute-start | bytes 1327112 | tf_op jit(solution)/shard_map/ppermute | solution.py:506
  100.8 15.9 %collective-permute-start.38 = (bf16[2,2,72,384]{3,2,1,0:T(8,128)(2,1)S(1)}, bf16[2,2,72,384]{3,2,1,0:T(8,128)(2,1)S(1)}, u32[]{:S(2)}, u32[]{:S(2)}) collective-permute-start(bf16[2,2,72,384]{3,2,1,0:T(8,128)(2,1)S(1)} %get-tuple-element.162), channel_id=1, source_target_pairs={{0,16},{1,17},{2,18},{3,19},{4,20},{5,21},{6,22},{7,23},{8,24},{9,... | collective-permute-start | bytes 663560 | tf_op jit(solution)/shard_map/ppermute | solution.py:506
  103.3 11.4 %collective-permute-start.35 = (bf16[2,2,72,384]{3,2,1,0:T(8,128)(2,1)S(1)}, bf16[2,2,72,384]{3,2,1,0:T(8,128)(2,1)S(1)}, u32[]{:S(2)}, u32[]{:S(2)}) collective-permute-start(bf16[2,2,72,384]{3,2,1,0:T(8,128)(2,1)S(1)} %get-tuple-element.163), channel_id=1, source_target_pairs={{0,8},{1,9},{2,10},{3,11},{4,12},{5,13},{6,14},{7,15},{8,0},{9,1},... | collective-permute-start | bytes 663560 | tf_op jit(solution)/shard_map/ppermute | solution.py:506
  103.9 11.2 %collective-permute-start.33 = (bf16[2,2,2,80,256]{4,3,2,1,0:T(8,128)(2,1)S(1)}, bf16[2,2,2,80,256]{4,3,2,1,0:T(8,128)(2,1)S(1)}, u32[]{:S(2)}, u32[]{:S(2)}) collective-permute-start(bf16[2,2,2,80,256]{4,3,2,1,0:T(8,128)(2,1)S(1)} %get-tuple-element.160), channel_id=1, source_target_pairs={{0,2},{1,3},{2,0},{3,1},{4,6},{5,7},{6,4},{7,5},{8,10},{9,11},{10,... | collective-permute-start | bytes 983048 | tf_op jit(solution)/shard_map/ppermute | solution.py:506
  105.6 11.8 %collective-permute-start.37 = (bf16[2,2,72,576]{3,2,1,0:T(8,128)(2,1)S(1)}, bf16[2,2,72,576]{3,2,1,0:T(8,128)(2,1)S(1)}, u32[]{:S(2)}, u32[]{:S(2)}) collective-permute-start(bf16[2,2,72,576]{3,2,1,0:T(8,128)(2,1)S(1)} %get-tuple-element.158), channel_id=1, source_target_pairs={{0,4},{1,5},{2,6},{3,7},{4,0},{5,1},{6,2},{7,3},{8,12},{9,13},{10,... | collective-permute-start | bytes 995336 | tf_op jit(solution)/shard_map/ppermute | solution.py:506
  106.8 15.5 %collective-permute-start.32 = (bf16[256,384]{1,0:T(8,128)(2,1)S(1)}, bf16[256,384]{1,0:T(8,128)(2,1)S(1)}, u32[]{:S(2)}, u32[]{:S(2)}) collective-permute-start(bf16[256,384]{1,0:T(8,128)(2,1)S(1)} %get-tuple-element.165), channel_id=1, source_target_pairs={{0,2},{1,3},{2,0},{3,1},{4,6},{5,7},{6,4},{7,5},{8,10},{9,11},{10,... | collective-permute-start | bytes 589832 | tf_op jit(solution)/shard_map/ppermute | solution.py:506
  114.7 9.5 %collective-permute-start.39 = (bf16[2,72,384]{2,1,0:T(8,128)(2,1)S(1)}, bf16[2,72,384]{2,1,0:T(8,128)(2,1)S(1)}, u32[]{:S(2)}, u32[]{:S(2)}) collective-permute-start(bf16[2,72,384]{2,1,0:T(8,128)(2,1)S(1)} %fusion.32), channel_id=1, source_target_pairs={{0,16},{1,17},{2,18},{3,19},{4,20},{5,21},{6,22},{7,23},{8,24},{9,... | collective-permute-start | bytes 331784 | tf_op jit(solution)/shard_map/ppermute | solution.py:506
  116.7 8.9 %collective-permute-start.43 = (bf16[2,72,384]{2,1,0:T(8,128)(2,1)S(1)}, bf16[2,72,384]{2,1,0:T(8,128)(2,1)S(1)}, u32[]{:S(2)}, u32[]{:S(2)}) collective-permute-start(bf16[2,72,384]{2,1,0:T(8,128)(2,1)S(1)} %fusion.33), channel_id=1, source_target_pairs={{0,4},{1,5},{2,6},{3,7},{4,0},{5,1},{6,2},{7,3},{8,12},{9,13},{10,... | collective-permute-start | bytes 331784 | tf_op jit(solution)/shard_map/ppermute | solution.py:506
  117.5 9.0 %collective-permute-start.42 = (bf16[2,72,576]{2,1,0:T(8,128)(2,1)S(1)}, bf16[2,72,576]{2,1,0:T(8,128)(2,1)S(1)}, u32[]{:S(2)}, u32[]{:S(2)}) collective-permute-start(bf16[2,72,576]{2,1,0:T(8,128)(2,1)S(1)} %get-tuple-element.168), channel_id=1, source_target_pairs={{0,8},{1,9},{2,10},{3,11},{4,12},{5,13},{6,14},{7,15},{8,0},{9,1},... | collective-permute-start | bytes 497672 | tf_op jit(solution)/shard_map/ppermute | solution.py:506
  121.6 7.6 %collective-permute-start.41 = (bf16[2,80,256]{2,1,0:T(8,128)(2,1)S(1)}, bf16[2,80,256]{2,1,0:T(8,128)(2,1)S(1)}, u32[]{:S(2)}, u32[]{:S(2)}) collective-permute-start(bf16[2,80,256]{2,1,0:T(8,128)(2,1)S(1)} %get-tuple-element.176), channel_id=1, source_target_pairs={{0,8},{1,9},{2,10},{3,11},{4,12},{5,13},{6,14},{7,15},{8,0},{9,1},... | collective-permute-start | bytes 245768 | tf_op jit(solution)/shard_map/ppermute | solution.py:506
  125.7 9.9 %collective-permute-start.45 = (bf16[2,72,384]{2,1,0:T(8,128)(2,1)S(1)}, bf16[2,72,384]{2,1,0:T(8,128)(2,1)S(1)}, u32[]{:S(2)}, u32[]{:S(2)}) collective-permute-start(bf16[2,72,384]{2,1,0:T(8,128)(2,1)S(1)} %fusion.17), channel_id=1, source_target_pairs={{0,2},{1,3},{2,0},{3,1},{4,6},{5,7},{6,4},{7,5},{8,10},{9,11},{10,... | collective-permute-start | bytes 331784 | tf_op jit(solution)/shard_map/ppermute | solution.py:506
  129.6 9.5 %collective-permute-start.44 = (bf16[2,72,384]{2,1,0:T(8,128)(2,1)S(1)}, bf16[2,72,384]{2,1,0:T(8,128)(2,1)S(1)}, u32[]{:S(2)}, u32[]{:S(2)}) collective-permute-start(bf16[2,72,384]{2,1,0:T(8,128)(2,1)S(1)} %add_convert_fusion.11.a_near), channel_id=1, source_target_pairs={{0,1},{1,0},{2,3},{3,2},{4,5},{5,4},{6,7},{7,6},{8,9},{9,8},{10,11... | collective-permute-start | bytes 331784 | tf_op jit(solution)/shard_map/ppermute | solution.py:506
  (51 other events, 285.9 us)

commit v13 on v12

--- a/solution.py
+++ b/solution.py
@@ -895,13 +895,13 @@
     down_got = net.swap(down_give, core)
     a_got = net.swap(after(a_give, down_got), core)
     b_got = net.swap(after(b_give, down_got), core)
-    a, a_give = halves(a_keep, a_got)
+    a_give, a_core = add(a_keep[1], a_got[1]), a_got
+    b_give, b_core = add(b_keep[1], b_got[1]), b_got
+    down_give, down_core = add(down_keep[1], down_got[1]), down_got
     a_got = net.swap(a_give, xbit)
-    b, b_give = halves(b_keep, b_got)
     b_got = net.swap(b_give, znear)
-    down, down_give = halves(down_keep, down_got)
+    down_got = net.swap(down_give, ybit)
     attended_grad = after(attended_grad, a_give, b_give, down_give)
-    down_got = net.swap(down_give, ybit)
 
     dq, dkv_keep, dkv_give, rest_keep, rest_give = call(
         functools.partial(attention_backward_pieces, order, length, d_rows),
@@ -918,6 +918,9 @@
         [(width, 1024), (1, qkv_w), (1, width), (n_fsdp, 8, 1024)],
         24,
     )
+    a = add(a_keep[0], after(a_core, dq)[0])
+    b = add(b_keep[0], after(b_core, dq)[0])
+    down = add(down_keep[0], after(down_core, dq)[0])
     b, b_give = halves(b, after(b_got, dq))
     a, a_give = halves(a, after(a_got, b_give))
     b_got = net.swap(b_give, zfar)

time: 143 us -> 145 us (1.014)
  starting transfers between devices: 42.8 us -> 44.7 us
  waiting for transfers between devices: 47 us -> 45.1 us
  other arithmetic: 5.99 us -> 7.82 us
    ppermute x54, starting transfers between devices: 42.8 us -> 44.7 us  [swap(): return lax.ppermute(value, ('fsdp', 'seq'), pairs)]
    ppermute x54, waiting for transfers between devices: 47 us -> 45.1 us  [swap(): return lax.ppermute(value, ('fsdp', 'seq'), pairs)]
    convert_element_type x21 -> x23, other arithmetic: 3.49 us -> 5.33 us  [add(): return (keep.astype(F32) + got.astype(F32)).astype(BF)]
    unnamed x60 -> x62, local copies, waits for them, and re-layouts: 4.2 us -> 4.76 us
  transfers between devices with their start and end apart: 54 -> 54, of which waited for: 18 -> 16; matrix products, arithmetic and copies ran while one was open for 6% -> 7% of each run, Pallas kernels for 17% -> 16%
where the time goes in v13:
time: 145 us
  waiting for transfers between devices  45.1 us (31%)
  starting transfers between devices  44.7 us (31%)
  Pallas kernels  40 us (28%)
  other arithmetic  7.82 us (5%)
  local copies, waits for them, and re-layouts  5.8 us (4%)
    ppermute x54, waiting for transfers between devices, swap(): return lax.ppermute(value, ('fsdp', 'seq'), pairs)  45.1 us
    ppermute x54, starting transfers between devices, swap(): return lax.ppermute(value, ('fsdp', 'seq'), pairs)  44.7 us
    pallas_call x5, Pallas kernels, call(): pl.pallas_call(kernel, out_shape=outs, in_specs=specs, out_specs=whole(*o...  39.1 us
    convert_element_type x23, other arithmetic, add(): return (keep.astype(F32) + got.astype(F32)).astype(BF)  5.33 us
    unnamed x62, local copies, waits for them, and re-layouts  4.76 us
  transfers between devices with their start and end apart: 54, of which 16 were waited for; matrix products, arithmetic and copies ran while one was open for 7% of the time, Pallas kernels for 16%

profile of v13, /device:TPU:0, one launch (start us, length us, event | category | flops | bytes accessed | tf_op | source)
XLA Modules:
  0.0 144.7 jit_solution(16097345274877723350)
XLA Ops:
  3.8 4.1 %collective-permute-start.3 = (bf16[40,960]{1,0:T(8,128)(2,1)S(1)}, bf16[40,960]{1,0:T(8,128)(2,1)S(1)}, u32[]{:S(2)}, u32[]{:S(2)}) collective-permute-start(bf16[40,960]{1,0:T(8,128)(2,1)S(1)} %shard_map.187), channel_id=1, source_target_pairs={{0,16},{1,17},{2,18},{3,19},{4,20},{5,21},{6,22},{7,23},{8,24},{9,... | collective-permute-start | bytes 230408 | tf_op jit(solution)/shard_map/ppermute | solution.py:506
  10.0 1.6 %collective-permute-start = (bf16[256,640]{1,0:T(8,128)(2,1)S(1)}, bf16[256,640]{1,0:T(8,128)(2,1)S(1)}, u32[]{:S(2)}, u32[]{:S(2)}) collective-permute-start(bf16[256,640]{1,0:T(8,128)(2,1)S(1)} %pad_maximum_fusion.3.b0), channel_id=1, source_target_pairs={{0,2},{1,3},{2,0},{3,1},{4,6},{5,7},{6,4},{7,5},{8,10},{9,11},{10,... | collective-permute-start | bytes 983048 | tf_op jit(solution)/shard_map/ppermute | solution.py:506
  12.6 1.6 %collective-permute-start.4 = (bf16[2,40,960]{2,1,0:T(8,128)(2,1)S(1)}, bf16[2,40,960]{2,1,0:T(8,128)(2,1)S(1)}, u32[]{:S(2)}, u32[]{:S(2)}) collective-permute-start(bf16[2,40,960]{2,1,0:T(8,128)(2,1)S(1)} %pad_maximum_fusion.6), channel_id=1, source_target_pairs={{0,8},{1,9},{2,10},{3,11},{4,12},{5,13},{6,14},{7,15},{8,0},{9,1},... | collective-permute-start | bytes 460808 | tf_op jit(solution)/shard_map/ppermute | solution.py:506
  14.3 2.7 %collective-permute-start.10 = (bf16[136,576]{1,0:T(8,128)(2,1)S(1)}, bf16[136,576]{1,0:T(8,128)(2,1)S(1)}, u32[]{:S(2)}, u32[]{:S(2)}) collective-permute-start(bf16[136,576]{1,0:T(8,128)(2,1)S(1)} %dynamic-slice_bitcast_fusion), channel_id=1, source_target_pairs={{0,16},{1,17},{2,18},{3,19},{4,20},{5,21},{6,22},{7,23},{8,24},{9,... | collective-permute-start | bytes 470024 | tf_op jit(solution)/shard_map/ppermute | solution.py:506
  17.0 4.1 %collective-permute-done.8 = bf16[72,768]{1,0:T(8,128)(2,1)S(1)} collective-permute-done((bf16[72,768]{1,0:T(8,128)(2,1)S(1)}, bf16[72,768]{1,0:T(8,128)(2,1)S(1)}, u32[]{:S(2)}, u32[]{:S(2)}) %collective-permute-start.8) | collective-permute-done | bytes 110624 | tf_op jit(solution)/shard_map/ppermute | solution.py:506
  21.1 2.2 %collective-permute-done.4 = bf16[2,40,960]{2,1,0:T(8,128)(2,1)S(1)} collective-permute-done((bf16[2,40,960]{2,1,0:T(8,128)(2,1)S(1)}, bf16[2,40,960]{2,1,0:T(8,128)(2,1)S(1)}, u32[]{:S(2)}, u32[]{:S(2)}) %collective-permute-start.4) | collective-permute-done | bytes 153632 | tf_op jit(solution)/shard_map/ppermute | solution.py:506
  23.4 1.6 %collective-permute-start.5 = (bf16[2,2,40,960]{3,2,1,0:T(8,128)(2,1)S(1)}, bf16[2,2,40,960]{3,2,1,0:T(8,128)(2,1)S(1)}, u32[]{:S(2)}, u32[]{:S(2)}) collective-permute-start(bf16[2,2,40,960]{3,2,1,0:T(8,128)(2,1)S(1)} %pad_maximum_fusion.4.a00), channel_id=1, source_target_pairs={{0,4},{1,5},{2,6},{3,7},{4,0},{5,1},{6,2},{7,3},{8,12},{9,13},{10,... | collective-permute-start | bytes 921608 | tf_op jit(solution)/shard_map/ppermute | solution.py:506
  25.0 2.7 %collective-permute-done.10 = bf16[136,576]{1,0:T(8,128)(2,1)S(1)} collective-permute-done((bf16[136,576]{1,0:T(8,128)(2,1)S(1)}, bf16[136,576]{1,0:T(8,128)(2,1)S(1)}, u32[]{:S(2)}, u32[]{:S(2)}) %collective-permute-start.10) | collective-permute-done | bytes 156704 | tf_op jit(solution)/shard_map/ppermute | solution.py:506
  27.8 1.6 %collective-permute-start.12 = (bf16[2,136,576]{2,1,0:T(8,128)(2,1)S(1)}, bf16[2,136,576]{2,1,0:T(8,128)(2,1)S(1)}, u32[]{:S(2)}, u32[]{:S(2)}) collective-permute-start(bf16[2,136,576]{2,1,0:T(8,128)(2,1)S(1)} %pad_maximum_fusion.2.refs_0_), channel_id=1, source_target_pairs={{0,4},{1,5},{2,6},{3,7},{4,0},{5,1},{6,2},{7,3},{8,12},{9,13},{10,... | collective-permute-start | bytes 940040 | tf_op jit(solution)/shard_map/ppermute | solution.py:506
  29.8 4.5 %collective-permute-done.9 = bf16[2,72,768]{2,1,0:T(8,128)(2,1)S(1)} collective-permute-done((bf16[2,72,768]{2,1,0:T(8,128)(2,1)S(1)}, bf16[2,72,768]{2,1,0:T(8,128)(2,1)S(1)}, u32[]{:S(2)}, u32[]{:S(2)}) %collective-permute-start.9) | collective-permute-done | bytes 221216 | tf_op jit(solution)/shard_map/ppermute | solution.py:506
  34.4 1.6 %collective-permute-start.21 = (bf16[2,2,72,768]{3,2,1,0:T(8,128)(2,1)S(1)}, bf16[2,2,72,768]{3,2,1,0:T(8,128)(2,1)}, u32[]{:S(2)}, u32[]{:S(2)}) collective-permute-start(bf16[2,2,72,768]{3,2,1,0:T(8,128)(2,1)S(1)} %pad_maximum_fusion.refs_8_), channel_id=1, source_target_pairs={{0,4},{1,5},{2,6},{3,7},{4,0},{5,1},{6,2},{7,3},{8,12},{9,13},{10,... | collective-permute-start | bytes 1327112 | tf_op jit(solution)/shard_map/ppermute | solution.py:506
  39.5 10.7 %shard_map.188 = (bf16[256,576]{1,0:T(8,128)(2,1)S(1)}, bf16[2,3,384,64]{3,2,1,0:T(8,128)(2,1)}, bf16[2,3,512,64]{3,2,1,0:T(8,128)(2,1)}, bf16[2,3,512,64]{3,2,1...) custom-call(s32[2]{0:T(128)S(1)} %pad_add_fusion.meta, bf16[256,640]{1,0:T(8,128)(2,1)S(1)} %pad_maximum_fusion.3.b0, ...), custom_call_target="tpu_custom_call" | custom-call | flops 12000000000 | bytes 6074880 | tf_op jit(solution)/shard_map/pallas_call | solution.py:55
  54.0 8.7 %collective-permute-done.23.refs_14_ = bf16[2,2,72,768]{3,2,1,0:T(8,128)(2,1)} collective-permute-done((bf16[2,2,72,768]{3,2,1,0:T(8,128)(2,1)}, bf16[2,2,72,768]{3,2,1,0:T(8,128)(2,1)}, u32[]{:S(2)}, u32[]{:S(2)}) %collective-permute-start.23) | collective-permute-done | bytes 442400 | tf_op jit(solution)/shard_map/ppermute | solution.py:506
  63.8 1.5 %collective-permute-done.16.refs_5_ = bf16[2,136,576]{2,1,0:T(8,128)(2,1)} collective-permute-done((bf16[2,136,576]{2,1,0:T(8,128)(2,1)}, bf16[2,136,576]{2,1,0:T(8,128)(2,1)}, u32[]{:S(2)}, u32[]{:S(2)}) %collective-permute-start.16) | collective-permute-done | bytes 313376 | tf_op jit(solution)/shard_map/ppermute | solution.py:506
  65.8 13.3 %shard_map.189 = (bf16[2,576,128]{2,1,0:T(8,128)(2,1)}, bf16[2,2,2,2,72,384]{5,4,3,2,1,0:T(8,128)(2,1)}, bf16[2,2,2,2,72,384]{5,4,3,2,1,0:T(8,128)(2,1)}, bf16[2...) custom-call(s32[2]{0:T(128)S(1)} %pad_add_fusion.meta, ...), custom_call_target="tpu_custom_call" | custom-call | flops 14000000000 | bytes 14311168 | tf_op jit(solution)/shard_map/pallas_call | solution.py:55
  79.3 3.4 %collective-permute-done.25 = bf16[2,2,2,2,72,576]{5,4,3,2,1,0:T(8,128)(2,1)S(1)} collective-permute-done((bf16[2,2,2,2,72,576]{5,4,3,2,1,0:T(8,128)(2,1)}, bf16[2,2,2,2,72,576]{5,4,3,2,1,0:T(8,128)(2,1)S(1)}, u32[]{:S(2)}, u32[]{:S(2)}) %collective-permute-start.25) | collective-permute-done | bytes 1327136 | tf_op jit(solution)/shard_map/ppermute | solution.py:506
  83.2 1.4 fusion
  84.7 1.5 %collective-permute-start.29 = (bf16[2,2,2,72,576]{4,3,2,1,0:T(8,128)(2,1)S(1)}, bf16[2,2,2,72,576]{4,3,2,1,0:T(8,128)(2,1)S(1)}, u32[]{:S(2)}, u32[]{:S(2)}) collective-permute-start(bf16[2,2,2,72,576]{4,3,2,1,0:T(8,128)(2,1)S(1)} %fusion), channel_id=1, source_target_pairs={{0,2},{1,3},{2,0},{3,1},{4,6},{5,7},{6,4},{7,5},{8,10},{9,11},{10,... | collective-permute-start | bytes 1990664 | tf_op jit(solution)/shard_map/ppermute | solution.py:506
  90.2 11.2 %shard_map.190 = (bf16[256,640]{1,0:T(8,128)(2,1)S(1)}, bf16[2,256,384]{2,1,0:T(8,128)(2,1)S(1)}, bf16[2,256,384]{2,1,0:T(8,128)(2,1)S(1)}, bf16[2,2,2,2,80,256]...) custom-call(s32[2]{0:T(128)S(1)} %pad_add_fusion.meta, bf16[256,640]{1,0:T(8,128)(2,1)S(1)} %pad_maximum_fusion.3.b0, ...), custom_call_target="tpu_custom_call" | custom-call | flops 14000000000 | bytes 7273216 | tf_op jit(solution)/shard_map/pallas_call | solution.py:55
  103.1 2.3 %collective-permute-start.38 = (bf16[2,2,72,384]{3,2,1,0:T(8,128)(2,1)S(1)}, bf16[2,2,72,384]{3,2,1,0:T(8,128)(2,1)S(1)}, u32[]{:S(2)}, u32[]{:S(2)}) collective-permute-start(bf16[2,2,72,384]{3,2,1,0:T(8,128)(2,1)S(1)} %get-tuple-element.162), channel_id=1, source_target_pairs={{0,16},{1,17},{2,18},{3,19},{4,20},{5,21},{6,22},{7,23},{8,24},{9,... | collective-permute-start | bytes 663560 | tf_op jit(solution)/shard_map/ppermute | solution.py:506
  108.6 1.4 collective-permute-start.32
  110.0 6.2 %collective-permute-done.35 = bf16[2,2,72,384]{3,2,1,0:T(8,128)(2,1)S(1)} collective-permute-done((bf16[2,2,72,384]{3,2,1,0:T(8,128)(2,1)S(1)}, bf16[2,2,72,384]{3,2,1,0:T(8,128)(2,1)S(1)}, u32[]{:S(2)}, u32[]{:S(2)}) %collective-permute-start.35) | collective-permute-done | bytes 221216 | tf_op jit(solution)/shard_map/ppermute | solution.py:506
  117.2 1.3 collective-permute-start.36
  119.5 1.5 %collective-permute-start.42 = (bf16[2,72,576]{2,1,0:T(8,128)(2,1)S(1)}, bf16[2,72,576]{2,1,0:T(8,128)(2,1)S(1)}, u32[]{:S(2)}, u32[]{:S(2)}) collective-permute-start(bf16[2,72,576]{2,1,0:T(8,128)(2,1)S(1)} %get-tuple-element.168), channel_id=1, source_target_pairs={{0,8},{1,9},{2,10},{3,11},{4,12},{5,13},{6,14},{7,15},{8,0},{9,1},... | collective-permute-start | bytes 497672 | tf_op jit(solution)/shard_map/ppermute | solution.py:506
  121.0 1.9 %collective-permute-done.36 = bf16[2,2,80,256]{3,2,1,0:T(8,128)(2,1)S(1)} collective-permute-done((bf16[2,2,80,256]{3,2,1,0:T(8,128)(2,1)S(1)}, bf16[2,2,80,256]{3,2,1,0:T(8,128)(2,1)S(1)}, u32[]{:S(2)}, u32[]{:S(2)}) %collective-permute-start.36) | collective-permute-done | bytes 163872 | tf_op jit(solution)/shard_map/ppermute | solution.py:506
  124.2 1.9 %shard_map.191 = f32[2,576,128]{2,1,0:T(8,128)} custom-call(bf16[256,640]{1,0:T(8,128)(2,1)S(1)} %get-tuple-element.103.dq, bf16[256,384]{1,0:T(8,128)(2,1)S(1)} %get-tuple-element.166.own, bf16[256,384]{1,0:T(8,128)(2,1)S(1)} %collective-permute-done.32.other, bf16[256,576]{1,0:T(8,128)(2,1)S(1)} %bitcast.213, f32[256,576]{1,0:T(8,128)S(1)} %copy-done.9, ...), custom_call_target="tpu_custom_call" | custom-call | flops 3000000000 | bytes 3305984 | tf_op jit(solution)/shard_map/pallas_call | solution.py:55
  126.2 1.4 collective-permute-start.40
  128.4 2.0 %collective-permute-start.47 = (bf16[72,576]{1,0:T(8,128)(2,1)S(1)}, bf16[72,576]{1,0:T(8,128)(2,1)S(1)}, u32[]{:S(2)}, u32[]{:S(2)}) collective-permute-start(bf16[72,576]{1,0:T(8,128)(2,1)S(1)} %fusion.36), channel_id=1, source_target_pairs={{0,16},{1,17},{2,18},{3,19},{4,20},{5,21},{6,22},{7,23},{8,24},{9,... | collective-permute-start | bytes 248840 | tf_op jit(solution)/shard_map/ppermute | solution.py:506
  131.6 3.3 %collective-permute-done.47 = bf16[72,576]{1,0:T(8,128)(2,1)S(1)} collective-permute-done((bf16[72,576]{1,0:T(8,128)(2,1)S(1)}, bf16[72,576]{1,0:T(8,128)(2,1)S(1)}, u32[]{:S(2)}, u32[]{:S(2)}) %collective-permute-start.47) | collective-permute-done | bytes 82976 | tf_op jit(solution)/shard_map/ppermute | solution.py:506
  135.0 1.8 %collective-permute-start.48 = (bf16[72,576]{1,0:T(8,128)(2,1)S(1)}, bf16[72,576]{1,0:T(8,128)(2,1)S(1)}, u32[]{:S(2)}, u32[]{:S(2)}) collective-permute-start(bf16[72,576]{1,0:T(8,128)(2,1)S(1)} %fusion.26.d0), channel_id=1, source_target_pairs={{0,2},{1,3},{2,0},{3,1},{4,6},{5,7},{6,4},{7,5},{8,10},{9,11},{10,... | collective-permute-start | bytes 248840 | tf_op jit(solution)/shard_map/ppermute | solution.py:506
  137.3 3.6 %collective-permute-done.51.r1 = bf16[80,256]{1,0:T(8,128)(2,1)S(1)} collective-permute-done((bf16[80,256]{1,0:T(8,128)(2,1)S(1)}, bf16[80,256]{1,0:T(8,128)(2,1)S(1)}, u32[]{:S(2)}, u32[]{:S(2)}) %collective-permute-start.51) | collective-permute-done | bytes 40992 | tf_op jit(solution)/shard_map/ppermute | solution.py:506
  142.7 1.9 %shard_map.192 = (f32[72,3072]{1,0:T(8,128)}, f32[192,576]{1,0:T(8,128)}, f32[72,576]{1,0:T(8,128)}, f32[72,960]{1,0:T(8,128)}, f32[1,96]{1,0:T(1,128)}, /*index=5*/f32[1,24]{1,0:T(1,128)}, f32[2,72]{1,0:T(2,128)}) custom-call(s32[2]{0:T(128)S(1)} %pad_add_fusion.meta, bf16[2,72,384]{2,1,0:T(8,128)(2,1)S(1)} %add_convert_fusion.11.a_near, ...), custom_call_target="tpu_custom_call" | custom-call | flops 3000000000 | bytes 2708512 | tf_op jit(solution)/shard_map/pallas_call | solution.py:55
  (199 shorter events, 32.9 us)
Async XLA Ops:
  3.8 8.8 %collective-permute-start.3 = (bf16[40,960]{1,0:T(8,128)(2,1)S(1)}, bf16[40,960]{1,0:T(8,128)(2,1)S(1)}, u32[]{:S(2)}, u32[]{:S(2)}) collective-permute-start(bf16[40,960]{1,0:T(8,128)(2,1)S(1)} %shard_map.187), channel_id=1, source_target_pairs={{0,16},{1,17},{2,18},{3,19},{4,20},{5,21},{6,22},{7,23},{8,24},{9,... | collective-permute-start | bytes 230408 | tf_op jit(solution)/shard_map/ppermute | solution.py:506
  10.0 19.6 %collective-permute-start.1 = (bf16[256,640]{1,0:T(8,128)(2,1)S(1)}, bf16[256,640]{1,0:T(8,128)(2,1)S(1)}, u32[]{:S(2)}, u32[]{:S(2)}) collective-permute-start(bf16[256,640]{1,0:T(8,128)(2,1)S(1)} %pad_maximum_fusion.3.b0), channel_id=1, source_target_pairs={{0,1},{1,0},{2,3},{3,2},{4,5},{5,4},{6,7},{7,6},{8,9},{9,8},{10,11... | collective-permute-start | bytes 983048 | tf_op jit(solution)/shard_map/ppermute | solution.py:506
  10.0 17.7 %collective-permute-start = (bf16[256,640]{1,0:T(8,128)(2,1)S(1)}, bf16[256,640]{1,0:T(8,128)(2,1)S(1)}, u32[]{:S(2)}, u32[]{:S(2)}) collective-permute-start(bf16[256,640]{1,0:T(8,128)(2,1)S(1)} %pad_maximum_fusion.3.b0), channel_id=1, source_target_pairs={{0,2},{1,3},{2,0},{3,1},{4,6},{5,7},{6,4},{7,5},{8,10},{9,11},{10,... | collective-permute-start | bytes 983048 | tf_op jit(solution)/shard_map/ppermute | solution.py:506
  11.6 9.4 %collective-permute-start.8 = (bf16[72,768]{1,0:T(8,128)(2,1)S(1)}, bf16[72,768]{1,0:T(8,128)(2,1)S(1)}, u32[]{:S(2)}, u32[]{:S(2)}) collective-permute-start(bf16[72,768]{1,0:T(8,128)(2,1)S(1)} %constant_dynamic-slice_fusion), channel_id=1, source_target_pairs={{0,16},{1,17},{2,18},{3,19},{4,20},{5,21},{6,22},{7,23},{8,24},{9,... | collective-permute-start | bytes 331784 | tf_op jit(solution)/shard_map/ppermute | solution.py:506
  12.6 10.6 %collective-permute-start.4 = (bf16[2,40,960]{2,1,0:T(8,128)(2,1)S(1)}, bf16[2,40,960]{2,1,0:T(8,128)(2,1)S(1)}, u32[]{:S(2)}, u32[]{:S(2)}) collective-permute-start(bf16[2,40,960]{2,1,0:T(8,128)(2,1)S(1)} %pad_maximum_fusion.6), channel_id=1, source_target_pairs={{0,8},{1,9},{2,10},{3,11},{4,12},{5,13},{6,14},{7,15},{8,0},{9,1},... | collective-permute-start | bytes 460808 | tf_op jit(solution)/shard_map/ppermute | solution.py:506
  14.3 13.4 %collective-permute-start.10 = (bf16[136,576]{1,0:T(8,128)(2,1)S(1)}, bf16[136,576]{1,0:T(8,128)(2,1)S(1)}, u32[]{:S(2)}, u32[]{:S(2)}) collective-permute-start(bf16[136,576]{1,0:T(8,128)(2,1)S(1)} %dynamic-slice_bitcast_fusion), channel_id=1, source_target_pairs={{0,16},{1,17},{2,18},{3,19},{4,20},{5,21},{6,22},{7,23},{8,24},{9,... | collective-permute-start | bytes 470024 | tf_op jit(solution)/shard_map/ppermute | solution.py:506
  23.4 15.4 %collective-permute-start.6 = (bf16[2,2,40,960]{3,2,1,0:T(8,128)(2,1)S(1)}, bf16[2,2,40,960]{3,2,1,0:T(8,128)(2,1)S(1)}, u32[]{:S(2)}, u32[]{:S(2)}) collective-permute-start(bf16[2,2,40,960]{3,2,1,0:T(8,128)(2,1)S(1)} %pad_maximum_fusion.4.a00), channel_id=1, source_target_pairs={{0,1},{1,0},{2,3},{3,2},{4,5},{5,4},{6,7},{7,6},{8,9},{9,8},{10,11... | collective-permute-start | bytes 921608 | tf_op jit(solution)/shard_map/ppermute | solution.py:506
  23.4 12.6 %collective-permute-start.5 = (bf16[2,2,40,960]{3,2,1,0:T(8,128)(2,1)S(1)}, bf16[2,2,40,960]{3,2,1,0:T(8,128)(2,1)S(1)}, u32[]{:S(2)}, u32[]{:S(2)}) collective-permute-start(bf16[2,2,40,960]{3,2,1,0:T(8,128)(2,1)S(1)} %pad_maximum_fusion.4.a00), channel_id=1, source_target_pairs={{0,4},{1,5},{2,6},{3,7},{4,0},{5,1},{6,2},{7,3},{8,12},{9,13},{10,... | collective-permute-start | bytes 921608 | tf_op jit(solution)/shard_map/ppermute | solution.py:506
  27.8 24.0 %collective-permute-start.12 = (bf16[2,136,576]{2,1,0:T(8,128)(2,1)S(1)}, bf16[2,136,576]{2,1,0:T(8,128)(2,1)S(1)}, u32[]{:S(2)}, u32[]{:S(2)}) collective-permute-start(bf16[2,136,576]{2,1,0:T(8,128)(2,1)S(1)} %pad_maximum_fusion.2.refs_0_), channel_id=1, source_target_pairs={{0,4},{1,5},{2,6},{3,7},{4,0},{5,1},{6,2},{7,3},{8,12},{9,13},{10,... | collective-permute-start | bytes 940040 | tf_op jit(solution)/shard_map/ppermute | solution.py:506
  34.4 16.2 %collective-permute-start.21 = (bf16[2,2,72,768]{3,2,1,0:T(8,128)(2,1)S(1)}, bf16[2,2,72,768]{3,2,1,0:T(8,128)(2,1)}, u32[]{:S(2)}, u32[]{:S(2)}) collective-permute-start(bf16[2,2,72,768]{3,2,1,0:T(8,128)(2,1)S(1)} %pad_maximum_fusion.refs_8_), channel_id=1, source_target_pairs={{0,4},{1,5},{2,6},{3,7},{4,0},{5,1},{6,2},{7,3},{8,12},{9,13},{10,... | collective-permute-start | bytes 1327112 | tf_op jit(solution)/shard_map/ppermute | solution.py:506
  36.0 17.6 %collective-permute-start.19 = (bf16[2,2,72,768]{3,2,1,0:T(8,128)(2,1)S(1)}, bf16[2,2,72,768]{3,2,1,0:T(8,128)(2,1)S(1)}, u32[]{:S(2)}, u32[]{:S(2)}) collective-permute-start(bf16[2,2,72,768]{3,2,1,0:T(8,128)(2,1)S(1)} %pad_maximum_fusion.refs_8_), channel_id=1, source_target_pairs={{0,1},{1,0},{2,3},{3,2},{4,5},{5,4},{6,7},{7,6},{8,9},{9,8},{10,11... | collective-permute-start | bytes 1327112 | tf_op jit(solution)/shard_map/ppermute | solution.py:506
  38.3 12.3 %collective-permute-start.13 = (bf16[2,2,72,768]{3,2,1,0:T(8,128)(2,1)S(1)}, bf16[2,2,72,768]{3,2,1,0:T(8,128)(2,1)}, u32[]{:S(2)}, u32[]{:S(2)}) collective-permute-start(bf16[2,2,72,768]{3,2,1,0:T(8,128)(2,1)S(1)} %pad_maximum_fusion.refs_8_), channel_id=1, source_target_pairs={{0,2},{1,3},{2,0},{3,1},{4,6},{5,7},{6,4},{7,5},{8,10},{9,11},{10,... | collective-permute-start | bytes 1327112 | tf_op jit(solution)/shard_map/ppermute | solution.py:506
  38.8 13.6 %collective-permute-start.15 = (bf16[2,136,576]{2,1,0:T(8,128)(2,1)S(1)}, bf16[2,136,576]{2,1,0:T(8,128)(2,1)}, u32[]{:S(2)}, u32[]{:S(2)}) collective-permute-start(bf16[2,136,576]{2,1,0:T(8,128)(2,1)S(1)} %pad_maximum_fusion.2.refs_0_), channel_id=1, source_target_pairs={{0,8},{1,9},{2,10},{3,11},{4,12},{5,13},{6,14},{7,15},{8,0},{9,1},... | collective-permute-start | bytes 940040 | tf_op jit(solution)/shard_map/ppermute | solution.py:506
  50.6 12.0 %collective-permute-start.23 = (bf16[2,2,72,768]{3,2,1,0:T(8,128)(2,1)}, bf16[2,2,72,768]{3,2,1,0:T(8,128)(2,1)}, u32[]{:S(2)}, u32[]{:S(2)}) collective-permute-start(bf16[2,2,72,768]{3,2,1,0:T(8,128)(2,1)} %collective-permute-done.21.refs_12_), channel_id=1, source_target_pairs={{0,2},{1,3},{2,0},{3,1},{4,6},{5,7},{6,4},{7,5},{8,10},{9,11},{10,... | collective-permute-start | bytes 1327112 | tf_op jit(solution)/shard_map/ppermute | solution.py:506
  51.8 10.8 %collective-permute-start.14 = (bf16[2,136,576]{2,1,0:T(8,128)(2,1)S(1)}, bf16[2,136,576]{2,1,0:T(8,128)(2,1)S(1)}, u32[]{:S(2)}, u32[]{:S(2)}) collective-permute-start(bf16[2,136,576]{2,1,0:T(8,128)(2,1)S(1)} %collective-permute-done.12.refs_2_), channel_id=1, source_target_pairs={{0,1},{1,0},{2,3},{3,2},{4,5},{5,4},{6,7},{7,6},{8,9},{9,8},{10,11... | collective-permute-start | bytes 940040 | tf_op jit(solution)/shard_map/ppermute | solution.py:506
  52.4 10.8 %collective-permute-start.17 = (bf16[2,136,576]{2,1,0:T(8,128)(2,1)}, bf16[2,136,576]{2,1,0:T(8,128)(2,1)}, u32[]{:S(2)}, u32[]{:S(2)}) collective-permute-start(bf16[2,136,576]{2,1,0:T(8,128)(2,1)} %collective-permute-done.15.refs_4_), channel_id=1, source_target_pairs={{0,4},{1,5},{2,6},{3,7},{4,0},{5,1},{6,2},{7,3},{8,12},{9,13},{10,... | collective-permute-start | bytes 940040 | tf_op jit(solution)/shard_map/ppermute | solution.py:506
  53.5 11.8 %collective-permute-start.22 = (bf16[2,2,72,768]{3,2,1,0:T(8,128)(2,1)}, bf16[2,2,72,768]{3,2,1,0:T(8,128)(2,1)}, u32[]{:S(2)}, u32[]{:S(2)}) collective-permute-start(bf16[2,2,72,768]{3,2,1,0:T(8,128)(2,1)} %collective-permute-done.21.refs_12_), channel_id=1, source_target_pairs={{0,1},{1,0},{2,3},{3,2},{4,5},{5,4},{6,7},{7,6},{8,9},{9,8},{10,11... | collective-permute-start | bytes 1327112 | tf_op jit(solution)/shard_map/ppermute | solution.py:506
  53.6 11.7 %collective-permute-start.20 = (bf16[2,2,72,768]{3,2,1,0:T(8,128)(2,1)}, bf16[2,2,72,768]{3,2,1,0:T(8,128)(2,1)}, u32[]{:S(2)}, u32[]{:S(2)}) collective-permute-start(bf16[2,2,72,768]{3,2,1,0:T(8,128)(2,1)} %collective-permute-done.13.refs_10_), channel_id=1, source_target_pairs={{0,1},{1,0},{2,3},{3,2},{4,5},{5,4},{6,7},{7,6},{8,9},{9,8},{10,11... | collective-permute-start | bytes 1327112 | tf_op jit(solution)/shard_map/ppermute | solution.py:506
  84.7 21.2 %collective-permute-start.29 = (bf16[2,2,2,72,576]{4,3,2,1,0:T(8,128)(2,1)S(1)}, bf16[2,2,2,72,576]{4,3,2,1,0:T(8,128)(2,1)S(1)}, u32[]{:S(2)}, u32[]{:S(2)}) collective-permute-start(bf16[2,2,2,72,576]{4,3,2,1,0:T(8,128)(2,1)S(1)} %fusion), channel_id=1, source_target_pairs={{0,2},{1,3},{2,0},{3,1},{4,6},{5,7},{6,4},{7,5},{8,10},{9,11},{10,... | collective-permute-start | bytes 1990664 | tf_op jit(solution)/shard_map/ppermute | solution.py:506
  87.3 18.2 %collective-permute-start.34 = (bf16[2,2,2,72,384]{4,3,2,1,0:T(8,128)(2,1)S(1)}, bf16[2,2,2,72,384]{4,3,2,1,0:T(8,128)(2,1)S(1)}, u32[]{:S(2)}, u32[]{:S(2)}) collective-permute-start(bf16[2,2,2,72,384]{4,3,2,1,0:T(8,128)(2,1)S(1)} %fusion.3), channel_id=1, source_target_pairs={{0,4},{1,5},{2,6},{3,7},{4,0},{5,1},{6,2},{7,3},{8,12},{9,13},{10,... | collective-permute-start | bytes 1327112 | tf_op jit(solution)/shard_map/ppermute | solution.py:506
  89.3 13.7 %collective-permute-start.31 = (bf16[2,2,2,72,384]{4,3,2,1,0:T(8,128)(2,1)S(1)}, bf16[2,2,2,72,384]{4,3,2,1,0:T(8,128)(2,1)S(1)}, u32[]{:S(2)}, u32[]{:S(2)}) collective-permute-start(bf16[2,2,2,72,384]{4,3,2,1,0:T(8,128)(2,1)S(1)} %fusion.4), channel_id=1, source_target_pairs={{0,8},{1,9},{2,10},{3,11},{4,12},{5,13},{6,14},{7,15},{8,0},{9,1},... | collective-permute-start | bytes 1327112 | tf_op jit(solution)/shard_map/ppermute | solution.py:506
  103.1 15.4 %collective-permute-start.38 = (bf16[2,2,72,384]{3,2,1,0:T(8,128)(2,1)S(1)}, bf16[2,2,72,384]{3,2,1,0:T(8,128)(2,1)S(1)}, u32[]{:S(2)}, u32[]{:S(2)}) collective-permute-start(bf16[2,2,72,384]{3,2,1,0:T(8,128)(2,1)S(1)} %get-tuple-element.162), channel_id=1, source_target_pairs={{0,16},{1,17},{2,18},{3,19},{4,20},{5,21},{6,22},{7,23},{8,24},{9,... | collective-permute-start | bytes 663560 | tf_op jit(solution)/shard_map/ppermute | solution.py:506
  105.6 10.6 %collective-permute-start.35 = (bf16[2,2,72,384]{3,2,1,0:T(8,128)(2,1)S(1)}, bf16[2,2,72,384]{3,2,1,0:T(8,128)(2,1)S(1)}, u32[]{:S(2)}, u32[]{:S(2)}) collective-permute-start(bf16[2,2,72,384]{3,2,1,0:T(8,128)(2,1)S(1)} %get-tuple-element.163), channel_id=1, source_target_pairs={{0,8},{1,9},{2,10},{3,11},{4,12},{5,13},{6,14},{7,15},{8,0},{9,1},... | collective-permute-start | bytes 663560 | tf_op jit(solution)/shard_map/ppermute | solution.py:506
  106.0 11.1 %collective-permute-start.33 = (bf16[2,2,2,80,256]{4,3,2,1,0:T(8,128)(2,1)S(1)}, bf16[2,2,2,80,256]{4,3,2,1,0:T(8,128)(2,1)S(1)}, u32[]{:S(2)}, u32[]{:S(2)}) collective-permute-start(bf16[2,2,2,80,256]{4,3,2,1,0:T(8,128)(2,1)S(1)} %get-tuple-element.160), channel_id=1, source_target_pairs={{0,2},{1,3},{2,0},{3,1},{4,6},{5,7},{6,4},{7,5},{8,10},{9,11},{10,... | collective-permute-start | bytes 983048 | tf_op jit(solution)/shard_map/ppermute | solution.py:506
  107.4 11.9 %collective-permute-start.37 = (bf16[2,2,72,576]{3,2,1,0:T(8,128)(2,1)S(1)}, bf16[2,2,72,576]{3,2,1,0:T(8,128)(2,1)S(1)}, u32[]{:S(2)}, u32[]{:S(2)}) collective-permute-start(bf16[2,2,72,576]{3,2,1,0:T(8,128)(2,1)S(1)} %get-tuple-element.158), channel_id=1, source_target_pairs={{0,4},{1,5},{2,6},{3,7},{4,0},{5,1},{6,2},{7,3},{8,12},{9,13},{10,... | collective-permute-start | bytes 995336 | tf_op jit(solution)/shard_map/ppermute | solution.py:506
  108.6 15.6 %collective-permute-start.32 = (bf16[256,384]{1,0:T(8,128)(2,1)S(1)}, bf16[256,384]{1,0:T(8,128)(2,1)S(1)}, u32[]{:S(2)}, u32[]{:S(2)}) collective-permute-start(bf16[256,384]{1,0:T(8,128)(2,1)S(1)} %get-tuple-element.165), channel_id=1, source_target_pairs={{0,2},{1,3},{2,0},{3,1},{4,6},{5,7},{6,4},{7,5},{8,10},{9,11},{10,... | collective-permute-start | bytes 589832 | tf_op jit(solution)/shard_map/ppermute | solution.py:506
  116.3 9.8 %collective-permute-start.39 = (bf16[2,72,384]{2,1,0:T(8,128)(2,1)S(1)}, bf16[2,72,384]{2,1,0:T(8,128)(2,1)S(1)}, u32[]{:S(2)}, u32[]{:S(2)}) collective-permute-start(bf16[2,72,384]{2,1,0:T(8,128)(2,1)S(1)} %fusion.32), channel_id=1, source_target_pairs={{0,16},{1,17},{2,18},{3,19},{4,20},{5,21},{6,22},{7,23},{8,24},{9,... | collective-permute-start | bytes 331784 | tf_op jit(solution)/shard_map/ppermute | solution.py:506
  118.6 9.0 %collective-permute-start.43 = (bf16[2,72,384]{2,1,0:T(8,128)(2,1)S(1)}, bf16[2,72,384]{2,1,0:T(8,128)(2,1)S(1)}, u32[]{:S(2)}, u32[]{:S(2)}) collective-permute-start(bf16[2,72,384]{2,1,0:T(8,128)(2,1)S(1)} %fusion.33), channel_id=1, source_target_pairs={{0,4},{1,5},{2,6},{3,7},{4,0},{5,1},{6,2},{7,3},{8,12},{9,13},{10,... | collective-permute-start | bytes 331784 | tf_op jit(solution)/shard_map/ppermute | solution.py:506
  119.5 8.9 %collective-permute-start.42 = (bf16[2,72,576]{2,1,0:T(8,128)(2,1)S(1)}, bf16[2,72,576]{2,1,0:T(8,128)(2,1)S(1)}, u32[]{:S(2)}, u32[]{:S(2)}) collective-permute-start(bf16[2,72,576]{2,1,0:T(8,128)(2,1)S(1)} %get-tuple-element.168), channel_id=1, source_target_pairs={{0,8},{1,9},{2,10},{3,11},{4,12},{5,13},{6,14},{7,15},{8,0},{9,1},... | collective-permute-start | bytes 497672 | tf_op jit(solution)/shard_map/ppermute | solution.py:506
  123.0 7.5 %collective-permute-start.41 = (bf16[2,80,256]{2,1,0:T(8,128)(2,1)S(1)}, bf16[2,80,256]{2,1,0:T(8,128)(2,1)S(1)}, u32[]{:S(2)}, u32[]{:S(2)}) collective-permute-start(bf16[2,80,256]{2,1,0:T(8,128)(2,1)S(1)} %get-tuple-element.176), channel_id=1, source_target_pairs={{0,8},{1,9},{2,10},{3,11},{4,12},{5,13},{6,14},{7,15},{8,0},{9,1},... | collective-permute-start | bytes 245768 | tf_op jit(solution)/shard_map/ppermute | solution.py:506
  127.6 9.6 %collective-permute-start.45 = (bf16[2,72,384]{2,1,0:T(8,128)(2,1)S(1)}, bf16[2,72,384]{2,1,0:T(8,128)(2,1)S(1)}, u32[]{:S(2)}, u32[]{:S(2)}) collective-permute-start(bf16[2,72,384]{2,1,0:T(8,128)(2,1)S(1)} %fusion.17), channel_id=1, source_target_pairs={{0,2},{1,3},{2,0},{3,1},{4,6},{5,7},{6,4},{7,5},{8,10},{9,11},{10,... | collective-permute-start | bytes 331784 | tf_op jit(solution)/shard_map/ppermute | solution.py:506
  131.5 10.0 %collective-permute-start.44 = (bf16[2,72,384]{2,1,0:T(8,128)(2,1)S(1)}, bf16[2,72,384]{2,1,0:T(8,128)(2,1)S(1)}, u32[]{:S(2)}, u32[]{:S(2)}) collective-permute-start(bf16[2,72,384]{2,1,0:T(8,128)(2,1)S(1)} %add_convert_fusion.11.a_near), channel_id=1, source_target_pairs={{0,1},{1,0},{2,3},{3,2},{4,5},{5,4},{6,7},{7,6},{8,9},{9,8},{10,11... | collective-permute-start | bytes 331784 | tf_op jit(solution)/shard_map/ppermute | solution.py:506
  (52 other events, 332.2 us)

commit v14 on v12

--- a/solution.py
+++ b/solution.py
@@ -881,6 +881,7 @@
         ],
         1.4e10,
         [(units // 2, width), (n_fsdp, d_rows + d_rows // 3, width)],
+        mib=36,
         fetched=pieces,
         landing=[(2, 2, 2, 2) + b1.shape[1:], (2, 2, 2, 2, 2, d_rows, units // 2)],
     )

time: 143 us -> 145 us (1.014)
  local copies, waits for them, and re-layouts: 5.24 us -> 13.9 us
  waiting for transfers between devices: 47 us -> 42.7 us
  Pallas kernels: 40.1 us -> 37.9 us
    unnamed x60 -> x68, local copies, waits for them, and re-layouts: 4.2 us -> 12.8 us
    ppermute x54, waiting for transfers between devices: 47 us -> 42.7 us  [swap(): return lax.ppermute(value, ('fsdp', 'seq'), pairs)]
    pallas_call x5, Pallas kernels: 39.2 us -> 37.1 us  [call(): pl.pallas_call(kernel, out_shape=outs, in_specs=specs, out_specs=whole(*o...]
  transfers between devices with their start and end apart: 54 -> 54, of which waited for: 18 -> 15; matrix products, arithmetic and copies ran while one was open for 6% -> 5% of each run, Pallas kernels for 17% -> 17%
where the time goes in v14:
time: 145 us; the launch traced here: 144 us
  starting transfers between devices  43.9 us (30%)
  waiting for transfers between devices  42.7 us (29%)
  Pallas kernels  37.9 us (26%)
  local copies, waits for them, and re-layouts  13.9 us (10%)
  other arithmetic  4.63 us (3%)
    ppermute x54, starting transfers between devices, swap(): return lax.ppermute(value, ('fsdp', 'seq'), pairs)  43.9 us
    ppermute x54, waiting for transfers between devices, swap(): return lax.ppermute(value, ('fsdp', 'seq'), pairs)  42.7 us
    pallas_call x5, Pallas kernels, call(): pl.pallas_call(kernel, out_shape=outs, in_specs=specs, out_specs=whole(*o...  37.1 us
    unnamed x68, local copies, waits for them, and re-layouts  12.8 us
  transfers between devices with their start and end apart: 54, of which 15 were waited for; matrix products, arithmetic and copies ran while one was open for 5% of the time, Pallas kernels for 17%

profile of v14, /device:TPU:0, one launch (start us, length us, event | category | flops | bytes accessed | tf_op | source)
XLA Modules:
  0.0 144.3 jit_solution(16592359527311033325)
XLA Ops:
  3.8 4.1 %collective-permute-start.3 = (bf16[40,960]{1,0:T(8,128)(2,1)S(1)}, bf16[40,960]{1,0:T(8,128)(2,1)S(1)}, u32[]{:S(2)}, u32[]{:S(2)}) collective-permute-start(bf16[40,960]{1,0:T(8,128)(2,1)S(1)} %shard_map.187), channel_id=1, source_target_pairs={{0,16},{1,17},{2,18},{3,19},{4,20},{5,21},{6,22},{7,23},{8,24},{9,... | collective-permute-start | bytes 230408 | tf_op jit(solution)/shard_map/ppermute | solution.py:506
  10.0 1.6 %collective-permute-start = (bf16[256,640]{1,0:T(8,128)(2,1)S(1)}, bf16[256,640]{1,0:T(8,128)(2,1)S(1)}, u32[]{:S(2)}, u32[]{:S(2)}) collective-permute-start(bf16[256,640]{1,0:T(8,128)(2,1)S(1)} %pad_maximum_fusion.3.b0), channel_id=1, source_target_pairs={{0,2},{1,3},{2,0},{3,1},{4,6},{5,7},{6,4},{7,5},{8,10},{9,11},{10,... | collective-permute-start | bytes 983048 | tf_op jit(solution)/shard_map/ppermute | solution.py:506
  12.6 1.6 %collective-permute-start.4 = (bf16[2,40,960]{2,1,0:T(8,128)(2,1)S(1)}, bf16[2,40,960]{2,1,0:T(8,128)(2,1)S(1)}, u32[]{:S(2)}, u32[]{:S(2)}) collective-permute-start(bf16[2,40,960]{2,1,0:T(8,128)(2,1)S(1)} %pad_maximum_fusion.6), channel_id=1, source_target_pairs={{0,8},{1,9},{2,10},{3,11},{4,12},{5,13},{6,14},{7,15},{8,0},{9,1},... | collective-permute-start | bytes 460808 | tf_op jit(solution)/shard_map/ppermute | solution.py:506
  14.3 2.7 %collective-permute-start.10 = (bf16[136,576]{1,0:T(8,128)(2,1)S(1)}, bf16[136,576]{1,0:T(8,128)(2,1)S(1)}, u32[]{:S(2)}, u32[]{:S(2)}) collective-permute-start(bf16[136,576]{1,0:T(8,128)(2,1)S(1)} %dynamic-slice_bitcast_fusion), channel_id=1, source_target_pairs={{0,16},{1,17},{2,18},{3,19},{4,20},{5,21},{6,22},{7,23},{8,24},{9,... | collective-permute-start | bytes 470024 | tf_op jit(solution)/shard_map/ppermute | solution.py:506
  17.0 4.1 %collective-permute-done.8 = bf16[72,768]{1,0:T(8,128)(2,1)S(1)} collective-permute-done((bf16[72,768]{1,0:T(8,128)(2,1)S(1)}, bf16[72,768]{1,0:T(8,128)(2,1)S(1)}, u32[]{:S(2)}, u32[]{:S(2)}) %collective-permute-start.8) | collective-permute-done | bytes 110624 | tf_op jit(solution)/shard_map/ppermute | solution.py:506
  21.1 2.2 %collective-permute-done.4 = bf16[2,40,960]{2,1,0:T(8,128)(2,1)S(1)} collective-permute-done((bf16[2,40,960]{2,1,0:T(8,128)(2,1)S(1)}, bf16[2,40,960]{2,1,0:T(8,128)(2,1)S(1)}, u32[]{:S(2)}, u32[]{:S(2)}) %collective-permute-start.4) | collective-permute-done | bytes 153632 | tf_op jit(solution)/shard_map/ppermute | solution.py:506
  23.4 1.6 %collective-permute-start.5 = (bf16[2,2,40,960]{3,2,1,0:T(8,128)(2,1)S(1)}, bf16[2,2,40,960]{3,2,1,0:T(8,128)(2,1)S(1)}, u32[]{:S(2)}, u32[]{:S(2)}) collective-permute-start(bf16[2,2,40,960]{3,2,1,0:T(8,128)(2,1)S(1)} %pad_maximum_fusion.4.a00), channel_id=1, source_target_pairs={{0,4},{1,5},{2,6},{3,7},{4,0},{5,1},{6,2},{7,3},{8,12},{9,13},{10,... | collective-permute-start | bytes 921608 | tf_op jit(solution)/shard_map/ppermute | solution.py:506
  25.0 2.7 %collective-permute-done.10 = bf16[136,576]{1,0:T(8,128)(2,1)S(1)} collective-permute-done((bf16[136,576]{1,0:T(8,128)(2,1)S(1)}, bf16[136,576]{1,0:T(8,128)(2,1)S(1)}, u32[]{:S(2)}, u32[]{:S(2)}) %collective-permute-start.10) | collective-permute-done | bytes 156704 | tf_op jit(solution)/shard_map/ppermute | solution.py:506
  27.8 1.6 %collective-permute-start.12 = (bf16[2,136,576]{2,1,0:T(8,128)(2,1)S(1)}, bf16[2,136,576]{2,1,0:T(8,128)(2,1)S(1)}, u32[]{:S(2)}, u32[]{:S(2)}) collective-permute-start(bf16[2,136,576]{2,1,0:T(8,128)(2,1)S(1)} %pad_maximum_fusion.2.refs_0_), channel_id=1, source_target_pairs={{0,4},{1,5},{2,6},{3,7},{4,0},{5,1},{6,2},{7,3},{8,12},{9,13},{10,... | collective-permute-start | bytes 940040 | tf_op jit(solution)/shard_map/ppermute | solution.py:506
  29.8 4.5 %collective-permute-done.9 = bf16[2,72,768]{2,1,0:T(8,128)(2,1)S(1)} collective-permute-done((bf16[2,72,768]{2,1,0:T(8,128)(2,1)S(1)}, bf16[2,72,768]{2,1,0:T(8,128)(2,1)S(1)}, u32[]{:S(2)}, u32[]{:S(2)}) %collective-permute-start.9) | collective-permute-done | bytes 221216 | tf_op jit(solution)/shard_map/ppermute | solution.py:506
  34.4 1.6 %collective-permute-start.21 = (bf16[2,2,72,768]{3,2,1,0:T(8,128)(2,1)S(1)}, bf16[2,2,72,768]{3,2,1,0:T(8,128)(2,1)S(1)}, u32[]{:S(2)}, u32[]{:S(2)}) collective-permute-start(bf16[2,2,72,768]{3,2,1,0:T(8,128)(2,1)S(1)} %pad_maximum_fusion.refs_8_), channel_id=1, source_target_pairs={{0,4},{1,5},{2,6},{3,7},{4,0},{5,1},{6,2},{7,3},{8,12},{9,13},{10,... | collective-permute-start | bytes 1327112 | tf_op jit(solution)/shard_map/ppermute | solution.py:506
  39.5 10.7 %shard_map.188 = (bf16[256,576]{1,0:T(8,128)(2,1)S(1)}, bf16[2,3,384,64]{3,2,1,0:T(8,128)(2,1)}, bf16[2,3,512,64]{3,2,1,0:T(8,128)(2,1)}, bf16[2,3,512,64]{3,2,1...) custom-call(s32[2]{0:T(128)S(1)} %pad_add_fusion.meta, bf16[256,640]{1,0:T(8,128)(2,1)S(1)} %pad_maximum_fusion.3.b0, ...), custom_call_target="tpu_custom_call" | custom-call | flops 12000000000 | bytes 6074880 | tf_op jit(solution)/shard_map/pallas_call | solution.py:55
  50.9 1.5 %collective-permute-start.23 = (bf16[2,2,72,768]{3,2,1,0:T(8,128)(2,1)S(1)}, bf16[2,2,72,768]{3,2,1,0:T(8,128)(2,1)}, u32[]{:S(2)}, u32[]{:S(2)}) collective-permute-start(bf16[2,2,72,768]{3,2,1,0:T(8,128)(2,1)S(1)} %collective-permute-done.21.refs_12_), channel_id=1, source_target_pairs={{0,2},{1,3},{2,0},{3,1},{4,6},{5,7},{6,4},{7,5},{8,10},{9,11},{10,... | collective-permute-start | bytes 1327112 | tf_op jit(solution)/shard_map/ppermute | solution.py:506
  56.3 6.6 %collective-permute-done.23.refs_14_ = bf16[2,2,72,768]{3,2,1,0:T(8,128)(2,1)} collective-permute-done((bf16[2,2,72,768]{3,2,1,0:T(8,128)(2,1)S(1)}, bf16[2,2,72,768]{3,2,1,0:T(8,128)(2,1)}, u32[]{:S(2)}, u32[]{:S(2)}) %collective-permute-start.23) | collective-permute-done | bytes 442400 | tf_op jit(solution)/shard_map/ppermute | solution.py:506
  71.3 11.3 %shard_map.189 = (bf16[2,576,128]{2,1,0:T(8,128)(2,1)}, bf16[2,2,2,2,72,384]{5,4,3,2,1,0:T(8,128)(2,1)S(1)}, bf16[2,2,2,2,72,384]{5,4,3,2,1,0:T(8,128)(2,1)S(1)}...) custom-call(s32[2]{0:T(128)S(1)} %pad_add_fusion.meta, ...), custom_call_target="tpu_custom_call" | custom-call | flops 14000000000 | bytes 14311168 | tf_op jit(solution)/shard_map/pallas_call | solution.py:55
  83.1 2.9 %collective-permute-done.25 = bf16[2,2,2,2,72,576]{5,4,3,2,1,0:T(8,128)(2,1)S(1)} collective-permute-done((bf16[2,2,2,2,72,576]{5,4,3,2,1,0:T(8,128)(2,1)S(1)}, bf16[2,2,2,2,72,576]{5,4,3,2,1,0:T(8,128)(2,1)S(1)}, u32[]{:S(2)}, u32[]{:S(2)}) %collective-permute-start.25) | collective-permute-done | bytes 1327136 | tf_op jit(solution)/shard_map/ppermute | solution.py:506
  86.9 1.6 %collective-permute-start.29 = (bf16[2,2,2,72,576]{4,3,2,1,0:T(8,128)(2,1)S(1)}, bf16[2,2,2,72,576]{4,3,2,1,0:T(8,128)(2,1)S(1)}, u32[]{:S(2)}, u32[]{:S(2)}) collective-permute-start(bf16[2,2,2,72,576]{4,3,2,1,0:T(8,128)(2,1)S(1)} %get-tuple-element.152), channel_id=1, source_target_pairs={{0,2},{1,3},{2,0},{3,1},{4,6},{5,7},{6,4},{7,5},{8,10},{9,11},{10,... | collective-permute-start | bytes 1990664 | tf_op jit(solution)/shard_map/ppermute | solution.py:506
  91.1 11.2 %shard_map.190 = (bf16[256,640]{1,0:T(8,128)(2,1)S(1)}, bf16[2,256,384]{2,1,0:T(8,128)(2,1)S(1)}, bf16[2,256,384]{2,1,0:T(8,128)(2,1)S(1)}, bf16[2,2,2,2,80,256]...) custom-call(s32[2]{0:T(128)S(1)} %pad_add_fusion.meta, bf16[256,640]{1,0:T(8,128)(2,1)S(1)} %pad_maximum_fusion.3.b0, ...), custom_call_target="tpu_custom_call" | custom-call | flops 14000000000 | bytes 7273216 | tf_op jit(solution)/shard_map/pallas_call | solution.py:55
  103.0 2.0 %collective-permute-start.38 = (bf16[2,2,72,384]{3,2,1,0:T(8,128)(2,1)S(1)}, bf16[2,2,72,384]{3,2,1,0:T(8,128)(2,1)S(1)}, u32[]{:S(2)}, u32[]{:S(2)}) collective-permute-start(bf16[2,2,72,384]{3,2,1,0:T(8,128)(2,1)S(1)} %get-tuple-element.162), channel_id=1, source_target_pairs={{0,16},{1,17},{2,18},{3,19},{4,20},{5,21},{6,22},{7,23},{8,24},{9,... | collective-permute-start | bytes 663560 | tf_op jit(solution)/shard_map/ppermute | solution.py:506
  106.0 1.5 %collective-permute-start.33 = (bf16[2,2,2,80,256]{4,3,2,1,0:T(8,128)(2,1)S(1)}, bf16[2,2,2,80,256]{4,3,2,1,0:T(8,128)(2,1)S(1)}, u32[]{:S(2)}, u32[]{:S(2)}) collective-permute-start(bf16[2,2,2,80,256]{4,3,2,1,0:T(8,128)(2,1)S(1)} %get-tuple-element.160), channel_id=1, source_target_pairs={{0,2},{1,3},{2,0},{3,1},{4,6},{5,7},{6,4},{7,5},{8,10},{9,11},{10,... | collective-permute-start | bytes 983048 | tf_op jit(solution)/shard_map/ppermute | solution.py:506
  109.7 6.9 %collective-permute-done.35 = bf16[2,2,72,384]{3,2,1,0:T(8,128)(2,1)S(1)} collective-permute-done((bf16[2,2,72,384]{3,2,1,0:T(8,128)(2,1)S(1)}, bf16[2,2,72,384]{3,2,1,0:T(8,128)(2,1)S(1)}, u32[]{:S(2)}, u32[]{:S(2)}) %collective-permute-start.35) | collective-permute-done | bytes 221216 | tf_op jit(solution)/shard_map/ppermute | solution.py:506
  117.4 1.2 collective-permute-start.36
  120.6 3.1 %collective-permute-done.36 = bf16[2,2,80,256]{3,2,1,0:T(8,128)(2,1)S(1)} collective-permute-done((bf16[2,2,80,256]{3,2,1,0:T(8,128)(2,1)S(1)}, bf16[2,2,80,256]{3,2,1,0:T(8,128)(2,1)S(1)}, u32[]{:S(2)}, u32[]{:S(2)}) %collective-permute-start.36) | collective-permute-done | bytes 163872 | tf_op jit(solution)/shard_map/ppermute | solution.py:506
  124.2 1.9 %shard_map.191 = f32[2,576,128]{2,1,0:T(8,128)} custom-call(bf16[256,640]{1,0:T(8,128)(2,1)S(1)} %get-tuple-element.100.dq, bf16[256,384]{1,0:T(8,128)(2,1)S(1)} %get-tuple-element.166.own, bf16[256,384]{1,0:T(8,128)(2,1)S(1)} %collective-permute-done.32.other, bf16[256,576]{1,0:T(8,128)(2,1)S(1)} %bitcast.213, f32[256,576]{1,0:T(8,128)S(1)} %get-tuple-element.116.mid, ...), custom_call_target="tpu_custom_call" | custom-call | flops 3000000000 | bytes 3305984 | tf_op jit(solution)/shard_map/pallas_call | solution.py:55
  126.1 1.3 collective-permute-start.40
  128.4 2.7 %collective-permute-start.47 = (bf16[72,576]{1,0:T(8,128)(2,1)S(1)}, bf16[72,576]{1,0:T(8,128)(2,1)S(1)}, u32[]{:S(2)}, u32[]{:S(2)}) collective-permute-start(bf16[72,576]{1,0:T(8,128)(2,1)S(1)} %fusion.36), channel_id=1, source_target_pairs={{0,16},{1,17},{2,18},{3,19},{4,20},{5,21},{6,22},{7,23},{8,24},{9,... | collective-permute-start | bytes 248840 | tf_op jit(solution)/shard_map/ppermute | solution.py:506
  131.6 2.3 %collective-permute-done.47 = bf16[72,576]{1,0:T(8,128)(2,1)S(1)} collective-permute-done((bf16[72,576]{1,0:T(8,128)(2,1)S(1)}, bf16[72,576]{1,0:T(8,128)(2,1)S(1)}, u32[]{:S(2)}, u32[]{:S(2)}) %collective-permute-start.47) | collective-permute-done | bytes 82976 | tf_op jit(solution)/shard_map/ppermute | solution.py:506
  134.0 1.3 collective-permute-start.48
  136.4 1.2 collective-permute-start.51
  137.7 2.8 %collective-permute-done.51.r1 = bf16[80,256]{1,0:T(8,128)(2,1)S(1)} collective-permute-done((bf16[80,256]{1,0:T(8,128)(2,1)S(1)}, bf16[80,256]{1,0:T(8,128)(2,1)S(1)}, u32[]{:S(2)}, u32[]{:S(2)}) %collective-permute-start.51) | collective-permute-done | bytes 40992 | tf_op jit(solution)/shard_map/ppermute | solution.py:506
  141.1 1.2 collective-permute-done.53.far
  142.3 1.9 %shard_map.192 = (f32[72,3072]{1,0:T(8,128)}, f32[192,576]{1,0:T(8,128)}, f32[72,576]{1,0:T(8,128)}, f32[72,960]{1,0:T(8,128)}, f32[1,96]{1,0:T(1,128)}, /*index=5*/f32[1,24]{1,0:T(1,128)}, f32[2,72]{1,0:T(2,128)}) custom-call(s32[2]{0:T(128)S(1)} %pad_add_fusion.meta, bf16[2,72,384]{2,1,0:T(8,128)(2,1)S(1)} %add_convert_fusion.11.a_near, ...), custom_call_target="tpu_custom_call" | custom-call | flops 3000000000 | bytes 2708512 | tf_op jit(solution)/shard_map/pallas_call | solution.py:55
  (203 shorter events, 37.6 us)
Async XLA Ops:
  3.8 8.8 %collective-permute-start.3 = (bf16[40,960]{1,0:T(8,128)(2,1)S(1)}, bf16[40,960]{1,0:T(8,128)(2,1)S(1)}, u32[]{:S(2)}, u32[]{:S(2)}) collective-permute-start(bf16[40,960]{1,0:T(8,128)(2,1)S(1)} %shard_map.187), channel_id=1, source_target_pairs={{0,16},{1,17},{2,18},{3,19},{4,20},{5,21},{6,22},{7,23},{8,24},{9,... | collective-permute-start | bytes 230408 | tf_op jit(solution)/shard_map/ppermute | solution.py:506
  10.0 19.6 %collective-permute-start.1 = (bf16[256,640]{1,0:T(8,128)(2,1)S(1)}, bf16[256,640]{1,0:T(8,128)(2,1)S(1)}, u32[]{:S(2)}, u32[]{:S(2)}) collective-permute-start(bf16[256,640]{1,0:T(8,128)(2,1)S(1)} %pad_maximum_fusion.3.b0), channel_id=1, source_target_pairs={{0,1},{1,0},{2,3},{3,2},{4,5},{5,4},{6,7},{7,6},{8,9},{9,8},{10,11... | collective-permute-start | bytes 983048 | tf_op jit(solution)/shard_map/ppermute | solution.py:506
  10.0 17.7 %collective-permute-start = (bf16[256,640]{1,0:T(8,128)(2,1)S(1)}, bf16[256,640]{1,0:T(8,128)(2,1)S(1)}, u32[]{:S(2)}, u32[]{:S(2)}) collective-permute-start(bf16[256,640]{1,0:T(8,128)(2,1)S(1)} %pad_maximum_fusion.3.b0), channel_id=1, source_target_pairs={{0,2},{1,3},{2,0},{3,1},{4,6},{5,7},{6,4},{7,5},{8,10},{9,11},{10,... | collective-permute-start | bytes 983048 | tf_op jit(solution)/shard_map/ppermute | solution.py:506
  11.6 9.4 %collective-permute-start.8 = (bf16[72,768]{1,0:T(8,128)(2,1)S(1)}, bf16[72,768]{1,0:T(8,128)(2,1)S(1)}, u32[]{:S(2)}, u32[]{:S(2)}) collective-permute-start(bf16[72,768]{1,0:T(8,128)(2,1)S(1)} %constant_dynamic-slice_fusion), channel_id=1, source_target_pairs={{0,16},{1,17},{2,18},{3,19},{4,20},{5,21},{6,22},{7,23},{8,24},{9,... | collective-permute-start | bytes 331784 | tf_op jit(solution)/shard_map/ppermute | solution.py:506
  12.6 10.6 %collective-permute-start.4 = (bf16[2,40,960]{2,1,0:T(8,128)(2,1)S(1)}, bf16[2,40,960]{2,1,0:T(8,128)(2,1)S(1)}, u32[]{:S(2)}, u32[]{:S(2)}) collective-permute-start(bf16[2,40,960]{2,1,0:T(8,128)(2,1)S(1)} %pad_maximum_fusion.6), channel_id=1, source_target_pairs={{0,8},{1,9},{2,10},{3,11},{4,12},{5,13},{6,14},{7,15},{8,0},{9,1},... | collective-permute-start | bytes 460808 | tf_op jit(solution)/shard_map/ppermute | solution.py:506
  14.3 13.4 %collective-permute-start.10 = (bf16[136,576]{1,0:T(8,128)(2,1)S(1)}, bf16[136,576]{1,0:T(8,128)(2,1)S(1)}, u32[]{:S(2)}, u32[]{:S(2)}) collective-permute-start(bf16[136,576]{1,0:T(8,128)(2,1)S(1)} %dynamic-slice_bitcast_fusion), channel_id=1, source_target_pairs={{0,16},{1,17},{2,18},{3,19},{4,20},{5,21},{6,22},{7,23},{8,24},{9,... | collective-permute-start | bytes 470024 | tf_op jit(solution)/shard_map/ppermute | solution.py:506
  23.4 15.4 %collective-permute-start.6 = (bf16[2,2,40,960]{3,2,1,0:T(8,128)(2,1)S(1)}, bf16[2,2,40,960]{3,2,1,0:T(8,128)(2,1)S(1)}, u32[]{:S(2)}, u32[]{:S(2)}) collective-permute-start(bf16[2,2,40,960]{3,2,1,0:T(8,128)(2,1)S(1)} %pad_maximum_fusion.4.a00), channel_id=1, source_target_pairs={{0,1},{1,0},{2,3},{3,2},{4,5},{5,4},{6,7},{7,6},{8,9},{9,8},{10,11... | collective-permute-start | bytes 921608 | tf_op jit(solution)/shard_map/ppermute | solution.py:506
  23.4 12.5 %collective-permute-start.5 = (bf16[2,2,40,960]{3,2,1,0:T(8,128)(2,1)S(1)}, bf16[2,2,40,960]{3,2,1,0:T(8,128)(2,1)S(1)}, u32[]{:S(2)}, u32[]{:S(2)}) collective-permute-start(bf16[2,2,40,960]{3,2,1,0:T(8,128)(2,1)S(1)} %pad_maximum_fusion.4.a00), channel_id=1, source_target_pairs={{0,4},{1,5},{2,6},{3,7},{4,0},{5,1},{6,2},{7,3},{8,12},{9,13},{10,... | collective-permute-start | bytes 921608 | tf_op jit(solution)/shard_map/ppermute | solution.py:506
  27.8 24.7 %collective-permute-start.12 = (bf16[2,136,576]{2,1,0:T(8,128)(2,1)S(1)}, bf16[2,136,576]{2,1,0:T(8,128)(2,1)S(1)}, u32[]{:S(2)}, u32[]{:S(2)}) collective-permute-start(bf16[2,136,576]{2,1,0:T(8,128)(2,1)S(1)} %pad_maximum_fusion.2.refs_0_), channel_id=1, source_target_pairs={{0,4},{1,5},{2,6},{3,7},{4,0},{5,1},{6,2},{7,3},{8,12},{9,13},{10,... | collective-permute-start | bytes 940040 | tf_op jit(solution)/shard_map/ppermute | solution.py:506
  34.4 16.5 %collective-permute-start.21 = (bf16[2,2,72,768]{3,2,1,0:T(8,128)(2,1)S(1)}, bf16[2,2,72,768]{3,2,1,0:T(8,128)(2,1)S(1)}, u32[]{:S(2)}, u32[]{:S(2)}) collective-permute-start(bf16[2,2,72,768]{3,2,1,0:T(8,128)(2,1)S(1)} %pad_maximum_fusion.refs_8_), channel_id=1, source_target_pairs={{0,4},{1,5},{2,6},{3,7},{4,0},{5,1},{6,2},{7,3},{8,12},{9,13},{10,... | collective-permute-start | bytes 1327112 | tf_op jit(solution)/shard_map/ppermute | solution.py:506
  36.0 19.1 %collective-permute-start.19 = (bf16[2,2,72,768]{3,2,1,0:T(8,128)(2,1)S(1)}, bf16[2,2,72,768]{3,2,1,0:T(8,128)(2,1)S(1)}, u32[]{:S(2)}, u32[]{:S(2)}) collective-permute-start(bf16[2,2,72,768]{3,2,1,0:T(8,128)(2,1)S(1)} %pad_maximum_fusion.refs_8_), channel_id=1, source_target_pairs={{0,1},{1,0},{2,3},{3,2},{4,5},{5,4},{6,7},{7,6},{8,9},{9,8},{10,11... | collective-permute-start | bytes 1327112 | tf_op jit(solution)/shard_map/ppermute | solution.py:506
  38.3 12.7 %collective-permute-start.13 = (bf16[2,2,72,768]{3,2,1,0:T(8,128)(2,1)S(1)}, bf16[2,2,72,768]{3,2,1,0:T(8,128)(2,1)}, u32[]{:S(2)}, u32[]{:S(2)}) collective-permute-start(bf16[2,2,72,768]{3,2,1,0:T(8,128)(2,1)S(1)} %pad_maximum_fusion.refs_8_), channel_id=1, source_target_pairs={{0,2},{1,3},{2,0},{3,1},{4,6},{5,7},{6,4},{7,5},{8,10},{9,11},{10,... | collective-permute-start | bytes 1327112 | tf_op jit(solution)/shard_map/ppermute | solution.py:506
  38.8 15.0 %collective-permute-start.15 = (bf16[2,136,576]{2,1,0:T(8,128)(2,1)S(1)}, bf16[2,136,576]{2,1,0:T(8,128)(2,1)}, u32[]{:S(2)}, u32[]{:S(2)}) collective-permute-start(bf16[2,136,576]{2,1,0:T(8,128)(2,1)S(1)} %pad_maximum_fusion.2.refs_0_), channel_id=1, source_target_pairs={{0,8},{1,9},{2,10},{3,11},{4,12},{5,13},{6,14},{7,15},{8,0},{9,1},... | collective-permute-start | bytes 940040 | tf_op jit(solution)/shard_map/ppermute | solution.py:506
  50.9 12.0 %collective-permute-start.23 = (bf16[2,2,72,768]{3,2,1,0:T(8,128)(2,1)S(1)}, bf16[2,2,72,768]{3,2,1,0:T(8,128)(2,1)}, u32[]{:S(2)}, u32[]{:S(2)}) collective-permute-start(bf16[2,2,72,768]{3,2,1,0:T(8,128)(2,1)S(1)} %collective-permute-done.21.refs_12_), channel_id=1, source_target_pairs={{0,2},{1,3},{2,0},{3,1},{4,6},{5,7},{6,4},{7,5},{8,10},{9,11},{10,... | collective-permute-start | bytes 1327112 | tf_op jit(solution)/shard_map/ppermute | solution.py:506
  52.5 10.5 %collective-permute-start.14 = (bf16[2,136,576]{2,1,0:T(8,128)(2,1)S(1)}, bf16[2,136,576]{2,1,0:T(8,128)(2,1)S(1)}, u32[]{:S(2)}, u32[]{:S(2)}) collective-permute-start(bf16[2,136,576]{2,1,0:T(8,128)(2,1)S(1)} %collective-permute-done.12.refs_2_), channel_id=1, source_target_pairs={{0,1},{1,0},{2,3},{3,2},{4,5},{5,4},{6,7},{7,6},{8,9},{9,8},{10,11... | collective-permute-start | bytes 940040 | tf_op jit(solution)/shard_map/ppermute | solution.py:506
  53.7 10.5 %collective-permute-start.17 = (bf16[2,136,576]{2,1,0:T(8,128)(2,1)}, bf16[2,136,576]{2,1,0:T(8,128)(2,1)}, u32[]{:S(2)}, u32[]{:S(2)}) collective-permute-start(bf16[2,136,576]{2,1,0:T(8,128)(2,1)} %collective-permute-done.15.refs_4_), channel_id=1, source_target_pairs={{0,4},{1,5},{2,6},{3,7},{4,0},{5,1},{6,2},{7,3},{8,12},{9,13},{10,... | collective-permute-start | bytes 940040 | tf_op jit(solution)/shard_map/ppermute | solution.py:506
  55.0 10.8 %collective-permute-start.22 = (bf16[2,2,72,768]{3,2,1,0:T(8,128)(2,1)S(1)}, bf16[2,2,72,768]{3,2,1,0:T(8,128)(2,1)}, u32[]{:S(2)}, u32[]{:S(2)}) collective-permute-start(bf16[2,2,72,768]{3,2,1,0:T(8,128)(2,1)S(1)} %collective-permute-done.21.refs_12_), channel_id=1, source_target_pairs={{0,1},{1,0},{2,3},{3,2},{4,5},{5,4},{6,7},{7,6},{8,9},{9,8},{10,11... | collective-permute-start | bytes 1327112 | tf_op jit(solution)/shard_map/ppermute | solution.py:506
  55.8 10.1 %collective-permute-start.20 = (bf16[2,2,72,768]{3,2,1,0:T(8,128)(2,1)}, bf16[2,2,72,768]{3,2,1,0:T(8,128)(2,1)}, u32[]{:S(2)}, u32[]{:S(2)}) collective-permute-start(bf16[2,2,72,768]{3,2,1,0:T(8,128)(2,1)} %collective-permute-done.13.refs_10_), channel_id=1, source_target_pairs={{0,1},{1,0},{2,3},{3,2},{4,5},{5,4},{6,7},{7,6},{8,9},{9,8},{10,11... | collective-permute-start | bytes 1327112 | tf_op jit(solution)/shard_map/ppermute | solution.py:506
  86.9 18.9 %collective-permute-start.29 = (bf16[2,2,2,72,576]{4,3,2,1,0:T(8,128)(2,1)S(1)}, bf16[2,2,2,72,576]{4,3,2,1,0:T(8,128)(2,1)S(1)}, u32[]{:S(2)}, u32[]{:S(2)}) collective-permute-start(bf16[2,2,2,72,576]{4,3,2,1,0:T(8,128)(2,1)S(1)} %get-tuple-element.152), channel_id=1, source_target_pairs={{0,2},{1,3},{2,0},{3,1},{4,6},{5,7},{6,4},{7,5},{8,10},{9,11},{10,... | collective-permute-start | bytes 1990664 | tf_op jit(solution)/shard_map/ppermute | solution.py:506
  88.8 16.2 %collective-permute-start.34 = (bf16[2,2,2,72,384]{4,3,2,1,0:T(8,128)(2,1)S(1)}, bf16[2,2,2,72,384]{4,3,2,1,0:T(8,128)(2,1)S(1)}, u32[]{:S(2)}, u32[]{:S(2)}) collective-permute-start(bf16[2,2,2,72,384]{4,3,2,1,0:T(8,128)(2,1)S(1)} %get-tuple-element.154), channel_id=1, source_target_pairs={{0,4},{1,5},{2,6},{3,7},{4,0},{5,1},{6,2},{7,3},{8,12},{9,13},{10,... | collective-permute-start | bytes 1327112 | tf_op jit(solution)/shard_map/ppermute | solution.py:506
  89.9 13.0 %collective-permute-start.31 = (bf16[2,2,2,72,384]{4,3,2,1,0:T(8,128)(2,1)S(1)}, bf16[2,2,2,72,384]{4,3,2,1,0:T(8,128)(2,1)S(1)}, u32[]{:S(2)}, u32[]{:S(2)}) collective-permute-start(bf16[2,2,2,72,384]{4,3,2,1,0:T(8,128)(2,1)S(1)} %get-tuple-element.156), channel_id=1, source_target_pairs={{0,8},{1,9},{2,10},{3,11},{4,12},{5,13},{6,14},{7,15},{8,0},{9,1},... | collective-permute-start | bytes 1327112 | tf_op jit(solution)/shard_map/ppermute | solution.py:506
  103.0 15.6 %collective-permute-start.38 = (bf16[2,2,72,384]{3,2,1,0:T(8,128)(2,1)S(1)}, bf16[2,2,72,384]{3,2,1,0:T(8,128)(2,1)S(1)}, u32[]{:S(2)}, u32[]{:S(2)}) collective-permute-start(bf16[2,2,72,384]{3,2,1,0:T(8,128)(2,1)S(1)} %get-tuple-element.162), channel_id=1, source_target_pairs={{0,16},{1,17},{2,18},{3,19},{4,20},{5,21},{6,22},{7,23},{8,24},{9,... | collective-permute-start | bytes 663560 | tf_op jit(solution)/shard_map/ppermute | solution.py:506
  105.2 11.4 %collective-permute-start.35 = (bf16[2,2,72,384]{3,2,1,0:T(8,128)(2,1)S(1)}, bf16[2,2,72,384]{3,2,1,0:T(8,128)(2,1)S(1)}, u32[]{:S(2)}, u32[]{:S(2)}) collective-permute-start(bf16[2,2,72,384]{3,2,1,0:T(8,128)(2,1)S(1)} %get-tuple-element.163), channel_id=1, source_target_pairs={{0,8},{1,9},{2,10},{3,11},{4,12},{5,13},{6,14},{7,15},{8,0},{9,1},... | collective-permute-start | bytes 663560 | tf_op jit(solution)/shard_map/ppermute | solution.py:506
  106.0 11.3 %collective-permute-start.33 = (bf16[2,2,2,80,256]{4,3,2,1,0:T(8,128)(2,1)S(1)}, bf16[2,2,2,80,256]{4,3,2,1,0:T(8,128)(2,1)S(1)}, u32[]{:S(2)}, u32[]{:S(2)}) collective-permute-start(bf16[2,2,2,80,256]{4,3,2,1,0:T(8,128)(2,1)S(1)} %get-tuple-element.160), channel_id=1, source_target_pairs={{0,2},{1,3},{2,0},{3,1},{4,6},{5,7},{6,4},{7,5},{8,10},{9,11},{10,... | collective-permute-start | bytes 983048 | tf_op jit(solution)/shard_map/ppermute | solution.py:506
  107.7 11.8 %collective-permute-start.37 = (bf16[2,2,72,576]{3,2,1,0:T(8,128)(2,1)S(1)}, bf16[2,2,72,576]{3,2,1,0:T(8,128)(2,1)S(1)}, u32[]{:S(2)}, u32[]{:S(2)}) collective-permute-start(bf16[2,2,72,576]{3,2,1,0:T(8,128)(2,1)S(1)} %get-tuple-element.158), channel_id=1, source_target_pairs={{0,4},{1,5},{2,6},{3,7},{4,0},{5,1},{6,2},{7,3},{8,12},{9,13},{10,... | collective-permute-start | bytes 995336 | tf_op jit(solution)/shard_map/ppermute | solution.py:506
  109.0 15.2 %collective-permute-start.32 = (bf16[256,384]{1,0:T(8,128)(2,1)S(1)}, bf16[256,384]{1,0:T(8,128)(2,1)S(1)}, u32[]{:S(2)}, u32[]{:S(2)}) collective-permute-start(bf16[256,384]{1,0:T(8,128)(2,1)S(1)} %get-tuple-element.165), channel_id=1, source_target_pairs={{0,2},{1,3},{2,0},{3,1},{4,6},{5,7},{6,4},{7,5},{8,10},{9,11},{10,... | collective-permute-start | bytes 589832 | tf_op jit(solution)/shard_map/ppermute | solution.py:506
  116.6 9.5 %collective-permute-start.39 = (bf16[2,72,384]{2,1,0:T(8,128)(2,1)S(1)}, bf16[2,72,384]{2,1,0:T(8,128)(2,1)S(1)}, u32[]{:S(2)}, u32[]{:S(2)}) collective-permute-start(bf16[2,72,384]{2,1,0:T(8,128)(2,1)S(1)} %fusion.32), channel_id=1, source_target_pairs={{0,16},{1,17},{2,18},{3,19},{4,20},{5,21},{6,22},{7,23},{8,24},{9,... | collective-permute-start | bytes 331784 | tf_op jit(solution)/shard_map/ppermute | solution.py:506
  118.6 8.8 %collective-permute-start.43 = (bf16[2,72,384]{2,1,0:T(8,128)(2,1)S(1)}, bf16[2,72,384]{2,1,0:T(8,128)(2,1)S(1)}, u32[]{:S(2)}, u32[]{:S(2)}) collective-permute-start(bf16[2,72,384]{2,1,0:T(8,128)(2,1)S(1)} %fusion.33), channel_id=1, source_target_pairs={{0,4},{1,5},{2,6},{3,7},{4,0},{5,1},{6,2},{7,3},{8,12},{9,13},{10,... | collective-permute-start | bytes 331784 | tf_op jit(solution)/shard_map/ppermute | solution.py:506
  119.7 8.7 %collective-permute-start.42 = (bf16[2,72,576]{2,1,0:T(8,128)(2,1)S(1)}, bf16[2,72,576]{2,1,0:T(8,128)(2,1)S(1)}, u32[]{:S(2)}, u32[]{:S(2)}) collective-permute-start(bf16[2,72,576]{2,1,0:T(8,128)(2,1)S(1)} %get-tuple-element.168), channel_id=1, source_target_pairs={{0,8},{1,9},{2,10},{3,11},{4,12},{5,13},{6,14},{7,15},{8,0},{9,1},... | collective-permute-start | bytes 497672 | tf_op jit(solution)/shard_map/ppermute | solution.py:506
  123.8 7.3 %collective-permute-start.41 = (bf16[2,80,256]{2,1,0:T(8,128)(2,1)S(1)}, bf16[2,80,256]{2,1,0:T(8,128)(2,1)S(1)}, u32[]{:S(2)}, u32[]{:S(2)}) collective-permute-start(bf16[2,80,256]{2,1,0:T(8,128)(2,1)S(1)} %get-tuple-element.176), channel_id=1, source_target_pairs={{0,8},{1,9},{2,10},{3,11},{4,12},{5,13},{6,14},{7,15},{8,0},{9,1},... | collective-permute-start | bytes 245768 | tf_op jit(solution)/shard_map/ppermute | solution.py:506
  127.5 10.0 %collective-permute-start.45 = (bf16[2,72,384]{2,1,0:T(8,128)(2,1)S(1)}, bf16[2,72,384]{2,1,0:T(8,128)(2,1)S(1)}, u32[]{:S(2)}, u32[]{:S(2)}) collective-permute-start(bf16[2,72,384]{2,1,0:T(8,128)(2,1)S(1)} %fusion.17), channel_id=1, source_target_pairs={{0,2},{1,3},{2,0},{3,1},{4,6},{5,7},{6,4},{7,5},{8,10},{9,11},{10,... | collective-permute-start | bytes 331784 | tf_op jit(solution)/shard_map/ppermute | solution.py:506
  131.5 9.6 %collective-permute-start.44 = (bf16[2,72,384]{2,1,0:T(8,128)(2,1)S(1)}, bf16[2,72,384]{2,1,0:T(8,128)(2,1)S(1)}, u32[]{:S(2)}, u32[]{:S(2)}) collective-permute-start(bf16[2,72,384]{2,1,0:T(8,128)(2,1)S(1)} %add_convert_fusion.11.a_near), channel_id=1, source_target_pairs={{0,1},{1,0},{2,3},{3,2},{4,5},{5,4},{6,7},{7,6},{8,9},{9,8},{10,11... | collective-permute-start | bytes 331784 | tf_op jit(solution)/shard_map/ppermute | solution.py:506
  (55 other events, 238.9 us)
